TPU v7x, 32 devices: a whole 2x2x4 slice. The times are simulated.
32 devices in a mesh: dp: 4 (over y, x), mp: 8 (over z, core).
Axes of the slice: x: 2, y: 2, z: 4, core: 2. Of those that a mesh axis runs over, the one named last changes fastest.
Arguments:
- token_ids: int32 [8192], P('dp'), may hold values from 0 to 50256
- targets: int32 [8192], P('dp'), may hold values from 0 to 50256
- starts: int32 [8192], P('dp'), may hold values from 0 to 1023, as said below
- sources: int32 [8192], P('dp'), may hold values from 0 to 3, as said below
- embedding: float32 [50304, 1024], P('mp', 'dp')
- w_qkv: float32 [1024, 3072], P('dp', 'mp'), may hold values from -0.1875 to 0.1875
- w_out: float32 [1024, 1024], P('mp', 'dp'), may hold values from -0.5 to 0.5
- w_fc: float32 [1024, 4096], P('dp', 'mp'), may hold values from -0.1875 to 0.1875
- w_proj: float32 [4096, 1024], P('mp', 'dp'), may hold values from -0.09375 to 0.09375
- norm_params: float32 [6, 1024], replicated
- rows_table: float32 [50304], P('mp'), may hold values from 1.4901161e-09 to 5.9604646e-09
- cols_table: float32 [1024], P('dp'), may hold values from 1.4901161e-09 to 5.9604646e-09
- rows_qkv: float32 [1024], P('dp'), may hold values from 4.7683717e-08 to 1.9073487e-07
- cols_qkv: float32 [3072], P('mp'), may hold values from 4.7683717e-08 to 1.9073487e-07
- rows_out: float32 [1024], P('mp'), may hold values from 4.7683717e-08 to 1.9073487e-07
- cols_out: float32 [1024], P('dp'), may hold values from 4.7683717e-08 to 1.9073487e-07
- rows_fc: float32 [1024], P('dp'), may hold values from 4.7683717e-08 to 1.9073487e-07
- cols_fc: float32 [4096], P('mp'), may hold values from 4.7683717e-08 to 1.9073487e-07
- rows_proj: float32 [4096], P('mp'), may hold values from 4.7683717e-08 to 1.9073487e-07
- cols_proj: float32 [1024], P('dp'), may hold values from 4.7683717e-08 to 1.9073487e-07
- second_norms: float32 [6, 1024], replicated, may hold values from 4.7683717e-08 to 1.9073487e-07
Outputs:
- loss_sums: float32 [4], replicated
- counts: float32 [4], replicated
- grad_table: float32 [50304, 1024], P('mp', 'dp')
- rows_table_new: float32 [50304], P('mp')
- cols_table_new: float32 [1024], P('dp')
- table_new: float32 [50304, 1024], P('mp', 'dp')
- grad_qkv: float32 [1024, 3072], P('dp', 'mp')
- rows_qkv_new: float32 [1024], P('dp')
- cols_qkv_new: float32 [3072], P('mp')
- qkv_new: float32 [1024, 3072], P('dp', 'mp')
- grad_out: float32 [1024, 1024], P('mp', 'dp')
- rows_out_new: float32 [1024], P('mp')
- cols_out_new: float32 [1024], P('dp')
- out_new: float32 [1024, 1024], P('mp', 'dp')
- grad_fc: float32 [1024, 4096], P('dp', 'mp')
- rows_fc_new: float32 [1024], P('dp')
- cols_fc_new: float32 [4096], P('mp')
- fc_new: float32 [1024, 4096], P('dp', 'mp')
- grad_proj: float32 [4096, 1024], P('mp', 'dp')
- rows_proj_new: float32 [4096], P('mp')
- cols_proj_new: float32 [1024], P('dp')
- proj_new: float32 [4096, 1024], P('mp', 'dp')
- grad_norms: float32 [6, 1024], replicated
- second_norms_new: float32 [6, 1024], replicated
- norms_new: float32 [6, 1024], replicated
Inputs may be any that keep to these rules, and one draw needn't show every extreme that they name: starts[t] is the position within its sequence of 1024 tokens of the first token of t's document: at most t's own position, never falling along a sequence, and 0 at the first token of every sequence. One of the sources 1 to 2, which one drawn from the seed, has no token in the step.
All inputs are finite; a program needn't handle non-finite values.
Results may differ from a plain program's by a relative error of at most 0.015.
Values may be sent and summed in bfloat16 or wider, within the bound.
A program may use at most 256 MiB of HBM per device.

v0:
```python
import jax
import jax.numpy as jnp
from jax import lax
from jax.sharding import PartitionSpec as P

HD = 64
VREAL = 50257
LEN = 1024
NSRC = 4
STEP = 10


EPS_NORM = 1e-05
EPS_ONE = 1e-30
CLIP = 1.0
RHO = 0.5
MASKED = -1e30


def layer_norm(values, gain, shift):
    centre = jnp.mean(values, axis=-1, keepdims=True)
    centred = values - centre
    spread = jnp.mean(centred * centred, axis=-1, keepdims=True)
    return centred * lax.rsqrt(spread + EPS_NORM) * gain + shift


def row_slice(values, start, count):
    return lax.dynamic_slice_in_dim(values, start, count, 0)


def own_rows(values):
    share = values.shape[0] // lax.axis_size("mp")
    return row_slice(values, lax.axis_index("mp") * share, share)


def sum_branch(term, tokens):
    return lax.psum(term(0, tokens).astype(jnp.bfloat16), "mp").astype(jnp.float32)


def sum_grads(term, tokens):
    return lax.psum(term(0, tokens).astype(jnp.bfloat16), "mp").astype(jnp.float32)


def norm_back(values, gain, upstream):
    centre = jnp.mean(values, axis=-1, keepdims=True)
    centred = values - centre
    scale = lax.rsqrt(jnp.mean(centred * centred, axis=-1, keepdims=True) + EPS_NORM)
    normed = centred * scale
    weighted = upstream * gain
    dvalues = scale * (
        weighted
        - jnp.mean(weighted, axis=-1, keepdims=True)
        - normed * jnp.mean(weighted * normed, axis=-1, keepdims=True)
    )
    dgain = jnp.sum(own_rows(upstream * normed), axis=0)
    dshift = jnp.sum(own_rows(upstream), axis=0)
    return (dvalues, dgain, dshift)


def gelu_tanh(values):
    return jax.nn.gelu(values, approximate=True)


def score_block(mixed_seq, start_seq):
    place = jnp.arange(mixed_seq.shape[0], dtype=jnp.int32)
    allowed = (place[None, :] <= place[:, None]) & (place[None, :] >= start_seq[:, None])
    raw = jnp.einsum(
        "qhe,khe->hqk", mixed_seq[:, :, 0], mixed_seq[:, :, 1], preferred_element_type=jnp.float32
    )
    return jnp.where(allowed[None], raw * HD ** (-0.5), MASKED)


def attend_forward(mixed_seq, start_seq):
    scores = score_block(mixed_seq, start_seq)
    highest = jnp.max(scores, axis=-1, keepdims=True)
    weights = jnp.exp(scores - highest)
    totals = jnp.sum(weights, axis=-1, keepdims=True)
    probs = (weights / totals).astype(jnp.bfloat16)
    result = jnp.einsum(
        "hqk,khe->qhe", probs, mixed_seq[:, :, 2], preferred_element_type=jnp.float32
    )
    return (result.astype(jnp.bfloat16), highest[:, :, 0] + jnp.log(totals[:, :, 0]))


def attend_backward(mixed_seq, start_seq, log_rows, upstream):
    scores = score_block(mixed_seq, start_seq)
    probs = jnp.exp(scores - log_rows[:, :, None])
    dprobs = jnp.einsum(
        "qhe,khe->hqk", upstream, mixed_seq[:, :, 2], preferred_element_type=jnp.float32
    )
    dvalues = jnp.einsum(
        "hqk,qhe->khe", probs.astype(jnp.bfloat16), upstream, preferred_element_type=jnp.float32
    )
    inner = jnp.sum(probs * dprobs, axis=-1, keepdims=True)
    dscores = (probs * (dprobs - inner)).astype(jnp.bfloat16)
    dquery = jnp.einsum(
        "hqk,khe->qhe", dscores, mixed_seq[:, :, 1], preferred_element_type=jnp.float32
    ) * HD ** (-0.5)
    dkeys = jnp.einsum(
        "hqk,qhe->khe", dscores, mixed_seq[:, :, 0], preferred_element_type=jnp.float32
    ) * HD ** (-0.5)
    return jnp.stack([dquery, dkeys, dvalues], axis=2).astype(jnp.bfloat16)


def layer_forward(stream0, norm_params, wide_qkv, wide_out, wide_fc, wide_proj, starts):
    tokens = starts.shape[0]
    heads = wide_qkv.shape[1] // (3 * HD)
    inner_one = layer_norm(stream0, norm_params[0], norm_params[1]).astype(jnp.bfloat16)
    mixed = jnp.dot(inner_one, wide_qkv, preferred_element_type=jnp.float32).astype(jnp.bfloat16)
    mixed = mixed.reshape(tokens // LEN, LEN, heads, 3, HD)
    start_seqs = starts.reshape(tokens // LEN, LEN)
    attended, log_sums = lax.map(
        lambda paired: attend_forward(paired[0], paired[1]), (mixed, start_seqs)
    )
    attended = attended.reshape(tokens, heads * HD)

    def attn_term(start, count):
        return jnp.dot(
            row_slice(attended, start, count), wide_out, preferred_element_type=jnp.float32
        )

    stream1 = stream0 + sum_branch(attn_term, tokens)
    inner_two = layer_norm(stream1, norm_params[2], norm_params[3]).astype(jnp.bfloat16)
    before = jnp.dot(inner_two, wide_fc, preferred_element_type=jnp.float32)
    hidden = gelu_tanh(before).astype(jnp.bfloat16)

    def mlp_term(start, count):
        return jnp.dot(
            row_slice(hidden, start, count), wide_proj, preferred_element_type=jnp.float32
        )

    stream2 = stream1 + sum_branch(mlp_term, tokens)
    kept = (
        stream0,
        inner_one,
        mixed,
        start_seqs,
        log_sums,
        attended,
        stream1,
        inner_two,
        before,
        hidden,
    )
    return (stream2, kept)


def layer_backward(dstream2, kept, norm_params, wide_qkv, wide_out, wide_fc, wide_proj):
    (
        stream0,
        inner_one,
        mixed,
        start_seqs,
        log_sums,
        attended,
        stream1,
        inner_two,
        before,
        hidden,
    ) = kept
    tokens = inner_one.shape[0]
    heads = attended.shape[1] // HD
    dbranch = dstream2.astype(jnp.bfloat16)
    grad_proj = jnp.einsum("tf,td->fd", hidden, dbranch, preferred_element_type=jnp.float32)
    dhidden = jnp.einsum("td,fd->tf", dbranch, wide_proj, preferred_element_type=jnp.float32)
    unused, gelu_pull = jax.vjp(gelu_tanh, before)
    dbefore = gelu_pull(dhidden)[0].astype(jnp.bfloat16)
    grad_fc = jnp.einsum("td,tf->df", inner_two, dbefore, preferred_element_type=jnp.float32)

    def fc_term(start, count):
        return jnp.einsum(
            "tf,df->td",
            row_slice(dbefore, start, count),
            wide_fc,
            preferred_element_type=jnp.float32,
        )

    dinner_two = sum_grads(fc_term, tokens)
    dnorm_two, dgain_two, dshift_two = norm_back(stream1, norm_params[2], dinner_two)
    dstream1 = dstream2 + dnorm_two
    dbranch = dstream1.astype(jnp.bfloat16)
    grad_out = jnp.einsum("tf,td->fd", attended, dbranch, preferred_element_type=jnp.float32)
    dattended = jnp.einsum(
        "td,fd->tf", dbranch, wide_out, preferred_element_type=jnp.float32
    ).astype(jnp.bfloat16)
    dattended = dattended.reshape(tokens // LEN, LEN, heads, HD)
    dmixed = lax.map(
        lambda paired: attend_backward(paired[0], paired[1], paired[2], paired[3]),
        (mixed, start_seqs, log_sums, dattended),
    )
    dmixed = dmixed.reshape(tokens, heads * 3 * HD)
    grad_qkv = jnp.einsum("td,tc->dc", inner_one, dmixed, preferred_element_type=jnp.float32)

    def qkv_term(start, count):
        return jnp.einsum(
            "tc,dc->td",
            row_slice(dmixed, start, count),
            wide_qkv,
            preferred_element_type=jnp.float32,
        )

    dinner_one = sum_grads(qkv_term, tokens)
    dnorm_one, dgain_one, dshift_one = norm_back(stream0, norm_params[0], dinner_one)
    dstream0 = dstream1 + dnorm_one
    return (
        dstream0,
        (grad_qkv, grad_out, grad_fc, grad_proj),
        (dgain_one, dshift_one, dgain_two, dshift_two),
    )


def local(
    token_ids,
    targets,
    starts,
    sources,
    embedding,
    w_qkv,
    w_out,
    w_fc,
    w_proj,
    norm_params,
    rows_table,
    cols_table,
    rows_qkv,
    cols_qkv,
    rows_out,
    cols_out,
    rows_fc,
    cols_fc,
    rows_proj,
    cols_proj,
    second_norms,
):
    gathered_table, wide_qkv, wide_out, wide_fc, wide_proj = (
        lax.all_gather(embedding.astype(jnp.bfloat16), "dp", axis=1, tiled=True),
        lax.all_gather(w_qkv.astype(jnp.bfloat16), "dp", axis=0, tiled=True),
        lax.all_gather(w_out.astype(jnp.bfloat16), "dp", axis=1, tiled=True),
        lax.all_gather(w_fc.astype(jnp.bfloat16), "dp", axis=0, tiled=True),
        lax.all_gather(w_proj.astype(jnp.bfloat16), "dp", axis=1, tiled=True),
    )
    tokens = token_ids.shape[0]
    width = gathered_table.shape[1]
    vocab_rows = gathered_table.shape[0]
    first_row = lax.axis_index("mp") * vocab_rows
    local_ids = token_ids - first_row
    inside = (local_ids >= 0) & (local_ids < vocab_rows)
    safe_ids = jnp.clip(local_ids, 0, vocab_rows - 1)

    def lookup_term(start, count):
        picked_ids = row_slice(safe_ids, start, count)
        picked_inside = row_slice(inside, start, count)
        return jnp.where(
            picked_inside[:, None], gathered_table[picked_ids].astype(jnp.float32), 0.0
        )

    stream0 = sum_branch(lookup_term, tokens)
    stream2, kept = layer_forward(
        stream0, norm_params, wide_qkv, wide_out, wide_fc, wide_proj, starts
    )
    final = layer_norm(stream2, norm_params[4], norm_params[5]).astype(jnp.bfloat16)
    block = min(512, tokens)
    blocks = tokens // block
    column_ids = jnp.arange(vocab_rows, dtype=jnp.int32)
    valid = column_ids + first_row < VREAL
    final_blocks = final.reshape(blocks, block, width)
    wanted_blocks = (targets - first_row).reshape(blocks, block)

    def logits_of(rows):
        logits = jnp.einsum("bd,vd->bv", rows, gathered_table, preferred_element_type=jnp.float32)
        return jnp.where(valid[None, :], logits, MASKED)

    def head_stats(paired):
        logits = logits_of(paired[0])
        highest = jnp.max(logits, axis=1)
        exp_sums = jnp.sum(jnp.exp(logits - highest[:, None]), axis=1)
        picked = jnp.sum(jnp.where(column_ids[None, :] == paired[1][:, None], logits, 0.0), axis=1)
        return (highest, exp_sums, picked)

    highest, exp_sums, picked = lax.map(head_stats, (final_blocks, wanted_blocks))
    highest = highest.reshape(tokens)
    exp_sums = exp_sums.reshape(tokens)
    picked = picked.reshape(tokens)
    overall = lax.pmax(highest, "mp")
    exp_sums, picked = lax.psum((exp_sums * jnp.exp(highest - overall), picked), "mp")
    highest = overall
    log_total = highest + jnp.log(exp_sums)
    token_loss = log_total - picked
    member = (sources[:, None] == jnp.arange(NSRC, dtype=jnp.int32)[None, :]).astype(jnp.float32)
    loss_sums, counts = lax.psum(
        (jnp.sum(member * token_loss[:, None], axis=0), jnp.sum(member, axis=0)), "dp"
    )
    token_weight = jnp.sum(member / (NSRC * jnp.maximum(counts, 1.0))[None, :], axis=1)

    def head_back(table_grad, paired):
        rows, wanted, log_rows, weight_rows = paired
        logits = logits_of(rows)
        probs = jnp.exp(logits - log_rows[:, None])
        chosen = (column_ids[None, :] == wanted[:, None]).astype(jnp.float32)
        dlogits = ((probs - chosen) * weight_rows[:, None]).astype(jnp.bfloat16)
        table_grad = table_grad + jnp.einsum(
            "bv,bd->vd", dlogits, rows, preferred_element_type=jnp.float32
        )
        return (table_grad, jnp.dot(dlogits, gathered_table, preferred_element_type=jnp.float32))

    table_grad, dfinal = lax.scan(
        head_back,
        jnp.zeros((vocab_rows, width), jnp.float32),
        (
            final_blocks,
            wanted_blocks,
            log_total.reshape(blocks, block),
            token_weight.reshape(blocks, block),
        ),
    )
    dfinal = dfinal.reshape(tokens, width)

    def final_term(start, count):
        return row_slice(dfinal, start, count)

    dfinal_rows = sum_grads(final_term, tokens)
    dstream2, dgain_final, dshift_final = norm_back(stream2, norm_params[4], dfinal_rows)
    dstream0, layer_grads, norm_grads = layer_backward(
        dstream2, kept, norm_params, wide_qkv, wide_out, wide_fc, wide_proj
    )
    table_grad = table_grad + jax.ops.segment_sum(
        jnp.where(inside[:, None], dstream0, 0.0), safe_ids, num_segments=vocab_rows
    )
    norm_partial = jnp.stack(
        [norm_grads[0], norm_grads[1], norm_grads[2], norm_grads[3], dgain_final, dshift_final]
    )
    grad_table, grad_qkv, grad_out, grad_fc, grad_proj = (
        lax.psum_scatter(
            table_grad.astype(jnp.bfloat16), "dp", scatter_dimension=1, tiled=True
        ).astype(jnp.float32),
        lax.psum_scatter(
            layer_grads[0].astype(jnp.bfloat16), "dp", scatter_dimension=0, tiled=True
        ).astype(jnp.float32),
        lax.psum_scatter(
            layer_grads[1].astype(jnp.bfloat16), "dp", scatter_dimension=1, tiled=True
        ).astype(jnp.float32),
        lax.psum_scatter(
            layer_grads[2].astype(jnp.bfloat16), "dp", scatter_dimension=0, tiled=True
        ).astype(jnp.float32),
        lax.psum_scatter(
            layer_grads[3].astype(jnp.bfloat16), "dp", scatter_dimension=1, tiled=True
        ).astype(jnp.float32),
    )
    beta = 1.0 - STEP ** (-0.8)
    size_mp = lax.axis_size("mp")
    size_dp = lax.axis_size("dp")
    weights = (embedding, w_qkv, w_out, w_fc, w_proj)
    grads = (grad_table, grad_qkv, grad_out, grad_fc, grad_proj)
    rows_old = (rows_table, rows_qkv, rows_out, rows_fc, rows_proj)
    cols_old = (cols_table, cols_qkv, cols_out, cols_fc, cols_proj)
    row_span = (size_mp, size_dp, size_mp, size_dp, size_mp)
    col_span = (size_dp, size_mp, size_dp, size_mp, size_dp)
    squares = [gradient * gradient + EPS_ONE for gradient in grads]
    row_parts = [jnp.sum(square, axis=1) for square in squares]
    col_parts = [jnp.sum(square, axis=0) for square in squares]
    over_mp = lax.psum((row_parts[1], row_parts[3], col_parts[0], col_parts[2], col_parts[4]), "mp")
    over_dp = lax.psum((col_parts[1], col_parts[3], row_parts[0], row_parts[2], row_parts[4]), "dp")
    row_full = (over_dp[2], over_mp[0], over_dp[3], over_mp[1], over_dp[4])
    col_full = (over_mp[2], over_dp[0], over_mp[3], over_dp[1], over_mp[4])
    rows_new = []
    cols_new = []
    row_share = []
    weight_sq = []
    full_rows = []
    full_cols = []
    for index in range(5):
        full_rows.append(grads[index].shape[0] * row_span[index])
        full_cols.append(grads[index].shape[1] * col_span[index])
        rows_next = beta * rows_old[index] + (1.0 - beta) * row_full[index] / full_cols[index]
        cols_next = beta * cols_old[index] + (1.0 - beta) * col_full[index] / full_rows[index]
        rows_new.append(rows_next)
        cols_new.append(cols_next)
        row_share.append(jnp.sum(rows_next) / col_span[index])
        weight_sq.append(jnp.sum(weights[index] * weights[index]))
    summed, grad_norms = lax.psum((jnp.stack(row_share + weight_sq), norm_partial), ("dp", "mp"))
    steps = [
        grads[index]
        * lax.rsqrt(
            rows_new[index][:, None] * cols_new[index][None, :] * full_rows[index] / summed[index]
        )
        for index in range(5)
    ]
    step_sq = lax.psum(jnp.stack([jnp.sum(piece * piece) for piece in steps]), ("dp", "mp"))
    updated = []
    for index in range(5):
        entries = full_rows[index] * full_cols[index]
        clipped = steps[index] / jnp.maximum(1.0, jnp.sqrt(step_sq[index] / entries) / CLIP)
        rate = RHO * jnp.sqrt(summed[5 + index] / entries)
        updated.append(weights[index] - rate * clipped)
    second_new = beta * second_norms + (1.0 - beta) * (grad_norms * grad_norms + EPS_ONE)
    norm_steps = grad_norms * lax.rsqrt(second_new)
    norm_steps = norm_steps / jnp.maximum(1.0, jnp.sqrt(jnp.mean(norm_steps * norm_steps)) / CLIP)
    norms_new = norm_params - RHO * jnp.sqrt(jnp.mean(norm_params * norm_params)) * norm_steps
    return (
        loss_sums,
        counts,
        grad_table,
        rows_new[0],
        cols_new[0],
        updated[0],
        grad_qkv,
        rows_new[1],
        cols_new[1],
        updated[1],
        grad_out,
        rows_new[2],
        cols_new[2],
        updated[2],
        grad_fc,
        rows_new[3],
        cols_new[3],
        updated[3],
        grad_proj,
        rows_new[4],
        cols_new[4],
        updated[4],
        grad_norms,
        second_new,
        norms_new,
    )


def solution(mesh):
    placed = (
        P("dp"),
        P("dp"),
        P("dp"),
        P("dp"),
        P("mp", "dp"),
        P("dp", "mp"),
        P("mp", "dp"),
        P("dp", "mp"),
        P("mp", "dp"),
        P(),
        P("mp"),
        P("dp"),
        P("dp"),
        P("mp"),
        P("mp"),
        P("dp"),
        P("dp"),
        P("mp"),
        P("mp"),
        P("dp"),
        P(),
    )
    return jax.shard_map(
        local,
        mesh=mesh,
        in_specs=placed,
        out_specs=(
            P(),
            P(),
            P("mp", "dp"),
            P("mp"),
            P("dp"),
            P("mp", "dp"),
            P("dp", "mp"),
            P("dp"),
            P("mp"),
            P("dp", "mp"),
            P("mp", "dp"),
            P("mp"),
            P("dp"),
            P("mp", "dp"),
            P("dp", "mp"),
            P("dp"),
            P("mp"),
            P("dp", "mp"),
            P("mp", "dp"),
            P("mp"),
            P("dp"),
            P("mp", "dp"),
            P(),
            P(),
            P(),
        ),
        check_vma=False,
    )
```

profile of v0, /device:TPU:0, one launch (start us, length us, event | category | flops | bytes accessed | tf_op | source)
XLA Modules:
  0.0 1641.4 jit_solution(5035195346405216117)
XLA Ops:
  7.3 8.8 multiply_reduce_fusion.10
  16.8 127.0 %all-gather.4.cloned.1.call-done = bf16[6288,1024]{1,0:T(8,128)(2,1)} async-done(((bf16[6288,256]{1,0:T(8,128)(2,1)}), bf16[6288,1024]{1,0:T(8,128)(2,1)}) %all-gather.4.cloned.1.call-update) | async-done | bytes 12877840 | tf_op jit(solution)/shard_map/all_gather | solution.py:236
  143.8 17.2 %gather_fusion = bf16[2048,1024]{1,0:T(8,128)(2,1)} fusion(bf16[6288,1024]{1,0:T(8,128)(2,1)} %all-gather.4.cloned.1.call-done, s32[2048]{0:T(1024)S(1)} %get-tuple-element.401), kind=kCustom, calls=%fused_computation | custom fusion | bytes 8396800 | tf_op jit(solution)/shard_map/gather | solution.py:254
  165.9 10.0 all_gather.17
  176.6 10.6 all_gather.16
  187.3 74.6 %all-reduce.11.cloned.1.call-done = bf16[2048,1024]{1,0:T(8,128)(2,1)} async-done(((bf16[2048,1024]{1,0:T(8,128)(2,1)}), bf16[2048,1024]{1,0:T(8,128)(2,1)}) %all-reduce.11.cloned.1.call-update) | async-done | bytes 4194320 | tf_op jit(solution)/shard_map/psum | solution.py:37
  273.6 16.5 %while.50 = (s32[]{:T(128)}, bf16[2,1024,2,64]{1,3,2,0:T(8,128)(2,1)}, f32[2,2,1024]{2,1,0:T(2,128)S(1)}, bf16[2,1024,2,3,64]{1,4,2,3,0:T(8,128)(2,1)S(1)}, s32[2,1024]{1,0:T(2,128)S(1)}, /*index=5*/s32[]{:T(128)}) while((s32[]{:T(128)}, bf16[2,1024,2,64]{1,3,2,0:T(8,128)(2,1)}, f32[2,2,1024]{2,1,0:T(2,128)S(1)}, ...), condition=%wide.region_6.7_spmd, body=%wide.region_3.6_spmd.sunk | while | flops 565311488 | bytes 36253836 | solution.py:112
  299.6 93.5 %all-reduce.13.cloned.1.call-done = bf16[2048,1024]{1,0:T(8,128)(2,1)} async-done(((bf16[2048,1024]{1,0:T(8,128)(2,1)}), bf16[2048,1024]{1,0:T(8,128)(2,1)}) %all-reduce.13.cloned.1.call-update) | async-done | bytes 4194320 | tf_op jit(solution)/shard_map/psum | solution.py:37
  393.1 4.8 fusion.61
  405.5 16.6 %all-gather.6.cloned.1.call-done = bf16[1024,512]{1,0:T(8,128)(2,1)} async-done(((bf16[256,512]{1,0:T(8,128)(2,1)}), bf16[1024,512]{1,0:T(8,128)(2,1)}) %all-gather.6.cloned.1.call-update) | async-done | bytes 1048592 | tf_op jit(solution)/shard_map/all_gather | solution.py:239
  422.1 8.0 fusion.91
  430.1 20.8 %all-gather.8.cloned.1.call-done = bf16[512,1024]{1,0:T(8,128)(2,1)} async-done(((bf16[512,256]{1,0:T(8,128)(2,1)}), bf16[512,1024]{1,0:T(8,128)(2,1)}) %all-gather.8.cloned.1.call-update) | async-done | bytes 1048592 | tf_op jit(solution)/shard_map/all_gather | solution.py:240
  450.9 7.3 convolution_convert_fusion.2
  458.3 9.4 psum.167
  467.8 87.0 %all-reduce.15.cloned.1.call-done = bf16[2048,1024]{1,0:T(8,128)(2,1)} async-done(((bf16[2048,1024]{1,0:T(8,128)(2,1)}), bf16[2048,1024]{1,0:T(8,128)(2,1)}) %all-reduce.15.cloned.1.call-update) | async-done | bytes 4194320 | tf_op jit(solution)/shard_map/psum | solution.py:37
  554.8 6.5 fusion.75
  565.5 5.8 add_convert_fusion
  571.3 59.6 %while.52 = (s32[]{:T(128)}, f32[4,512]{1,0:T(4,128)S(1)}, f32[4,512]{1,0:T(4,128)S(1)}, f32[4,512]{1,0:T(4,128)S(1)}, bf16[4,512,1024]{2,1,0:T(8,128)(2,1)}, /*...) while((s32[]{:T(128)}, f32[4,512]{1,0:T(4,128)S(1)}, ...), condition=%wide.region_17.18_spmd.clone, body=%wide.region_13.17_spmd.clone.sunk | while | flops 6615993344 | bytes 39721880 | solution.py:280
  571.4 11.1 fusion.174
  586.3 11.1 fusion.174
  601.2 11.1 fusion.174
  616.0 11.1 fusion.174
  630.9 15.8 pmax.7
  646.8 26.1 %all-reduce.2 = (f32[2048]{0:T(1024)S(1)}, f32[2048]{0:T(1024)S(1)}) all-reduce(f32[2048]{0:T(1024)S(1)} %exponential_multiply_fusion, f32[2048]{0:T(1024)S(1)} %bitcast.271), channel_id=1, replica_groups=mesh['dp'=4,'mp'=8] {'mp'}, use_global_device_ids=true, to_apply=%region_19.20 | all-reduce | flops 4096 | bytes 32768 | tf_op jit(solution)/shard_map/psum | solution.py:285
  673.6 182.8 %while.53 = (s32[]{:T(128)}, f32[6288,1024]{1,0:T(8,128)}, bf16[4,512,1024]{2,1,0:T(8,128)(2,1)}, bf16[4,512,1024]{2,1,0:T(8,128)(2,1)}, bf16[6288,1024]{1,0:T(8...) while((s32[]{:T(128)}, f32[6288,1024]{1,0:T(8,128)}, ...), condition=%wide.region_27.28_spmd.clone, body=%wide.region_26.27_spmd.clone.sunk | while | flops 19815763968 | bytes 100810656 | solution.py:306
  673.6 15.2 multiply_convert_fusion.8
  688.8 14.2 select_add_fusion.2
  703.0 12.7 bitcast_dynamic-update-slice_fusion.5
  715.7 15.2 multiply_convert_fusion.8
  730.9 18.9 %select_add_fusion.2 = f32[6288,1024]{1,0:T(8,128)} fusion(f32[6288,1024]{1,0:T(8,128)} %get-tuple-element.697, bf16[512,6288]{0,1:T(8,128)(2,1)} %multiply_convert_fusion.8, pred[]{:T(512)S(6)} %compare.3, bf16[4,512,1024]{2,1,0:T(8,128)(2,1)} %get-tuple-element.710, s32[]{:T(128)} %get-tuple-element.696), kind=kOutput, calls=%fused_computation.70.clone.1 | convolution fusion | flops 6606323712 | bytes 58999296 | tf_op jit(solution)/shard_map/while/body/eval_jaxpr/bv,bd->vd/dot_general | solution.py:301
  749.9 12.7 bitcast_dynamic-update-slice_fusion.5
  762.6 15.2 multiply_convert_fusion.8
  777.8 18.9 %select_add_fusion.2 = f32[6288,1024]{1,0:T(8,128)} fusion(f32[6288,1024]{1,0:T(8,128)} %get-tuple-element.697, bf16[512,6288]{0,1:T(8,128)(2,1)} %multiply_convert_fusion.8, pred[]{:T(512)S(6)} %compare.3, bf16[4,512,1024]{2,1,0:T(8,128)(2,1)} %get-tuple-element.710, s32[]{:T(128)} %get-tuple-element.696), kind=kOutput, calls=%fused_computation.70.clone.1 | convolution fusion | flops 6606323712 | bytes 58999296 | tf_op jit(solution)/shard_map/while/body/eval_jaxpr/bv,bd->vd/dot_general | solution.py:301
  796.8 12.7 bitcast_dynamic-update-slice_fusion.5
  809.5 15.2 multiply_convert_fusion.8
  824.7 18.9 %select_add_fusion.2 = f32[6288,1024]{1,0:T(8,128)} fusion(f32[6288,1024]{1,0:T(8,128)} %get-tuple-element.697, bf16[512,6288]{0,1:T(8,128)(2,1)} %multiply_convert_fusion.8, pred[]{:T(512)S(6)} %compare.3, bf16[4,512,1024]{2,1,0:T(8,128)(2,1)} %get-tuple-element.710, s32[]{:T(128)} %get-tuple-element.696), kind=kOutput, calls=%fused_computation.70.clone.1 | convolution fusion | flops 6606323712 | bytes 58999296 | tf_op jit(solution)/shard_map/while/body/eval_jaxpr/bv,bd->vd/dot_general | solution.py:301
  843.7 12.7 bitcast_dynamic-update-slice_fusion.5
  856.6 94.6 %all-reduce.17.cloned.1.call-done = bf16[2048,1024]{1,0:T(8,128)(2,1)} async-done(((bf16[2048,1024]{1,0:T(8,128)(2,1)}), bf16[2048,1024]{1,0:T(8,128)(2,1)}) %all-reduce.17.cloned.1.call-update) | async-done | bytes 4194320 | tf_op jit(solution)/shard_map/psum | solution.py:41
  951.2 6.4 multiply_reduce_fusion.8
  958.3 7.6 fusion.70
  965.9 4.4 convolution_convert_fusion.1
  970.4 96.6 %all-reduce.19.cloned.1.call-done = bf16[2048,1024]{1,0:T(8,128)(2,1)} async-done(((bf16[2048,1024]{1,0:T(8,128)(2,1)}), bf16[2048,1024]{1,0:T(8,128)(2,1)}) %all-reduce.19.cloned.1.call-update) | async-done | bytes 4194320 | tf_op jit(solution)/shard_map/psum | solution.py:41
  1067.1 6.4 multiply_reduce_fusion.7
  1074.2 8.6 multiply_add_fusion
  1088.5 27.3 %while.51 = (s32[]{:T(128)}, bf16[2,1024,2,3,64]{1,4,2,3,0:T(8,128)(2,1)}, bf16[2,1024,2,3,64]{1,4,2,3,0:T(8,128)(2,1)S(1)}, s32[2,1024]{1,0:T(2,128)S(1)}, f32[...) while((s32[]{:T(128)}, bf16[2,1024,2,3,64]{1,4,2,3,0:T(8,128)(2,1)}, ...), condition=%wide.region_36.37_spmd, body=%wide.region_34.36_spmd.sunk | while | flops 1379792896 | bytes 72946272 | solution.py:187
  1119.3 4.4 convolution_convert_fusion
  1123.8 9.3 fusion.85
  1133.2 7.5 convolution_convert_fusion.6
  1140.8 4.9 fusion.88
  1146.0 6.1 convolution_convert_fusion.7
  1152.2 68.3 %all-reduce.21.cloned.1.call-done = bf16[2048,1024]{1,0:T(8,128)(2,1)} async-done(((bf16[2048,1024]{1,0:T(8,128)(2,1)}), bf16[2048,1024]{1,0:T(8,128)(2,1)}) %all-reduce.21.cloned.1.call-update) | async-done | bytes 4194320 | tf_op jit(solution)/shard_map/psum | solution.py:41
  1220.5 6.9 multiply_reduce_fusion.6
  1227.4 39.8 %scatter_custom_fusion = f32[6288,1024]{1,0:T(8,128)} fusion(f32[6288,1024]{1,0:T(8,128)} %get-tuple-element.191, s32[2048]{0:T(1024)} %get-tuple-element.402, f32[2048,1024]{1,0:T(8,128)} %copy-done.5, f32[2048]{0:T(1024)S(1)} %broadcast_multiply_fusion, f32[2048]{0:T(1024)S(1)} %copy-done.49, f32[]{:T(128)} %constant.213.clone.1, ...), kind=kCustom, calls=%fused_computation.90 | custom fusion | flops 25165824 | bytes 42572288 | tf_op jit(solution)/shard_map/scatter-add | solution.py:326
  1267.3 13.7 convert_element_type.175
  1292.8 17.0 %reduce-scatter.10.cloned.1.call-done = bf16[128,256]{1,0:T(8,128)(2,1)} async-done(((bf16[128,1024]{1,0:T(8,128)(2,1)}), bf16[128,256]{1,0:T(8,128)(2,1)}) %reduce-scatter.10.cloned.1.call-update) | async-done | bytes 65552 | tf_op jit(solution)/shard_map/reduce_scatter | solution.py:339
  1310.8 28.3 %reduce-scatter.8.cloned.1.call-done = bf16[256,384]{1,0:T(8,128)(2,1)} async-done(((bf16[1024,384]{1,0:T(8,128)(2,1)}), bf16[256,384]{1,0:T(8,128)(2,1)}) %reduce-scatter.8.cloned.1.call-update) | async-done | bytes 196624 | tf_op jit(solution)/shard_map/reduce_scatter | solution.py:336
  1345.2 121.1 %reduce-scatter.6.cloned.1.call-done = bf16[6288,256]{1,0:T(8,128)(2,1)} async-done(((bf16[6288,1024]{1,0:T(8,128)(2,1)}), bf16[6288,256]{1,0:T(8,128)(2,1)}) %reduce-scatter.6.cloned.1.call-update) | async-done | bytes 3219472 | tf_op jit(solution)/shard_map/reduce_scatter | solution.py:333
  1466.2 5.8 fusion.62
  1472.0 16.7 %all-reduce.1 = (f32[256]{0:T(256)S(1)}, f32[256]{0:T(256)S(1)}, f32[256]{0:T(256)S(1)}, f32[256]{0:T(256)S(1)}, f32[256]{0:T(256)S(1)}) all-reduce(f32[256]{0:T(256)S(1)} %get-tuple-element.291, f32[256]{0:T(256)S(1)} %get-tuple-element.304, f32[256]{0:T(256)S(1)} %get-tuple-element.302, ...), channel_id=1, replica_groups=mesh['dp'=4,'mp'=8] {'mp'}, use_global_device_ids=true, to_apply=%region_45.46 | all-reduce | flops 1280 | bytes 10240 | tf_op jit(solution)/shard_map/psum | solution.py:361
  1491.3 16.2 all-reduce.3
  1514.7 37.0 %psum.177 = f32[10]{0:T(128)S(1)} all-reduce(f32[10]{0:T(128)S(1)} %stack.94), channel_id=1, replica_groups=mesh['dp'=4,'mp'=8] {'dp','mp'}, use_global_device_ids=true, to_apply=%region_68.69 | all-reduce | flops 10 | bytes 80 | tf_op jit(solution)/shard_map/psum | solution.py:380
  1558.2 6.7 multiply_reduce_fusion.9
  1568.1 42.1 %all-reduce = (f32[5]{0:T(128)S(1)}, f32[6,1024]{1,0:T(8,128)S(1)}) all-reduce(f32[5]{0:T(128)S(1)} %stack.100, f32[6,1024]{1,0:T(8,128)S(1)} %stack.107), channel_id=1, replica_groups=mesh['dp'=4,'mp'=8] {'dp','mp'}, use_global_device_ids=true, to_apply=%region_82.83 | all-reduce | flops 6149 | bytes 49192 | tf_op jit(solution)/shard_map/psum | solution.py:388
  1625.2 8.5 multiply_subtract_fusion.1
  (383 shorter events, 151.7 us)
Async XLA Ops:
  7.2 136.6 %all-gather.4.cloned.1.call-start = ((), (), s32[]{:S(2)}) async-start(), calls=%async_computation.5 | async-start | bytes 16097280 | tf_op jit(solution)/shard_map/all_gather | solution.py:236
  16.1 245.8 %all-reduce.11.cloned.1.call-start = ((), (), s32[]{:S(2)}) async-start(), calls=%async_computation.6 | async-start | bytes 8388608 | tf_op jit(solution)/shard_map/psum | solution.py:37
  16.2 144.9 %copy-start.63 = (pred[2048]{0:T(1024)(128)(4,1)}, pred[2048]{0:T(1024)(128)(4,1)S(1)}, u32[]{:S(2)}) copy-start(pred[2048]{0:T(1024)(128)(4,1)S(1)} %compare_and_fusion) | copy-start | bytes 6148
  161.1 26.1 %copy-start.36 = (f32[6,1024]{1,0:T(8,128)S(1)}, f32[6,1024]{1,0:T(8,128)}, u32[]{:S(2)}) copy-start(f32[6,1024]{1,0:T(8,128)} %param.38) | copy-start | bytes 73732
  165.2 227.9 %all-reduce.13.cloned.1.call-start = ((), (), s32[]{:S(2)}) async-start(), calls=%async_computation.7 | async-start | bytes 8388608 | tf_op jit(solution)/shard_map/psum | solution.py:37
  175.9 116.3 %copy-start.18 = (bf16[128,1024]{1,0:T(8,128)(2,1)}, bf16[128,1024]{1,0:T(8,128)(2,1)S(1)}, u32[]{:S(2)}) copy-start(bf16[128,1024]{1,0:T(8,128)(2,1)S(1)} %all_gather.17) | copy-start | bytes 786436
  187.2 80.7 %copy-start.27 = (bf16[1024,384]{1,0:T(8,128)(2,1)}, bf16[1024,384]{1,0:T(8,128)(2,1)S(1)}, u32[]{:S(2)}) copy-start(bf16[1024,384]{1,0:T(8,128)(2,1)S(1)} %all_gather.16) | copy-start | bytes 2359300
  187.3 80.6 %copy-start.54 = (f32[1,1024]{1,0:T(1,128)}, f32[1,1024]{1,0:T(1,128)S(1)}, u32[]{:S(2)}) copy-start(f32[1,1024]{1,0:T(1,128)S(1)} %get-tuple-element.427) | copy-start | bytes 12292
  187.3 80.6 %copy-start.73 = (f32[1,1024]{1,0:T(1,128)}, f32[1,1024]{1,0:T(1,128)S(1)}, u32[]{:S(2)}) copy-start(f32[1,1024]{1,0:T(1,128)S(1)} %get-tuple-element.426) | copy-start | bytes 12292
  187.3 234.8 %copy-start.52 = (f32[1,1024]{1,0:T(1,128)}, f32[1,1024]{1,0:T(1,128)S(1)}, u32[]{:S(2)}) copy-start(f32[1,1024]{1,0:T(1,128)S(1)} %get-tuple-element.422) | copy-start | bytes 12292
  187.3 234.8 %copy-start.75 = (f32[1,1024]{1,0:T(1,128)}, f32[1,1024]{1,0:T(1,128)S(1)}, u32[]{:S(2)}) copy-start(f32[1,1024]{1,0:T(1,128)S(1)} %get-tuple-element.425) | copy-start | bytes 12292
  187.3 378.2 %copy-start.50 = (f32[1,1024]{1,0:T(1,128)}, f32[1,1024]{1,0:T(1,128)S(1)}, u32[]{:S(2)}) copy-start(f32[1,1024]{1,0:T(1,128)S(1)} %get-tuple-element.424) | copy-start | bytes 12292
  296.4 125.7 %all-gather.6.cloned.1.call-start = ((), (), s32[]{:S(2)}) async-start(), calls=%async_computation.8 | async-start | bytes 1310720 | tf_op jit(solution)/shard_map/all_gather | solution.py:239
  297.9 153.0 %all-gather.8.cloned.1.call-start = ((), (), s32[]{:S(2)}) async-start(), calls=%async_computation.9 | async-start | bytes 1310720 | tf_op jit(solution)/shard_map/all_gather | solution.py:240
  299.3 255.5 %all-reduce.15.cloned.1.call-start = ((), (), s32[]{:S(2)}) async-start(), calls=%async_computation.10 | async-start | bytes 8388608 | tf_op jit(solution)/shard_map/psum | solution.py:37
  430.1 28.1 %copy-start.58 = (s32[2048]{0:T(1024)S(1)}, s32[2048]{0:T(1024)}, u32[]{:S(2)}) copy-start(s32[2048]{0:T(1024)} %param.32) | copy-start | bytes 24580
  430.1 37.7 %copy-start.71 = (s32[2048]{0:T(1024)S(1)}, s32[2048]{0:T(1024)}, u32[]{:S(2)}) copy-start(s32[2048]{0:T(1024)} %param.30) | copy-start | bytes 24580
  458.1 493.0 %all-reduce.17.cloned.1.call-start = ((), (), s32[]{:S(2)}) async-start(), calls=%async_computation.11 | async-start | bytes 8388608 | tf_op jit(solution)/shard_map/psum | solution.py:41
  467.7 97.7 %copy-start.89 = (f32[4]{0:T(128)}, f32[4]{0:T(128)S(1)}, u32[]{:S(2)}) copy-start(f32[4]{0:T(128)S(1)} %psum.167) | copy-start | bytes 52
  673.6 277.6 %copy-start.51 = (f32[1,1024]{1,0:T(1,128)S(1)}, f32[1,1024]{1,0:T(1,128)}, u32[]{:S(2)}) copy-start(f32[1,1024]{1,0:T(1,128)} %copy-done.50) | copy-start | bytes 12292
  856.3 101.3 %copy-start.45 = (f32[2048]{0:T(1024)S(1)}, f32[2048]{0:T(1024)}, u32[]{:S(2)}) copy-start(f32[2048]{0:T(1024)} %copy-done.44) | copy-start | bytes 24580
  856.3 101.3 %copy-start.88 = (bf16[512,1024]{1,0:T(8,128)(2,1)S(1)}, bf16[512,1024]{1,0:T(8,128)(2,1)}, u32[]{:S(2)}) copy-start(bf16[512,1024]{1,0:T(8,128)(2,1)} %all-gather.8.cloned.1.call-done) | copy-start | bytes 3145732
  856.3 210.7 %all-reduce.19.cloned.1.call-start = ((), (), s32[]{:S(2)}) async-start(), calls=%async_computation.12 | async-start | bytes 8388608 | tf_op jit(solution)/shard_map/psum | solution.py:41
  965.9 101.2 %copy-start.53 = (f32[1,1024]{1,0:T(1,128)S(1)}, f32[1,1024]{1,0:T(1,128)}, u32[]{:S(2)}) copy-start(f32[1,1024]{1,0:T(1,128)} %copy-done.52) | copy-start | bytes 12292
  970.3 103.2 %copy-start.47 = (f32[2048]{0:T(1024)S(1)}, f32[2048]{0:T(1024)}, u32[]{:S(2)}) copy-start(f32[2048]{0:T(1024)} %copy-done.46) | copy-start | bytes 24580
  970.3 250.1 %all-reduce.21.cloned.1.call-start = ((), (), s32[]{:S(2)}) async-start(), calls=%async_computation.13 | async-start | bytes 8388608 | tf_op jit(solution)/shard_map/psum | solution.py:41
  1088.5 30.8 %copy-start.28 = (bf16[1024,384]{1,0:T(8,128)(2,1)S(1)}, bf16[1024,384]{1,0:T(8,128)(2,1)}, u32[]{:S(2)}) copy-start(bf16[1024,384]{1,0:T(8,128)(2,1)} %copy-done.27) | copy-start | bytes 2359300
  1123.8 166.6 %reduce-scatter.14.cloned.1.call-start = ((), (), s32[]{:S(2)}) async-start(), calls=%async_computation.18 | async-start | bytes 1310720 | tf_op jit(solution)/shard_map/reduce_scatter | solution.py:345
  1133.1 158.3 %reduce-scatter.12.cloned.1.call-start = ((), (), s32[]{:S(2)}) async-start(), calls=%async_computation.17 | async-start | bytes 1310720 | tf_op jit(solution)/shard_map/reduce_scatter | solution.py:342
  1140.7 169.1 %reduce-scatter.10.cloned.1.call-start = ((), (), s32[]{:S(2)}) async-start(), calls=%async_computation.16 | async-start | bytes 327680 | tf_op jit(solution)/shard_map/reduce_scatter | solution.py:339
  1145.7 193.4 %reduce-scatter.8.cloned.1.call-start = ((), (), s32[]{:S(2)}) async-start(), calls=%async_computation.15 | async-start | bytes 983040 | tf_op jit(solution)/shard_map/reduce_scatter | solution.py:336
  1152.2 75.3 %copy-start.64 = (pred[2048]{0:T(1024)(128)(4,1)S(1)}, pred[2048]{0:T(1024)(128)(4,1)}, u32[]{:S(2)}) copy-start(pred[2048]{0:T(1024)(128)(4,1)} %copy-done.63) | copy-start | bytes 6148
  1152.2 314.1 %reduce-scatter.6.cloned.1.call-start = ((), (), s32[]{:S(2)}) async-start(), calls=%async_computation.14 | async-start | bytes 16097280 | tf_op jit(solution)/shard_map/reduce_scatter | solution.py:333
  1291.4 327.5 %copy-start.15 = (f32[512,256]{1,0:T(8,128)}, f32[512,256]{1,0:T(8,128)S(1)}, u32[]{:S(2)}) copy-start(f32[512,256]{1,0:T(8,128)S(1)} %get-tuple-element.394) | copy-start | bytes 1572868
  1292.8 327.8 %copy-start.16 = (f32[256,512]{1,0:T(8,128)}, f32[256,512]{1,0:T(8,128)S(1)}, u32[]{:S(2)}) copy-start(f32[256,512]{1,0:T(8,128)S(1)} %get-tuple-element.392) | copy-start | bytes 1572868
  1310.8 311.5 %copy-start.26 = (f32[128,256]{1,0:T(8,128)}, f32[128,256]{1,0:T(8,128)S(1)}, u32[]{:S(2)}) copy-start(f32[128,256]{1,0:T(8,128)S(1)} %get-tuple-element.395) | copy-start | bytes 393220
  1340.2 283.5 %copy-start.17 = (f32[256,384]{1,0:T(8,128)}, f32[256,384]{1,0:T(8,128)S(1)}, u32[]{:S(2)}) copy-start(f32[256,384]{1,0:T(8,128)S(1)} %get-tuple-element.393) | copy-start | bytes 1179652
  1343.5 145.2 %copy-start.81 = (f32[256]{0:T(256)S(1)}, f32[256]{0:T(256)}, u32[]{:S(2)}) copy-start(f32[256]{0:T(256)} %param.41) | copy-start | bytes 3076
  1343.6 146.5 %copy-start.82 = (f32[256]{0:T(256)S(1)}, f32[256]{0:T(256)}, u32[]{:S(2)}) copy-start(f32[256]{0:T(256)} %param.45) | copy-start | bytes 3076
  1343.6 147.7 %copy-start.77 = (f32[4]{0:T(128)S(1)}, f32[4]{0:T(128)}, u32[]{:S(2)}) copy-start(f32[4]{0:T(128)} %get-tuple-element.308) | copy-start | bytes 52
  1343.6 163.9 %copy-start.59 = (f32[6288]{0:T(1024)S(1)}, f32[6288]{0:T(1024)}, u32[]{:S(2)}) copy-start(f32[6288]{0:T(1024)} %param.39) | copy-start | bytes 75460
  1343.6 165.2 %copy-start.80 = (f32[512]{0:T(512)S(1)}, f32[512]{0:T(512)}, u32[]{:S(2)}) copy-start(f32[512]{0:T(512)} %param.47) | copy-start | bytes 6148
  1343.6 166.4 %copy-start.86 = (f32[128]{0:T(128)S(1)}, f32[128]{0:T(128)}, u32[]{:S(2)}) copy-start(f32[128]{0:T(128)} %param.43) | copy-start | bytes 1540
  1343.6 208.7 %copy-start.83 = (f32[256]{0:T(256)S(1)}, f32[256]{0:T(256)}, u32[]{:S(2)}) copy-start(f32[256]{0:T(256)} %param.48) | copy-start | bytes 3076
  1343.6 208.7 %copy-start.78 = (f32[512]{0:T(512)S(1)}, f32[512]{0:T(512)}, u32[]{:S(2)}) copy-start(f32[512]{0:T(512)} %param.46) | copy-start | bytes 6148
  1343.6 208.7 %copy-start.84 = (f32[256]{0:T(256)S(1)}, f32[256]{0:T(256)}, u32[]{:S(2)}) copy-start(f32[256]{0:T(256)} %param.44) | copy-start | bytes 3076
  1343.7 208.8 %copy-start.79 = (f32[384]{0:T(512)S(1)}, f32[384]{0:T(512)}, u32[]{:S(2)}) copy-start(f32[384]{0:T(512)} %param.42) | copy-start | bytes 4612
  1343.7 208.8 %copy-start.85 = (f32[256]{0:T(256)S(1)}, f32[256]{0:T(256)}, u32[]{:S(2)}) copy-start(f32[256]{0:T(256)} %param.40) | copy-start | bytes 3076
  1345.1 265.2 %copy-start.56 = (f32[6,1024]{1,0:T(8,128)S(1)}, f32[6,1024]{1,0:T(8,128)}, u32[]{:S(2)}) copy-start(f32[6,1024]{1,0:T(8,128)} %param.49) | copy-start | bytes 73732
  1345.1 273.8 %copy-start.21 = (f32[512,256]{1,0:T(8,128)S(1)}, f32[512,256]{1,0:T(8,128)}, u32[]{:S(2)}) copy-start(f32[512,256]{1,0:T(8,128)} %param.37) | copy-start | bytes 1572868
  1345.1 275.5 %copy-start.23 = (f32[256,512]{1,0:T(8,128)S(1)}, f32[256,512]{1,0:T(8,128)}, u32[]{:S(2)}) copy-start(f32[256,512]{1,0:T(8,128)} %param.36) | copy-start | bytes 1572868
  1345.2 277.1 %copy-start.30 = (f32[128,256]{1,0:T(8,128)S(1)}, f32[128,256]{1,0:T(8,128)}, u32[]{:S(2)}) copy-start(f32[128,256]{1,0:T(8,128)} %param.35) | copy-start | bytes 393220
  1472.0 151.6 %copy-start.25 = (f32[256,384]{1,0:T(8,128)S(1)}, f32[256,384]{1,0:T(8,128)}, u32[]{:S(2)}) copy-start(f32[256,384]{1,0:T(8,128)} %param.34) | copy-start | bytes 1179652
  1489.4 144.3 %copy-start.66 = (f32[256]{0:T(256)}, f32[256]{0:T(256)S(1)}, u32[]{:S(2)}) copy-start(f32[256]{0:T(256)S(1)} %get-tuple-element.389) | copy-start | bytes 3076
  1490.6 143.0 %copy-start.67 = (f32[256]{0:T(256)}, f32[256]{0:T(256)S(1)}, u32[]{:S(2)}) copy-start(f32[256]{0:T(256)S(1)} %get-tuple-element.385) | copy-start | bytes 3076
  1508.1 125.6 %copy-start.35 = (f32[6288]{0:T(1024)}, f32[6288]{0:T(1024)S(1)}, u32[]{:S(2)}) copy-start(f32[6288]{0:T(1024)S(1)} %get-tuple-element.391) | copy-start | bytes 75460
  1509.4 124.3 %copy-start.62 = (f32[512]{0:T(512)}, f32[512]{0:T(512)S(1)}, u32[]{:S(2)}) copy-start(f32[512]{0:T(512)S(1)} %get-tuple-element.383) | copy-start | bytes 6148
  1510.6 123.0 %copy-start.72 = (f32[128]{0:T(128)}, f32[128]{0:T(128)S(1)}, u32[]{:S(2)}) copy-start(f32[128]{0:T(128)S(1)} %get-tuple-element.387) | copy-start | bytes 1540
  1552.3 81.4 %copy-start.68 = (f32[256]{0:T(256)}, f32[256]{0:T(256)S(1)}, u32[]{:S(2)}) copy-start(f32[256]{0:T(256)S(1)} %multiply_add_fusion.11) | copy-start | bytes 3076
  1552.4 81.3 %copy-start.60 = (f32[512]{0:T(512)}, f32[512]{0:T(512)S(1)}, u32[]{:S(2)}) copy-start(f32[512]{0:T(512)S(1)} %multiply_add_fusion.8) | copy-start | bytes 6148
  1552.4 81.3 %copy-start.65 = (f32[256]{0:T(256)}, f32[256]{0:T(256)S(1)}, u32[]{:S(2)}) copy-start(f32[256]{0:T(256)S(1)} %multiply_add_fusion.12) | copy-start | bytes 3076
  1552.4 81.3 %copy-start.61 = (f32[384]{0:T(512)}, f32[384]{0:T(512)S(1)}, u32[]{:S(2)}) copy-start(f32[384]{0:T(512)S(1)} %multiply_add_fusion.9) | copy-start | bytes 4612
  1552.5 81.3 %copy-start.69 = (f32[256]{0:T(256)}, f32[256]{0:T(256)S(1)}, u32[]{:S(2)}) copy-start(f32[256]{0:T(256)S(1)} %multiply_add_fusion.15) | copy-start | bytes 3076
  1610.3 23.5 %copy-start.38 = (f32[6,1024]{1,0:T(8,128)}, f32[6,1024]{1,0:T(8,128)S(1)}, u32[]{:S(2)}) copy-start(f32[6,1024]{1,0:T(8,128)S(1)} %get-tuple-element.366) | copy-start | bytes 73732
  (44 other events, 262.0 us)
Sparse Core Ops, SparseCore 0:
  16.2 127.5 all-gather.3
  165.3 96.5 all-reduce.10
  296.5 96.5 all-reduce.12
  395.4 26.6 all-gather.5
  424.3 26.4 all-gather.7
  458.3 96.4 all-reduce.14
  856.5 94.6 all-reduce.16
  970.5 96.5 all-reduce.18
  1123.9 96.5 all-reduce.20
  1223.2 27.7 reduce-scatter.13
  1254.8 27.7 reduce-scatter.11
  1285.7 24.0 reduce-scatter.9
  1313.0 26.0 reduce-scatter.7
  1342.4 123.7 reduce-scatter.5
where the time goes:
time: 1650 us; the launch traced here: 1640 us
  waiting for transfers between devices  846 us (51%)
  matrix products  321 us (19%)
  other arithmetic  214 us (13%)
  blocking collectives  184 us (11%)
  local copies, waits for them, and re-layouts  47.6 us (3%)
  between operations  27.1 us (2%)
    psum x3, waiting for transfers between devices, sum_grads(): lax.psum(term(0, tokens).astype(jnp.bfloat16), 'mp').astype(jnp.float32)  259 us
    psum x3, waiting for transfers between devices, sum_branch(): lax.psum(term(0, tokens).astype(jnp.bfloat16), 'mp').astype(jnp.float32)  255 us
    all_gather x1, waiting for transfers between devices, local(): lax.all_gather(embedding.astype(jnp.bfloat16), 'dp', axis=1, tiled=True)  127 us
    reduce_scatter x1, waiting for transfers between devices, local(): lax.psum_scatter(table_grad.astype(jnp.bfloat16), 'dp', scatter_dimension...  121 us
    dot_general x8, matrix products, logits_of(): jnp.einsum('bd,vd->bv', rows, gathered_table, preferred_element_type=jnp....  105 us
    dot_general x4, matrix products, head_back(): jnp.einsum('bv,bd->vd', dlogits, rows, preferred_element_type=jnp.float32)  71 us
    dot_general x4, matrix products, head_back(): jnp.dot(dlogits, gathered_table, preferred_element_type=jnp.float32)  50.7 us
    psum x1, blocking collectives, local(): lax.psum(jnp.stack([jnp.sum(piece * piece) for piece in steps]), ('dp', '...  42.1 us
  transfers between devices with their start and end apart: 14, of which 12 were waited for; matrix products, arithmetic and copies ran while one was open for 8% of the time, Pallas kernels for 0%

commit v1 on v0

v1 whole, which is shorter than its diff:
```python
import functools
import math

import jax
import jax.numpy as jnp
from jax import lax
from jax.experimental import pallas as pl
from jax.experimental.pallas import tpu as pltpu
from jax.sharding import PartitionSpec as P

HD = 64
VREAL = 50257
LEN = 1024
NSRC = 4
STEP = 10


EPS_NORM = 1e-05
EPS_ONE = 1e-30
CLIP = 1.0
RHO = 0.5
MASKED = -1e30
MESH = pl.DeviceIdType.MESH
VMEM_CAP = 56 * 2**20


def row_slice(values, start, count):
    return lax.dynamic_slice_in_dim(values, start, count, 0)


def line_kernel(nr, ng, chunks, rows, width, n_in, n_out, step, *refs):
    part = refs[0] if nr else None
    first = 1 if nr else 0
    ins = refs[first : first + n_in]
    refs = refs[first + n_in :]
    if ng:
        whole, refs = refs[0], refs[1:]
    outs = refs[:n_out]
    scratch = refs[n_out:]
    dp = lax.axis_index("dp")
    mp = lax.axis_index("mp")
    z = mp // 2
    core = lax.rem(mp, 2)
    other = mp + 1 - 2 * core
    piece = rows // chunks
    most = max(nr, ng)
    zb = lax.rem(z, most)
    if nr:
        zr = lax.rem(z, nr)
        last_r = nr - 1
    if ng:
        zg = lax.rem(z, ng)
        last_g = ng - 1

    barrier = pltpu.get_barrier_semaphore()
    pl.semaphore_signal(barrier, inc=1, device_id=(dp, other), device_id_type=MESH)

    @pl.when(zb > 0)
    def _():
        pl.semaphore_signal(barrier, inc=1, device_id=(dp, mp - 2), device_id_type=MESH)

    @pl.when(zb < most - 1)
    def _():
        pl.semaphore_signal(barrier, inc=1, device_id=(dp, mp + 2), device_id_type=MESH)

    greeted = 1 + (zb > 0).astype(jnp.int32) + (zb < most - 1).astype(jnp.int32)
    pl.semaphore_wait(barrier, greeted)

    if nr:
        half, from_left, from_right, going = scratch[:4]
        half_send, half_recv, rs_send, left_recv, right_recv = scratch[4:9]
        scratch = scratch[9:]
    if ng:
        core_send, core_recv, to_right, to_left, ag_left, ag_right = scratch[:6]

    def part_rows(block, k):
        return pl.ds(pl.multiple_of(block * rows + k * piece, piece), piece)

    def remote(src, dst, send, recv, target):
        return pltpu.make_async_remote_copy(
            src_ref=src,
            dst_ref=dst,
            send_sem=send,
            recv_sem=recv,
            device_id=(dp, target),
            device_id_type=MESH,
        )

    if nr:

        def half_copy(dest, k):
            return remote(
                part.at[part_rows(2 * dest + 1 - core, k)],
                half.at[dest, k],
                half_send.at[dest, k],
                half_recv.at[dest, k],
                other,
            )

        def send_halves(k, carry):
            for dest in range(nr):
                half_copy(dest, k).start()
            return carry

        lax.fori_loop(0, chunks, send_halves, 0)

        def right_copy(dest, k):
            return remote(
                going.at[dest, k],
                from_left.at[dest, k],
                rs_send.at[dest, k],
                left_recv.at[dest, k],
                mp + 2,
            )

        def left_copy(dest, k):
            return remote(
                going.at[dest, k],
                from_right.at[dest, k],
                rs_send.at[dest, k],
                right_recv.at[dest, k],
                mp - 2,
            )

        def chip_sum(dest, k):
            half_copy(dest, k).wait_recv()
            mine = part[part_rows(2 * dest + core, k), :].astype(jnp.float32)
            return mine + half[dest, k].astype(jnp.float32)

        def pass_right(dest, k):
            total = chip_sum(dest, k)

            @pl.when(zr == 0)
            def _():
                going[dest, k] = total.astype(jnp.bfloat16)

            @pl.when(zr > 0)
            def _():
                right_copy(dest, k).wait_recv()
                both = total + from_left[dest, k].astype(jnp.float32)
                going[dest, k] = both.astype(jnp.bfloat16)

            right_copy(dest, k).start()

        def pass_left(dest, k):
            total = chip_sum(dest, k)

            @pl.when(zr == last_r)
            def _():
                going[dest, k] = total.astype(jnp.bfloat16)

            @pl.when(zr < last_r)
            def _():
                left_copy(dest, k).wait_recv()
                both = total + from_right[dest, k].astype(jnp.float32)
                going[dest, k] = both.astype(jnp.bfloat16)

            left_copy(dest, k).start()

    if ng:

        def gathered(block, k, send, recv, target):
            where = whole.at[part_rows(2 * block + core, k)]
            return remote(where, where, send.at[block, k], recv.at[block, k], target)

        def core_copy(block, k):
            return gathered(block, k, core_send, core_recv, other)

        def ag_right_copy(block, k):
            return gathered(block, k, to_right, ag_left, mp + 2)

        def ag_left_copy(block, k):
            return gathered(block, k, to_left, ag_right, mp - 2)

    def own_rows(k):
        total = None
        if nr:
            total = chip_sum(zr, k)
            zero = jnp.zeros((piece, width), jnp.float32)

            @pl.when(zr > 0)
            def _():
                right_copy(zr, k).wait_recv()

            @pl.when(zr < last_r)
            def _():
                left_copy(zr, k).wait_recv()

            total += jnp.where(zr > 0, from_left[zr, k].astype(jnp.float32), zero)
            total += jnp.where(zr < last_r, from_right[zr, k].astype(jnp.float32), zero)
        at = pl.ds(pl.multiple_of(k * piece, piece), piece)
        ready = step(total, at, ins, outs)
        if ng:
            whole[part_rows(2 * zg + core, k), :] = ready.astype(whole.dtype)
            core_copy(zg, k).start()

            @pl.when(zg < last_g)
            def _():
                ag_right_copy(zg, k).start()

            @pl.when(zg > 0)
            def _():
                ag_left_copy(zg, k).start()

    def inside(k):
        return (k >= 0) & (k < chunks)

    def own_lag(chip):
        if not nr:
            return 0
        at = lax.rem(chip, nr)
        return jnp.maximum(at, last_r - at)

    def tick(now, carry):
        if nr:
            k_right = now - zr
            k_left = now - (last_r - zr)
            for far in range(last_r):

                @pl.when(inside(k_right) & (last_r - far > zr))
                def _():
                    pass_right(last_r - far, k_right)

                @pl.when(inside(k_left) & (far < zr))
                def _():
                    pass_left(far, k_left)

        k_own = now - own_lag(z)

        @pl.when(inside(k_own))
        def _():
            own_rows(k_own)

        if ng:
            for block in range(ng):
                k = now - (own_lag(z - zg + block) + jnp.abs(zg - block))

                @pl.when(inside(k) & (block < zg))
                def _():
                    ag_right_copy(block, k).wait_recv()
                    core_copy(block, k).start()

                    @pl.when(zg < last_g)
                    def _():
                        ag_right_copy(block, k).start()

                @pl.when(inside(k) & (block > zg))
                def _():
                    ag_left_copy(block, k).wait_recv()
                    core_copy(block, k).start()

                    @pl.when(zg > 0)
                    def _():
                        ag_left_copy(block, k).start()

        return carry

    ticks = chunks + (nr - 1 if nr else 0) + (ng - 1 if ng else 0)
    lax.fori_loop(0, ticks, tick, 0)

    def finish(k, carry):
        if nr:
            for block in range(nr):
                half_copy(block, k).wait_send()

                @pl.when(block != zr)
                def _():
                    right_copy(block, k).wait_send()

        if ng:
            for block in range(ng):
                core_copy(block, k).wait()

                @pl.when((zg < last_g) & (block <= zg))
                def _():
                    ag_right_copy(block, k).wait_send()

                @pl.when((zg > 0) & (block >= zg))
                def _():
                    ag_left_copy(block, k).wait_send()

        return carry

    lax.fori_loop(0, chunks, finish, 0)


def line_call(name, cid, partial, ins, out_types, step, rows, width, chunks, nr, ng):
    piece = rows // chunks
    out_shape = []
    if ng:
        out_shape.append(jax.ShapeDtypeStruct((2 * ng * rows, width), jnp.bfloat16))
    out_shape += out_types
    dma = pltpu.SemaphoreType.DMA
    scratch = []
    if nr:
        scratch += [pltpu.VMEM((nr, chunks, piece, width), jnp.bfloat16)] * 4
        scratch += [dma((nr, chunks))] * 5
    if ng:
        scratch += [dma((ng, chunks))] * 6
    args = ([partial] if nr else []) + list(ins)
    vmem = pl.BlockSpec(memory_space=pltpu.VMEM)
    call = pl.pallas_call(
        functools.partial(
            line_kernel, nr, ng, chunks, rows, width, len(ins), len(out_types), step
        ),
        out_shape=out_shape,
        in_specs=[vmem] * len(args),
        out_specs=[vmem] * len(out_shape),
        scratch_shapes=scratch,
        compiler_params=pltpu.CompilerParams(
            collective_id=cid, has_side_effects=True, vmem_limit_bytes=VMEM_CAP
        ),
        name=name,
    )
    return list(call(*args))


def head_stats_kernel(block, tile, table_ref, final_ref, wanted_ref, edge_ref, exp_ref, top_ref, sum_ref, pick_ref):
    j = pl.program_id(0)
    tokens = final_ref.shape[0]
    place = j * block + lax.broadcasted_iota(jnp.int32, (block, 1), 0)
    valid = place < edge_ref[0]

    def one(i, carry):
        at = pl.ds(i * tile, tile)
        logits = lax.dot_general(
            table_ref[...],
            final_ref[at, :],
            (((1,), (1,)), ((), ())),
            preferred_element_type=jnp.float32,
        )
        logits = jnp.where(valid, logits, MASKED)
        top = jnp.max(logits, axis=0, keepdims=True)
        weights = jnp.exp(logits - top)
        exp_ref[:, at] = weights.astype(jnp.bfloat16)
        top_ref[0, :, at] = top
        sum_ref[0, :, at] = jnp.sum(weights, axis=0, keepdims=True)
        pick_ref[0, :, at] = jnp.sum(
            jnp.where(place == wanted_ref[:, at], logits, 0.0), axis=0, keepdims=True
        )
        return carry

    for i in range(tokens // tile):
        one(i, 0)


def head_stats(table, final, wanted, edge, block, tile=512):
    rows, width = table.shape
    tokens = final.shape[0]
    steps = pl.cdiv(rows, block)
    row = jax.ShapeDtypeStruct((steps, 1, tokens), jnp.float32)
    row_spec = pl.BlockSpec((1, 1, tokens), lambda j: (j, 0, 0))
    return pl.pallas_call(
        functools.partial(head_stats_kernel, block, tile),
        grid=(steps,),
        out_shape=[jax.ShapeDtypeStruct((steps * block, tokens), jnp.bfloat16), row, row, row],
        in_specs=[
            pl.BlockSpec((block, width), lambda j: (j, 0)),
            pl.BlockSpec((tokens, width), lambda j: (0, 0)),
            pl.BlockSpec((1, tokens), lambda j: (0, 0)),
            pl.BlockSpec(memory_space=pltpu.SMEM),
        ],
        out_specs=[pl.BlockSpec((block, tokens), lambda j: (j, 0)), row_spec, row_spec, row_spec],
        compiler_params=pltpu.CompilerParams(vmem_limit_bytes=56 * 2**20),
        cost_estimate=pl.CostEstimate(
            flops=2 * rows * width * tokens,
            bytes_accessed=2 * rows * (width + tokens),
            transcendentals=rows * tokens,
        ),
        name="head_stats",
    )(table, final, wanted, edge)


def head_back_kernel(rows, block, tile, exp_ref, table_ref, final_ref, scale_ref, weight_ref, wanted_ref, grad_ref, dfinal_ref, dl_ref):
    j = pl.program_id(0)
    tokens = final_ref.shape[0]
    place = j * block + lax.broadcasted_iota(jnp.int32, (block, 1), 0)

    @pl.when(j == 0)
    def _():
        dfinal_ref[...] = jnp.zeros_like(dfinal_ref)

    table = jnp.where(place < rows, table_ref[...], jnp.zeros_like(table_ref))

    def one(i, carry):
        at = pl.ds(i * tile, tile)
        weight = weight_ref[:, at]
        dl = exp_ref[:, at].astype(jnp.float32) * scale_ref[0, :, at]
        dl = dl - jnp.where(place == wanted_ref[:, at], weight, 0.0)
        dl = dl.astype(jnp.bfloat16)
        dl_ref[:, at] = dl
        dfinal_ref[at, :] += lax.dot_general(
            dl, table, (((0,), (0,)), ((), ())), preferred_element_type=jnp.float32
        )
        return carry

    for i in range(tokens // tile):
        one(i, 0)

    strip = block // max(1, block // 256)

    def two(i, carry):
        at = pl.ds(i * strip, strip)
        grad_ref[at, :] = jnp.dot(
            dl_ref[at, :], final_ref[...], preferred_element_type=jnp.float32
        ).astype(jnp.bfloat16)
        return carry

    for i in range(block // strip):
        two(i, 0)


def head_back(exps, table, final, scale, weight, wanted, block, tile=256):
    rows, width = table.shape
    tokens = final.shape[0]
    steps = pl.cdiv(rows, block)
    return pl.pallas_call(
        functools.partial(head_back_kernel, rows, block, tile),
        grid=(steps,),
        out_shape=[
            jax.ShapeDtypeStruct((rows, width), jnp.bfloat16),
            jax.ShapeDtypeStruct((tokens, width), jnp.float32),
        ],
        in_specs=[
            pl.BlockSpec((block, tokens), lambda j: (j, 0)),
            pl.BlockSpec((block, width), lambda j: (j, 0)),
            pl.BlockSpec((tokens, width), lambda j: (0, 0)),
            pl.BlockSpec((1, 1, tokens), lambda j: (j, 0, 0)),
            pl.BlockSpec((1, tokens), lambda j: (0, 0)),
            pl.BlockSpec((1, tokens), lambda j: (0, 0)),
        ],
        out_specs=[
            pl.BlockSpec((block, width), lambda j: (j, 0)),
            pl.BlockSpec((tokens, width), lambda j: (0, 0)),
        ],
        scratch_shapes=[pltpu.VMEM((block, tokens), jnp.bfloat16)],
        compiler_params=pltpu.CompilerParams(vmem_limit_bytes=60 * 2**20),
        cost_estimate=pl.CostEstimate(
            flops=4 * rows * width * tokens,
            bytes_accessed=2 * rows * (2 * width + tokens),
            transcendentals=0,
        ),
        name="head_back",
    )(exps, table, final, scale, weight, wanted)


def small_gather_kernel(axis, count, src_ref, out_ref, send, recv):
    dp = lax.axis_index("dp")
    mp = lax.axis_index("mp")
    me = dp if axis == "dp" else mp

    def device(peer):
        return (peer, mp) if axis == "dp" else (dp, peer)

    barrier = pltpu.get_barrier_semaphore()
    for hop in range(1, count):
        pl.semaphore_signal(
            barrier, inc=1, device_id=device(lax.rem(me + hop, count)), device_id_type=MESH
        )
    pl.semaphore_wait(barrier, count - 1)
    copies = []
    for hop in range(1, count):
        peer = lax.rem(me + hop, count)
        copy = pltpu.make_async_remote_copy(
            src_ref=src_ref,
            dst_ref=out_ref.at[me],
            send_sem=send.at[hop],
            recv_sem=recv.at[hop],
            device_id=device(peer),
            device_id_type=MESH,
        )
        copy.start()
        copies.append(copy)
    out_ref[me] = src_ref[...]
    for copy in copies:
        copy.wait()


def small_gather(name, cid, values, axis):
    count = lax.axis_size(axis)
    vmem = pl.BlockSpec(memory_space=pltpu.VMEM)
    return pl.pallas_call(
        functools.partial(small_gather_kernel, axis, count),
        out_shape=jax.ShapeDtypeStruct((count,) + values.shape, values.dtype),
        in_specs=[vmem],
        out_specs=vmem,
        scratch_shapes=[pltpu.SemaphoreType.DMA((count,)), pltpu.SemaphoreType.DMA((count,))],
        compiler_params=pltpu.CompilerParams(collective_id=cid, has_side_effects=True),
        name=name,
    )(values)


def packed(pieces):
    flat = []
    for piece in pieces:
        piece = piece.reshape(-1)
        flat.append(jnp.pad(piece, (0, -piece.size % 128)))
    flat = jnp.concatenate(flat)
    return jnp.pad(flat, (0, -flat.size % 1024)).reshape(-1, 128)


def unpacked(rows, shapes):
    flat = rows.reshape(-1)
    pieces, at = [], 0
    for shape in shapes:
        size = math.prod(shape)
        pieces.append(flat[at : at + size].reshape(shape))
        at += size + -size % 128
    return pieces


def small_sum(name, cid, over_dp, over_mp, over_all):
    first = small_gather(name + "_dp", cid, packed(over_dp + over_all), "dp")
    first = unpacked(jnp.sum(first, axis=0), [v.shape for v in over_dp + over_all])
    rest = first[len(over_dp) :]
    second = small_gather(name + "_mp", cid + 1, packed(over_mp + rest), "mp")
    second = unpacked(jnp.sum(second, axis=0), [v.shape for v in over_mp + over_all])
    return first[: len(over_dp)], second[: len(over_mp)], second[len(over_mp) :]


def lookup_kernel(count_ref, key_ref, table_ref, out_ref, rows_ref):
    spots = rows_ref.shape[0]
    rows_ref[...] = jnp.zeros_like(rows_ref)

    def one(i, carry):
        key = key_ref[i]
        rows_ref[pl.ds(key % spots, 1), :] = table_ref[pl.ds(key // spots, 1), :]
        return carry

    lax.fori_loop(0, count_ref[0], one, 0)

    def narrow(i, carry):
        at = pl.ds(pl.multiple_of(i * 256, 256), 256)
        out_ref[at, :] = rows_ref[at, :].astype(jnp.bfloat16)
        return carry

    lax.fori_loop(0, spots // 256, narrow, 0)


def lookup(keys, count, table, spots):
    width = table.shape[1]
    smem = pl.BlockSpec(memory_space=pltpu.SMEM)
    vmem = pl.BlockSpec(memory_space=pltpu.VMEM)
    return pl.pallas_call(
        lookup_kernel,
        out_shape=jax.ShapeDtypeStruct((spots, width), jnp.bfloat16),
        in_specs=[smem, smem, vmem],
        out_specs=vmem,
        scratch_shapes=[pltpu.VMEM((spots, width), jnp.float32)],
        compiler_params=pltpu.CompilerParams(vmem_limit_bytes=VMEM_CAP),
        cost_estimate=pl.CostEstimate(flops=0, bytes_accessed=8 * spots * width, transcendentals=0),
        name="lookup",
    )(count, keys, table)


def scatter_kernel(count_ref, key_ref, head_ref, rows_in_ref, grad_ref, rows_ref):
    spots = rows_ref.shape[0]
    vocab = grad_ref.shape[0]

    def widen(i, carry):
        at = pl.ds(pl.multiple_of(i * 256, 256), 256)
        rows_ref[at, :] = rows_in_ref[at, :].astype(jnp.float32)
        return carry

    lax.fori_loop(0, spots // 256, widen, 0)
    grad_ref[...] = head_ref[...].astype(jnp.float32)

    def one(i, carry):
        key = key_ref[i]
        grad_ref[pl.ds(key // spots, 1), :] += rows_ref[pl.ds(key % spots, 1), :]
        return carry

    lax.fori_loop(0, count_ref[0], one, 0)


def scatter(keys, count, head_grad, rows):
    spots, width = rows.shape
    vocab = head_grad.shape[0]
    smem = pl.BlockSpec(memory_space=pltpu.SMEM)
    vmem = pl.BlockSpec(memory_space=pltpu.VMEM)
    return pl.pallas_call(
        scatter_kernel,
        out_shape=jax.ShapeDtypeStruct((vocab, width), jnp.float32),
        in_specs=[smem, smem, vmem, vmem],
        out_specs=vmem,
        scratch_shapes=[pltpu.VMEM((spots, width), jnp.float32)],
        compiler_params=pltpu.CompilerParams(vmem_limit_bytes=VMEM_CAP),
        cost_estimate=pl.CostEstimate(flops=0, bytes_accessed=16 * spots * width, transcendentals=0),
        name="scatter",
    )(count, keys, head_grad, rows)


def norm_parts(values):
    centre = jnp.mean(values, axis=-1, keepdims=True)
    centred = values - centre
    scale = lax.rsqrt(jnp.mean(centred * centred, axis=-1, keepdims=True) + EPS_NORM)
    return centred * scale, scale


def norm_pull(values, gain, upstream):
    normed, scale = norm_parts(values)
    weighted = upstream * gain
    pulled = scale * (
        weighted
        - jnp.mean(weighted, axis=-1, keepdims=True)
        - normed * jnp.mean(weighted * normed, axis=-1, keepdims=True)
    )
    return (
        pulled,
        jnp.sum(upstream * normed, axis=0, keepdims=True),
        jnp.sum(upstream, axis=0, keepdims=True),
    )


def step_first(total, at, ins, outs):
    stream, norms = ins
    normed, scale = norm_parts(stream[at, :].astype(jnp.float32))
    return normed * norms[0:1, :] + norms[1:2, :]


def step_lookup(total, at, ins, outs):
    outs[0][at, :] = total.astype(jnp.bfloat16)


def step_forward(row, total, at, ins, outs):
    stream, norms = ins
    values = stream[at, :].astype(jnp.float32) + total
    outs[0][at, :] = values
    normed, scale = norm_parts(values)
    return normed * norms[row : row + 1, :] + norms[row + 1 : row + 2, :]


def step_backward(row, total, at, ins, outs):
    stream, norms = ins[:2]
    pulled, dgain, dshift = norm_pull(
        stream[at, :].astype(jnp.float32), norms[row : row + 1, :], total
    )
    if len(ins) > 2:
        pulled = pulled + ins[2][at, :]
    outs[0][at, :] = pulled.astype(outs[0].dtype)
    first = at.start == 0

    @pl.when(first)
    def _():
        outs[1][...] = jnp.zeros_like(outs[1])

    outs[1][0:1, :] += dgain
    outs[1][1:2, :] += dshift
    return pulled


def step_pass(total, at, ins, outs):
    return ins[0][at, :]


def gelu_tanh(values):
    return jax.nn.gelu(values, approximate=True)


def score_block(mixed, starts):
    place = jnp.arange(mixed.shape[0], dtype=jnp.int32)
    allowed = (place[None, :] <= place[:, None]) & (place[None, :] >= starts[:, None])
    raw = jnp.einsum(
        "qhe,khe->hqk", mixed[:, :, 0], mixed[:, :, 1], preferred_element_type=jnp.float32
    )
    return jnp.where(allowed[None], raw * HD ** (-0.5), MASKED)


def attend_forward(mixed, starts):
    scores = score_block(mixed, starts)
    highest = jnp.max(scores, axis=-1, keepdims=True)
    weights = jnp.exp(scores - highest)
    totals = jnp.sum(weights, axis=-1, keepdims=True)
    probs = (weights / totals).astype(jnp.bfloat16)
    result = jnp.einsum(
        "hqk,khe->qhe", probs, mixed[:, :, 2], preferred_element_type=jnp.float32
    )
    return (result.astype(jnp.bfloat16), highest[:, :, 0] + jnp.log(totals[:, :, 0]))


def attend_backward(mixed, starts, log_rows, upstream):
    scores = score_block(mixed, starts)
    probs = jnp.exp(scores - log_rows[:, :, None])
    dprobs = jnp.einsum(
        "qhe,khe->hqk", upstream, mixed[:, :, 2], preferred_element_type=jnp.float32
    )
    dvalues = jnp.einsum(
        "hqk,qhe->khe", probs.astype(jnp.bfloat16), upstream, preferred_element_type=jnp.float32
    )
    inner = jnp.sum(probs * dprobs, axis=-1, keepdims=True)
    dscores = (probs * (dprobs - inner)).astype(jnp.bfloat16)
    dquery = jnp.einsum(
        "hqk,khe->qhe", dscores, mixed[:, :, 1], preferred_element_type=jnp.float32
    ) * HD ** (-0.5)
    dkeys = jnp.einsum(
        "hqk,qhe->khe", dscores, mixed[:, :, 0], preferred_element_type=jnp.float32
    ) * HD ** (-0.5)
    return jnp.stack([dquery, dkeys, dvalues], axis=2).astype(jnp.bfloat16)


def local(
    token_ids,
    targets,
    starts,
    sources,
    embedding,
    w_qkv,
    w_out,
    w_fc,
    w_proj,
    norm_params,
    rows_table,
    cols_table,
    rows_qkv,
    cols_qkv,
    rows_out,
    cols_out,
    rows_fc,
    cols_fc,
    rows_proj,
    cols_proj,
    second_norms,
):
    bf16 = jnp.bfloat16
    f32 = jnp.float32
    size_mp = lax.axis_size("mp")
    size_dp = lax.axis_size("dp")
    dp = lax.axis_index("dp")
    mp = lax.axis_index("mp")
    tokens = token_ids.shape[0]
    seqs = tokens // LEN
    chips = size_mp // 2
    near = chips // seqs
    sharers = size_mp // seqs
    rows = tokens // size_mp
    vocab, part_width = embedding.shape
    width = part_width * size_dp
    first_row = mp * vocab
    spots = tokens * size_dp
    chunks_full = max(1, min(8, rows // 32))
    chunks_near = max(1, min(4, rows // 32))

    both = jnp.stack([token_ids, sources]).reshape(-1, 128)
    both = small_gather("gather_ids", 0, both, "dp").reshape(size_dp, 2, tokens)
    all_ids = both[:, 0]
    all_sources = both[:, 1].reshape(-1)
    counts = jnp.sum(
        (all_sources[:, None] == jnp.arange(NSRC, dtype=jnp.int32)[None, :]).astype(f32), axis=0
    )


    def own_and_twins(weight, axis):
        weight = weight.astype(bf16)
        found = [weight]
        for turn in range(1, seqs):
            shift = [(i, (i + turn * sharers) % size_mp) for i in range(size_mp)]
            found.append(lax.ppermute(weight, "mp", shift))
        return jnp.concatenate(found, axis=axis) if seqs > 1 else weight

    wide_qkv = lax.all_gather(own_and_twins(w_qkv, 1), "dp", axis=0, tiled=True)
    wide_out = lax.all_gather(own_and_twins(w_out, 0), "dp", axis=1, tiled=True)
    wide_fc = lax.all_gather(own_and_twins(w_fc, 1), "dp", axis=0, tiled=True)
    wide_proj = lax.all_gather(own_and_twins(w_proj, 0), "dp", axis=1, tiled=True)
    wide_table = lax.all_gather(embedding.astype(bf16), "dp", axis=1, tiled=True)

    place = (
        (jnp.arange(size_mp, dtype=jnp.int32) * size_dp)[None, :, None] * rows
        + (jnp.arange(size_dp, dtype=jnp.int32) * rows)[:, None, None]
        + jnp.arange(rows, dtype=jnp.int32)[None, None, :]
    ).reshape(size_dp, tokens)
    local_ids = all_ids - first_row
    inside = (local_ids >= 0) & (local_ids < vocab)
    keys = jnp.where(inside, local_ids * spots + place, jnp.iinfo(jnp.int32).max)
    keys = jnp.sort(keys.reshape(-1))
    owned = jnp.sum(inside.astype(jnp.int32)).reshape(1)
    found = lookup(keys, owned, embedding, spots)
    (picked_rows,) = line_call(
        "rs_lookup",
        1,
        found,
        [],
        [jax.ShapeDtypeStruct((size_dp * rows, part_width), bf16)],
        step_lookup,
        size_dp * rows,
        part_width,
        chunks_full,
        chips,
        0,
    )
    stream0 = lax.all_to_all(
        picked_rows.reshape(size_dp, rows, part_width), "dp", 0, 0, tiled=False
    )
    stream0 = jnp.swapaxes(stream0, 0, 1).reshape(rows, width)

    row_f32 = jax.ShapeDtypeStruct((rows, width), f32)
    pair_f32 = jax.ShapeDtypeStruct((8, width), f32)
    (inner_one,) = line_call(
        "ag_inner1", 2, None, [stream0, norm_params], [], step_first, rows, width, chunks_near, 0, near
    )
    heads = wide_qkv.shape[1] // (3 * HD)
    my_starts = row_slice(starts, (mp // sharers) * LEN, LEN)
    mixed = jnp.dot(inner_one, wide_qkv, preferred_element_type=f32).astype(bf16)
    mixed = mixed.reshape(LEN, heads, 3, HD)
    attended, log_sums = attend_forward(mixed, my_starts)
    attended = attended.reshape(LEN, heads * HD)
    partial = jnp.dot(attended, wide_out, preferred_element_type=f32).astype(bf16)
    inner_two, stream1 = line_call(
        "attn_sum",
        3,
        partial,
        [stream0, norm_params],
        [row_f32],
        functools.partial(step_forward, 2),
        rows,
        width,
        chunks_near,
        near,
        near,
    )
    before = jnp.dot(inner_two, wide_fc, preferred_element_type=f32)
    hidden = gelu_tanh(before).astype(bf16)
    partial = jnp.dot(hidden, wide_proj, preferred_element_type=f32).astype(bf16)
    final, stream2 = line_call(
        "mlp_sum",
        4,
        partial,
        [stream1, norm_params],
        [row_f32],
        functools.partial(step_forward, 4),
        rows,
        width,
        chunks_full,
        near,
        chips,
    )

    edge = jnp.clip(VREAL - first_row, 0, vocab).astype(jnp.int32).reshape(1)
    wanted = targets - first_row
    wanted = jnp.where((wanted >= 0) & (wanted < vocab), wanted, -1).reshape(1, tokens)
    block = 640
    exps, tops, sums, picks = head_stats(wide_table, final, wanted, edge, block)
    tops = tops[:, 0]
    top = jnp.max(tops, axis=0)
    total = jnp.sum(sums[:, 0] * jnp.exp(tops - top[None, :]), axis=0)
    pick = jnp.sum(picks[:, 0], axis=0)
    stats = small_gather("gather_stats", 5, packed([top, total, pick]), "mp")
    stats = stats.reshape(size_mp, -1)[:, : 3 * tokens].reshape(size_mp, 3, tokens)
    highest = jnp.max(stats[:, 0], axis=0)
    log_total = highest + jnp.log(
        jnp.sum(stats[:, 1] * jnp.exp(stats[:, 0] - highest[None, :]), axis=0)
    )
    token_loss = log_total - jnp.sum(stats[:, 2], axis=0)
    member = (sources[:, None] == jnp.arange(NSRC, dtype=jnp.int32)[None, :]).astype(f32)
    loss_part = jnp.sum(member * token_loss[:, None], axis=0)
    weight = jnp.sum(member / (NSRC * jnp.maximum(counts, 1.0))[None, :], axis=1)
    scale = jnp.exp(tops - log_total[None, :]) * weight[None, :]
    table_grad, dfinal = head_back(
        exps, wide_table, final, scale[:, None, :], weight[None, :], wanted, block
    )
    head_grad = lax.psum_scatter(table_grad, "dp", scatter_dimension=1, tiled=True)

    dbranch2, dstream2, norm3 = line_call(
        "final_back",
        6,
        dfinal.astype(bf16),
        [stream2, norm_params],
        [row_f32, pair_f32],
        functools.partial(step_backward, 4),
        rows,
        width,
        chunks_full,
        chips,
        near,
    )
    grad_proj = jnp.einsum("tf,td->fd", hidden, dbranch2, preferred_element_type=f32).astype(bf16)
    dhidden = jnp.einsum("td,fd->tf", dbranch2, wide_proj, preferred_element_type=f32)
    unused, gelu_pull = jax.vjp(gelu_tanh, before)
    dbefore = gelu_pull(dhidden)[0].astype(bf16)
    partial = jnp.einsum("tf,df->td", dbefore, wide_fc, preferred_element_type=f32).astype(bf16)
    dbranch1, dstream1, norm2 = line_call(
        "mlp_back",
        7,
        partial,
        [stream1, norm_params, dstream2],
        [row_f32, pair_f32],
        functools.partial(step_backward, 2),
        rows,
        width,
        chunks_near,
        near,
        near,
    )
    grad_fc = jnp.einsum("td,tf->df", inner_two, dbefore, preferred_element_type=f32).astype(bf16)
    grad_out = jnp.einsum("tf,td->fd", attended, dbranch1, preferred_element_type=f32).astype(bf16)
    dattended = jnp.einsum("td,fd->tf", dbranch1, wide_out, preferred_element_type=f32)
    dattended = dattended.astype(bf16).reshape(LEN, heads, HD)
    dmixed = attend_backward(mixed, my_starts, log_sums, dattended)
    dmixed = dmixed.reshape(LEN, heads * 3 * HD)
    partial = jnp.einsum("tc,dc->td", dmixed, wide_qkv, preferred_element_type=f32).astype(bf16)
    dstream0, norm1 = line_call(
        "attn_back",
        8,
        partial,
        [stream0, norm_params, dstream1],
        [jax.ShapeDtypeStruct((rows, width), bf16), pair_f32],
        functools.partial(step_backward, 0),
        rows,
        width,
        chunks_near,
        near,
        0,
    )
    grad_qkv = jnp.einsum("td,tc->dc", inner_one, dmixed, preferred_element_type=f32).astype(bf16)

    def to_owner(gradient, cut, axis):
        share = lax.psum_scatter(gradient, "dp", scatter_dimension=cut, tiled=True)
        pieces = jnp.split(share, seqs, axis=axis)
        mine = pieces[0].astype(f32)
        for turn in range(1, seqs):
            back = [(i, (i - turn * sharers) % size_mp) for i in range(size_mp)]
            mine = mine + lax.ppermute(pieces[turn], "mp", back).astype(f32)
        return mine

    grad_proj = to_owner(grad_proj, 1, 0)
    grad_fc = to_owner(grad_fc, 0, 1)
    grad_out = to_owner(grad_out, 1, 0)
    grad_qkv = to_owner(grad_qkv, 0, 1)

    sent = jnp.swapaxes(dstream0.reshape(rows, size_dp, part_width), 0, 1)
    sent = lax.all_to_all(sent, "dp", 0, 0, tiled=False).reshape(size_dp * rows, part_width)
    (drows,) = line_call(
        "ag_lookup",
        9,
        None,
        [sent],
        [],
        step_pass,
        size_dp * rows,
        part_width,
        chunks_full,
        0,
        chips,
    )
    grad_table = scatter(keys, owned, head_grad, drows)

    beta = 1.0 - STEP ** (-0.8)
    weights = (embedding, w_qkv, w_out, w_fc, w_proj)
    grads = (grad_table, grad_qkv, grad_out, grad_fc, grad_proj)
    rows_old = (rows_table, rows_qkv, rows_out, rows_fc, rows_proj)
    cols_old = (cols_table, cols_qkv, cols_out, cols_fc, cols_proj)
    row_span = (size_mp, size_dp, size_mp, size_dp, size_mp)
    col_span = (size_dp, size_mp, size_dp, size_mp, size_dp)
    squares = [gradient * gradient + EPS_ONE for gradient in grads]
    row_parts = [jnp.sum(square, axis=1) for square in squares]
    col_parts = [jnp.sum(square, axis=0) for square in squares]
    square_sums = jnp.stack([jnp.sum(part) for part in col_parts])
    weight_sums = jnp.stack([jnp.sum(value * value) for value in weights])
    old_sums = jnp.stack([jnp.sum(old) / span for old, span in zip(rows_old, col_span)])
    norm_partial = jnp.concatenate([norm1[:2], norm2[:2], norm3[:2]])
    on_dp, on_mp, on_all = small_sum(
        "sum_squares",
        10,
        [col_parts[1], col_parts[3], row_parts[0], row_parts[2], row_parts[4], loss_part],
        [row_parts[1], row_parts[3], col_parts[0], col_parts[2], col_parts[4]],
        [square_sums, weight_sums, old_sums, norm_partial],
    )
    square_sums, weight_sums, old_sums, grad_norms = on_all
    loss_sums = on_dp[5]
    row_full = (on_dp[2], on_mp[0], on_dp[3], on_mp[1], on_dp[4])
    col_full = (on_mp[2], on_dp[0], on_mp[3], on_dp[1], on_mp[4])
    rows_new = []
    cols_new = []
    steps = []
    entries = []
    for index in range(5):
        full_rows = grads[index].shape[0] * row_span[index]
        full_cols = grads[index].shape[1] * col_span[index]
        entries.append(full_rows * full_cols)
        rows_next = beta * rows_old[index] + (1.0 - beta) * row_full[index] / full_cols
        cols_next = beta * cols_old[index] + (1.0 - beta) * col_full[index] / full_rows
        mean = beta * old_sums[index] / full_rows + (1.0 - beta) * (
            square_sums[index] / (full_rows * full_cols)
        )
        rows_new.append(rows_next)
        cols_new.append(cols_next)
        steps.append(
            grads[index] * lax.rsqrt(rows_next[:, None] * cols_next[None, :] / mean)
        )
    step_part = jnp.stack([jnp.sum(piece * piece) for piece in steps])
    unused, unused, (step_sq,) = small_sum("sum_steps", 12, [], [], [step_part])
    updated = []
    for index in range(5):
        clipped = steps[index] / jnp.maximum(1.0, jnp.sqrt(step_sq[index] / entries[index]) / CLIP)
        rate = RHO * jnp.sqrt(weight_sums[index] / entries[index])
        updated.append(weights[index] - rate * clipped)
    second_new = beta * second_norms + (1.0 - beta) * (grad_norms * grad_norms + EPS_ONE)
    norm_steps = grad_norms * lax.rsqrt(second_new)
    norm_steps = norm_steps / jnp.maximum(1.0, jnp.sqrt(jnp.mean(norm_steps * norm_steps)) / CLIP)
    norms_new = norm_params - RHO * jnp.sqrt(jnp.mean(norm_params * norm_params)) * norm_steps
    return (
        loss_sums,
        counts,
        grad_table,
        rows_new[0],
        cols_new[0],
        updated[0],
        grad_qkv,
        rows_new[1],
        cols_new[1],
        updated[1],
        grad_out,
        rows_new[2],
        cols_new[2],
        updated[2],
        grad_fc,
        rows_new[3],
        cols_new[3],
        updated[3],
        grad_proj,
        rows_new[4],
        cols_new[4],
        updated[4],
        grad_norms,
        second_new,
        norms_new,
    )


def solution(mesh):
    placed = (
        P("dp"),
        P("dp"),
        P("dp"),
        P("dp"),
        P("mp", "dp"),
        P("dp", "mp"),
        P("mp", "dp"),
        P("dp", "mp"),
        P("mp", "dp"),
        P(),
        P("mp"),
        P("dp"),
        P("dp"),
        P("mp"),
        P("mp"),
        P("dp"),
        P("dp"),
        P("mp"),
        P("mp"),
        P("dp"),
        P(),
    )
    return jax.shard_map(
        local,
        mesh=mesh,
        in_specs=placed,
        out_specs=(
            P(),
            P(),
            P("mp", "dp"),
            P("mp"),
            P("dp"),
            P("mp", "dp"),
            P("dp", "mp"),
            P("dp"),
            P("mp"),
            P("dp", "mp"),
            P("mp", "dp"),
            P("mp"),
            P("dp"),
            P("mp", "dp"),
            P("dp", "mp"),
            P("dp"),
            P("mp"),
            P("dp", "mp"),
            P("mp", "dp"),
            P("mp"),
            P("dp"),
            P("mp", "dp"),
            P(),
            P(),
            P(),
        ),
        check_vma=False,
    )
```

time: 1650 us -> 1030 us (0.62)
  waiting for transfers between devices: 846 us -> 178 us
  Pallas kernels: 0 us -> 531 us
  matrix products: 321 us -> 94.8 us
  blocking collectives: 184 us -> 23.9 us
  other arithmetic: 214 us -> 99.7 us
  starting transfers between devices: 1.26 us -> 19.8 us
    pallas_call x0 -> x18, Pallas kernels: none -> 531 us  [the longest x8 307 us: line_call(): return list(call(*args))]
    psum x6 -> x0, waiting for transfers between devices: 515 us -> none  [the longest x3 259 us: sum_grads(): lax.psum(term(0, tokens).astype(jnp.bfloat16), 'mp').astype(jnp.float32)]
    dot_general x40 -> x17, matrix products: 316 us -> 92 us  [the longest x1 14 us: attend_backward(): jnp.einsum('qhe,khe->hqk', upstream, mixed[:, :, 2], preferred_element_ty...]
    all_gather x3 -> x4, waiting for transfers between devices: 164 us -> 0.06 us  [the longest x1 0.02 us: local(): lax.all_gather(embedding.astype(bf16), 'dp', axis=1, tiled=True)]
    psum x6 -> x0, blocking collectives: 147 us -> none  [the longest x1 42.1 us: local(): lax.psum(jnp.stack([jnp.sum(piece * piece) for piece in steps]), ('dp', '...]
    ppermute x0 -> x8, waiting for transfers between devices: none -> 61.7 us  [the longest x4 38.8 us: own_and_twins(): found.append(lax.ppermute(weight, 'mp', shift))]
    reduce_sum x33 -> x28, other arithmetic: 88.9 us -> 36.6 us  [the longest x5 13.9 us: local(): weight_sums = jnp.stack([jnp.sum(value * value) for value in weights])]
    reduce_scatter x5, waiting for transfers between devices: 166 us -> 116 us  [the longest x1 110 us: local(): lax.psum_scatter(table_grad, 'dp', scatter_dimension=1, tiled=True)]
  transfers between devices with their start and end apart: 14 -> 19, of which waited for: 12 -> 8; matrix products, arithmetic and copies ran while one was open for 8% -> 11% of each run, Pallas kernels for 0% -> 25%
where the time goes in v1:
time: 1030 us; the launch traced here: 1010 us
  Pallas kernels  531 us (52%)
  waiting for transfers between devices  178 us (17%)
  other arithmetic  99.7 us (10%)
  matrix products  94.8 us (9%)
  local copies, waits for them, and re-layouts  33.6 us (3%)
  between operations  33.4 us (3%)
  blocking collectives  23.9 us (2%)
  starting transfers between devices  19.8 us (2%)
    pallas_call x8, Pallas kernels, line_call(): return list(call(*args))  307 us
    reduce_scatter x1, waiting for transfers between devices, local(): lax.psum_scatter(table_grad, 'dp', scatter_dimension=1, tiled=True)  110 us
    pallas_call x1, Pallas kernels, head_back(): pl.pallas_call(functools.partial(head_back_kernel, rows, block, tile), gr...  70.6 us
    pallas_call x1, Pallas kernels, head_stats(): pl.pallas_call(functools.partial(head_stats_kernel, block, tile), grid=(s...  47.1 us
    pallas_call x6, Pallas kernels, small_gather(): pl.pallas_call(functools.partial(small_gather_kernel, axis, count), out_s...  43.9 us
    ppermute x4, waiting for transfers between devices, own_and_twins(): found.append(lax.ppermute(weight, 'mp', shift))  38.8 us
    pallas_call x1, Pallas kernels, scatter(): pl.pallas_call(scatter_kernel, out_shape=jax.ShapeDtypeStruct((vocab, wid...  31.7 us
    pallas_call x1, Pallas kernels, lookup(): pl.pallas_call(lookup_kernel, out_shape=jax.ShapeDtypeStruct((spots, widt...  30.4 us
  transfers between devices with their start and end apart: 19, of which 8 were waited for; matrix products, arithmetic and copies ran while one was open for 11% of the time, Pallas kernels for 25%

profile of v1, /device:TPU:0, one launch (start us, length us, event | category | flops | bytes accessed | tf_op | source)
XLA Modules:
  0.0 1014.3 jit_solution(5355602809659384416)
XLA Ops:
  7.3 1.9 multiply_reduce_fusion.8
  9.1 4.0 collective-permute-start
  13.2 9.1 collective-permute-done
  23.1 1.9 multiply_reduce_fusion.6
  25.1 14.0 %collective-permute-done.2 = bf16[256,512]{1,0:T(8,128)(2,1)S(1)} collective-permute-done((bf16[256,512]{1,0:T(8,128)(2,1)S(1)}, bf16[256,512]{1,0:T(8,128)(2,1)S(1)}, u32[]{:S(2)}, u32[]{:S(2)}) %collective-permute-start.2) | collective-permute-done | bytes 262176 | tf_op jit(solution)/shard_map/ppermute | solution.py:757
  40.8 13.1 %collective-permute-done.3 = bf16[512,256]{1,0:T(8,128)(2,1)S(1)} collective-permute-done((bf16[512,256]{1,0:T(8,128)(2,1)S(1)}, bf16[512,256]{1,0:T(8,128)(2,1)S(1)}, u32[]{:S(2)}, u32[]{:S(2)}) %collective-permute-start.3) | collective-permute-done | bytes 262176 | tf_op jit(solution)/shard_map/ppermute | solution.py:757
  54.8 8.7 multiply_reduce_fusion.2
  64.2 6.2 gather_ids.1
  72.4 6.8 sort.14
  79.1 30.4 %lookup.1.refs_0_ = bf16[8192,256]{1,0:T(8,128)(2,1)} custom-call(s32[1]{0:T(128)} %bitcast.2.count_ref, s32[8192]{0:T(1024)} %get-tuple-element.45.key_ref, f32[6288,256]{1,0:T(8,128)} %table_ref.1), custom_call_target="tpu_custom_call" | custom-call | bytes 16777216 | tf_op jit(solution)/shard_map/lookup/pallas_call | solution.py:544
  109.6 45.5 %rs_lookup.1 = bf16[1024,256]{1,0:T(8,128)(2,1)} custom-call(bf16[8192,256]{1,0:T(8,128)(2,1)} %lookup.1.refs_0_), custom_call_target="tpu_custom_call" | custom-call | tf_op jit(solution)/shard_map/rs_lookup/pallas_call | solution.py:315
  155.0 3.9 all-to-all-start
  162.9 2.6 collective-permute-done.1
  165.5 23.9 %all_gather.17 = bf16[256,1024]{1,0:T(8,128)(2,1)S(1)} all-gather(bf16[256,256]{1,0:T(8,128)(2,1)S(1)} %pad_maximum_fusion.4), channel_id=1, replica_groups=mesh['dp'=4,'mp'=8] {'dp'}, dimensions={1}, use_global_device_ids=true | all-gather | bytes 655360 | tf_op jit(solution)/shard_map/all_gather | solution.py:761
  190.3 16.7 %ag_inner1.1 = bf16[1024,1024]{1,0:T(8,128)(2,1)} custom-call(bf16[256,1024]{1,0:T(8,128)(2,1)} %bitcast.218, f32[6,1024]{1,0:T(8,128)} %refs_2_.9), custom_call_target="tpu_custom_call" | custom-call | tf_op jit(solution)/shard_map/ag_inner1/pallas_call | solution.py:315
  207.0 4.1 convolution_convert_fusion.7
  211.1 7.6 fusion.74
  218.7 8.0 fusion
  226.7 7.4 fusion.22
  234.1 2.1 convolution_convert_fusion.4.refs_0_
  236.2 32.3 %attn_sum.1 = (bf16[1024,1024]{1,0:T(8,128)(2,1)}, f32[256,1024]{1,0:T(8,128)}) custom-call(bf16[1024,1024]{1,0:T(8,128)(2,1)} %convolution_convert_fusion.4.refs_0_, bf16[256,1024]{1,0:T(8,128)(2,1)} %bitcast.219, f32[6,1024]{1,0:T(8,128)} %refs_2_.9), custom_call_target="tpu_custom_call" | custom-call | tf_op jit(solution)/shard_map/attn_sum/pallas_call | solution.py:315
  268.6 6.6 fusion.75
  275.2 6.8 convolution_convert_fusion.3.refs_0_
  282.0 58.0 %mlp_sum.1 = (bf16[2048,1024]{1,0:T(8,128)(2,1)}, f32[256,1024]{1,0:T(8,128)}) custom-call(bf16[1024,1024]{1,0:T(8,128)(2,1)} %convolution_convert_fusion.3.refs_0_, f32[256,1024]{1,0:T(8,128)} %get-tuple-element.47.refs_1_, f32[6,1024]{1,0:T(8,128)} %refs_2_.9), custom_call_target="tpu_custom_call" | custom-call | tf_op jit(solution)/shard_map/mlp_sum/pallas_call | solution.py:315
  340.1 47.1 %head_stats.1 = (bf16[6400,2048]{1,0:T(8,128)(2,1)}, f32[10,1,2048]{2,1,0:T(1,128)}, f32[10,1,2048]{2,1,0:T(1,128)}, f32[10,1,2048]{2,1,0:T(1,128)}) custom-call(bf16[6288,1024]{1,0:T(8,128)(2,1)} %all-gather.7.cloned.1.call-done.table_ref, bf16[2048,1024]{1,0:T(8,128)(2,1)} %get-tuple-element.48.final_ref, s32[1,2048]{1,0:T(1,128)} %bitcast.253, ...), custom_call_target="tpu_custom_call" | custom-call | flops 26373783552 | bytes 38633472 | tf_op jit(solution)/shard_map/head_stats/pallas_call | solution.py:353
  390.7 7.9 gather_stats.1
  401.7 70.6 %head_back.1 = (bf16[6288,1024]{1,0:T(8,128)(2,1)}, f32[2048,1024]{1,0:T(8,128)}) custom-call(bf16[6400,2048]{1,0:T(8,128)(2,1)} %get-tuple-element.49.exp_ref, bf16[6288,1024]{1,0:T(8,128)(2,1)} %all-gather.7.cloned.1.call-done.table_ref, bf16[2048,1024]{1,0:T(8,128)(2,1)} %get-tuple-element.48.final_ref, ...), custom_call_target="tpu_custom_call" | custom-call | flops 52747567104 | bytes 51511296 | tf_op jit(solution)/shard_map/head_back/pallas_call | solution.py:417
  472.2 6.1 convert_element_type.143.refs_0_
  478.3 59.1 %final_back.1 = (bf16[1024,1024]{1,0:T(8,128)(2,1)}, f32[256,1024]{1,0:T(8,128)}, f32[8,1024]{1,0:T(8,128)}) custom-call(bf16[2048,1024]{1,0:T(8,128)(2,1)} %convert_element_type.143.refs_0_, f32[256,1024]{1,0:T(8,128)} %get-tuple-element.54.refs_1_, f32[6,1024]{1,0:T(8,128)} %refs_2_.9), custom_call_target="tpu_custom_call" | custom-call | tf_op jit(solution)/shard_map/final_back/pallas_call | solution.py:315
  537.4 7.2 fusion.15
  544.6 3.8 convolution_convert_fusion.2.refs_0_
  548.4 34.1 %mlp_back.1 = (bf16[1024,1024]{1,0:T(8,128)(2,1)}, f32[256,1024]{1,0:T(8,128)}, f32[8,1024]{1,0:T(8,128)}) custom-call(bf16[1024,1024]{1,0:T(8,128)(2,1)} %convolution_convert_fusion.2.refs_0_, f32[256,1024]{1,0:T(8,128)} %get-tuple-element.47.refs_1_, f32[6,1024]{1,0:T(8,128)} %refs_2_.9, f32[256,1024]{1,0:T(8,128)} %get-tuple-element.56.refs_3_), custom_call_target="tpu_custom_call" | custom-call | tf_op jit(solution)/shard_map/mlp_back/pallas_call | solution.py:315
  582.5 2.5 convolution_convert_fusion.9
  585.0 14.0 %multiply_reduce_fusion = (f32[4,1024]{1,0:T(4,128)}, f32[4,1024,1024]{1,2,0:T(8,128)}) fusion(f32[4,1024,1024]{1,2,0:T(8,128)} %get-tuple-element.139, f32[4,1024]{1,0:T(4,128)S(1)} %log_add_fusion, bf16[1024,4,64]{0,2,1:T(8,128)(2,1)S(1)} %bitcast.221, bf16[1024,4,3,64]{0,3,2,1:T(8,128)(2,1)S(1)} %bitcast.228), kind=kOutput, calls=%fused_computation.1 | convolution fusion | flops 549449728 | bytes 34635776 | tf_op jit(solution)/shard_map/qhe,khe->hqk/dot_general | solution.py:684
  600.2 2.8 fusion.23
  603.0 3.1 convolution_convert_fusion.8
  606.1 11.8 %multiply_convert_fusion = bf16[4,1024,1024]{1,2,0:T(8,128)(2,1)S(1)} fusion(f32[4,1024,1024]{1,2,0:T(8,128)} %get-tuple-element.141, f32[4,1024,1024]{1,2,0:T(8,128)} %get-tuple-element.139, f32[4,1024]{1,0:T(4,128)} %get-tuple-element.140, f32[4,1024]{1,0:T(4,128)S(1)} %log_add_fusion), kind=kLoop, calls=%fused_computation | loop fusion | flops 16777216 | bytes 41975808 | tf_op jit(solution)/shard_map/convert_element_type | solution.py:691
  618.0 3.2 copy-done
  622.9 6.0 fusion.26
  630.5 3.1 convolution_convert_fusion.6
  633.8 6.0 convolution_convert_fusion.1
  639.9 7.1 convolution_convert_fusion
  648.4 3.2 convolution_convert_fusion.5.refs_0_
  651.6 19.5 %attn_back.1 = (bf16[256,1024]{1,0:T(8,128)(2,1)}, f32[8,1024]{1,0:T(8,128)}) custom-call(bf16[1024,1024]{1,0:T(8,128)(2,1)} %convolution_convert_fusion.5.refs_0_, bf16[256,1024]{1,0:T(8,128)(2,1)} %bitcast.220, f32[6,1024]{1,0:T(8,128)} %refs_2_.9, f32[256,1024]{1,0:T(8,128)} %get-tuple-element.59.refs_3_), custom_call_target="tpu_custom_call" | custom-call | tf_op jit(solution)/shard_map/attn_back/pallas_call | solution.py:315
  671.1 1.9 copy.131
  673.0 3.5 all-to-all-start.1
  684.1 3.3 stack.115
  693.0 42.1 %ag_lookup.1.rows_in_ref = bf16[8192,256]{1,0:T(8,128)(2,1)} custom-call(bf16[1024,256]{1,0:T(8,128)(2,1)} %bitcast.224), custom_call_target="tpu_custom_call" | custom-call | tf_op jit(solution)/shard_map/ag_lookup/pallas_call | solution.py:315
  737.8 3.0 collective-permute-start.5
  740.8 12.6 %collective-permute-done.4 = bf16[256,384]{1,0:T(8,128)(2,1)S(1)} collective-permute-done((bf16[256,384]{1,0:T(8,128)(2,1)S(1)}, bf16[256,384]{1,0:T(8,128)(2,1)S(1)}, u32[]{:S(2)}, u32[]{:S(2)}) %collective-permute-start.4) | collective-permute-done | bytes 196640 | tf_op jit(solution)/shard_map/ppermute | solution.py:921
  755.1 5.6 reduce-scatter.14.cloned.1.call-done
  761.7 2.5 collective-permute-start.7
  766.0 10.3 %collective-permute-done.7 = bf16[512,256]{1,0:T(8,128)(2,1)S(1)} collective-permute-done((bf16[512,256]{1,0:T(8,128)(2,1)S(1)}, bf16[512,256]{1,0:T(8,128)(2,1)S(1)}, u32[]{:S(2)}, u32[]{:S(2)}) %collective-permute-start.7) | collective-permute-done | bytes 262176 | tf_op jit(solution)/shard_map/ppermute | solution.py:921
  778.1 110.0 %reduce-scatter.10.cloned.1.call-done.head_ref = bf16[6288,256]{1,0:T(8,128)(2,1)} async-done(((bf16[6288,1024]{1,0:T(8,128)(2,1)}), bf16[6288,256]{1,0:T(8,128)(2,1)}) %reduce-scatter.10.cloned.1.call-update) | async-done | bytes 3219472 | tf_op jit(solution)/shard_map/reduce_scatter | solution.py:860
  888.0 31.7 %scatter.1 = f32[6288,256]{1,0:T(8,128)} custom-call(s32[1]{0:T(128)} %bitcast.2.count_ref, s32[8192]{0:T(1024)} %get-tuple-element.45.key_ref, bf16[6288,256]{1,0:T(8,128)(2,1)} %reduce-scatter.10.cloned.1.call-done.head_ref, bf16[8192,256]{1,0:T(8,128)(2,1)} %ag_lookup.1.rows_in_ref), custom_call_target="tpu_custom_call" | custom-call | bytes 33554432 | tf_op jit(solution)/shard_map/scatter/pallas_call | solution.py:581
  919.8 6.6 fusion.6
  926.4 3.3 stack.109
  930.4 7.2 sum_squares_dp.1
  939.8 9.3 sum_squares_mp.1
  958.9 6.2 multiply_reduce_fusion.1
  968.4 3.2 stack.127
  972.3 5.9 sum_steps_dp.1
  979.5 7.5 sum_steps_mp.1
  998.9 7.8 multiply_subtract_fusion
  (261 shorter events, 58.1 us)
Async XLA Ops:
  7.2 32.8 %copy-start.7 = (f32[512,256]{1,0:T(8,128)S(1)}, f32[512,256]{1,0:T(8,128)}, u32[]{:S(2)}) copy-start(f32[512,256]{1,0:T(8,128)} %param.29) | copy-start | bytes 1572868
  7.2 199.8 %all-gather.5.cloned.1.call-start = ((), (), s32[]{:S(2)}) async-start(), calls=%async_computation.7 | async-start | bytes 1966080 | tf_op jit(solution)/shard_map/all_gather | solution.py:760
  9.1 13.1 %collective-permute-start = (bf16[256,384]{1,0:T(8,128)(2,1)S(1)}, bf16[256,384]{1,0:T(8,128)(2,1)S(1)}, u32[]{:S(2)}, u32[]{:S(2)}) collective-permute-start(bf16[256,384]{1,0:T(8,128)(2,1)S(1)} %get-tuple-element.100), channel_id=1, source_target_pairs={{0,4},{1,5},{2,6},{3,7},{4,0},{5,1},{6,2},{7,3},{8,12},{9,13},{10,... | collective-permute-start | bytes 589832 | tf_op jit(solution)/shard_map/ppermute | solution.py:757
  23.1 245.5 %all-gather.9.cloned.1.call-start = ((), (), s32[]{:S(2)}) async-start(), calls=%async_computation.9 | async-start | bytes 2621440 | tf_op jit(solution)/shard_map/all_gather | solution.py:762
  25.1 14.0 %collective-permute-start.2 = (bf16[256,512]{1,0:T(8,128)(2,1)S(1)}, bf16[256,512]{1,0:T(8,128)(2,1)S(1)}, u32[]{:S(2)}, u32[]{:S(2)}) collective-permute-start(bf16[256,512]{1,0:T(8,128)(2,1)S(1)} %get-tuple-element.98), channel_id=1, source_target_pairs={{0,4},{1,5},{2,6},{3,7},{4,0},{5,1},{6,2},{7,3},{8,12},{9,13},{10,... | collective-permute-start | bytes 786440 | tf_op jit(solution)/shard_map/ppermute | solution.py:757
  40.0 235.2 %all-gather.11.cloned.1.call-start = ((), (), s32[]{:S(2)}) async-start(), calls=%async_computation.10 | async-start | bytes 2621440 | tf_op jit(solution)/shard_map/all_gather | solution.py:763
  40.8 13.1 %collective-permute-start.3 = (bf16[512,256]{1,0:T(8,128)(2,1)S(1)}, bf16[512,256]{1,0:T(8,128)(2,1)S(1)}, u32[]{:S(2)}, u32[]{:S(2)}) collective-permute-start(bf16[512,256]{1,0:T(8,128)(2,1)S(1)} %get-tuple-element.96), channel_id=1, source_target_pairs={{0,4},{1,5},{2,6},{3,7},{4,0},{5,1},{6,2},{7,3},{8,12},{9,13},{10,... | collective-permute-start | bytes 786440 | tf_op jit(solution)/shard_map/ppermute | solution.py:757
  54.7 8.9 copy-start.24
  54.7 285.3 %all-gather.7.cloned.1.call-start = ((), (), s32[]{:S(2)}) async-start(), calls=%async_computation.8 | async-start | bytes 16097280 | tf_op jit(solution)/shard_map/all_gather | solution.py:764
  109.6 49.4 %copy-start.13 = (f32[128,256]{1,0:T(8,128)S(1)}, f32[128,256]{1,0:T(8,128)}, u32[]{:S(2)}) copy-start(f32[128,256]{1,0:T(8,128)} %param.27) | copy-start | bytes 393220
  109.6 51.0 %copy-start.40 = (s32[2048]{0:T(1024)S(1)}, s32[2048]{0:T(1024)}, u32[]{:S(2)}) copy-start(s32[2048]{0:T(1024)} %param.23) | copy-start | bytes 24580
  109.6 51.2 %copy-start.33 = (s32[2048]{0:T(1024)S(1)}, s32[2048]{0:T(1024)}, u32[]{:S(2)}) copy-start(s32[2048]{0:T(1024)} %param.22) | copy-start | bytes 24580
  155.0 34.4 %all-to-all-start = ((bf16[4,256,256]{2,1,0:T(8,128)(2,1)}), bf16[4,256,256]{2,1,0:T(8,128)(2,1)S(1)}, u32[]{:S(2)}, u32[]{:S(2)}) async-start(bf16[4,256,256]{2,1,0:T(8,128)(2,1)} %bitcast.223), calls=%async_computation | async-start | bytes 1048576 | tf_op jit(solution)/shard_map/all_to_all | solution.py:790
  159.0 530.8 %reduce-scatter.12.cloned.1.call-start = ((), (), s32[]{:S(2)}) async-start(), calls=%async_computation.14 | async-start | bytes 655360 | tf_op jit(solution)/shard_map/reduce_scatter | solution.py:916
  159.6 5.9 collective-permute-start.1
  234.1 41.0 %copy-start.15 = (bf16[4,64,1024]{2,1,0:T(8,128)(2,1)}, bf16[4,64,1024]{2,1,0:T(8,128)(2,1)S(1)}, u32[]{:S(2)}) copy-start(bf16[4,64,1024]{2,1,0:T(8,128)(2,1)S(1)} %fusion.22) | copy-start | bytes 1572868
  478.3 59.1 %copy-start.47 = (bf16[1024,1024]{1,0:T(8,128)(2,1)S(1)}, bf16[1024,1024]{1,0:T(8,128)(2,1)}, u32[]{:S(2)}) copy-start(bf16[1024,1024]{1,0:T(8,128)(2,1)} %all-gather.11.cloned.1.call-done) | copy-start | bytes 6291460
  582.5 16.5 %slice-start = ((s8[16777216]{0:T(1024)(128)(4,1)}), s8[4194304]{0:T(1024)(128)(4,1)S(1)}, s32[]{:S(2)}) async-start(s8[16777216]{0:T(1024)(128)(4,1)} %bitcast.216), calls=%async_computation.16 | async-start | bytes 8388608
  585.0 14.0 %slice-start.1 = ((s8[16777216]{0:T(1024)(128)(4,1)}), s8[4194304]{0:T(1024)(128)(4,1)S(1)}, s32[]{:S(2)}) async-start(s8[16777216]{0:T(1024)(128)(4,1)} %bitcast.216), calls=%async_computation.17 | async-start | bytes 8388608
  585.0 14.0 %slice-start.2 = ((s8[16777216]{0:T(1024)(128)(4,1)}), s8[4194304]{0:T(1024)(128)(4,1)S(1)}, s32[]{:S(2)}) async-start(s8[16777216]{0:T(1024)(128)(4,1)} %bitcast.216), calls=%async_computation.18 | async-start | bytes 8388608
  585.0 15.2 %slice-start.3 = ((s8[16777216]{0:T(1024)(128)(4,1)}), s8[4194304]{0:T(1024)(128)(4,1)S(1)}, s32[]{:S(2)}) async-start(s8[16777216]{0:T(1024)(128)(4,1)} %bitcast.216), calls=%async_computation.19 | async-start | bytes 8388608
  622.8 112.3 %reduce-scatter.6.cloned.1.call-start = ((), (), s32[]{:S(2)}) async-start(), calls=%async_computation.11 | async-start | bytes 1966080 | tf_op jit(solution)/shard_map/reduce_scatter | solution.py:916
  633.6 103.2 %reduce-scatter.8.cloned.1.call-start = ((), (), s32[]{:S(2)}) async-start(), calls=%async_computation.12 | async-start | bytes 2621440 | tf_op jit(solution)/shard_map/reduce_scatter | solution.py:916
  639.8 120.9 %reduce-scatter.14.cloned.1.call-start = ((), (), s32[]{:S(2)}) async-start(), calls=%async_computation.15 | async-start | bytes 2621440 | tf_op jit(solution)/shard_map/reduce_scatter | solution.py:916
  647.0 241.0 %reduce-scatter.10.cloned.1.call-start = ((), (), s32[]{:S(2)}) async-start(), calls=%async_computation.13 | async-start | bytes 16097280 | tf_op jit(solution)/shard_map/reduce_scatter | solution.py:860
  651.6 24.9 %copy-start.21 = (f32[6288]{0:T(1024)S(1)}, f32[6288]{0:T(1024)}, u32[]{:S(2)}) copy-start(f32[6288]{0:T(1024)} %param.31) | copy-start | bytes 75460
  651.6 25.5 %copy-start.36 = (f32[256]{0:T(256)S(1)}, f32[256]{0:T(256)}, u32[]{:S(2)}) copy-start(f32[256]{0:T(256)} %param.33) | copy-start | bytes 3076
  651.6 26.1 %copy-start.49 = (f32[128]{0:T(128)S(1)}, f32[128]{0:T(128)}, u32[]{:S(2)}) copy-start(f32[128]{0:T(128)} %param.35) | copy-start | bytes 1540
  651.6 28.0 %copy-start.37 = (f32[256]{0:T(256)S(1)}, f32[256]{0:T(256)}, u32[]{:S(2)}) copy-start(f32[256]{0:T(256)} %param.37) | copy-start | bytes 3076
  651.6 29.9 %copy-start.34 = (f32[512]{0:T(512)S(1)}, f32[512]{0:T(512)}, u32[]{:S(2)}) copy-start(f32[512]{0:T(512)} %param.39) | copy-start | bytes 6148
  651.6 31.2 %copy-start.4 = (f32[6,1024]{1,0:T(8,128)S(1)}, f32[6,1024]{1,0:T(8,128)}, u32[]{:S(2)}) copy-start(f32[6,1024]{1,0:T(8,128)} %refs_2_.9) | copy-start | bytes 73732
  673.0 19.2 %all-to-all-start.1 = ((bf16[4,256,256]{2,1,0:T(8,128)(2,1)}), bf16[4,256,256]{2,1,0:T(8,128)(2,1)S(1)}, u32[]{:S(2)}, u32[]{:S(2)}) async-start(bf16[4,256,256]{2,1,0:T(8,128)(2,1)} %bitcast.215), calls=%async_computation.4 | async-start | bytes 1048576 | tf_op jit(solution)/shard_map/all_to_all | solution.py:930
  689.8 46.3 %copy-start.20 = (bf16[256,256]{1,0:T(8,128)(2,1)S(1)}, bf16[256,256]{1,0:T(8,128)(2,1)}, u32[]{:S(2)}) copy-start(bf16[256,256]{1,0:T(8,128)(2,1)} %reduce-scatter.12.cloned.1.call-done) | copy-start | bytes 393220
  690.7 45.4 %collective-permute-start.6 = (bf16[128,256]{1,0:T(8,128)(2,1)S(1)}, bf16[128,256]{1,0:T(8,128)(2,1)S(1)}, u32[]{:S(2)}, u32[]{:S(2)}) collective-permute-start(bf16[128,256]{1,0:T(8,128)(2,1)S(1)} %split.37), channel_id=1, source_target_pairs={{0,4},{1,5},{2,6},{3,7},{4,0},{5,1},{6,2},{7,3},{8,12},{9,13},{10,... | collective-permute-start | bytes 196616 | tf_op jit(solution)/shard_map/ppermute | solution.py:921
  736.0 17.3 %collective-permute-start.4 = (bf16[256,384]{1,0:T(8,128)(2,1)S(1)}, bf16[256,384]{1,0:T(8,128)(2,1)S(1)}, u32[]{:S(2)}, u32[]{:S(2)}) collective-permute-start(bf16[256,384]{1,0:T(8,128)(2,1)S(1)} %split.33), channel_id=1, source_target_pairs={{0,4},{1,5},{2,6},{3,7},{4,0},{5,1},{6,2},{7,3},{8,12},{9,13},{10,... | collective-permute-start | bytes 589832 | tf_op jit(solution)/shard_map/ppermute | solution.py:921
  736.8 260.5 %copy-start.11 = (f32[128,256]{1,0:T(8,128)}, f32[128,256]{1,0:T(8,128)S(1)}, u32[]{:S(2)}) copy-start(f32[128,256]{1,0:T(8,128)S(1)} %get-tuple-element.86) | copy-start | bytes 393220
  737.8 26.3 %collective-permute-start.5 = (bf16[256,512]{1,0:T(8,128)(2,1)S(1)}, bf16[256,512]{1,0:T(8,128)(2,1)S(1)}, u32[]{:S(2)}, u32[]{:S(2)}) collective-permute-start(bf16[256,512]{1,0:T(8,128)(2,1)S(1)} %split.35), channel_id=1, source_target_pairs={{0,4},{1,5},{2,6},{3,7},{4,0},{5,1},{6,2},{7,3},{8,12},{9,13},{10,... | collective-permute-start | bytes 786440 | tf_op jit(solution)/shard_map/ppermute | solution.py:921
  755.1 242.9 %copy-start.3 = (f32[256,384]{1,0:T(8,128)}, f32[256,384]{1,0:T(8,128)S(1)}, u32[]{:S(2)}) copy-start(f32[256,384]{1,0:T(8,128)S(1)} %get-tuple-element.88) | copy-start | bytes 1179652
  761.7 14.6 %collective-permute-start.7 = (bf16[512,256]{1,0:T(8,128)(2,1)S(1)}, bf16[512,256]{1,0:T(8,128)(2,1)S(1)}, u32[]{:S(2)}, u32[]{:S(2)}) collective-permute-start(bf16[512,256]{1,0:T(8,128)(2,1)S(1)} %split.39), channel_id=1, source_target_pairs={{0,4},{1,5},{2,6},{3,7},{4,0},{5,1},{6,2},{7,3},{8,12},{9,13},{10,... | collective-permute-start | bytes 786440 | tf_op jit(solution)/shard_map/ppermute | solution.py:921
  765.9 230.3 %copy-start.1 = (f32[256,512]{1,0:T(8,128)}, f32[256,512]{1,0:T(8,128)S(1)}, u32[]{:S(2)}) copy-start(f32[256,512]{1,0:T(8,128)S(1)} %get-tuple-element.87) | copy-start | bytes 1572868
  778.1 217.1 %copy-start.2 = (f32[512,256]{1,0:T(8,128)}, f32[512,256]{1,0:T(8,128)S(1)}, u32[]{:S(2)}) copy-start(f32[512,256]{1,0:T(8,128)S(1)} %get-tuple-element.85) | copy-start | bytes 1572868
  919.7 30.4 %copy-start.22 = (f32[6,1024]{1,0:T(8,128)S(1)}, f32[6,1024]{1,0:T(8,128)}, u32[]{:S(2)}) copy-start(f32[6,1024]{1,0:T(8,128)} %param.41) | copy-start | bytes 73732
  919.7 32.5 %copy-start.41 = (f32[512]{0:T(512)S(1)}, f32[512]{0:T(512)}, u32[]{:S(2)}) copy-start(f32[512]{0:T(512)} %param.38) | copy-start | bytes 6148
  919.7 35.8 %copy-start.39 = (f32[384]{0:T(512)S(1)}, f32[384]{0:T(512)}, u32[]{:S(2)}) copy-start(f32[384]{0:T(512)} %param.34) | copy-start | bytes 4612
  919.7 39.0 %copy-start.42 = (f32[256]{0:T(256)S(1)}, f32[256]{0:T(256)}, u32[]{:S(2)}) copy-start(f32[256]{0:T(256)} %param.40) | copy-start | bytes 3076
  919.7 39.0 %copy-start.43 = (f32[256]{0:T(256)S(1)}, f32[256]{0:T(256)}, u32[]{:S(2)}) copy-start(f32[256]{0:T(256)} %param.36) | copy-start | bytes 3076
  919.7 39.0 %copy-start.44 = (f32[256]{0:T(256)S(1)}, f32[256]{0:T(256)}, u32[]{:S(2)}) copy-start(f32[256]{0:T(256)} %param.32) | copy-start | bytes 3076
  938.6 58.7 %copy-start.38 = (f32[128]{0:T(128)}, f32[128]{0:T(128)S(1)}, u32[]{:S(2)}) copy-start(f32[128]{0:T(128)S(1)} %fusion.68) | copy-start | bytes 1540
  938.6 60.3 %copy-start.18 = (f32[6288]{0:T(1024)}, f32[6288]{0:T(1024)S(1)}, u32[]{:S(2)}) copy-start(f32[6288]{0:T(1024)S(1)} %fusion.49) | copy-start | bytes 75460
  950.1 28.8 %copy-start.50 = (pred[1,128]{1,0:T(4,128)(4,1)S(1)}, pred[1,128]{1,0:T(4,128)(4,1)}, u32[]{:S(2)}) copy-start(pred[1,128]{1,0:T(4,128)(4,1)} %constant.207.clone.1) | copy-start | bytes 388
  950.1 56.6 %copy-start.17 = (f32[6,1024]{1,0:T(8,128)}, f32[6,1024]{1,0:T(8,128)S(1)}, u32[]{:S(2)}) copy-start(f32[6,1024]{1,0:T(8,128)S(1)} %reshape.400) | copy-start | bytes 73732
  950.8 55.9 %copy-start.19 = (f32[6,1024]{1,0:T(8,128)}, f32[6,1024]{1,0:T(8,128)S(1)}, u32[]{:S(2)}) copy-start(f32[6,1024]{1,0:T(8,128)S(1)} %get-tuple-element.84) | copy-start | bytes 73732
  952.2 44.0 %copy-start.26 = (f32[512]{0:T(512)}, f32[512]{0:T(512)S(1)}, u32[]{:S(2)}) copy-start(f32[512]{0:T(512)S(1)} %get-tuple-element.107) | copy-start | bytes 6148
  952.2 44.0 %copy-start.27 = (f32[512]{0:T(512)}, f32[512]{0:T(512)S(1)}, u32[]{:S(2)}) copy-start(f32[512]{0:T(512)S(1)} %get-tuple-element.108) | copy-start | bytes 6148
  952.2 43.0 %copy-start.8 = (f32[512,256]{1,0:T(8,128)S(1)}, f32[512,256]{1,0:T(8,128)}, u32[]{:S(2)}) copy-start(f32[512,256]{1,0:T(8,128)} %param.29) | copy-start | bytes 1572868
  955.5 42.5 %copy-start.25 = (f32[384]{0:T(512)}, f32[384]{0:T(512)S(1)}, u32[]{:S(2)}) copy-start(f32[384]{0:T(512)S(1)} %fusion.56) | copy-start | bytes 4612
  958.8 37.4 %copy-start.29 = (f32[256]{0:T(256)}, f32[256]{0:T(256)S(1)}, u32[]{:S(2)}) copy-start(f32[256]{0:T(256)S(1)} %get-tuple-element.127) | copy-start | bytes 3076
  958.8 37.4 %copy-start.30 = (f32[256]{0:T(256)}, f32[256]{0:T(256)S(1)}, u32[]{:S(2)}) copy-start(f32[256]{0:T(256)S(1)} %get-tuple-element.128) | copy-start | bytes 3076
  958.8 38.4 %copy-start.28 = (f32[256]{0:T(256)}, f32[256]{0:T(256)S(1)}, u32[]{:S(2)}) copy-start(f32[256]{0:T(256)S(1)} %get-tuple-element.129) | copy-start | bytes 3076
  958.9 39.2 %copy-start.31 = (f32[256]{0:T(256)}, f32[256]{0:T(256)S(1)}, u32[]{:S(2)}) copy-start(f32[256]{0:T(256)S(1)} %get-tuple-element.130) | copy-start | bytes 3076
  958.9 40.1 %copy-start.32 = (f32[256]{0:T(256)}, f32[256]{0:T(256)S(1)}, u32[]{:S(2)}) copy-start(f32[256]{0:T(256)S(1)} %get-tuple-element.131) | copy-start | bytes 3076
  958.9 37.3 %copy-start.9 = (f32[256,512]{1,0:T(8,128)S(1)}, f32[256,512]{1,0:T(8,128)}, u32[]{:S(2)}) copy-start(f32[256,512]{1,0:T(8,128)} %param.28) | copy-start | bytes 1572868
  958.9 38.3 %copy-start.14 = (f32[128,256]{1,0:T(8,128)S(1)}, f32[128,256]{1,0:T(8,128)}, u32[]{:S(2)}) copy-start(f32[128,256]{1,0:T(8,128)} %param.27) | copy-start | bytes 393220
  965.1 32.9 %copy-start.10 = (f32[256,384]{1,0:T(8,128)S(1)}, f32[256,384]{1,0:T(8,128)}, u32[]{:S(2)}) copy-start(f32[256,384]{1,0:T(8,128)} %param.26) | copy-start | bytes 1179652
  (11 other events, 40.2 us)
Sparse Core Ops, SparseCore 0:
  23.2 32.2 all-gather.4
  57.9 35.5 all-gather.8
  95.9 35.1 all-gather.10
  133.3 135.5 all-gather.6
  622.9 22.7 reduce-scatter.11
  648.8 31.0 reduce-scatter.5
  683.8 38.7 reduce-scatter.7
  725.5 35.1 reduce-scatter.13
  764.1 123.8 reduce-scatter.9

commit v2 on v1

--- a/solution.py
+++ b/solution.py
@@ -24,19 +24,29 @@
 VMEM_CAP = 56 * 2**20
 
 
+def cost_of(time):
+    return pl.CostEstimate(
+        flops=time * 1000000000, bytes_accessed=time * 3000000, transcendentals=0
+    )
+
+
 def row_slice(values, start, count):
     return lax.dynamic_slice_in_dim(values, start, count, 0)
 
 
-def line_kernel(nr, ng, chunks, rows, width, n_in, n_out, step, *refs):
+def line_kernel(nr, ng, chunks, rows, width, n_in, n_out, step, sides, *refs):
     part = refs[0] if nr else None
     first = 1 if nr else 0
     ins = refs[first : first + n_in]
     refs = refs[first + n_in :]
+    side_ins, refs = refs[: len(sides)], refs[len(sides) :]
     if ng:
         whole, refs = refs[0], refs[1:]
     outs = refs[:n_out]
-    scratch = refs[n_out:]
+    refs = refs[n_out:]
+    side_outs, scratch = refs[: len(sides)], refs[len(sides) :]
+    side_scratch, scratch = scratch[: 3 * len(sides)], scratch[3 * len(sides) :]
+    size_dp = lax.axis_size("dp")
     dp = lax.axis_index("dp")
     mp = lax.axis_index("mp")
     z = mp // 2
@@ -63,8 +73,43 @@
     def _():
         pl.semaphore_signal(barrier, inc=1, device_id=(dp, mp + 2), device_id_type=MESH)
 
-    greeted = 1 + (zb > 0).astype(jnp.int32) + (zb < most - 1).astype(jnp.int32)
+    if sides:
+        for hop in range(1, size_dp):
+            pl.semaphore_signal(
+                barrier,
+                inc=1,
+                device_id=(lax.rem(dp + hop, size_dp), mp),
+                device_id_type=MESH,
+            )
+    greeted = (size_dp if sides else 1) + (zb > 0).astype(jnp.int32) + (zb < most - 1).astype(jnp.int32)
     pl.semaphore_wait(barrier, greeted)
+
+    def share(axis, length, which):
+        at = pl.ds(pl.multiple_of(which * length, length), length)
+        return (at, slice(None)) if axis == 0 else (slice(None), at)
+
+    side_copies = []
+    for index, (kind, axis) in enumerate(sides):
+        src, dst = side_ins[index], side_outs[index]
+        send, recv, slots = side_scratch[3 * index : 3 * index + 3]
+        length = (src if kind == "gather" else dst).shape[axis]
+        for hop in range(1, size_dp):
+            peer = lax.rem(dp + hop, size_dp)
+            if kind == "gather":
+                source, target = src, dst.at[share(axis, length, dp)]
+            else:
+                source, target = src.at[share(axis, length, peer)], slots.at[hop]
+            copy = pltpu.make_async_remote_copy(
+                src_ref=source,
+                dst_ref=target,
+                send_sem=send.at[hop],
+                recv_sem=recv.at[hop],
+                device_id=(peer, mp),
+                device_id_type=MESH,
+            )
+            side_copies.append(copy)
+            if nr == 0:
+                copy.start()
 
     if nr:
         half, from_left, from_right, going = scratch[:4]
@@ -103,6 +148,8 @@
             return carry
 
         lax.fori_loop(0, chunks, send_halves, 0)
+        for copy in side_copies:
+            copy.start()
 
         def right_copy(dest, k):
             return remote(
@@ -282,9 +329,39 @@
         return carry
 
     lax.fori_loop(0, chunks, finish, 0)
-
-
-def line_call(name, cid, partial, ins, out_types, step, rows, width, chunks, nr, ng):
+    for index, (kind, axis) in enumerate(sides):
+        if kind == "gather":
+            length = side_ins[index].shape[axis]
+            side_outs[index][share(axis, length, dp)] = side_ins[index][...]
+    for copy in side_copies:
+        copy.wait()
+    for index, (kind, axis) in enumerate(sides):
+        if kind == "scatter":
+            src, dst = side_ins[index], side_outs[index]
+            slots = side_scratch[3 * index + 2]
+            strip = 128
+            height = dst.shape[0]
+
+            def add(i, carry):
+                at = pl.ds(pl.multiple_of(i * strip, strip), strip)
+                length = dst.shape[axis]
+                if axis == 0:
+                    start = pl.multiple_of(dp * length + i * strip, strip)
+                    total = src[pl.ds(start, strip), :].astype(jnp.float32)
+                else:
+                    start = pl.multiple_of(dp * length, length)
+                    total = src[at, pl.ds(start, length)].astype(jnp.float32)
+                for hop in range(1, size_dp):
+                    total += slots[hop, at, :].astype(jnp.float32)
+                dst[at, :] = total
+                return carry
+
+            lax.fori_loop(0, height // strip, add, 0)
+
+
+def line_call(
+    name, cid, partial, ins, out_types, step, rows, width, chunks, nr, ng, time, sides=()
+):
     piece = rows // chunks
     out_shape = []
     if ng:
@@ -292,16 +369,37 @@
     out_shape += out_types
     dma = pltpu.SemaphoreType.DMA
     scratch = []
+    size_dp = lax.axis_size("dp")
+    for kind, axis, values in sides:
+        shape = list(values.shape)
+        scratch += [dma((size_dp,)), dma((size_dp,))]
+        if kind == "gather":
+            shape[axis] *= size_dp
+            out_shape.append(jax.ShapeDtypeStruct(tuple(shape), values.dtype))
+            scratch.append(pltpu.VMEM((16, 128), values.dtype))
+        else:
+            shape[axis] //= size_dp
+            out_shape.append(jax.ShapeDtypeStruct(tuple(shape), jnp.float32))
+            scratch.append(pltpu.VMEM((size_dp, *shape), values.dtype))
     if nr:
         scratch += [pltpu.VMEM((nr, chunks, piece, width), jnp.bfloat16)] * 4
         scratch += [dma((nr, chunks))] * 5
     if ng:
         scratch += [dma((ng, chunks))] * 6
-    args = ([partial] if nr else []) + list(ins)
+    args = ([partial] if nr else []) + list(ins) + [side[2] for side in sides]
     vmem = pl.BlockSpec(memory_space=pltpu.VMEM)
     call = pl.pallas_call(
         functools.partial(
-            line_kernel, nr, ng, chunks, rows, width, len(ins), len(out_types), step
+            line_kernel,
+            nr,
+            ng,
+            chunks,
+            rows,
+            width,
+            len(ins),
+            len(out_types),
+            step,
+            tuple(side[:2] for side in sides),
         ),
         out_shape=out_shape,
         in_specs=[vmem] * len(args),
@@ -310,6 +408,7 @@
         compiler_params=pltpu.CompilerParams(
             collective_id=cid, has_side_effects=True, vmem_limit_bytes=VMEM_CAP
         ),
+        cost_estimate=cost_of(time),
         name=name,
     )
     return list(call(*args))
@@ -371,14 +470,14 @@
     )(table, final, wanted, edge)
 
 
-def head_back_kernel(rows, block, tile, exp_ref, table_ref, final_ref, scale_ref, weight_ref, wanted_ref, grad_ref, dfinal_ref, dl_ref):
+def head_back_kernel(rows, block, tile, exp_ref, table_ref, final_ref, scale_ref, weight_ref, wanted_ref, grad_ref, dfinal_ref, dl_ref, sum_ref):
     j = pl.program_id(0)
     tokens = final_ref.shape[0]
     place = j * block + lax.broadcasted_iota(jnp.int32, (block, 1), 0)
 
     @pl.when(j == 0)
     def _():
-        dfinal_ref[...] = jnp.zeros_like(dfinal_ref)
+        sum_ref[...] = jnp.zeros_like(sum_ref)
 
     table = jnp.where(place < rows, table_ref[...], jnp.zeros_like(table_ref))
 
@@ -389,7 +488,7 @@
         dl = dl - jnp.where(place == wanted_ref[:, at], weight, 0.0)
         dl = dl.astype(jnp.bfloat16)
         dl_ref[:, at] = dl
-        dfinal_ref[at, :] += lax.dot_general(
+        sum_ref[at, :] += lax.dot_general(
             dl, table, (((0,), (0,)), ((), ())), preferred_element_type=jnp.float32
         )
         return carry
@@ -408,6 +507,10 @@
 
     for i in range(block // strip):
         two(i, 0)
+
+    @pl.when(j == pl.num_programs(0) - 1)
+    def _():
+        dfinal_ref[...] = sum_ref[...].astype(jnp.bfloat16)
 
 
 def head_back(exps, table, final, scale, weight, wanted, block, tile=256):
@@ -419,7 +522,7 @@
         grid=(steps,),
         out_shape=[
             jax.ShapeDtypeStruct((rows, width), jnp.bfloat16),
-            jax.ShapeDtypeStruct((tokens, width), jnp.float32),
+            jax.ShapeDtypeStruct((tokens, width), jnp.bfloat16),
         ],
         in_specs=[
             pl.BlockSpec((block, tokens), lambda j: (j, 0)),
@@ -433,7 +536,10 @@
             pl.BlockSpec((block, width), lambda j: (j, 0)),
             pl.BlockSpec((tokens, width), lambda j: (0, 0)),
         ],
-        scratch_shapes=[pltpu.VMEM((block, tokens), jnp.bfloat16)],
+        scratch_shapes=[
+            pltpu.VMEM((block, tokens), jnp.bfloat16),
+            pltpu.VMEM((tokens, width), jnp.float32),
+        ],
         compiler_params=pltpu.CompilerParams(vmem_limit_bytes=60 * 2**20),
         cost_estimate=pl.CostEstimate(
             flops=4 * rows * width * tokens,
@@ -486,6 +592,7 @@
         out_specs=vmem,
         scratch_shapes=[pltpu.SemaphoreType.DMA((count,)), pltpu.SemaphoreType.DMA((count,))],
         compiler_params=pltpu.CompilerParams(collective_id=cid, has_side_effects=True),
+        cost_estimate=cost_of(6),
         name=name,
     )(values)
 
@@ -548,7 +655,7 @@
         out_specs=vmem,
         scratch_shapes=[pltpu.VMEM((spots, width), jnp.float32)],
         compiler_params=pltpu.CompilerParams(vmem_limit_bytes=VMEM_CAP),
-        cost_estimate=pl.CostEstimate(flops=0, bytes_accessed=8 * spots * width, transcendentals=0),
+        cost_estimate=cost_of(20),
         name="lookup",
     )(count, keys, table)
 
@@ -585,7 +692,7 @@
         out_specs=vmem,
         scratch_shapes=[pltpu.VMEM((spots, width), jnp.float32)],
         compiler_params=pltpu.CompilerParams(vmem_limit_bytes=VMEM_CAP),
-        cost_estimate=pl.CostEstimate(flops=0, bytes_accessed=16 * spots * width, transcendentals=0),
+        cost_estimate=cost_of(23),
         name="scatter",
     )(count, keys, head_grad, rows)
 
@@ -757,10 +864,10 @@
             found.append(lax.ppermute(weight, "mp", shift))
         return jnp.concatenate(found, axis=axis) if seqs > 1 else weight
 
-    wide_qkv = lax.all_gather(own_and_twins(w_qkv, 1), "dp", axis=0, tiled=True)
-    wide_out = lax.all_gather(own_and_twins(w_out, 0), "dp", axis=1, tiled=True)
-    wide_fc = lax.all_gather(own_and_twins(w_fc, 1), "dp", axis=0, tiled=True)
-    wide_proj = lax.all_gather(own_and_twins(w_proj, 0), "dp", axis=1, tiled=True)
+    pair_qkv = own_and_twins(w_qkv, 1)
+    pair_out = own_and_twins(w_out, 0)
+    pair_fc = own_and_twins(w_fc, 1)
+    pair_proj = own_and_twins(w_proj, 0)
     wide_table = lax.all_gather(embedding.astype(bf16), "dp", axis=1, tiled=True)
 
     place = (
@@ -774,7 +881,7 @@
     keys = jnp.sort(keys.reshape(-1))
     owned = jnp.sum(inside.astype(jnp.int32)).reshape(1)
     found = lookup(keys, owned, embedding, spots)
-    (picked_rows,) = line_call(
+    picked_rows, wide_qkv, wide_out, wide_fc = line_call(
         "rs_lookup",
         1,
         found,
@@ -786,6 +893,8 @@
         chunks_full,
         chips,
         0,
+        50,
+        [("gather", 0, pair_qkv), ("gather", 1, pair_out), ("gather", 0, pair_fc)],
     )
     stream0 = lax.all_to_all(
         picked_rows.reshape(size_dp, rows, part_width), "dp", 0, 0, tiled=False
@@ -795,7 +904,18 @@
     row_f32 = jax.ShapeDtypeStruct((rows, width), f32)
     pair_f32 = jax.ShapeDtypeStruct((8, width), f32)
     (inner_one,) = line_call(
-        "ag_inner1", 2, None, [stream0, norm_params], [], step_first, rows, width, chunks_near, 0, near
+        "ag_inner1",
+        2,
+        None,
+        [stream0, norm_params],
+        [],
+        step_first,
+        rows,
+        width,
+        chunks_near,
+        0,
+        near,
+        17,
     )
     heads = wide_qkv.shape[1] // (3 * HD)
     my_starts = row_slice(starts, (mp // sharers) * LEN, LEN)
@@ -804,7 +924,7 @@
     attended, log_sums = attend_forward(mixed, my_starts)
     attended = attended.reshape(LEN, heads * HD)
     partial = jnp.dot(attended, wide_out, preferred_element_type=f32).astype(bf16)
-    inner_two, stream1 = line_call(
+    inner_two, stream1, wide_proj = line_call(
         "attn_sum",
         3,
         partial,
@@ -816,6 +936,8 @@
         chunks_near,
         near,
         near,
+        32,
+        [("gather", 1, pair_proj)],
     )
     before = jnp.dot(inner_two, wide_fc, preferred_element_type=f32)
     hidden = gelu_tanh(before).astype(bf16)
@@ -832,6 +954,7 @@
         chunks_full,
         near,
         chips,
+        58,
     )
 
     edge = jnp.clip(VREAL - first_row, 0, vocab).astype(jnp.int32).reshape(1)
@@ -862,7 +985,7 @@
     dbranch2, dstream2, norm3 = line_call(
         "final_back",
         6,
-        dfinal.astype(bf16),
+        dfinal,
         [stream2, norm_params],
         [row_f32, pair_f32],
         functools.partial(step_backward, 4),
@@ -871,6 +994,7 @@
         chunks_full,
         chips,
         near,
+        60,
     )
     grad_proj = jnp.einsum("tf,td->fd", hidden, dbranch2, preferred_element_type=f32).astype(bf16)
     dhidden = jnp.einsum("td,fd->tf", dbranch2, wide_proj, preferred_element_type=f32)
@@ -889,6 +1013,7 @@
         chunks_near,
         near,
         near,
+        34,
     )
     grad_fc = jnp.einsum("td,tf->df", inner_two, dbefore, preferred_element_type=f32).astype(bf16)
     grad_out = jnp.einsum("tf,td->fd", attended, dbranch1, preferred_element_type=f32).astype(bf16)
@@ -897,7 +1022,7 @@
     dmixed = attend_backward(mixed, my_starts, log_sums, dattended)
     dmixed = dmixed.reshape(LEN, heads * 3 * HD)
     partial = jnp.einsum("tc,dc->td", dmixed, wide_qkv, preferred_element_type=f32).astype(bf16)
-    dstream0, norm1 = line_call(
+    dstream0, norm1, grad_proj, grad_out = line_call(
         "attn_back",
         8,
         partial,
@@ -909,26 +1034,14 @@
         chunks_near,
         near,
         0,
+        28,
+        [("scatter", 1, grad_proj), ("scatter", 1, grad_out)],
     )
     grad_qkv = jnp.einsum("td,tc->dc", inner_one, dmixed, preferred_element_type=f32).astype(bf16)
-
-    def to_owner(gradient, cut, axis):
-        share = lax.psum_scatter(gradient, "dp", scatter_dimension=cut, tiled=True)
-        pieces = jnp.split(share, seqs, axis=axis)
-        mine = pieces[0].astype(f32)
-        for turn in range(1, seqs):
-            back = [(i, (i - turn * sharers) % size_mp) for i in range(size_mp)]
-            mine = mine + lax.ppermute(pieces[turn], "mp", back).astype(f32)
-        return mine
-
-    grad_proj = to_owner(grad_proj, 1, 0)
-    grad_fc = to_owner(grad_fc, 0, 1)
-    grad_out = to_owner(grad_out, 1, 0)
-    grad_qkv = to_owner(grad_qkv, 0, 1)
 
     sent = jnp.swapaxes(dstream0.reshape(rows, size_dp, part_width), 0, 1)
     sent = lax.all_to_all(sent, "dp", 0, 0, tiled=False).reshape(size_dp * rows, part_width)
-    (drows,) = line_call(
+    drows, grad_fc, grad_qkv = line_call(
         "ag_lookup",
         9,
         None,
@@ -940,7 +1053,22 @@
         chunks_full,
         0,
         chips,
-    )
+        45,
+        [("scatter", 0, grad_fc), ("scatter", 0, grad_qkv)],
+    )
+
+    def to_owner(share, axis):
+        pieces = jnp.split(share, seqs, axis=axis)
+        mine = pieces[0]
+        for turn in range(1, seqs):
+            back = [(i, (i - turn * sharers) % size_mp) for i in range(size_mp)]
+            mine = mine + lax.ppermute(pieces[turn].astype(bf16), "mp", back).astype(f32)
+        return mine
+
+    grad_proj = to_owner(grad_proj, 0)
+    grad_out = to_owner(grad_out, 0)
+    grad_fc = to_owner(grad_fc, 1)
+    grad_qkv = to_owner(grad_qkv, 1)
     grad_table = scatter(keys, owned, head_grad, drows)
 
     beta = 1.0 - STEP ** (-0.8)

time: 1030 us -> 922 us (0.90)
  waiting for transfers between devices: 178 us -> 18.9 us
  Pallas kernels: 531 us -> 605 us
  local copies, waits for them, and re-layouts: 33.6 us -> 58.1 us
  blocking collectives: 23.9 us -> 0 us
  matrix products: 94.8 us -> 82 us
    reduce_scatter x1, waiting for transfers between devices: 110 us -> 0.01 us  [local(): lax.psum_scatter(table_grad, 'dp', scatter_dimension=1, tiled=True)]
    pallas_call x8, Pallas kernels: 307 us -> 392 us  [line_call(): return list(call(*args))]
    ppermute x4, waiting for transfers between devices: 38.8 us -> 0.01 us  [own_and_twins(): found.append(lax.ppermute(weight, 'mp', shift))]
    all_gather x1 -> x0, blocking collectives: 23.9 us -> none  [local(): wide_out = lax.all_gather(own_and_twins(w_out, 0), 'dp', axis=1, tiled=True)]
    unnamed x137 -> x181, local copies, waits for them, and re-layouts: 7.67 us -> 26.9 us
  transfers between devices with their start and end apart: 19 -> 12, of which waited for: 8 -> 4; matrix products, arithmetic and copies ran while one was open for 11% -> 17% of each run, Pallas kernels for 25% -> 46%
where the time goes in v2:
time: 922 us; the launch traced here: 910 us
  Pallas kernels  605 us (66%)
  other arithmetic  92.5 us (10%)
  matrix products  82 us (9%)
  local copies, waits for them, and re-layouts  58.1 us (6%)
  between operations  33.3 us (4%)
  starting transfers between devices  20.5 us (2%)
  waiting for transfers between devices  18.9 us (2%)
    pallas_call x8, Pallas kernels, line_call(): return list(call(*args))  392 us
    pallas_call x1, Pallas kernels, head_back(): pl.pallas_call(functools.partial(head_back_kernel, rows, block, tile), gr...  69.7 us
    pallas_call x6, Pallas kernels, small_gather(): pl.pallas_call(functools.partial(small_gather_kernel, axis, count), out_s...  53.2 us
    pallas_call x1, Pallas kernels, head_stats(): pl.pallas_call(functools.partial(head_stats_kernel, block, tile), grid=(s...  47.1 us
    unnamed x181, local copies, waits for them, and re-layouts  26.9 us
    pallas_call x1, Pallas kernels, scatter(): pl.pallas_call(scatter_kernel, out_shape=jax.ShapeDtypeStruct((vocab, wid...  22 us
    pallas_call x1, Pallas kernels, lookup(): pl.pallas_call(lookup_kernel, out_shape=jax.ShapeDtypeStruct((spots, widt...  21.2 us
  transfers between devices with their start and end apart: 12, of which 4 were waited for; matrix products, arithmetic and copies ran while one was open for 17% of the time, Pallas kernels for 46%

profile of v2, /device:TPU:0, one launch (start us, length us, event | category | flops | bytes accessed | tf_op | source)
XLA Modules:
  0.0 910.2 jit_solution(3887256981082029594)
XLA Ops:
  7.2 1.9 multiply_reduce_fusion.6
  9.2 4.0 collective-permute-start.2
  13.2 1.9 multiply_reduce_fusion.8
  15.1 1.6 multiply_reduce_fusion.10
  16.7 2.9 collective-permute-start.1
  19.6 1.9 multiply_reduce_fusion.5
  21.6 8.8 multiply_reduce_fusion.2
  31.8 6.6 gather_ids.1
  40.5 6.8 sort.14
  47.3 21.2 %lookup.1.refs_0_ = bf16[8192,256]{1,0:T(8,128)(2,1)} custom-call(s32[1]{0:T(128)} %bitcast.2.count_ref, s32[8192]{0:T(1024)} %get-tuple-element.55.key_ref, f32[6288,256]{1,0:T(8,128)} %table_ref.1), custom_call_target="tpu_custom_call" | custom-call | flops 20000000000 | bytes 60000000 | tf_op jit(solution)/shard_map/lookup/pallas_call | solution.py:651
  71.4 86.9 %rs_lookup.1 = (bf16[1024,256]{1,0:T(8,128)(2,1)}, bf16[1024,768]{1,0:T(8,128)(2,1)}, bf16[256,1024]{1,0:T(8,128)(2,1)}, bf16[1024,1024]{1,0:T(8,128)(2,1)}) custom-call(bf16[8192,256]{1,0:T(8,128)(2,1)} %lookup.1.refs_0_, bf16[256,768]{1,0:T(8,128)(2,1)} %pad_maximum_fusion.3.refs_1_, bf16[256,256]{1,0:T(8,128)(2,1)} %pad_maximum_fusion.4.refs_2_, ...), custom_call_target="tpu_custom_call" | custom-call | flops 49999998976 | bytes 150000000 | tf_op jit(solution)/shard_map/rs_lookup/pallas_call | solution.py:414
  158.3 3.5 all-to-all-start
  169.4 3.8 stack.115
  176.8 29.2 %ag_inner1.1 = bf16[1024,1024]{1,0:T(8,128)(2,1)} custom-call(bf16[256,1024]{1,0:T(8,128)(2,1)} %bitcast.228, f32[6,1024]{1,0:T(8,128)} %refs_2_.9), custom_call_target="tpu_custom_call" | custom-call | flops 16999999488 | bytes 51000000 | tf_op jit(solution)/shard_map/ag_inner1/pallas_call | solution.py:414
  206.0 3.4 convolution_convert_fusion.7
  209.4 7.6 fusion.74
  217.0 8.0 fusion
  225.6 7.4 fusion.22
  233.9 2.1 convolution_convert_fusion.4.refs_0_
  236.0 34.3 %attn_sum.1 = (bf16[1024,1024]{1,0:T(8,128)(2,1)}, f32[256,1024]{1,0:T(8,128)}, bf16[1024,1024]{1,0:T(8,128)(2,1)}) custom-call(bf16[1024,1024]{1,0:T(8,128)(2,1)} %convolution_convert_fusion.4.refs_0_, bf16[256,1024]{1,0:T(8,128)(2,1)} %bitcast.229, f32[6,1024]{1,0:T(8,128)} %refs_2_.9, bf16[1024,256]{1,0:T(8,128)(2,1)} %pad_maximum_fusion.2.refs_3_), custom_call_target="tpu_custom_call" | custom-call | flops 32000000000 | bytes 96000000 | tf_op jit(solution)/shard_map/attn_sum/pallas_call | solution.py:414
  270.3 4.1 fusion.75
  274.4 4.0 convolution_convert_fusion.3.refs_0_
  278.4 62.6 %mlp_sum.1 = (bf16[2048,1024]{1,0:T(8,128)(2,1)}, f32[256,1024]{1,0:T(8,128)}) custom-call(bf16[1024,1024]{1,0:T(8,128)(2,1)} %convolution_convert_fusion.3.refs_0_, f32[256,1024]{1,0:T(8,128)} %get-tuple-element.62.refs_1_, f32[6,1024]{1,0:T(8,128)} %refs_2_.9), custom_call_target="tpu_custom_call" | custom-call | flops 57999998976 | bytes 174000000 | tf_op jit(solution)/shard_map/mlp_sum/pallas_call | solution.py:414
  341.0 47.1 %head_stats.1 = (bf16[6400,2048]{1,0:T(8,128)(2,1)}, f32[10,1,2048]{2,1,0:T(1,128)}, f32[10,1,2048]{2,1,0:T(1,128)}, f32[10,1,2048]{2,1,0:T(1,128)}) custom-call(bf16[6288,1024]{1,0:T(8,128)(2,1)} %all-gather.2.cloned.1.call-done.table_ref, bf16[2048,1024]{1,0:T(8,128)(2,1)} %get-tuple-element.63.final_ref, s32[1,2048]{1,0:T(1,128)} %bitcast.253, ...), custom_call_target="tpu_custom_call" | custom-call | flops 26373783552 | bytes 38633472 | tf_op jit(solution)/shard_map/head_stats/pallas_call | solution.py:452
  391.6 8.4 gather_stats.1
  402.8 69.7 %head_back.1 = (bf16[6288,1024]{1,0:T(8,128)(2,1)}, bf16[2048,1024]{1,0:T(8,128)(2,1)}) custom-call(bf16[6400,2048]{1,0:T(8,128)(2,1)} %get-tuple-element.64.exp_ref, bf16[6288,1024]{1,0:T(8,128)(2,1)} %all-gather.2.cloned.1.call-done.table_ref, bf16[2048,1024]{1,0:T(8,128)(2,1)} %get-tuple-element.63.final_ref, ...), custom_call_target="tpu_custom_call" | custom-call | flops 52747567104 | bytes 51511296 | tf_op jit(solution)/shard_map/head_back/pallas_call | solution.py:520
  472.5 58.7 %final_back.1 = (bf16[1024,1024]{1,0:T(8,128)(2,1)}, f32[256,1024]{1,0:T(8,128)}, f32[8,1024]{1,0:T(8,128)}) custom-call(bf16[2048,1024]{1,0:T(8,128)(2,1)} %get-tuple-element.68.refs_0_, f32[256,1024]{1,0:T(8,128)} %get-tuple-element.69.refs_1_, f32[6,1024]{1,0:T(8,128)} %refs_2_.9), custom_call_target="tpu_custom_call" | custom-call | flops 60000002048 | bytes 180000000 | tf_op jit(solution)/shard_map/final_back/pallas_call | solution.py:414
  531.2 6.5 fusion.15
  537.8 3.7 convolution_convert_fusion.2.refs_0_
  541.5 34.5 %mlp_back.1 = (bf16[1024,1024]{1,0:T(8,128)(2,1)}, f32[256,1024]{1,0:T(8,128)}, f32[8,1024]{1,0:T(8,128)}) custom-call(bf16[1024,1024]{1,0:T(8,128)(2,1)} %convolution_convert_fusion.2.refs_0_, f32[256,1024]{1,0:T(8,128)} %get-tuple-element.62.refs_1_, f32[6,1024]{1,0:T(8,128)} %refs_2_.9, f32[256,1024]{1,0:T(8,128)} %get-tuple-element.71.refs_3_), custom_call_target="tpu_custom_call" | custom-call | flops 33999998976 | bytes 102000000 | tf_op jit(solution)/shard_map/mlp_back/pallas_call | solution.py:414
  576.0 2.4 convolution_convert_fusion.9
  578.5 15.3 %multiply_reduce_fusion = (f32[4,1024]{1,0:T(4,128)S(1)}, f32[4,1024,1024]{1,2,0:T(8,128)}) fusion(f32[4,1024,1024]{1,2,0:T(8,128)} %get-tuple-element.159, f32[4,1024]{1,0:T(4,128)S(1)} %copy-done.18, bf16[1024,4,64]{0,2,1:T(8,128)(2,1)S(1)} %bitcast.218, bf16[1024,4,3,64]{0,3,2,1:T(8,128)(2,1)S(1)} %bitcast.223), kind=kOutput, calls=%fused_computation.1 | convolution fusion | flops 549449728 | bytes 34635776 | tf_op jit(solution)/shard_map/qhe,khe->hqk/dot_general | solution.py:791
  595.2 7.9 multiply_convert_fusion
  603.1 1.6 fusion.27
  604.7 2.7 fusion.26
  607.4 3.2 fusion.23
  612.4 1.5 convolution_convert_fusion.8.refs_5_
  613.9 3.2 convolution_convert_fusion.5.refs_0_
  617.1 4.1 convolution_convert_fusion.1.refs_4_
  621.2 36.0 %attn_back.1 = (bf16[256,1024]{1,0:T(8,128)(2,1)}, f32[8,1024]{1,0:T(8,128)}, f32[1024,256]{1,0:T(8,128)}, f32[256,256]{1,0:T(8,128)}) custom-call(bf16[1024,1024]{1,0:T(8,128)(2,1)} %convolution_convert_fusion.5.refs_0_, bf16[256,1024]{1,0:T(8,128)(2,1)} %bitcast.230, f32[6,1024]{1,0:T(8,128)} %refs_2_.9, f32[256,1024]{1,0:T(8,128)} %get-tuple-element.73.refs_3_, ...), custom_call_target="tpu_custom_call" | custom-call | flops 28000000000 | bytes 84000000 | tf_op jit(solution)/shard_map/attn_back/pallas_call | solution.py:414
  657.2 1.9 copy.131
  659.1 3.9 all-to-all-start.1
  662.9 6.1 convolution_convert_fusion.refs_1_
  669.0 3.0 convolution_convert_fusion.6.refs_2_
  672.9 1.9 collective-permute-start.6
  678.9 6.1 collective-permute-done.6
  685.1 1.6 fusion.41
  687.5 49.7 %ag_lookup.1 = (bf16[8192,256]{1,0:T(8,128)(2,1)}, f32[256,1024]{1,0:T(8,128)}, f32[256,768]{1,0:T(8,128)}) custom-call(bf16[1024,256]{1,0:T(8,128)(2,1)} %bitcast.232, bf16[1024,1024]{1,0:T(8,128)(2,1)} %convolution_convert_fusion.refs_1_, bf16[1024,768]{1,0:T(8,128)(2,1)} %convolution_convert_fusion.6.refs_2_), custom_call_target="tpu_custom_call" | custom-call | flops 44999999488 | bytes 135000000 | tf_op jit(solution)/shard_map/ag_lookup/pallas_call | solution.py:414
  740.5 3.0 collective-permute-start.5
  743.4 10.9 %collective-permute-done.4 = bf16[256,384]{1,0:T(8,128)(2,1)S(1)} collective-permute-done((bf16[256,384]{1,0:T(8,128)(2,1)S(1)}, bf16[256,384]{1,0:T(8,128)(2,1)S(1)}, u32[]{:S(2)}, u32[]{:S(2)}) %collective-permute-start.4) | collective-permute-done | bytes 196640 | tf_op jit(solution)/shard_map/ppermute | solution.py:1065
  754.3 1.8 fusion.35
  759.8 1.9 fusion.29
  764.3 22.0 %scatter.1 = f32[6288,256]{1,0:T(8,128)} custom-call(s32[1]{0:T(128)} %bitcast.2.count_ref, s32[8192]{0:T(1024)} %get-tuple-element.55.key_ref, bf16[6288,256]{1,0:T(8,128)(2,1)} %reduce-scatter.2.cloned.1.call-done.head_ref, bf16[8192,256]{1,0:T(8,128)(2,1)} %get-tuple-element.78.rows_in_ref), custom_call_target="tpu_custom_call" | custom-call | flops 23000000512 | bytes 69000000 | tf_op jit(solution)/shard_map/scatter/pallas_call | solution.py:688
  786.3 6.5 fusion.6
  798.1 3.3 stack.109
  806.6 1.5 pad_bitcast_fusion.src_ref
  808.1 7.8 sum_squares_dp.1
  826.7 1.4 pad_bitcast_fusion.1.src_ref
  828.1 16.2 %sum_squares_mp.1 = f32[8,64,128]{2,1,0:T(8,128)} custom-call(f32[64,128]{1,0:T(8,128)} %pad_bitcast_fusion.1.src_ref), custom_call_target="tpu_custom_call" | custom-call | flops 6000000000 | bytes 18000000 | tf_op jit(solution)/shard_map/sum_squares_mp/pallas_call | solution.py:588
  854.1 6.1 multiply_reduce_fusion.1
  863.5 3.2 stack.127
  867.4 5.9 sum_steps_dp.1
  874.6 8.2 sum_steps_mp.1
  894.8 7.8 multiply_subtract_fusion
  (282 shorter events, 74.1 us)
Async XLA Ops:
  7.2 333.8 %all-gather.2.cloned.1.call-start = ((), (), s32[]{:S(2)}) async-start(), calls=%async_computation.3 | async-start | bytes 16097280 | tf_op jit(solution)/shard_map/all_gather | solution.py:871
  9.2 61.3 %collective-permute-start.2 = (bf16[256,512]{1,0:T(8,128)(2,1)S(1)}, bf16[256,512]{1,0:T(8,128)(2,1)S(1)}, u32[]{:S(2)}, u32[]{:S(2)}) collective-permute-start(bf16[256,512]{1,0:T(8,128)(2,1)S(1)} %get-tuple-element.118), channel_id=1, source_target_pairs={{0,4},{1,5},{2,6},{3,7},{4,0},{5,1},{6,2},{7,3},{8,12},{9,13},{10,... | collective-permute-start | bytes 786440 | tf_op jit(solution)/shard_map/ppermute | solution.py:864
  15.1 54.6 %collective-permute-start = (bf16[256,384]{1,0:T(8,128)(2,1)S(1)}, bf16[256,384]{1,0:T(8,128)(2,1)S(1)}, u32[]{:S(2)}, u32[]{:S(2)}) collective-permute-start(bf16[256,384]{1,0:T(8,128)(2,1)S(1)} %get-tuple-element.120), channel_id=1, source_target_pairs={{0,4},{1,5},{2,6},{3,7},{4,0},{5,1},{6,2},{7,3},{8,12},{9,13},{10,... | collective-permute-start | bytes 589832 | tf_op jit(solution)/shard_map/ppermute | solution.py:864
  16.7 52.3 %collective-permute-start.1 = (bf16[128,256]{1,0:T(8,128)(2,1)S(1)}, bf16[128,256]{1,0:T(8,128)(2,1)S(1)}, u32[]{:S(2)}, u32[]{:S(2)}) collective-permute-start(bf16[128,256]{1,0:T(8,128)(2,1)S(1)} %get-tuple-element.124), channel_id=1, source_target_pairs={{0,4},{1,5},{2,6},{3,7},{4,0},{5,1},{6,2},{7,3},{8,12},{9,13},{10,... | collective-permute-start | bytes 196616 | tf_op jit(solution)/shard_map/ppermute | solution.py:864
  21.6 152.9 %collective-permute-start.3 = (bf16[512,256]{1,0:T(8,128)(2,1)S(1)}, bf16[512,256]{1,0:T(8,128)(2,1)S(1)}, u32[]{:S(2)}, u32[]{:S(2)}) collective-permute-start(bf16[512,256]{1,0:T(8,128)(2,1)S(1)} %get-tuple-element.116), channel_id=1, source_target_pairs={{0,4},{1,5},{2,6},{3,7},{4,0},{5,1},{6,2},{7,3},{8,12},{9,13},{10,... | collective-permute-start | bytes 786440 | tf_op jit(solution)/shard_map/ppermute | solution.py:864
  40.4 28.0 %copy-start.53 = (f32[4]{0:T(128)}, f32[4]{0:T(128)S(1)}, u32[]{:S(2)}) copy-start(f32[4]{0:T(128)S(1)} %convert_reduce_fusion) | copy-start | bytes 52
  71.3 90.5 %copy-start.21 = (f32[6,1024]{1,0:T(8,128)S(1)}, f32[6,1024]{1,0:T(8,128)}, u32[]{:S(2)}) copy-start(f32[6,1024]{1,0:T(8,128)} %refs_2_.9) | copy-start | bytes 73732
  71.3 91.1 %copy-start.23 = (f32[6288]{0:T(1024)S(1)}, f32[6288]{0:T(1024)}, u32[]{:S(2)}) copy-start(f32[6288]{0:T(1024)} %param.31) | copy-start | bytes 75460
  71.3 91.8 %copy-start.42 = (f32[256]{0:T(256)S(1)}, f32[256]{0:T(256)}, u32[]{:S(2)}) copy-start(f32[256]{0:T(256)} %param.33) | copy-start | bytes 3076
  71.3 92.4 %copy-start.58 = (f32[128]{0:T(128)S(1)}, f32[128]{0:T(128)}, u32[]{:S(2)}) copy-start(f32[128]{0:T(128)} %param.35) | copy-start | bytes 1540
  71.3 94.3 %copy-start.44 = (f32[256]{0:T(256)S(1)}, f32[256]{0:T(256)}, u32[]{:S(2)}) copy-start(f32[256]{0:T(256)} %param.37) | copy-start | bytes 3076
  71.3 96.1 %copy-start.39 = (f32[512]{0:T(512)S(1)}, f32[512]{0:T(512)}, u32[]{:S(2)}) copy-start(f32[512]{0:T(512)} %param.39) | copy-start | bytes 6148
  71.3 102.5 %copy-start.38 = (s32[2048]{0:T(1024)S(1)}, s32[2048]{0:T(1024)}, u32[]{:S(2)}) copy-start(s32[2048]{0:T(1024)} %param.22) | copy-start | bytes 24580
  158.3 17.6 %all-to-all-start = ((bf16[4,256,256]{2,1,0:T(8,128)(2,1)}), bf16[4,256,256]{2,1,0:T(8,128)(2,1)S(1)}, u32[]{:S(2)}, u32[]{:S(2)}) async-start(bf16[4,256,256]{2,1,0:T(8,128)(2,1)} %bitcast.231), calls=%async_computation | async-start | bytes 1048576 | tf_op jit(solution)/shard_map/all_to_all | solution.py:899
  161.8 602.5 %reduce-scatter.2.cloned.1.call-start = ((), (), s32[]{:S(2)}) async-start(), calls=%async_computation.4 | async-start | bytes 16097280 | tf_op jit(solution)/shard_map/reduce_scatter | solution.py:983
  176.8 29.2 %copy-start.69 = (bf16[1024,768]{1,0:T(8,128)(2,1)S(1)}, bf16[1024,768]{1,0:T(8,128)(2,1)}, u32[]{:S(2)}) copy-start(bf16[1024,768]{1,0:T(8,128)(2,1)} %get-tuple-element.57) | copy-start | bytes 4718596
  209.4 16.2 %copy-start.5 = (bf16[1024,768]{0,1:T(8,128)(2,1)}, bf16[1024,768]{0,1:T(8,128)(2,1)S(1)}, u32[]{:S(2)}) copy-start(bf16[1024,768]{0,1:T(8,128)(2,1)S(1)} %convolution_convert_fusion.7) | copy-start | bytes 4718596
  236.0 34.3 %copy-start.65 = (bf16[1024,1024]{1,0:T(8,128)(2,1)S(1)}, bf16[1024,1024]{1,0:T(8,128)(2,1)}, u32[]{:S(2)}) copy-start(bf16[1024,1024]{1,0:T(8,128)(2,1)} %get-tuple-element.60) | copy-start | bytes 6291460
  391.6 10.4 %copy-start.9 = (f32[10,1,2048]{2,1,0:T(1,128)S(1)}, f32[10,1,2048]{2,1,0:T(1,128)}, u32[]{:S(2)}) copy-start(f32[10,1,2048]{2,1,0:T(1,128)} %get-tuple-element.65) | copy-start | bytes 245764
  472.5 58.7 %copy-start.63 = (f32[1024,1024]{1,0:T(8,128)S(1)}, f32[1024,1024]{1,0:T(8,128)}, u32[]{:S(2)}) copy-start(f32[1024,1024]{1,0:T(8,128)} %copy-done.62) | copy-start | bytes 12582916
  472.5 58.7 %copy-start.73 = (bf16[1024,1024]{1,0:T(8,128)(2,1)S(1)}, bf16[1024,1024]{1,0:T(8,128)(2,1)}, u32[]{:S(2)}) copy-start(bf16[1024,1024]{1,0:T(8,128)(2,1)} %get-tuple-element.61) | copy-start | bytes 6291460
  541.5 34.5 %copy-start.14 = (bf16[256,1024]{1,0:T(8,128)(2,1)S(1)}, bf16[256,1024]{1,0:T(8,128)(2,1)}, u32[]{:S(2)}) copy-start(bf16[256,1024]{1,0:T(8,128)(2,1)} %get-tuple-element.58) | copy-start | bytes 1572868
  578.5 15.4 %slice-start = ((s8[16777216]{0:T(1024)(128)(4,1)}), s8[4194304]{0:T(1024)(128)(4,1)S(1)}, s32[]{:S(2)}) async-start(s8[16777216]{0:T(1024)(128)(4,1)} %bitcast.216), calls=%async_computation.5 | async-start | bytes 8388608
  578.5 15.4 %slice-start.1 = ((s8[16777216]{0:T(1024)(128)(4,1)}), s8[4194304]{0:T(1024)(128)(4,1)S(1)}, s32[]{:S(2)}) async-start(s8[16777216]{0:T(1024)(128)(4,1)} %bitcast.216), calls=%async_computation.6 | async-start | bytes 8388608
  578.5 15.4 %slice-start.2 = ((s8[16777216]{0:T(1024)(128)(4,1)}), s8[4194304]{0:T(1024)(128)(4,1)S(1)}, s32[]{:S(2)}) async-start(s8[16777216]{0:T(1024)(128)(4,1)} %bitcast.216), calls=%async_computation.7 | async-start | bytes 8388608
  578.5 16.7 %slice-start.3 = ((s8[16777216]{0:T(1024)(128)(4,1)}), s8[4194304]{0:T(1024)(128)(4,1)S(1)}, s32[]{:S(2)}) async-start(s8[16777216]{0:T(1024)(128)(4,1)} %bitcast.216), calls=%async_computation.8 | async-start | bytes 8388608
  659.1 27.7 %all-to-all-start.1 = ((bf16[4,256,256]{2,1,0:T(8,128)(2,1)}), bf16[4,256,256]{2,1,0:T(8,128)(2,1)S(1)}, u32[]{:S(2)}, u32[]{:S(2)}) async-start(bf16[4,256,256]{2,1,0:T(8,128)(2,1)} %bitcast.215), calls=%async_computation.1 | async-start | bytes 1048576 | tf_op jit(solution)/shard_map/all_to_all | solution.py:1043
  672.9 12.1 %collective-permute-start.6 = (bf16[128,256]{1,0:T(8,128)(2,1)S(1)}, bf16[128,256]{1,0:T(8,128)(2,1)S(1)}, u32[]{:S(2)}, u32[]{:S(2)}) collective-permute-start(bf16[128,256]{1,0:T(8,128)(2,1)S(1)} %split.51), channel_id=1, source_target_pairs={{0,4},{1,5},{2,6},{3,7},{4,0},{5,1},{6,2},{7,3},{8,12},{9,13},{10,... | collective-permute-start | bytes 196616 | tf_op jit(solution)/shard_map/ppermute | solution.py:1065
  674.9 63.5 %collective-permute-start.7 = (bf16[512,256]{1,0:T(8,128)(2,1)S(1)}, bf16[512,256]{1,0:T(8,128)(2,1)S(1)}, u32[]{:S(2)}, u32[]{:S(2)}) collective-permute-start(bf16[512,256]{1,0:T(8,128)(2,1)S(1)} %split.48), channel_id=1, source_target_pairs={{0,4},{1,5},{2,6},{3,7},{4,0},{5,1},{6,2},{7,3},{8,12},{9,13},{10,... | collective-permute-start | bytes 786440 | tf_op jit(solution)/shard_map/ppermute | solution.py:1065
  686.7 206.4 %copy-start.8 = (f32[128,256]{1,0:T(8,128)}, f32[128,256]{1,0:T(8,128)S(1)}, u32[]{:S(2)}) copy-start(f32[128,256]{1,0:T(8,128)S(1)} %get-tuple-element.106) | copy-start | bytes 393220
  738.3 16.0 %collective-permute-start.4 = (bf16[256,384]{1,0:T(8,128)(2,1)S(1)}, bf16[256,384]{1,0:T(8,128)(2,1)S(1)}, u32[]{:S(2)}, u32[]{:S(2)}) collective-permute-start(bf16[256,384]{1,0:T(8,128)(2,1)S(1)} %split.50), channel_id=1, source_target_pairs={{0,4},{1,5},{2,6},{3,7},{4,0},{5,1},{6,2},{7,3},{8,12},{9,13},{10,... | collective-permute-start | bytes 589832 | tf_op jit(solution)/shard_map/ppermute | solution.py:1065
  739.2 151.8 %copy-start = (f32[512,256]{1,0:T(8,128)}, f32[512,256]{1,0:T(8,128)S(1)}, u32[]{:S(2)}) copy-start(f32[512,256]{1,0:T(8,128)S(1)} %get-tuple-element.105) | copy-start | bytes 1572868
  740.5 19.4 %collective-permute-start.5 = (bf16[256,512]{1,0:T(8,128)(2,1)S(1)}, bf16[256,512]{1,0:T(8,128)(2,1)S(1)}, u32[]{:S(2)}, u32[]{:S(2)}) collective-permute-start(bf16[256,512]{1,0:T(8,128)(2,1)S(1)} %split.49), channel_id=1, source_target_pairs={{0,4},{1,5},{2,6},{3,7},{4,0},{5,1},{6,2},{7,3},{8,12},{9,13},{10,... | collective-permute-start | bytes 786440 | tf_op jit(solution)/shard_map/ppermute | solution.py:1065
  756.1 137.8 %copy-start.2 = (f32[256,384]{1,0:T(8,128)}, f32[256,384]{1,0:T(8,128)S(1)}, u32[]{:S(2)}) copy-start(f32[256,384]{1,0:T(8,128)S(1)} %get-tuple-element.108) | copy-start | bytes 1179652
  761.7 130.4 %copy-start.1 = (f32[256,512]{1,0:T(8,128)}, f32[256,512]{1,0:T(8,128)S(1)}, u32[]{:S(2)}) copy-start(f32[256,512]{1,0:T(8,128)S(1)} %get-tuple-element.107) | copy-start | bytes 1572868
  786.3 10.5 %copy-start.54 = (f32[4]{0:T(128)S(1)}, f32[4]{0:T(128)}, u32[]{:S(2)}) copy-start(f32[4]{0:T(128)} %get-tuple-element.101) | copy-start | bytes 52
  786.3 16.4 %copy-start.56 = (f32[5]{0:T(128)S(1)}, f32[5]{0:T(128)}, u32[]{:S(2)}) copy-start(f32[5]{0:T(128)} %stack.115) | copy-start | bytes 64
  786.3 17.7 %copy-start.57 = (f32[5]{0:T(128)S(1)}, f32[5]{0:T(128)}, u32[]{:S(2)}) copy-start(f32[5]{0:T(128)} %stack.121) | copy-start | bytes 64
  786.3 19.0 %copy-start.25 = (f32[6144]{0:T(1024)S(1)}, f32[6144]{0:T(1024)}, u32[]{:S(2)}) copy-start(f32[6144]{0:T(1024)} %reshape.392) | copy-start | bytes 73732
  816.9 76.2 %copy-start.46 = (f32[128]{0:T(128)}, f32[128]{0:T(128)S(1)}, u32[]{:S(2)}) copy-start(f32[128]{0:T(128)S(1)} %fusion.68) | copy-start | bytes 1540
  817.0 77.8 %copy-start.19 = (f32[6288]{0:T(1024)}, f32[6288]{0:T(1024)S(1)}, u32[]{:S(2)}) copy-start(f32[6288]{0:T(1024)S(1)} %fusion.49) | copy-start | bytes 75460
  828.0 17.3 %copy-start.26 = (f32[6,1024]{1,0:T(8,128)S(1)}, f32[6,1024]{1,0:T(8,128)}, u32[]{:S(2)}) copy-start(f32[6,1024]{1,0:T(8,128)} %param.41) | copy-start | bytes 73732
  828.0 19.4 %copy-start.40 = (f32[512]{0:T(512)S(1)}, f32[512]{0:T(512)}, u32[]{:S(2)}) copy-start(f32[512]{0:T(512)} %param.39) | copy-start | bytes 6148
  828.0 19.4 %copy-start.49 = (f32[512]{0:T(512)S(1)}, f32[512]{0:T(512)}, u32[]{:S(2)}) copy-start(f32[512]{0:T(512)} %param.38) | copy-start | bytes 6148
  828.0 22.7 %copy-start.47 = (f32[384]{0:T(512)S(1)}, f32[384]{0:T(512)}, u32[]{:S(2)}) copy-start(f32[384]{0:T(512)} %param.34) | copy-start | bytes 4612
  828.0 25.9 %copy-start.43 = (f32[256]{0:T(256)S(1)}, f32[256]{0:T(256)}, u32[]{:S(2)}) copy-start(f32[256]{0:T(256)} %param.33) | copy-start | bytes 3076
  828.1 25.9 %copy-start.45 = (f32[256]{0:T(256)S(1)}, f32[256]{0:T(256)}, u32[]{:S(2)}) copy-start(f32[256]{0:T(256)} %param.37) | copy-start | bytes 3076
  828.1 25.9 %copy-start.50 = (f32[256]{0:T(256)S(1)}, f32[256]{0:T(256)}, u32[]{:S(2)}) copy-start(f32[256]{0:T(256)} %param.40) | copy-start | bytes 3076
  828.1 25.9 %copy-start.51 = (f32[256]{0:T(256)S(1)}, f32[256]{0:T(256)}, u32[]{:S(2)}) copy-start(f32[256]{0:T(256)} %param.36) | copy-start | bytes 3076
  828.1 25.9 %copy-start.52 = (f32[256]{0:T(256)S(1)}, f32[256]{0:T(256)}, u32[]{:S(2)}) copy-start(f32[256]{0:T(256)} %param.32) | copy-start | bytes 3076
  845.4 57.2 %copy-start.17 = (f32[6,1024]{1,0:T(8,128)}, f32[6,1024]{1,0:T(8,128)S(1)}, u32[]{:S(2)}) copy-start(f32[6,1024]{1,0:T(8,128)S(1)} %reshape.400) | copy-start | bytes 73732
  846.0 56.6 %copy-start.20 = (f32[6,1024]{1,0:T(8,128)}, f32[6,1024]{1,0:T(8,128)S(1)}, u32[]{:S(2)}) copy-start(f32[6,1024]{1,0:T(8,128)S(1)} %get-tuple-element.104) | copy-start | bytes 73732
  847.4 43.6 %copy-start.31 = (f32[512]{0:T(512)}, f32[512]{0:T(512)S(1)}, u32[]{:S(2)}) copy-start(f32[512]{0:T(512)S(1)} %get-tuple-element.127) | copy-start | bytes 6148
  847.4 44.6 %copy-start.32 = (f32[512]{0:T(512)}, f32[512]{0:T(512)S(1)}, u32[]{:S(2)}) copy-start(f32[512]{0:T(512)S(1)} %get-tuple-element.128) | copy-start | bytes 6148
  850.7 43.1 %copy-start.30 = (f32[384]{0:T(512)}, f32[384]{0:T(512)S(1)}, u32[]{:S(2)}) copy-start(f32[384]{0:T(512)S(1)} %fusion.56) | copy-start | bytes 4612
  854.0 37.0 %copy-start.34 = (f32[256]{0:T(256)}, f32[256]{0:T(256)S(1)}, u32[]{:S(2)}) copy-start(f32[256]{0:T(256)S(1)} %get-tuple-element.147) | copy-start | bytes 3076
  854.0 38.0 %copy-start.35 = (f32[256]{0:T(256)}, f32[256]{0:T(256)S(1)}, u32[]{:S(2)}) copy-start(f32[256]{0:T(256)S(1)} %get-tuple-element.148) | copy-start | bytes 3076
  854.0 39.0 %copy-start.33 = (f32[256]{0:T(256)}, f32[256]{0:T(256)S(1)}, u32[]{:S(2)}) copy-start(f32[256]{0:T(256)S(1)} %get-tuple-element.149) | copy-start | bytes 3076
  854.0 39.8 %copy-start.36 = (f32[256]{0:T(256)}, f32[256]{0:T(256)S(1)}, u32[]{:S(2)}) copy-start(f32[256]{0:T(256)S(1)} %get-tuple-element.150) | copy-start | bytes 3076
  854.1 40.7 %copy-start.37 = (f32[256]{0:T(256)}, f32[256]{0:T(256)S(1)}, u32[]{:S(2)}) copy-start(f32[256]{0:T(256)S(1)} %get-tuple-element.151) | copy-start | bytes 3076
  874.6 16.5 %copy-start.3 = (f32[512,256]{1,0:T(8,128)S(1)}, f32[512,256]{1,0:T(8,128)}, u32[]{:S(2)}) copy-start(f32[512,256]{1,0:T(8,128)} %param.29) | copy-start | bytes 1572868
  874.6 17.5 %copy-start.4 = (f32[256,512]{1,0:T(8,128)S(1)}, f32[256,512]{1,0:T(8,128)}, u32[]{:S(2)}) copy-start(f32[256,512]{1,0:T(8,128)} %param.28) | copy-start | bytes 1572868
  874.6 18.5 %copy-start.11 = (f32[128,256]{1,0:T(8,128)S(1)}, f32[128,256]{1,0:T(8,128)}, u32[]{:S(2)}) copy-start(f32[128,256]{1,0:T(8,128)} %param.27) | copy-start | bytes 393220
  874.6 19.3 %copy-start.7 = (f32[256,384]{1,0:T(8,128)S(1)}, f32[256,384]{1,0:T(8,128)}, u32[]{:S(2)}) copy-start(f32[256,384]{1,0:T(8,128)} %param.26) | copy-start | bytes 1179652
  (26 other events, 120.2 us)
Sparse Core Ops, SparseCore 0:
  30.6 169.3 all-gather.1
  472.6 123.1 reduce-scatter.1

commit v3 on v2

--- a/solution.py
+++ b/solution.py
@@ -597,44 +597,327 @@
     )(values)
 
 
-def packed(pieces):
-    flat = []
-    for piece in pieces:
-        piece = piece.reshape(-1)
-        flat.append(jnp.pad(piece, (0, -piece.size % 128)))
-    flat = jnp.concatenate(flat)
-    return jnp.pad(flat, (0, -flat.size % 1024)).reshape(-1, 128)
-
-
-def unpacked(rows, shapes):
-    flat = rows.reshape(-1)
-    pieces, at = [], 0
-    for shape in shapes:
-        size = math.prod(shape)
-        pieces.append(flat[at : at + size].reshape(shape))
-        at += size + -size % 128
-    return pieces
-
-
-def small_sum(name, cid, over_dp, over_mp, over_all):
-    first = small_gather(name + "_dp", cid, packed(over_dp + over_all), "dp")
-    first = unpacked(jnp.sum(first, axis=0), [v.shape for v in over_dp + over_all])
-    rest = first[len(over_dp) :]
-    second = small_gather(name + "_mp", cid + 1, packed(over_mp + rest), "mp")
-    second = unpacked(jnp.sum(second, axis=0), [v.shape for v in over_mp + over_all])
-    return first[: len(over_dp)], second[: len(over_mp)], second[len(over_mp) :]
-
-
-def lookup_kernel(count_ref, key_ref, table_ref, out_ref, rows_ref):
-    spots = rows_ref.shape[0]
+def exchange(axis, me, here, source, slots, send, recv, first):
+    count = slots.shape[0]
+    copies = []
+    for hop in range(1, count):
+        peer = lax.rem(me + hop, count)
+        copy = pltpu.make_async_remote_copy(
+            src_ref=source,
+            dst_ref=slots.at[me],
+            send_sem=send.at[first + hop],
+            recv_sem=recv.at[first + hop],
+            device_id=(peer, here) if axis == "dp" else (here, peer),
+            device_id_type=MESH,
+        )
+        copy.start()
+        copies.append(copy)
+    slots[me] = source[...]
+    for copy in copies:
+        copy.wait()
+    total = slots[0]
+    for index in range(1, count):
+        total = total + slots[index]
+    return total
+
+
+def greet_all(dp, mp, size_dp, size_mp):
+    barrier = pltpu.get_barrier_semaphore()
+    for hop in range(1, size_dp):
+        pl.semaphore_signal(
+            barrier, inc=1, device_id=(lax.rem(dp + hop, size_dp), mp), device_id_type=MESH
+        )
+    for hop in range(1, size_mp):
+        pl.semaphore_signal(
+            barrier, inc=1, device_id=(dp, lax.rem(mp + hop, size_mp)), device_id_type=MESH
+        )
+    pl.semaphore_wait(barrier, size_dp + size_mp - 2)
+
+
+def lane_rows(values):
+    values = values.reshape(-1)
+    return jnp.pad(values, (0, -values.size % 128)).reshape(-1, 128)
+
+
+def fold(values):
+    return jnp.sum(values, axis=0, keepdims=True)
+
+
+def stats_kernel(full, size_dp, size_mp, *refs):
+    row_part, row_old, col_part, col_old, weight_sq = (refs[5 * n : 5 * n + 5] for n in range(5))
+    loss_part, norm_one, norm_two, norm_three, norms, second_old = refs[25:31]
+    refs = refs[31:]
+    row_out, col_out = refs[0:5], refs[5:10]
+    loss_out, grads_out, second_out, norms_out, rate_out = refs[10:15]
+    send_dp, slots_dp, send_mp, slots_mp, parts, part_slots, whole, send, recv = refs[15:]
+    dp = lax.axis_index("dp")
+    mp = lax.axis_index("mp")
+    greet_all(dp, mp, size_dp, size_mp)
+    beta = 1.0 - STEP ** (-0.8)
+    width = norms.shape[1]
+
+    at = 0
+    marks = []
+
+    def put(values):
+        nonlocal at
+        rows = values.shape[0]
+        send_dp[at : at + rows, :] = values
+        marks.append((at, rows))
+        at += rows
+
+    norm_rows = width // 128
+    for ref in (norm_one, norm_two, norm_three):
+        for which in range(2):
+            for piece in range(norm_rows):
+                put(ref[which : which + 1, piece * 128 : piece * 128 + 128])
+    marks.clear()
+    count_norm = at
+    for index in (0, 2, 4):
+        put(row_part[index][...])
+    for index in (1, 3):
+        put(col_part[index][...])
+    put(loss_part[...])
+    for index in (1, 3):
+        put(fold(row_old[index][...]))
+    for index in range(5):
+        put(fold(weight_sq[index][...]))
+    if at < send_dp.shape[0]:
+        send_dp[at:, :] = jnp.zeros((send_dp.shape[0] - at, 128), jnp.float32)
+    over_dp = exchange("dp", dp, mp, send_dp, slots_dp, send, recv, 0)
+    taken = [over_dp[start : start + rows] for start, rows in marks]
+    loss_out[...] = taken[5]
+    row_full = {0: taken[0], 2: taken[1], 4: taken[2]}
+    col_full = {1: taken[3], 3: taken[4]}
+    old_total = {1: taken[6], 3: taken[7]}
+    weight_rows = taken[8:13]
+
+    at = 0
+    marks = []
+
+    def put_mp(values):
+        nonlocal at
+        rows = values.shape[0]
+        send_mp[at : at + rows, :] = values
+        marks.append((at, rows))
+        at += rows
+
+    for index in (0, 2, 4):
+        put_mp(col_part[index][...])
+    for index in (1, 3):
+        put_mp(row_part[index][...])
+    for index in range(5):
+        put_mp(fold(row_full[index] if index in row_full else col_full[index]))
+    for index in (0, 2, 4):
+        put_mp(fold(row_old[index][...]))
+    for index in range(5):
+        put_mp(weight_rows[index])
+    if at < send_mp.shape[0]:
+        send_mp[at:, :] = jnp.zeros((send_mp.shape[0] - at, 128), jnp.float32)
+    each = count_norm // size_mp
+    for index in range(size_mp):
+        parts[index] = over_dp[index * each : index * each + each]
+    first = size_dp + size_mp
+    copies = []
+    for hop in range(1, size_mp):
+        peer = lax.rem(mp + hop, size_mp)
+        copy = pltpu.make_async_remote_copy(
+            src_ref=parts.at[peer],
+            dst_ref=part_slots.at[mp],
+            send_sem=send.at[first + hop],
+            recv_sem=recv.at[first + hop],
+            device_id=(dp, peer),
+            device_id_type=MESH,
+        )
+        copy.start()
+        copies.append(copy)
+    part_slots[mp] = parts[mp]
+    over_mp = exchange("mp", mp, dp, send_mp, slots_mp, send, recv, size_dp)
+    for copy in copies:
+        copy.wait()
+    summed = part_slots[0]
+    for index in range(1, size_mp):
+        summed = summed + part_slots[index]
+    whole[mp] = summed
+    first += size_mp
+    copies = []
+    for hop in range(1, size_mp):
+        peer = lax.rem(mp + hop, size_mp)
+        copy = pltpu.make_async_remote_copy(
+            src_ref=whole.at[mp],
+            dst_ref=whole.at[mp],
+            send_sem=send.at[first + hop],
+            recv_sem=recv.at[first + hop],
+            device_id=(dp, peer),
+            device_id_type=MESH,
+        )
+        copies.append(copy)
+    for copy in copies:
+        copy.start()
+    taken = [over_mp[start : start + rows] for start, rows in marks]
+    for slot, index in enumerate((0, 2, 4)):
+        col_full[index] = taken[slot]
+        old_total[index] = taken[10 + slot]
+    for slot, index in enumerate((1, 3)):
+        row_full[index] = taken[3 + slot]
+    square_total = taken[5:10]
+    weight_total = taken[13:18]
+    for index in range(5):
+        full_rows, full_cols = full[index]
+        row_new = beta * row_old[index][...] + (1.0 - beta) * row_full[index] / full_cols
+        col_new = beta * col_old[index][...] + (1.0 - beta) * col_full[index] / full_rows
+        row_out[index][...] = row_new
+        col_out[index][...] = col_new
+        mean = (
+            beta * jnp.sum(old_total[index], axis=1, keepdims=True)
+            + (1.0 - beta) * jnp.sum(square_total[index], axis=1, keepdims=True) / full_cols
+        ) / full_rows
+        rate = RHO * jnp.sqrt(
+            jnp.sum(weight_total[index], axis=1, keepdims=True) / (full_rows * full_cols)
+        )
+        rate_out[index : index + 1, :] = jnp.broadcast_to(mean, (1, 128))
+        rate_out[8 + index : 9 + index, :] = jnp.broadcast_to(rate, (1, 128))
+    for copy in copies:
+        copy.wait()
+    for row in range(6):
+        for piece in range(norm_rows):
+            place = row * norm_rows + piece
+            grads_out[row : row + 1, piece * 128 : piece * 128 + 128] = whole[
+                place // each, place % each : place % each + 1, :
+            ]
+    grad = grads_out[...]
+    second = beta * second_old[...] + (1.0 - beta) * (grad * grad + EPS_ONE)
+    second_out[...] = second
+    step = grad * lax.rsqrt(second)
+    entries = step.size
+
+    def mean_square(values):
+        return jnp.sum(jnp.sum(values * values, axis=0, keepdims=True), axis=1, keepdims=True) / (
+            entries
+        )
+
+    step = step / jnp.maximum(1.0, jnp.sqrt(mean_square(step)) / CLIP)
+    old = norms[...]
+    norms_out[...] = old - RHO * jnp.sqrt(mean_square(old)) * step
+
+
+def update_stats(cid, row_parts, rows_old, col_parts, cols_old, weight_sq, loss, norm_parts, norms, second, full):
+    size_dp = lax.axis_size("dp")
+    size_mp = lax.axis_size("mp")
+    f32 = jnp.float32
+    rows_old2 = [lane_rows(v) for v in rows_old]
+    cols_old2 = [lane_rows(v) for v in cols_old]
+    args = (
+        [lane_rows(v) for v in row_parts]
+        + rows_old2
+        + [lane_rows(v) for v in col_parts]
+        + cols_old2
+        + [v if v.ndim == 2 else lane_rows(v) for v in weight_sq]
+        + [lane_rows(loss)]
+        + list(norm_parts)
+        + [norms, second]
+    )
+    width = norms.shape[1]
+    count_norm = 6 * width // 128
+    size_a = count_norm + sum(rows_old2[n].shape[0] for n in (0, 2, 4))
+    size_a += sum(cols_old2[n].shape[0] for n in (1, 3)) + 8
+    size_a += -size_a % 8
+    size_b = sum(cols_old2[n].shape[0] for n in (0, 2, 4))
+    size_b += sum(rows_old2[n].shape[0] for n in (1, 3)) + 13
+    size_b += -size_b % 8
+    each = count_norm // size_mp
+    out_shape = [jax.ShapeDtypeStruct(v.shape, f32) for v in rows_old2 + cols_old2]
+    out_shape += [
+        jax.ShapeDtypeStruct((1, 128), f32),
+        jax.ShapeDtypeStruct(norms.shape, f32),
+        jax.ShapeDtypeStruct(norms.shape, f32),
+        jax.ShapeDtypeStruct(norms.shape, f32),
+        jax.ShapeDtypeStruct((16, 128), f32),
+    ]
+    sems = size_dp + 3 * size_mp
+    vmem = pl.BlockSpec(memory_space=pltpu.VMEM)
+    found = pl.pallas_call(
+        functools.partial(stats_kernel, full, size_dp, size_mp),
+        out_shape=out_shape,
+        in_specs=[vmem] * len(args),
+        out_specs=[vmem] * len(out_shape),
+        scratch_shapes=[
+            pltpu.VMEM((size_a, 128), f32),
+            pltpu.VMEM((size_dp, size_a, 128), f32),
+            pltpu.VMEM((size_b, 128), f32),
+            pltpu.VMEM((size_mp, size_b, 128), f32),
+            pltpu.VMEM((size_mp, each, 128), f32),
+            pltpu.VMEM((size_mp, each, 128), f32),
+            pltpu.VMEM((size_mp, each, 128), f32),
+            pltpu.SemaphoreType.DMA((sems,)),
+            pltpu.SemaphoreType.DMA((sems,)),
+        ],
+        compiler_params=pltpu.CompilerParams(collective_id=cid, has_side_effects=True),
+        cost_estimate=cost_of(12),
+        name="update_stats",
+    )(*args)
+    rows_new = [found[n].reshape(-1)[: rows_old[n].size] for n in range(5)]
+    cols_new = [found[5 + n].reshape(-1)[: cols_old[n].size] for n in range(5)]
+    loss_sums = found[10][0, :NSRC]
+    return rows_new, cols_new, loss_sums, found[11], found[12], found[13], found[14]
+
+
+def clip_kernel(entries, size_dp, size_mp, *refs):
+    parts, rate = refs[:5], refs[5]
+    out, mine, slots_dp, slots_mp, send, recv = refs[6:]
+    dp = lax.axis_index("dp")
+    mp = lax.axis_index("mp")
+    greet_all(dp, mp, size_dp, size_mp)
+    mine[...] = jnp.zeros_like(mine)
+    for index in range(5):
+        mine[index : index + 1, :] = fold(parts[index][...])
+    mine[...] = exchange("dp", dp, mp, mine, slots_dp, send, recv, 0)
+    total = exchange("mp", mp, dp, mine, slots_mp, send, recv, size_dp)
+    total = jnp.sum(total, axis=1, keepdims=True)
+    for index in range(5):
+        clip = jnp.maximum(1.0, jnp.sqrt(total[index : index + 1] / entries[index]) / CLIP)
+        out[index : index + 1, :] = rate[8 + index : 9 + index, :] / clip
+
+
+def clip_rates(cid, step_parts, rate, entries):
+    size_dp = lax.axis_size("dp")
+    size_mp = lax.axis_size("mp")
+    vmem = pl.BlockSpec(memory_space=pltpu.VMEM)
+    sems = size_dp + size_mp
+    return pl.pallas_call(
+        functools.partial(clip_kernel, entries, size_dp, size_mp),
+        out_shape=jax.ShapeDtypeStruct((8, 128), jnp.float32),
+        in_specs=[vmem] * 6,
+        out_specs=vmem,
+        scratch_shapes=[
+            pltpu.VMEM((8, 128), jnp.float32),
+            pltpu.VMEM((size_dp, 8, 128), jnp.float32),
+            pltpu.VMEM((size_mp, 8, 128), jnp.float32),
+            pltpu.SemaphoreType.DMA((sems,)),
+            pltpu.SemaphoreType.DMA((sems,)),
+        ],
+        compiler_params=pltpu.CompilerParams(collective_id=cid, has_side_effects=True),
+        cost_estimate=cost_of(8),
+        name="clip_rates",
+    )(*[lane_rows(v) for v in step_parts], rate)
+
+
+UNROLL = 8
+
+
+def lookup_kernel(shift, count_ref, key_ref, table_ref, out_ref, low_ref, square_ref, rows_ref):
+    spots = out_ref.shape[0]
+    vocab, width = table_ref.shape
     rows_ref[...] = jnp.zeros_like(rows_ref)
 
-    def one(i, carry):
-        key = key_ref[i]
-        rows_ref[pl.ds(key % spots, 1), :] = table_ref[pl.ds(key // spots, 1), :]
+    def some(i, carry):
+        for j in range(UNROLL):
+            key = key_ref[i * UNROLL + j]
+            place = key & ((1 << shift) - 1)
+            rows_ref[pl.ds(place, 1), :] = table_ref[pl.ds(key >> shift, 1), :]
         return carry
 
-    lax.fori_loop(0, count_ref[0], one, 0)
+    lax.fori_loop(0, (count_ref[0] + UNROLL - 1) // UNROLL, some, 0)
 
     def narrow(i, carry):
         at = pl.ds(pl.multiple_of(i * 256, 256), 256)
@@ -642,27 +925,47 @@
         return carry
 
     lax.fori_loop(0, spots // 256, narrow, 0)
-
-
-def lookup(keys, count, table, spots):
-    width = table.shape[1]
+    strip = 48 if vocab % 48 == 0 else 8
+
+    def lower(i, total):
+        at = pl.ds(pl.multiple_of(i * strip, strip), strip)
+        values = table_ref[at, :]
+        low_ref[at, :] = values.astype(jnp.bfloat16)
+        for row in range(0, strip, 8):
+            piece = values[row : row + 8, :]
+            total = total + piece * piece
+        return total
+
+    total = lax.fori_loop(0, vocab // strip, lower, jnp.zeros((8, width), jnp.float32))
+    folded = total[:, 0:128]
+    for start in range(128, width, 128):
+        folded = folded + total[:, start : start + 128]
+    square_ref[...] = folded
+
+
+def lookup(keys, count, table, spots, shift):
+    vocab, width = table.shape
     smem = pl.BlockSpec(memory_space=pltpu.SMEM)
     vmem = pl.BlockSpec(memory_space=pltpu.VMEM)
     return pl.pallas_call(
-        lookup_kernel,
-        out_shape=jax.ShapeDtypeStruct((spots, width), jnp.bfloat16),
+        functools.partial(lookup_kernel, shift),
+        out_shape=[
+            jax.ShapeDtypeStruct((spots, width), jnp.bfloat16),
+            jax.ShapeDtypeStruct((vocab, width), jnp.bfloat16),
+            jax.ShapeDtypeStruct((8, 128), jnp.float32),
+        ],
         in_specs=[smem, smem, vmem],
-        out_specs=vmem,
-        scratch_shapes=[pltpu.VMEM((spots, width), jnp.float32)],
+        out_specs=[vmem] * 3,
+        scratch_shapes=[pltpu.VMEM((spots + 8, width), jnp.float32)],
         compiler_params=pltpu.CompilerParams(vmem_limit_bytes=VMEM_CAP),
         cost_estimate=cost_of(20),
         name="lookup",
     )(count, keys, table)
 
 
-def scatter_kernel(count_ref, key_ref, head_ref, rows_in_ref, grad_ref, rows_ref):
-    spots = rows_ref.shape[0]
-    vocab = grad_ref.shape[0]
+def scatter_kernel(shift, count_ref, key_ref, head_ref, rows_in_ref, grad_ref, rows_ref):
+    spots = rows_in_ref.shape[0]
+    width = grad_ref.shape[1]
 
     def widen(i, carry):
         at = pl.ds(pl.multiple_of(i * 256, 256), 256)
@@ -670,27 +973,30 @@
         return carry
 
     lax.fori_loop(0, spots // 256, widen, 0)
+    rows_ref[spots:, :] = jnp.zeros((8, width), jnp.float32)
     grad_ref[...] = head_ref[...].astype(jnp.float32)
 
-    def one(i, carry):
-        key = key_ref[i]
-        grad_ref[pl.ds(key // spots, 1), :] += rows_ref[pl.ds(key % spots, 1), :]
+    def some(i, carry):
+        for j in range(UNROLL):
+            key = key_ref[i * UNROLL + j]
+            place = key & ((1 << shift) - 1)
+            grad_ref[pl.ds(key >> shift, 1), :] += rows_ref[pl.ds(place, 1), :]
         return carry
 
-    lax.fori_loop(0, count_ref[0], one, 0)
-
-
-def scatter(keys, count, head_grad, rows):
+    lax.fori_loop(0, (count_ref[0] + UNROLL - 1) // UNROLL, some, 0)
+
+
+def scatter(keys, count, head_grad, rows, shift):
     spots, width = rows.shape
     vocab = head_grad.shape[0]
     smem = pl.BlockSpec(memory_space=pltpu.SMEM)
     vmem = pl.BlockSpec(memory_space=pltpu.VMEM)
     return pl.pallas_call(
-        scatter_kernel,
+        functools.partial(scatter_kernel, shift),
         out_shape=jax.ShapeDtypeStruct((vocab, width), jnp.float32),
         in_specs=[smem, smem, vmem, vmem],
         out_specs=vmem,
-        scratch_shapes=[pltpu.VMEM((spots, width), jnp.float32)],
+        scratch_shapes=[pltpu.VMEM((spots + 8, width), jnp.float32)],
         compiler_params=pltpu.CompilerParams(vmem_limit_bytes=VMEM_CAP),
         cost_estimate=cost_of(23),
         name="scatter",
@@ -855,6 +1161,10 @@
         (all_sources[:, None] == jnp.arange(NSRC, dtype=jnp.int32)[None, :]).astype(f32), axis=0
     )
 
+    w_qkv, w_out, w_fc, w_proj, all_ids = lax.optimization_barrier(
+        (w_qkv, w_out, w_fc, w_proj, all_ids)
+    )
+
 
     def own_and_twins(weight, axis):
         weight = weight.astype(bf16)
@@ -868,8 +1178,6 @@
     pair_out = own_and_twins(w_out, 0)
     pair_fc = own_and_twins(w_fc, 1)
     pair_proj = own_and_twins(w_proj, 0)
-    wide_table = lax.all_gather(embedding.astype(bf16), "dp", axis=1, tiled=True)
-
     place = (
         (jnp.arange(size_mp, dtype=jnp.int32) * size_dp)[None, :, None] * rows
         + (jnp.arange(size_dp, dtype=jnp.int32) * rows)[:, None, None]
@@ -877,10 +1185,12 @@
     ).reshape(size_dp, tokens)
     local_ids = all_ids - first_row
     inside = (local_ids >= 0) & (local_ids < vocab)
-    keys = jnp.where(inside, local_ids * spots + place, jnp.iinfo(jnp.int32).max)
+    shift = spots.bit_length()
+    idle = ((vocab - 1) << shift) + spots
+    keys = jnp.where(inside, (local_ids << shift) + place, idle)
     keys = jnp.sort(keys.reshape(-1))
     owned = jnp.sum(inside.astype(jnp.int32)).reshape(1)
-    found = lookup(keys, owned, embedding, spots)
+    found, low_table, table_sq = lookup(keys, owned, embedding, spots, shift)
     picked_rows, wide_qkv, wide_out, wide_fc = line_call(
         "rs_lookup",
         1,
@@ -901,6 +1211,8 @@
     )
     stream0 = jnp.swapaxes(stream0, 0, 1).reshape(rows, width)
 
+    low_table, picked_rows = lax.optimization_barrier((low_table, picked_rows))
+    wide_table = lax.all_gather(low_table, "dp", axis=1, tiled=True)
     row_f32 = jax.ShapeDtypeStruct((rows, width), f32)
     pair_f32 = jax.ShapeDtypeStruct((8, width), f32)
     (inner_one,) = line_call(
@@ -966,8 +1278,8 @@
     top = jnp.max(tops, axis=0)
     total = jnp.sum(sums[:, 0] * jnp.exp(tops - top[None, :]), axis=0)
     pick = jnp.sum(picks[:, 0], axis=0)
-    stats = small_gather("gather_stats", 5, packed([top, total, pick]), "mp")
-    stats = stats.reshape(size_mp, -1)[:, : 3 * tokens].reshape(size_mp, 3, tokens)
+    stats = jnp.concatenate([v.reshape(-1, 128) for v in (top, total, pick)])
+    stats = small_gather("gather_stats", 5, stats, "mp").reshape(size_mp, 3, tokens)
     highest = jnp.max(stats[:, 0], axis=0)
     log_total = highest + jnp.log(
         jnp.sum(stats[:, 1] * jnp.exp(stats[:, 0] - highest[None, :]), axis=0)
@@ -1057,74 +1369,55 @@
         [("scatter", 0, grad_fc), ("scatter", 0, grad_qkv)],
     )
 
-    def to_owner(share, axis):
+    def to_twins(share, axis):
         pieces = jnp.split(share, seqs, axis=axis)
-        mine = pieces[0]
+        found = []
         for turn in range(1, seqs):
             back = [(i, (i - turn * sharers) % size_mp) for i in range(size_mp)]
-            mine = mine + lax.ppermute(pieces[turn].astype(bf16), "mp", back).astype(f32)
-        return mine
-
-    grad_proj = to_owner(grad_proj, 0)
-    grad_out = to_owner(grad_out, 0)
-    grad_fc = to_owner(grad_fc, 1)
-    grad_qkv = to_owner(grad_qkv, 1)
-    grad_table = scatter(keys, owned, head_grad, drows)
-
-    beta = 1.0 - STEP ** (-0.8)
+            found.append(lax.ppermute(pieces[turn].astype(bf16), "mp", back))
+        return pieces[0], found
+
+    shares = [
+        to_twins(grad_qkv, 1),
+        to_twins(grad_out, 0),
+        to_twins(grad_fc, 1),
+        to_twins(grad_proj, 0),
+    ]
+    grad_table = scatter(keys, owned, head_grad, drows, shift)
+    shares, grad_table = lax.optimization_barrier((shares, grad_table))
+    grad_qkv, grad_out, grad_fc, grad_proj = [
+        sum((piece.astype(f32) for piece in found), mine) for mine, found in shares
+    ]
+
     weights = (embedding, w_qkv, w_out, w_fc, w_proj)
     grads = (grad_table, grad_qkv, grad_out, grad_fc, grad_proj)
-    rows_old = (rows_table, rows_qkv, rows_out, rows_fc, rows_proj)
-    cols_old = (cols_table, cols_qkv, cols_out, cols_fc, cols_proj)
     row_span = (size_mp, size_dp, size_mp, size_dp, size_mp)
     col_span = (size_dp, size_mp, size_dp, size_mp, size_dp)
+    full = tuple(
+        (g.shape[0] * r, g.shape[1] * c) for g, r, c in zip(grads, row_span, col_span)
+    )
     squares = [gradient * gradient + EPS_ONE for gradient in grads]
-    row_parts = [jnp.sum(square, axis=1) for square in squares]
-    col_parts = [jnp.sum(square, axis=0) for square in squares]
-    square_sums = jnp.stack([jnp.sum(part) for part in col_parts])
-    weight_sums = jnp.stack([jnp.sum(value * value) for value in weights])
-    old_sums = jnp.stack([jnp.sum(old) / span for old, span in zip(rows_old, col_span)])
-    norm_partial = jnp.concatenate([norm1[:2], norm2[:2], norm3[:2]])
-    on_dp, on_mp, on_all = small_sum(
-        "sum_squares",
+    rows_new, cols_new, loss_sums, grad_norms, second_new, norms_new, rates = update_stats(
         10,
-        [col_parts[1], col_parts[3], row_parts[0], row_parts[2], row_parts[4], loss_part],
-        [row_parts[1], row_parts[3], col_parts[0], col_parts[2], col_parts[4]],
-        [square_sums, weight_sums, old_sums, norm_partial],
-    )
-    square_sums, weight_sums, old_sums, grad_norms = on_all
-    loss_sums = on_dp[5]
-    row_full = (on_dp[2], on_mp[0], on_dp[3], on_mp[1], on_dp[4])
-    col_full = (on_mp[2], on_dp[0], on_mp[3], on_dp[1], on_mp[4])
-    rows_new = []
-    cols_new = []
-    steps = []
-    entries = []
-    for index in range(5):
-        full_rows = grads[index].shape[0] * row_span[index]
-        full_cols = grads[index].shape[1] * col_span[index]
-        entries.append(full_rows * full_cols)
-        rows_next = beta * rows_old[index] + (1.0 - beta) * row_full[index] / full_cols
-        cols_next = beta * cols_old[index] + (1.0 - beta) * col_full[index] / full_rows
-        mean = beta * old_sums[index] / full_rows + (1.0 - beta) * (
-            square_sums[index] / (full_rows * full_cols)
-        )
-        rows_new.append(rows_next)
-        cols_new.append(cols_next)
-        steps.append(
-            grads[index] * lax.rsqrt(rows_next[:, None] * cols_next[None, :] / mean)
-        )
-    step_part = jnp.stack([jnp.sum(piece * piece) for piece in steps])
-    unused, unused, (step_sq,) = small_sum("sum_steps", 12, [], [], [step_part])
-    updated = []
-    for index in range(5):
-        clipped = steps[index] / jnp.maximum(1.0, jnp.sqrt(step_sq[index] / entries[index]) / CLIP)
-        rate = RHO * jnp.sqrt(weight_sums[index] / entries[index])
-        updated.append(weights[index] - rate * clipped)
-    second_new = beta * second_norms + (1.0 - beta) * (grad_norms * grad_norms + EPS_ONE)
-    norm_steps = grad_norms * lax.rsqrt(second_new)
-    norm_steps = norm_steps / jnp.maximum(1.0, jnp.sqrt(jnp.mean(norm_steps * norm_steps)) / CLIP)
-    norms_new = norm_params - RHO * jnp.sqrt(jnp.mean(norm_params * norm_params)) * norm_steps
+        [jnp.sum(square, axis=1) for square in squares],
+        (rows_table, rows_qkv, rows_out, rows_fc, rows_proj),
+        [jnp.sum(square, axis=0) for square in squares],
+        (cols_table, cols_qkv, cols_out, cols_fc, cols_proj),
+        [table_sq] + [jnp.sum(value * value, axis=0) for value in weights[1:]],
+        loss_part,
+        (norm1, norm2, norm3),
+        norm_params,
+        second_norms,
+        full,
+    )
+    steps = [
+        grads[n] * lax.rsqrt(rows_new[n][:, None] * cols_new[n][None, :] / rates[n, 0])
+        for n in range(5)
+    ]
+    factors = clip_rates(
+        11, [jnp.sum(step * step, axis=0) for step in steps], rates, [r * c for r, c in full]
+    )
+    updated = [weights[n] - factors[n, 0] * steps[n] for n in range(5)]
     return (
         loss_sums,
         counts,

time: 922 us -> 800 us (0.87)
  Pallas kernels: 605 us -> 553 us
  local copies, waits for them, and re-layouts: 58.1 us -> 31.7 us
  between operations: 33.3 us -> 15.3 us
  other arithmetic: 92.5 us -> 75.1 us
    pallas_call x6 -> x2, Pallas kernels: 53.2 us -> 16.6 us  [small_gather(): pl.pallas_call(functools.partial(small_gather_kernel, axis, count), out_s...]
    pallas_call x8, Pallas kernels: 392 us -> 367 us  [line_call(): return list(call(*args))]
    reduce_sum x27 -> x14, other arithmetic: 46.6 us -> 22.8 us  [the longest x5 11 us: local(): jnp.sum(step * step, axis=0)]
    unnamed x181 -> x143, local copies, waits for them, and re-layouts: 26.9 us -> 12.9 us
    another operation x6 -> x1, local copies, waits for them, and re-layouts: 12 us -> 0.01 us  [the longest x1 3.83 us: local(): weight_sums = jnp.stack([jnp.sum(value * value) for value in weights])]
    ppermute x4, waiting for transfers between devices: 18.2 us -> 7.24 us  [to_twins(): found.append(lax.ppermute(pieces[turn].astype(bf16), 'mp', back))]
    pallas_call x2 -> x4, Pallas kernels: 43.2 us -> 52.5 us  [the longest x1 17 us: update_stats(): pl.pallas_call(functools.partial(stats_kernel, full, size_dp, size_mp), o...]
  transfers between devices with their start and end apart: 12 -> 12, of which waited for: 4 -> 4; matrix products, arithmetic and copies ran while one was open for 17% -> 16% of each run, Pallas kernels for 46% -> 42%
where the time goes in v3:
time: 800 us; the launch traced here: 793 us
  Pallas kernels  553 us (69%)
  matrix products  82.8 us (10%)
  other arithmetic  75.1 us (9%)
  local copies, waits for them, and re-layouts  31.7 us (4%)
  starting transfers between devices  18.6 us (2%)
  waiting for transfers between devices  17 us (2%)
  between operations  15.3 us (2%)
    pallas_call x8, Pallas kernels, line_call(): return list(call(*args))  367 us
    pallas_call x1, Pallas kernels, head_back(): pl.pallas_call(functools.partial(head_back_kernel, rows, block, tile), gr...  69.7 us
    pallas_call x1, Pallas kernels, head_stats(): pl.pallas_call(functools.partial(head_stats_kernel, block, tile), grid=(s...  47.1 us
    sub x5, other arithmetic, local(): updated = [weights[n] - factors[n, 0] * steps[n] for n in range(5)]  17.8 us
    pallas_call x1, Pallas kernels, update_stats(): pl.pallas_call(functools.partial(stats_kernel, full, size_dp, size_mp), o...  17 us
    pallas_call x2, Pallas kernels, small_gather(): pl.pallas_call(functools.partial(small_gather_kernel, axis, count), out_s...  16.6 us
  transfers between devices with their start and end apart: 12, of which 4 were waited for; matrix products, arithmetic and copies ran while one was open for 16% of the time, Pallas kernels for 42%

profile of v3, /device:TPU:0, one launch (start us, length us, event | category | flops | bytes accessed | tf_op | source)
XLA Modules:
  0.0 793.4 jit_solution(7295419956289438730)
XLA Ops:
  8.6 7.8 gather_ids.1
  18.0 2.6 collective-permute-start.1
  22.2 2.6 collective-permute-start.2
  25.7 6.8 sort.14
  32.5 12.7 %lookup.1 = (bf16[8192,256]{1,0:T(8,128)(2,1)}, bf16[6288,256]{1,0:T(8,128)(2,1)}, f32[8,128]{1,0:T(8,128)}) custom-call(s32[1]{0:T(128)} %bitcast.2.count_ref, s32[8192]{0:T(1024)} %get-tuple-element.89.key_ref, f32[6288,256]{1,0:T(8,128)} %table_ref.1), custom_call_target="tpu_custom_call" | custom-call | flops 20000000000 | bytes 60000000 | tf_op jit(solution)/shard_map/lookup/pallas_call | solution.py:950
  47.5 56.2 %rs_lookup.1 = (bf16[1024,256]{1,0:T(8,128)(2,1)}, bf16[1024,768]{1,0:T(8,128)(2,1)}, bf16[256,1024]{1,0:T(8,128)(2,1)}, bf16[1024,1024]{1,0:T(8,128)(2,1)}) custom-call(bf16[8192,256]{1,0:T(8,128)(2,1)} %get-tuple-element.90.refs_0_, bf16[256,768]{1,0:T(8,128)(2,1)} %pad_maximum_fusion.3.refs_1_, bf16[256,256]{1,0:T(8,128)(2,1)} %pad_maximum_fusion.4.refs_2_, ...), custom_call_target="tpu_custom_call" | custom-call | flops 49999998976 | bytes 150000000 | tf_op jit(solution)/shard_map/rs_lookup/pallas_call | solution.py:414
  105.1 3.5 all-to-all-start
  109.8 8.2 %collective-permute-done.3 = bf16[512,256]{1,0:T(8,128)(2,1)S(1)} collective-permute-done((bf16[512,256]{1,0:T(8,128)(2,1)S(1)}, bf16[512,256]{1,0:T(8,128)(2,1)S(1)}, u32[]{:S(2)}, u32[]{:S(2)}) %collective-permute-start.3) | collective-permute-done | bytes 262176 | tf_op jit(solution)/shard_map/ppermute | solution.py:1174
  118.8 1.5 all-to-all-done
  121.1 16.9 %ag_inner1.1 = bf16[1024,1024]{1,0:T(8,128)(2,1)} custom-call(bf16[256,1024]{1,0:T(8,128)(2,1)} %bitcast.192, f32[6,1024]{1,0:T(8,128)} %refs_29_.1), custom_call_target="tpu_custom_call" | custom-call | flops 16999999488 | bytes 51000000 | tf_op jit(solution)/shard_map/ag_inner1/pallas_call | solution.py:414
  138.1 3.4 convolution_convert_fusion.7
  141.6 7.6 fusion.48
  149.2 8.0 %fusion = f32[4,1024]{1,0:T(4,128)S(1)} fusion(f32[4,1024,1024]{1,2,0:T(8,128)} %get-tuple-element.195, f32[4,1024]{1,0:T(4,128)S(1)} %get-tuple-element.194), kind=kLoop, calls=%fused_computation.6 | loop fusion | flops 8384512 | bytes 16809984 | tf_op jit(solution)/shard_map/reduce_sum | solution.py:1086
  157.2 8.1 %fusion.21 = bf16[4,64,1024]{2,1,0:T(8,128)(2,1)S(1)} fusion(f32[4,1024,1024]{1,2,0:T(8,128)} %get-tuple-element.195, f32[4,1024]{1,0:T(4,128)S(1)} %fusion, f32[4,1024]{1,0:T(4,128)S(1)} %get-tuple-element.194, bf16[1024,4,3,64]{0,3,2,1:T(8,128)(2,1)S(1)} %bitcast.186), kind=kOutput, calls=%fused_computation.46 | convolution fusion | flops 549715968 | bytes 17858560 | tf_op jit(solution)/shard_map/hqk,khe->qhe/dot_general | solution.py:1088
  166.2 2.1 convolution_convert_fusion.4.refs_0_
  168.2 54.8 %attn_sum.1 = (bf16[1024,1024]{1,0:T(8,128)(2,1)}, f32[256,1024]{1,0:T(8,128)}, bf16[1024,1024]{1,0:T(8,128)(2,1)}) custom-call(bf16[1024,1024]{1,0:T(8,128)(2,1)} %convolution_convert_fusion.4.refs_0_, bf16[256,1024]{1,0:T(8,128)(2,1)} %bitcast.193, f32[6,1024]{1,0:T(8,128)} %refs_29_.1, bf16[1024,256]{1,0:T(8,128)(2,1)} %pad_maximum_fusion.2.refs_3_), custom_call_target="tpu_custom_call" | custom-call | flops 32000000000 | bytes 96000000 | tf_op jit(solution)/shard_map/attn_sum/pallas_call | solution.py:414
  223.1 4.1 fusion.49
  227.2 4.0 convolution_convert_fusion.3.refs_0_
  231.2 58.4 %mlp_sum.1 = (bf16[2048,1024]{1,0:T(8,128)(2,1)}, f32[256,1024]{1,0:T(8,128)}) custom-call(bf16[1024,1024]{1,0:T(8,128)(2,1)} %convolution_convert_fusion.3.refs_0_, f32[256,1024]{1,0:T(8,128)} %get-tuple-element.103.refs_1_, f32[6,1024]{1,0:T(8,128)} %refs_29_.1), custom_call_target="tpu_custom_call" | custom-call | flops 57999998976 | bytes 174000000 | tf_op jit(solution)/shard_map/mlp_sum/pallas_call | solution.py:414
  289.6 47.1 %head_stats.1 = (bf16[6400,2048]{1,0:T(8,128)(2,1)}, f32[10,1,2048]{2,1,0:T(1,128)}, f32[10,1,2048]{2,1,0:T(1,128)}, f32[10,1,2048]{2,1,0:T(1,128)}) custom-call(bf16[6288,1024]{1,0:T(8,128)(2,1)} %all-gather.2.cloned.1.call-done.table_ref, bf16[2048,1024]{1,0:T(8,128)(2,1)} %get-tuple-element.104.final_ref, s32[1,2048]{1,0:T(1,128)} %bitcast.236, ...), custom_call_target="tpu_custom_call" | custom-call | flops 26373783552 | bytes 38633472 | tf_op jit(solution)/shard_map/head_stats/pallas_call | solution.py:452
  340.2 8.7 %gather_stats.1 = f32[8,48,128]{2,1,0:T(8,128)} custom-call(f32[48,128]{1,0:T(8,128)} %pad_maximum_fusion.5.src_ref), custom_call_target="tpu_custom_call" | custom-call | flops 6000000000 | bytes 18000000 | tf_op jit(solution)/shard_map/gather_stats/pallas_call | solution.py:588
  351.7 69.7 %head_back.1 = (bf16[6288,1024]{1,0:T(8,128)(2,1)}, bf16[2048,1024]{1,0:T(8,128)(2,1)}) custom-call(bf16[6400,2048]{1,0:T(8,128)(2,1)} %get-tuple-element.105.exp_ref, bf16[6288,1024]{1,0:T(8,128)(2,1)} %all-gather.2.cloned.1.call-done.table_ref, bf16[2048,1024]{1,0:T(8,128)(2,1)} %get-tuple-element.104.final_ref, ...), custom_call_target="tpu_custom_call" | custom-call | flops 52747567104 | bytes 51511296 | tf_op jit(solution)/shard_map/head_back/pallas_call | solution.py:520
  422.1 58.6 %final_back.1 = (bf16[1024,1024]{1,0:T(8,128)(2,1)}, f32[256,1024]{1,0:T(8,128)}, f32[8,1024]{1,0:T(8,128)}) custom-call(bf16[2048,1024]{1,0:T(8,128)(2,1)} %get-tuple-element.109.refs_0_, f32[256,1024]{1,0:T(8,128)} %get-tuple-element.110.refs_1_, f32[6,1024]{1,0:T(8,128)} %refs_29_.1), custom_call_target="tpu_custom_call" | custom-call | flops 60000002048 | bytes 180000000 | tf_op jit(solution)/shard_map/final_back/pallas_call | solution.py:414
  480.7 6.9 fusion.14
  487.6 3.7 convolution_convert_fusion.2.refs_0_
  491.3 34.8 %mlp_back.1 = (bf16[1024,1024]{1,0:T(8,128)(2,1)}, f32[256,1024]{1,0:T(8,128)}, f32[8,1024]{1,0:T(8,128)}) custom-call(bf16[1024,1024]{1,0:T(8,128)(2,1)} %convolution_convert_fusion.2.refs_0_, f32[256,1024]{1,0:T(8,128)} %get-tuple-element.103.refs_1_, f32[6,1024]{1,0:T(8,128)} %refs_29_.1, f32[256,1024]{1,0:T(8,128)} %get-tuple-element.112.refs_3_), custom_call_target="tpu_custom_call" | custom-call | flops 33999998976 | bytes 102000000 | tf_op jit(solution)/shard_map/mlp_back/pallas_call | solution.py:414
  526.1 2.4 convolution_convert_fusion.9
  528.6 15.3 %multiply_reduce_fusion = (f32[4,1024]{1,0:T(4,128)S(1)}, f32[4,1024,1024]{1,2,0:T(8,128)}) fusion(f32[4,1024,1024]{1,2,0:T(8,128)} %get-tuple-element.195, f32[4,1024]{1,0:T(4,128)S(1)} %log_add_fusion, bf16[1024,4,64]{0,2,1:T(8,128)(2,1)S(1)} %bitcast.182, bf16[1024,4,3,64]{0,3,2,1:T(8,128)(2,1)S(1)} %bitcast.187), kind=kOutput, calls=%fused_computation.1 | convolution fusion | flops 549449728 | bytes 34635776 | tf_op jit(solution)/shard_map/qhe,khe->hqk/dot_general | solution.py:1097
  543.9 1.4 slice-done.3
  545.3 7.8 multiply_convert_fusion
  553.1 2.7 fusion.25
  555.8 1.6 fusion.26
  557.4 3.1 fusion.22
  562.3 1.5 convolution_convert_fusion.8.refs_5_
  563.8 3.2 convolution_convert_fusion.5.refs_0_
  567.0 4.1 convolution_convert_fusion.1.refs_4_
  571.1 37.8 %attn_back.1 = (bf16[256,1024]{1,0:T(8,128)(2,1)}, f32[8,1024]{1,0:T(8,128)}, f32[1024,256]{1,0:T(8,128)}, f32[256,256]{1,0:T(8,128)}) custom-call(bf16[1024,1024]{1,0:T(8,128)(2,1)} %convolution_convert_fusion.5.refs_0_, bf16[256,1024]{1,0:T(8,128)(2,1)} %bitcast.194, f32[6,1024]{1,0:T(8,128)} %refs_29_.1, f32[256,1024]{1,0:T(8,128)} %get-tuple-element.114.refs_3_, ...), custom_call_target="tpu_custom_call" | custom-call | flops 28000000000 | bytes 84000000 | tf_op jit(solution)/shard_map/attn_back/pallas_call | solution.py:414
  612.8 1.9 copy.121
  614.7 3.5 all-to-all-start.1
  618.2 1.8 collective-permute-start.5
  621.7 6.1 convolution_convert_fusion.refs_1_
  627.8 3.0 convolution_convert_fusion.6.refs_2_
  631.6 49.7 %ag_lookup.1 = (bf16[8192,256]{1,0:T(8,128)(2,1)}, f32[256,1024]{1,0:T(8,128)}, f32[256,768]{1,0:T(8,128)}) custom-call(bf16[1024,256]{1,0:T(8,128)(2,1)} %bitcast.195, bf16[1024,1024]{1,0:T(8,128)(2,1)} %convolution_convert_fusion.refs_1_, bf16[1024,768]{1,0:T(8,128)(2,1)} %convolution_convert_fusion.6.refs_2_), custom_call_target="tpu_custom_call" | custom-call | flops 44999999488 | bytes 135000000 | tf_op jit(solution)/shard_map/ag_lookup/pallas_call | solution.py:414
  685.5 1.8 collective-permute-start.4
  688.5 11.9 %scatter.1 = f32[6288,256]{1,0:T(8,128)} custom-call(s32[1]{0:T(128)} %bitcast.2.count_ref, s32[8192]{0:T(1024)} %get-tuple-element.89.key_ref, bf16[6288,256]{1,0:T(8,128)(2,1)} %reduce-scatter.2.cloned.1.call-done.head_ref, bf16[8192,256]{1,0:T(8,128)(2,1)} %get-tuple-element.121.rows_in_ref), custom_call_target="tpu_custom_call" | custom-call | flops 23000000512 | bytes 69000000 | tf_op jit(solution)/shard_map/scatter/pallas_call | solution.py:994
  700.4 2.6 collective-permute-done.4
  703.0 4.6 collective-permute-done.6
  707.7 4.4 fusion.6
  713.5 1.5 fusion.37
  715.8 1.9 fusion.29
  717.7 17.0 %update_stats.1 = (f32[50,128]{1,0:T(8,128)}, f32[2,128]{1,0:T(2,128)}, f32[1,128]{1,0:T(1,128)}, f32[2,128]{1,0:T(2,128)}, f32[4,128]{1,0:T(4,128)}, /*index=5*...) custom-call(f32[50,128]{1,0:T(8,128)} %get-tuple-element.199.refs_0_, ...), custom_call_target="tpu_custom_call" | custom-call | flops 12000000000 | bytes 36000000 | tf_op jit(solution)/shard_map/update_stats/pallas_call | solution.py:839
  735.9 1.4 fusion.46
  737.3 5.5 multiply_reduce_fusion.1
  742.8 1.4 multiply_reduce_fusion.2
  744.2 1.3 multiply_reduce_fusion.8
  745.5 1.4 multiply_reduce_fusion.3
  747.0 1.4 multiply_reduce_fusion.6
  748.3 10.9 %clip_rates.1 = f32[8,128]{1,0:T(8,128)} custom-call(f32[2,128]{1,0:T(2,128)} %bitcast.258, f32[3,128]{1,0:T(4,128)} %bitcast.245, f32[2,128]{1,0:T(2,128)} %bitcast.255, f32[4,128]{1,0:T(4,128)} %bitcast.244, f32[2,128]{1,0:T(2,128)} %bitcast.254, f32[16,128]{1,0:T(8,128)} %get-tuple-element.138.refs_5_), custom_call_target="tpu_custom_call" | custom-call | flops 8000000000 | bytes 24000000 | tf_op jit(solution)/shard_map/clip_rates/pallas_call | solution.py:887
  759.3 1.4 fusion.47
  760.7 2.1 multiply_subtract_fusion.4
  762.8 2.2 multiply_subtract_fusion.3
  764.9 2.3 multiply_subtract_fusion.1
  767.2 2.3 multiply_subtract_fusion.2
  769.5 9.1 %multiply_subtract_fusion = f32[6288,256]{1,0:T(8,128)} fusion(f32[6288,256]{1,0:T(8,128)} %table_ref.1, f32[]{:T(128)} %bitcast.76, f32[6288,256]{1,0:T(8,128)} %scatter.1, f32[]{:T(128)} %bitcast.58, f32[256]{0:T(256)S(1)} %bitcast.234, f32[6288]{0:T(1024)S(1)} %bitcast.200), kind=kLoop, calls=%fused_computation.11 | loop fusion | flops 8048640 | bytes 19342920 | tf_op jit(solution)/shard_map/sub | solution.py:1420
  (208 shorter events, 44.4 us)
Async XLA Ops:
  7.2 282.4 %all-gather.2.cloned.1.call-start = ((), (), s32[]{:S(2)}) async-start(), calls=%async_computation.3 | async-start | bytes 16097280 | tf_op jit(solution)/shard_map/all_gather | solution.py:1215
  8.6 8.8 %copy-start.14 = (f32[128,256]{1,0:T(8,128)S(1)}, f32[128,256]{1,0:T(8,128)}, u32[]{:S(2)}) copy-start(f32[128,256]{1,0:T(8,128)} %param.27) | copy-start | bytes 393220
  8.6 12.0 %copy-start.9 = (f32[256,384]{1,0:T(8,128)S(1)}, f32[256,384]{1,0:T(8,128)}, u32[]{:S(2)}) copy-start(f32[256,384]{1,0:T(8,128)} %param.26) | copy-start | bytes 1179652
  8.6 13.0 %copy-start.5 = (f32[256,512]{1,0:T(8,128)S(1)}, f32[256,512]{1,0:T(8,128)}, u32[]{:S(2)}) copy-start(f32[256,512]{1,0:T(8,128)} %param.28) | copy-start | bytes 1572868
  18.0 27.1 %collective-permute-start.1 = (bf16[128,256]{1,0:T(8,128)(2,1)S(1)}, bf16[128,256]{1,0:T(8,128)(2,1)S(1)}, u32[]{:S(2)}, u32[]{:S(2)}) collective-permute-start(bf16[128,256]{1,0:T(8,128)(2,1)S(1)} %get-tuple-element.179), channel_id=1, source_target_pairs={{0,4},{1,5},{2,6},{3,7},{4,0},{5,1},{6,2},{7,3},{8,12},{9,13},{10,... | collective-permute-start | bytes 196616 | tf_op jit(solution)/shard_map/ppermute | solution.py:1174
  21.3 24.5 %collective-permute-start = (bf16[256,384]{1,0:T(8,128)(2,1)S(1)}, bf16[256,384]{1,0:T(8,128)(2,1)S(1)}, u32[]{:S(2)}, u32[]{:S(2)}) collective-permute-start(bf16[256,384]{1,0:T(8,128)(2,1)S(1)} %get-tuple-element.175), channel_id=1, source_target_pairs={{0,4},{1,5},{2,6},{3,7},{4,0},{5,1},{6,2},{7,3},{8,12},{9,13},{10,... | collective-permute-start | bytes 589832 | tf_op jit(solution)/shard_map/ppermute | solution.py:1174
  22.2 24.3 %collective-permute-start.2 = (bf16[256,512]{1,0:T(8,128)(2,1)S(1)}, bf16[256,512]{1,0:T(8,128)(2,1)S(1)}, u32[]{:S(2)}, u32[]{:S(2)}) collective-permute-start(bf16[256,512]{1,0:T(8,128)(2,1)S(1)} %get-tuple-element.173), channel_id=1, source_target_pairs={{0,4},{1,5},{2,6},{3,7},{4,0},{5,1},{6,2},{7,3},{8,12},{9,13},{10,... | collective-permute-start | bytes 786440 | tf_op jit(solution)/shard_map/ppermute | solution.py:1174
  47.4 56.2 %copy-start.3 = (f32[512,256]{1,0:T(8,128)S(1)}, f32[512,256]{1,0:T(8,128)}, u32[]{:S(2)}) copy-start(f32[512,256]{1,0:T(8,128)} %param.29) | copy-start | bytes 1572868
  47.4 56.9 %copy-start.42 = (s32[2048]{0:T(1024)S(1)}, s32[2048]{0:T(1024)}, u32[]{:S(2)}) copy-start(s32[2048]{0:T(1024)} %param.23) | copy-start | bytes 24580
  103.6 5.6 copy-start.40
  104.3 13.7 %collective-permute-start.3 = (bf16[512,256]{1,0:T(8,128)(2,1)S(1)}, bf16[512,256]{1,0:T(8,128)(2,1)S(1)}, u32[]{:S(2)}, u32[]{:S(2)}) collective-permute-start(bf16[512,256]{1,0:T(8,128)(2,1)S(1)} %get-tuple-element.171), channel_id=1, source_target_pairs={{0,4},{1,5},{2,6},{3,7},{4,0},{5,1},{6,2},{7,3},{8,12},{9,13},{10,... | collective-permute-start | bytes 786440 | tf_op jit(solution)/shard_map/ppermute | solution.py:1174
  104.5 33.6 %copy-start.43 = (f32[4]{0:T(128)}, f32[4]{0:T(128)S(1)}, u32[]{:S(2)}) copy-start(f32[4]{0:T(128)S(1)} %convert_reduce_fusion) | copy-start | bytes 52
  105.1 15.2 %all-to-all-start = ((bf16[4,256,256]{2,1,0:T(8,128)(2,1)}), bf16[4,256,256]{2,1,0:T(8,128)(2,1)S(1)}, u32[]{:S(2)}, u32[]{:S(2)}) async-start(bf16[4,256,256]{2,1,0:T(8,128)(2,1)} %bitcast.3), calls=%async_computation | async-start | bytes 1048576 | tf_op jit(solution)/shard_map/all_to_all | solution.py:1209
  108.6 579.9 %reduce-scatter.2.cloned.1.call-start = ((), (), s32[]{:S(2)}) async-start(), calls=%async_computation.4 | async-start | bytes 16097280 | tf_op jit(solution)/shard_map/reduce_scatter | solution.py:1295
  121.1 17.0 %copy-start.54 = (bf16[1024,768]{1,0:T(8,128)(2,1)S(1)}, bf16[1024,768]{1,0:T(8,128)(2,1)}, u32[]{:S(2)}) copy-start(bf16[1024,768]{1,0:T(8,128)(2,1)} %get-tuple-element.95) | copy-start | bytes 4718596
  141.5 15.6 %copy-start.7 = (bf16[1024,768]{0,1:T(8,128)(2,1)}, bf16[1024,768]{0,1:T(8,128)(2,1)S(1)}, u32[]{:S(2)}) copy-start(bf16[1024,768]{0,1:T(8,128)(2,1)S(1)} %convolution_convert_fusion.7) | copy-start | bytes 4718596
  149.2 8.0 %copy-start.22 = (f32[4,1024]{1,0:T(4,128)}, f32[4,1024]{1,0:T(4,128)S(1)}, u32[]{:S(2)}) copy-start(f32[4,1024]{1,0:T(4,128)S(1)} %get-tuple-element.194) | copy-start | bytes 49156
  157.2 8.2 %copy-start.24 = (f32[4,1024]{1,0:T(4,128)}, f32[4,1024]{1,0:T(4,128)S(1)}, u32[]{:S(2)}) copy-start(f32[4,1024]{1,0:T(4,128)S(1)} %fusion) | copy-start | bytes 49156
  157.2 9.0 %copy-start.16 = (bf16[256,1024]{1,0:T(8,128)(2,1)S(1)}, bf16[256,1024]{1,0:T(8,128)(2,1)}, u32[]{:S(2)}) copy-start(bf16[256,1024]{1,0:T(8,128)(2,1)} %get-tuple-element.98) | copy-start | bytes 1572868
  168.2 54.8 %copy-start.50 = (bf16[1024,1024]{1,0:T(8,128)(2,1)S(1)}, bf16[1024,1024]{1,0:T(8,128)(2,1)}, u32[]{:S(2)}) copy-start(bf16[1024,1024]{1,0:T(8,128)(2,1)} %get-tuple-element.101) | copy-start | bytes 6291460
  223.1 4.1 copy-start.57
  227.2 4.0 copy-start.47
  340.2 10.0 %copy-start.30 = (s32[2048]{0:T(1024)S(1)}, s32[2048]{0:T(1024)}, u32[]{:S(2)}) copy-start(s32[2048]{0:T(1024)} %param.24) | copy-start | bytes 24580
  340.2 10.1 %copy-start.45 = (f32[4]{0:T(128)S(1)}, f32[4]{0:T(128)}, u32[]{:S(2)}) copy-start(f32[4]{0:T(128)} %maximum_multiply_fusion) | copy-start | bytes 52
  340.2 10.7 %copy-start.12 = (f32[10,1,2048]{2,1,0:T(1,128)S(1)}, f32[10,1,2048]{2,1,0:T(1,128)}, u32[]{:S(2)}) copy-start(f32[10,1,2048]{2,1,0:T(1,128)} %get-tuple-element.106) | copy-start | bytes 245764
  422.1 58.6 %copy-start.48 = (f32[1024,1024]{1,0:T(8,128)S(1)}, f32[1024,1024]{1,0:T(8,128)}, u32[]{:S(2)}) copy-start(f32[1024,1024]{1,0:T(8,128)} %copy-done.47) | copy-start | bytes 12582916
  480.7 6.9 copy-start.51
  487.6 3.7 copy-start.53
  491.3 34.8 %copy-start.17 = (bf16[256,1024]{1,0:T(8,128)(2,1)S(1)}, bf16[256,1024]{1,0:T(8,128)(2,1)}, u32[]{:S(2)}) copy-start(bf16[256,1024]{1,0:T(8,128)(2,1)} %get-tuple-element.98) | copy-start | bytes 1572868
  528.6 15.3 %slice-start = ((s8[16777216]{0:T(1024)(128)(4,1)}), s8[4194304]{0:T(1024)(128)(4,1)S(1)}, s32[]{:S(2)}) async-start(s8[16777216]{0:T(1024)(128)(4,1)} %bitcast.180), calls=%async_computation.5 | async-start | bytes 8388608
  528.6 15.3 %slice-start.1 = ((s8[16777216]{0:T(1024)(128)(4,1)}), s8[4194304]{0:T(1024)(128)(4,1)S(1)}, s32[]{:S(2)}) async-start(s8[16777216]{0:T(1024)(128)(4,1)} %bitcast.180), calls=%async_computation.6 | async-start | bytes 8388608
  528.6 15.3 %slice-start.2 = ((s8[16777216]{0:T(1024)(128)(4,1)}), s8[4194304]{0:T(1024)(128)(4,1)S(1)}, s32[]{:S(2)}) async-start(s8[16777216]{0:T(1024)(128)(4,1)} %bitcast.180), calls=%async_computation.7 | async-start | bytes 8388608
  528.6 16.7 %slice-start.3 = ((s8[16777216]{0:T(1024)(128)(4,1)}), s8[4194304]{0:T(1024)(128)(4,1)S(1)}, s32[]{:S(2)}) async-start(s8[16777216]{0:T(1024)(128)(4,1)} %bitcast.180), calls=%async_computation.8 | async-start | bytes 8388608
  560.5 3.3 copy-start.55
  571.1 50.1 %copy-start.44 = (f32[4]{0:T(128)S(1)}, f32[4]{0:T(128)}, u32[]{:S(2)}) copy-start(f32[4]{0:T(128)} %get-tuple-element.162) | copy-start | bytes 52
  614.7 16.1 %all-to-all-start.1 = ((bf16[4,256,256]{2,1,0:T(8,128)(2,1)}), bf16[4,256,256]{2,1,0:T(8,128)(2,1)S(1)}, u32[]{:S(2)}, u32[]{:S(2)}) async-start(bf16[4,256,256]{2,1,0:T(8,128)(2,1)} %bitcast.177), calls=%async_computation.1 | async-start | bytes 1048576 | tf_op jit(solution)/shard_map/all_to_all | solution.py:1355
  618.2 82.2 %collective-permute-start.5 = (bf16[128,256]{1,0:T(8,128)(2,1)S(1)}, bf16[128,256]{1,0:T(8,128)(2,1)S(1)}, u32[]{:S(2)}, u32[]{:S(2)}) collective-permute-start(bf16[128,256]{1,0:T(8,128)(2,1)S(1)} %split.47), channel_id=1, source_target_pairs={{0,4},{1,5},{2,6},{3,7},{4,0},{5,1},{6,2},{7,3},{8,12},{9,13},{10,... | collective-permute-start | bytes 196616 | tf_op jit(solution)/shard_map/ppermute | solution.py:1377
  619.9 80.5 %collective-permute-start.7 = (bf16[512,256]{1,0:T(8,128)(2,1)S(1)}, bf16[512,256]{1,0:T(8,128)(2,1)}, u32[]{:S(2)}, u32[]{:S(2)}) collective-permute-start(bf16[512,256]{1,0:T(8,128)(2,1)S(1)} %split.44), channel_id=1, source_target_pairs={{0,4},{1,5},{2,6},{3,7},{4,0},{5,1},{6,2},{7,3},{8,12},{9,13},{10,... | collective-permute-start | bytes 786440 | tf_op jit(solution)/shard_map/ppermute | solution.py:1377
  621.7 6.1 copy-start.52
  685.5 17.5 %collective-permute-start.4 = (bf16[256,384]{1,0:T(8,128)(2,1)S(1)}, bf16[256,384]{1,0:T(8,128)(2,1)S(1)}, u32[]{:S(2)}, u32[]{:S(2)}) collective-permute-start(bf16[256,384]{1,0:T(8,128)(2,1)S(1)} %split.46), channel_id=1, source_target_pairs={{0,4},{1,5},{2,6},{3,7},{4,0},{5,1},{6,2},{7,3},{8,12},{9,13},{10,... | collective-permute-start | bytes 589832 | tf_op jit(solution)/shard_map/ppermute | solution.py:1377
  687.3 20.4 %collective-permute-start.6 = (bf16[256,512]{1,0:T(8,128)(2,1)S(1)}, bf16[256,512]{1,0:T(8,128)(2,1)S(1)}, u32[]{:S(2)}, u32[]{:S(2)}) collective-permute-start(bf16[256,512]{1,0:T(8,128)(2,1)S(1)} %split.45), channel_id=1, source_target_pairs={{0,4},{1,5},{2,6},{3,7},{4,0},{5,1},{6,2},{7,3},{8,12},{9,13},{10,... | collective-permute-start | bytes 786440 | tf_op jit(solution)/shard_map/ppermute | solution.py:1377
  700.4 12.4 %copy-start.31 = (f32[6288]{0:T(1024)S(1)}, f32[6288]{0:T(1024)}, u32[]{:S(2)}) copy-start(f32[6288]{0:T(1024)} %param.31) | copy-start | bytes 75460
  700.4 7.3 copy-start.21
  712.8 49.9 %copy-start.2 = (f32[256,384]{1,0:T(8,128)}, f32[256,384]{1,0:T(8,128)S(1)}, u32[]{:S(2)}) copy-start(f32[256,384]{1,0:T(8,128)S(1)} %get-tuple-element.231) | copy-start | bytes 1179652
  715.0 45.7 %copy-start.11 = (f32[128,256]{1,0:T(8,128)}, f32[128,256]{1,0:T(8,128)S(1)}, u32[]{:S(2)}) copy-start(f32[128,256]{1,0:T(8,128)S(1)} %get-tuple-element.235) | copy-start | bytes 393220
  715.8 51.4 %copy-start = (f32[256,512]{1,0:T(8,128)}, f32[256,512]{1,0:T(8,128)S(1)}, u32[]{:S(2)}) copy-start(f32[256,512]{1,0:T(8,128)S(1)} %get-tuple-element.239) | copy-start | bytes 1572868
  717.7 47.3 %copy-start.1 = (f32[512,256]{1,0:T(8,128)}, f32[512,256]{1,0:T(8,128)S(1)}, u32[]{:S(2)}) copy-start(f32[512,256]{1,0:T(8,128)S(1)} %get-tuple-element.243) | copy-start | bytes 1572868
  734.7 8.1 %copy-start.32 = (f32[4,128]{1,0:T(4,128)S(1)}, f32[4,128]{1,0:T(4,128)}, u32[]{:S(2)}) copy-start(f32[4,128]{1,0:T(4,128)} %get-tuple-element.145) | copy-start | bytes 6148
  734.7 8.1 %copy-start.35 = (f32[2,128]{1,0:T(2,128)S(1)}, f32[2,128]{1,0:T(2,128)}, u32[]{:S(2)}) copy-start(f32[2,128]{1,0:T(2,128)} %get-tuple-element.146) | copy-start | bytes 3076
  734.7 9.5 %copy-start.37 = (f32[2,128]{1,0:T(2,128)S(1)}, f32[2,128]{1,0:T(2,128)}, u32[]{:S(2)}) copy-start(f32[2,128]{1,0:T(2,128)} %get-tuple-element.142) | copy-start | bytes 3076
  734.7 9.5 %copy-start.41 = (f32[1,128]{1,0:T(1,128)S(1)}, f32[1,128]{1,0:T(1,128)}, u32[]{:S(2)}) copy-start(f32[1,128]{1,0:T(1,128)} %get-tuple-element.141) | copy-start | bytes 1540
  734.7 10.8 %copy-start.33 = (f32[4,128]{1,0:T(4,128)S(1)}, f32[4,128]{1,0:T(4,128)}, u32[]{:S(2)}) copy-start(f32[4,128]{1,0:T(4,128)} %get-tuple-element.144) | copy-start | bytes 6148
  734.7 10.8 %copy-start.36 = (f32[2,128]{1,0:T(2,128)S(1)}, f32[2,128]{1,0:T(2,128)}, u32[]{:S(2)}) copy-start(f32[2,128]{1,0:T(2,128)} %get-tuple-element.143) | copy-start | bytes 3076
  734.7 12.2 %copy-start.34 = (f32[3,128]{1,0:T(4,128)S(1)}, f32[3,128]{1,0:T(4,128)}, u32[]{:S(2)}) copy-start(f32[3,128]{1,0:T(4,128)} %get-tuple-element.140) | copy-start | bytes 4612
  734.7 12.2 %copy-start.38 = (f32[2,128]{1,0:T(2,128)S(1)}, f32[2,128]{1,0:T(2,128)}, u32[]{:S(2)}) copy-start(f32[2,128]{1,0:T(2,128)} %get-tuple-element.139) | copy-start | bytes 3076
  748.3 12.4 %copy-start.15 = (f32[128,256]{1,0:T(8,128)S(1)}, f32[128,256]{1,0:T(8,128)}, u32[]{:S(2)}) copy-start(f32[128,256]{1,0:T(8,128)} %param.27) | copy-start | bytes 393220
  748.3 14.4 %copy-start.10 = (f32[256,384]{1,0:T(8,128)S(1)}, f32[256,384]{1,0:T(8,128)}, u32[]{:S(2)}) copy-start(f32[256,384]{1,0:T(8,128)} %param.26) | copy-start | bytes 1179652
  748.3 16.6 %copy-start.4 = (f32[512,256]{1,0:T(8,128)S(1)}, f32[512,256]{1,0:T(8,128)}, u32[]{:S(2)}) copy-start(f32[512,256]{1,0:T(8,128)} %param.29) | copy-start | bytes 1572868
  748.3 18.9 %copy-start.6 = (f32[256,512]{1,0:T(8,128)S(1)}, f32[256,512]{1,0:T(8,128)}, u32[]{:S(2)}) copy-start(f32[256,512]{1,0:T(8,128)} %param.28) | copy-start | bytes 1572868
  759.3 10.2 %copy-start.20 = (f32[50,128]{1,0:T(8,128)S(1)}, f32[50,128]{1,0:T(8,128)}, u32[]{:S(2)}) copy-start(f32[50,128]{1,0:T(8,128)} %get-tuple-element.136) | copy-start | bytes 76804
  759.3 10.2 %copy-start.39 = (f32[2,128]{1,0:T(2,128)S(1)}, f32[2,128]{1,0:T(2,128)}, u32[]{:S(2)}) copy-start(f32[2,128]{1,0:T(2,128)} %get-tuple-element.137) | copy-start | bytes 3076
  769.5 14.8 %copy-start.29 = (f32[6,1024]{1,0:T(8,128)S(1)}, f32[6,1024]{1,0:T(8,128)}, u32[]{:S(2)}) copy-start(f32[6,1024]{1,0:T(8,128)} %get-tuple-element.247) | copy-start | bytes 73732
  769.5 15.4 %copy-start.28 = (f32[6,1024]{1,0:T(8,128)S(1)}, f32[6,1024]{1,0:T(8,128)}, u32[]{:S(2)}) copy-start(f32[6,1024]{1,0:T(8,128)} %get-tuple-element.248) | copy-start | bytes 73732
  769.5 16.0 %copy-start.27 = (f32[6,1024]{1,0:T(8,128)S(1)}, f32[6,1024]{1,0:T(8,128)}, u32[]{:S(2)}) copy-start(f32[6,1024]{1,0:T(8,128)} %get-tuple-element.249) | copy-start | bytes 73732
  (10 other events, 15.4 us)
Sparse Core Ops, SparseCore 0:
  103.8 146.2 all-gather.1
  421.5 123.8 reduce-scatter.1

commit v4 on v3

--- a/solution.py
+++ b/solution.py
@@ -20,6 +20,7 @@
 CLIP = 1.0
 RHO = 0.5
 MASKED = -1e30
+QUERIES = 256
 MESH = pl.DeviceIdType.MESH
 VMEM_CAP = 56 * 2**20
 
@@ -34,7 +35,8 @@
     return lax.dynamic_slice_in_dim(values, start, count, 0)
 
 
-def line_kernel(nr, ng, chunks, rows, width, n_in, n_out, step, sides, *refs):
+def line_kernel(nr, ng, chunks, shapes, n_in, n_out, step, sides, turn, relay_tick, *refs):
+    (rows_r, width_r), (rows_g, width_g) = shapes
     part = refs[0] if nr else None
     first = 1 if nr else 0
     ins = refs[first : first + n_in]
@@ -46,13 +48,18 @@
     refs = refs[n_out:]
     side_outs, scratch = refs[: len(sides)], refs[len(sides) :]
     side_scratch, scratch = scratch[: 3 * len(sides)], scratch[3 * len(sides) :]
+    if turn:
+        cast, turn_send, turn_recv = scratch[-3:]
     size_dp = lax.axis_size("dp")
     dp = lax.axis_index("dp")
     mp = lax.axis_index("mp")
     z = mp // 2
     core = lax.rem(mp, 2)
     other = mp + 1 - 2 * core
-    piece = rows // chunks
+    piece_r = rows_r // chunks
+    piece_g = rows_g // chunks
+    small = min(piece_r, piece_g)
+    late = 1 if turn else 0
     most = max(nr, ng)
     zb = lax.rem(z, most)
     if nr:
@@ -73,7 +80,7 @@
     def _():
         pl.semaphore_signal(barrier, inc=1, device_id=(dp, mp + 2), device_id_type=MESH)
 
-    if sides:
+    if sides or turn:
         for hop in range(1, size_dp):
             pl.semaphore_signal(
                 barrier,
@@ -81,35 +88,96 @@
                 device_id=(lax.rem(dp + hop, size_dp), mp),
                 device_id_type=MESH,
             )
-    greeted = (size_dp if sides else 1) + (zb > 0).astype(jnp.int32) + (zb < most - 1).astype(jnp.int32)
+    greeted = (size_dp if sides or turn else 1) + (zb > 0).astype(jnp.int32) + (zb < most - 1).astype(jnp.int32)
     pl.semaphore_wait(barrier, greeted)
 
     def share(axis, length, which):
         at = pl.ds(pl.multiple_of(which * length, length), length)
         return (at, slice(None)) if axis == 0 else (slice(None), at)
 
-    side_copies = []
+    def to_peer(src, dst, send, recv, peer):
+        return pltpu.make_async_remote_copy(
+            src_ref=src,
+            dst_ref=dst,
+            send_sem=send,
+            recv_sem=recv,
+            device_id=(peer, mp),
+            device_id_type=MESH,
+        )
+
+    relay = size_dp == 4
+    beside_x = dp + 1 - 2 * lax.rem(dp, 2)
+    beside_y = lax.rem(dp + 2, 4)
+    across = 3 - dp
+
+    def half_share(axis, length, which, height, part):
+        if axis == 0:
+            return (pl.ds(pl.multiple_of(which * length + part * height, height), height), slice(None))
+        at = pl.ds(pl.multiple_of(which * length, length), length)
+        return (pl.ds(part * height, height), at)
+
+    first_copies, more_copies, relays = [], [], []
     for index, (kind, axis) in enumerate(sides):
         src, dst = side_ins[index], side_outs[index]
         send, recv, slots = side_scratch[3 * index : 3 * index + 3]
-        length = (src if kind == "gather" else dst).shape[axis]
-        for hop in range(1, size_dp):
-            peer = lax.rem(dp + hop, size_dp)
+        shard = src if kind == "gather" else dst
+        length, height = shard.shape[axis], shard.shape[0] // 2
+        if not relay:
+            for hop in range(1, size_dp):
+                peer = lax.rem(dp + hop, size_dp)
+                if kind == "gather":
+                    source, target = src, dst.at[share(axis, length, dp)]
+                else:
+                    source, target = src.at[share(axis, length, peer)], slots.at[hop]
+                more_copies.append(to_peer(source, target, send.at[hop], recv.at[hop], peer))
+            continue
+        for side, near_one, far_one in ((0, beside_x, beside_y), (1, beside_y, beside_x)):
+            sems = [(send.at[3 * side + n], recv.at[3 * side + n]) for n in range(3)]
             if kind == "gather":
-                source, target = src, dst.at[share(axis, length, dp)]
+                mine = src.at[pl.ds(side * height, height)]
+                here = dst.at[half_share(axis, length, dp, height, side)]
+                passed = dst.at[half_share(axis, length, near_one, height, side)]
+                arrives = to_peer(mine, here, *sems[0], near_one)
+                first_copies.append(arrives)
+                more_copies.append(to_peer(mine, here, *sems[1], far_one))
+                relays.append((arrives, None, to_peer(passed, passed, *sems[2], far_one)))
             else:
-                source, target = src.at[share(axis, length, peer)], slots.at[hop]
-            copy = pltpu.make_async_remote_copy(
-                src_ref=source,
-                dst_ref=target,
-                send_sem=send.at[hop],
-                recv_sem=recv.at[hop],
-                device_id=(peer, mp),
-                device_id_type=MESH,
-            )
-            side_copies.append(copy)
-            if nr == 0:
-                copy.start()
+                arrives = to_peer(
+                    src.at[half_share(axis, length, across, height, side)],
+                    slots.at[4 * side],
+                    *sems[0],
+                    near_one,
+                )
+                first_copies.append(arrives)
+                more_copies.append(
+                    to_peer(
+                        src.at[half_share(axis, length, near_one, height, side)],
+                        slots.at[4 * side + 1],
+                        *sems[1],
+                        near_one,
+                    )
+                )
+                summed = to_peer(
+                    slots.at[4 * side + 2], slots.at[4 * side + 3], *sems[2], far_one
+                )
+                own = src.at[half_share(axis, length, far_one, height, side)]
+                relays.append((arrives, (own, slots, 4 * side, height), summed))
+
+    def start_sides():
+        for copy in first_copies + more_copies:
+            copy.start()
+
+    def pass_on():
+        for arrives, adding, copy in relays:
+            arrives.wait_recv()
+            if adding is not None:
+                own, slots, at, height = adding
+                both = own[...].astype(jnp.float32) + slots[at].astype(jnp.float32)
+                slots[at + 2] = both.astype(slots.dtype)
+            copy.start()
+
+    if nr == 0:
+        start_sides()
 
     if nr:
         half, from_left, from_right, going = scratch[:4]
@@ -119,7 +187,10 @@
         core_send, core_recv, to_right, to_left, ag_left, ag_right = scratch[:6]
 
     def part_rows(block, k):
-        return pl.ds(pl.multiple_of(block * rows + k * piece, piece), piece)
+        return pl.ds(pl.multiple_of(block * rows_r + k * piece_r, piece_r), piece_r)
+
+    def whole_rows(block, k):
+        return pl.ds(pl.multiple_of(block * rows_g + k * piece_g, piece_g), piece_g)
 
     def remote(src, dst, send, recv, target):
         return pltpu.make_async_remote_copy(
@@ -148,8 +219,7 @@
             return carry
 
         lax.fori_loop(0, chunks, send_halves, 0)
-        for copy in side_copies:
-            copy.start()
+        start_sides()
 
         def right_copy(dest, k):
             return remote(
@@ -207,7 +277,7 @@
     if ng:
 
         def gathered(block, k, send, recv, target):
-            where = whole.at[part_rows(2 * block + core, k)]
+            where = whole.at[whole_rows(2 * block + core, k)]
             return remote(where, where, send.at[block, k], recv.at[block, k], target)
 
         def core_copy(block, k):
@@ -223,7 +293,7 @@
         total = None
         if nr:
             total = chip_sum(zr, k)
-            zero = jnp.zeros((piece, width), jnp.float32)
+            zero = jnp.zeros((piece_r, width_r), jnp.float32)
 
             @pl.when(zr > 0)
             def _():
@@ -235,19 +305,64 @@
 
             total += jnp.where(zr > 0, from_left[zr, k].astype(jnp.float32), zero)
             total += jnp.where(zr < last_r, from_right[zr, k].astype(jnp.float32), zero)
-        at = pl.ds(pl.multiple_of(k * piece, piece), piece)
+        if turn == "gather":
+            cast[k] = total.astype(cast.dtype)
+            for hop in range(1, size_dp):
+                turn_copy(hop, k).start()
+            mine = pl.ds(pl.multiple_of(dp * small, small), small)
+            outs[0][own_place(k, dp)] = cast[k, mine, :]
+            return
+        at = pl.ds(pl.multiple_of(k * piece_r, piece_r), piece_r)
         ready = step(total, at, ins, outs)
-        if ng:
-            whole[part_rows(2 * zg + core, k), :] = ready.astype(whole.dtype)
-            core_copy(zg, k).start()
-
-            @pl.when(zg < last_g)
-            def _():
-                ag_right_copy(zg, k).start()
-
-            @pl.when(zg > 0)
-            def _():
-                ag_left_copy(zg, k).start()
+        if turn == "spread":
+            cast[k] = ready.astype(cast.dtype)
+            for hop in range(1, size_dp):
+                turn_copy(hop, k).start()
+            whole[own_place(k, dp)] = cast[
+                k, :, pl.ds(pl.multiple_of(dp * width_g, width_g), width_g)
+            ]
+        elif ng:
+            whole[whole_rows(2 * zg + core, k), :] = ready.astype(whole.dtype)
+            start_gather(k)
+
+    def own_place(k, peer):
+        if turn == "gather":
+            return (
+                pl.ds(pl.multiple_of(k * small, small), small),
+                pl.ds(pl.multiple_of(peer * width_r, width_r), width_r),
+            )
+        start = (2 * zg + core) * rows_g + k * piece_g + peer * small
+        return (pl.ds(pl.multiple_of(start, small), small), slice(None))
+
+    def turn_copy(hop, k):
+        peer = lax.rem(dp + hop, size_dp)
+        if turn == "gather":
+            src = cast.at[k, pl.ds(pl.multiple_of(peer * small, small), small)]
+            dst = outs[0].at[own_place(k, dp)]
+        else:
+            src = cast.at[k, :, pl.ds(pl.multiple_of(peer * width_g, width_g), width_g)]
+            dst = whole.at[own_place(k, dp)]
+        return to_peer(src, dst, turn_send.at[hop, k], turn_recv.at[hop, k], peer)
+
+    def turned_rows(k):
+        for hop in range(1, size_dp):
+            turn_copy(hop, k).wait_recv()
+        if turn == "gather":
+            at = pl.ds(pl.multiple_of(k * piece_g, piece_g), piece_g)
+            ready = step(None, at, ins, outs)
+            whole[whole_rows(2 * zg + core, k), :] = ready.astype(whole.dtype)
+        start_gather(k)
+
+    def start_gather(k):
+        core_copy(zg, k).start()
+
+        @pl.when(zg < last_g)
+        def _():
+            ag_right_copy(zg, k).start()
+
+        @pl.when(zg > 0)
+        def _():
+            ag_left_copy(zg, k).start()
 
     def inside(k):
         return (k >= 0) & (k < chunks)
@@ -278,9 +393,21 @@
         def _():
             own_rows(k_own)
 
+        if turn:
+
+            @pl.when(inside(k_own - 1))
+            def _():
+                turned_rows(k_own - 1)
+
+        if relays:
+
+            @pl.when(now == relay_tick)
+            def _():
+                pass_on()
+
         if ng:
             for block in range(ng):
-                k = now - (own_lag(z - zg + block) + jnp.abs(zg - block))
+                k = now - (own_lag(z - zg + block) + late + jnp.abs(zg - block))
 
                 @pl.when(inside(k) & (block < zg))
                 def _():
@@ -302,10 +429,13 @@
 
         return carry
 
-    ticks = chunks + (nr - 1 if nr else 0) + (ng - 1 if ng else 0)
+    ticks = chunks + (nr - 1 if nr else 0) + (ng - 1 if ng else 0) + late
     lax.fori_loop(0, ticks, tick, 0)
 
     def finish(k, carry):
+        if turn:
+            for hop in range(1, size_dp):
+                turn_copy(hop, k).wait_send()
         if nr:
             for block in range(nr):
                 half_copy(block, k).wait_send()
@@ -333,46 +463,65 @@
         if kind == "gather":
             length = side_ins[index].shape[axis]
             side_outs[index][share(axis, length, dp)] = side_ins[index][...]
-    for copy in side_copies:
+    for copy in first_copies:
+        copy.wait_send()
+    for copy in more_copies:
+        copy.wait()
+    for unused, unused, copy in relays:
         copy.wait()
     for index, (kind, axis) in enumerate(sides):
         if kind == "scatter":
             src, dst = side_ins[index], side_outs[index]
             slots = side_scratch[3 * index + 2]
-            strip = 128
-            height = dst.shape[0]
-
-            def add(i, carry):
-                at = pl.ds(pl.multiple_of(i * strip, strip), strip)
-                length = dst.shape[axis]
-                if axis == 0:
-                    start = pl.multiple_of(dp * length + i * strip, strip)
-                    total = src[pl.ds(start, strip), :].astype(jnp.float32)
-                else:
-                    start = pl.multiple_of(dp * length, length)
-                    total = src[at, pl.ds(start, length)].astype(jnp.float32)
+            length, height = dst.shape[axis], dst.shape[0] // 2
+            if relay:
+                for side in range(2):
+                    total = src[half_share(axis, length, dp, height, side)].astype(jnp.float32)
+                    total += slots[4 * side + 1].astype(jnp.float32)
+                    total += slots[4 * side + 3].astype(jnp.float32)
+                    dst[pl.ds(side * height, height), :] = total
+            else:
+                total = src[share(axis, length, dp)].astype(jnp.float32)
                 for hop in range(1, size_dp):
-                    total += slots[hop, at, :].astype(jnp.float32)
-                dst[at, :] = total
-                return carry
-
-            lax.fori_loop(0, height // strip, add, 0)
+                    total += slots[hop].astype(jnp.float32)
+                dst[...] = total
 
 
 def line_call(
-    name, cid, partial, ins, out_types, step, rows, width, chunks, nr, ng, time, sides=()
+    name,
+    cid,
+    partial,
+    ins,
+    out_types,
+    step,
+    rows,
+    width,
+    chunks,
+    nr,
+    ng,
+    time,
+    sides=(),
+    turn=None,
+    relay_tick=0,
 ):
     piece = rows // chunks
+    size_dp = lax.axis_size("dp")
+    reduced = gathered = (rows, width)
+    if turn == "gather":
+        gathered = (rows // size_dp, width * size_dp)
+    elif turn == "spread":
+        gathered = (rows * size_dp, width // size_dp)
     out_shape = []
     if ng:
-        out_shape.append(jax.ShapeDtypeStruct((2 * ng * rows, width), jnp.bfloat16))
+        out_shape.append(
+            jax.ShapeDtypeStruct((2 * ng * gathered[0], gathered[1]), jnp.bfloat16)
+        )
     out_shape += out_types
     dma = pltpu.SemaphoreType.DMA
     scratch = []
-    size_dp = lax.axis_size("dp")
     for kind, axis, values in sides:
         shape = list(values.shape)
-        scratch += [dma((size_dp,)), dma((size_dp,))]
+        scratch += [dma((max(size_dp, 6),)), dma((max(size_dp, 6),))]
         if kind == "gather":
             shape[axis] *= size_dp
             out_shape.append(jax.ShapeDtypeStruct(tuple(shape), values.dtype))
@@ -380,12 +529,16 @@
         else:
             shape[axis] //= size_dp
             out_shape.append(jax.ShapeDtypeStruct(tuple(shape), jnp.float32))
-            scratch.append(pltpu.VMEM((size_dp, *shape), values.dtype))
+            slots = (8, shape[0] // 2, shape[1]) if size_dp == 4 else (size_dp, *shape)
+            scratch.append(pltpu.VMEM(slots, values.dtype))
     if nr:
         scratch += [pltpu.VMEM((nr, chunks, piece, width), jnp.bfloat16)] * 4
         scratch += [dma((nr, chunks))] * 5
     if ng:
         scratch += [dma((ng, chunks))] * 6
+    if turn:
+        scratch.append(pltpu.VMEM((chunks, piece, width), jnp.bfloat16))
+        scratch += [dma((size_dp, chunks))] * 2
     args = ([partial] if nr else []) + list(ins) + [side[2] for side in sides]
     vmem = pl.BlockSpec(memory_space=pltpu.VMEM)
     call = pl.pallas_call(
@@ -394,12 +547,13 @@
             nr,
             ng,
             chunks,
-            rows,
-            width,
+            (reduced, gathered),
             len(ins),
             len(out_types),
             step,
             tuple(side[:2] for side in sides),
+            turn,
+            relay_tick,
         ),
         out_shape=out_shape,
         in_specs=[vmem] * len(args),
@@ -548,6 +702,108 @@
         ),
         name="head_back",
     )(exps, table, final, scale, weight, wanted)
+
+
+def head_weights(mixed_ref, starts_ref, base, at, seen):
+    query = mixed_ref[at : at + QUERIES, base : base + HD]
+    keys = mixed_ref[0:seen, base + HD : base + 2 * HD]
+    values = mixed_ref[0:seen, base + 2 * HD : base + 3 * HD]
+    scores = lax.dot_general(
+        query, keys, (((1,), (1,)), ((), ())), preferred_element_type=jnp.float32
+    )
+    row = at + lax.broadcasted_iota(jnp.int32, (QUERIES, seen), 0)
+    column = lax.broadcasted_iota(jnp.int32, (QUERIES, seen), 1)
+    allowed = (column <= row) & (column >= starts_ref[at : at + QUERIES, :])
+    scores = jnp.where(allowed, scores * HD ** (-0.5), MASKED)
+    weights = jnp.exp(scores - jnp.max(scores, axis=1, keepdims=True))
+    probs = weights / jnp.sum(weights, axis=1, keepdims=True)
+    return query, keys, values, probs
+
+
+def attend_kernel(mixed_ref, starts_ref, out_ref):
+    length = mixed_ref.shape[0]
+    for at in range(0, length, QUERIES):
+        found = []
+        for head in range(2):
+            unused, unused, values, probs = head_weights(
+                mixed_ref, starts_ref, head * 3 * HD, at, at + QUERIES
+            )
+            found.append(
+                jnp.dot(probs.astype(jnp.bfloat16), values, preferred_element_type=jnp.float32)
+            )
+        out_ref[at : at + QUERIES, :] = jnp.concatenate(found, axis=1).astype(jnp.bfloat16)
+
+
+def attend(mixed, starts):
+    length, columns = mixed.shape
+    pairs = columns // (6 * HD)
+    return pl.pallas_call(
+        attend_kernel,
+        grid=(pairs,),
+        out_shape=jax.ShapeDtypeStruct((length, pairs * 2 * HD), jnp.bfloat16),
+        in_specs=[
+            pl.BlockSpec((length, 6 * HD), lambda j: (0, j)),
+            pl.BlockSpec((length, 1), lambda j: (0, 0)),
+        ],
+        out_specs=pl.BlockSpec((length, 2 * HD), lambda j: (0, j)),
+        compiler_params=pltpu.CompilerParams(vmem_limit_bytes=40 * 2**20),
+        cost_estimate=pl.CostEstimate(
+            flops=8 * pairs * length * length * HD,
+            bytes_accessed=2 * length * columns,
+            transcendentals=pairs * length * length,
+        ),
+        name="attend",
+    )(mixed, starts)
+
+
+def attend_back_kernel(mixed_ref, starts_ref, upstream_ref, out_ref, sums_ref):
+    length = mixed_ref.shape[0]
+    sums_ref[...] = jnp.zeros_like(sums_ref)
+    rows = (((0,), (0,)), ((), ()))
+    for at in range(0, length, QUERIES):
+        seen = at + QUERIES
+        for head in range(2):
+            base = head * 3 * HD
+            query, keys, values, probs = head_weights(mixed_ref, starts_ref, base, at, seen)
+            upstream = upstream_ref[at:seen, head * HD : head * HD + HD]
+            dprobs = lax.dot_general(
+                upstream, values, (((1,), (1,)), ((), ())), preferred_element_type=jnp.float32
+            )
+            inner = jnp.sum(probs * dprobs, axis=1, keepdims=True)
+            dscores = (probs * (dprobs - inner)).astype(jnp.bfloat16)
+            dquery = jnp.dot(dscores, keys, preferred_element_type=jnp.float32)
+            dkeys = lax.dot_general(dscores, query, rows, preferred_element_type=jnp.float32)
+            dvalues = lax.dot_general(
+                probs.astype(jnp.bfloat16), upstream, rows, preferred_element_type=jnp.float32
+            )
+            sums_ref[at:seen, base : base + HD] = dquery * HD ** (-0.5)
+            sums_ref[0:seen, base + HD : base + 2 * HD] += dkeys * HD ** (-0.5)
+            sums_ref[0:seen, base + 2 * HD : base + 3 * HD] += dvalues
+    out_ref[...] = sums_ref[...].astype(jnp.bfloat16)
+
+
+def attend_back(mixed, starts, upstream):
+    length, columns = mixed.shape
+    pairs = columns // (6 * HD)
+    return pl.pallas_call(
+        attend_back_kernel,
+        grid=(pairs,),
+        out_shape=jax.ShapeDtypeStruct((length, columns), jnp.bfloat16),
+        in_specs=[
+            pl.BlockSpec((length, 6 * HD), lambda j: (0, j)),
+            pl.BlockSpec((length, 1), lambda j: (0, 0)),
+            pl.BlockSpec((length, 2 * HD), lambda j: (0, j)),
+        ],
+        out_specs=pl.BlockSpec((length, 6 * HD), lambda j: (0, j)),
+        scratch_shapes=[pltpu.VMEM((length, 6 * HD), jnp.float32)],
+        compiler_params=pltpu.CompilerParams(vmem_limit_bytes=40 * 2**20),
+        cost_estimate=pl.CostEstimate(
+            flops=20 * pairs * length * length * HD,
+            bytes_accessed=4 * length * columns,
+            transcendentals=pairs * length * length,
+        ),
+        name="attend_back",
+    )(mixed, starts, upstream)
 
 
 def small_gather_kernel(axis, count, src_ref, out_ref, send, recv):
@@ -1026,13 +1282,9 @@
 
 
 def step_first(total, at, ins, outs):
-    stream, norms = ins
+    stream, norms = outs[0], ins[0]
     normed, scale = norm_parts(stream[at, :].astype(jnp.float32))
     return normed * norms[0:1, :] + norms[1:2, :]
-
-
-def step_lookup(total, at, ins, outs):
-    outs[0][at, :] = total.astype(jnp.bfloat16)
 
 
 def step_forward(row, total, at, ins, outs):
@@ -1050,65 +1302,21 @@
     )
     if len(ins) > 2:
         pulled = pulled + ins[2][at, :]
-    outs[0][at, :] = pulled.astype(outs[0].dtype)
-    first = at.start == 0
-
-    @pl.when(first)
+    if len(outs) > 1:
+        outs[0][at, :] = pulled
+    sums = outs[-1]
+
+    @pl.when(at.start == 0)
     def _():
-        outs[1][...] = jnp.zeros_like(outs[1])
-
-    outs[1][0:1, :] += dgain
-    outs[1][1:2, :] += dshift
+        sums[...] = jnp.zeros_like(sums)
+
+    sums[0:1, :] += dgain
+    sums[1:2, :] += dshift
     return pulled
-
-
-def step_pass(total, at, ins, outs):
-    return ins[0][at, :]
 
 
 def gelu_tanh(values):
     return jax.nn.gelu(values, approximate=True)
-
-
-def score_block(mixed, starts):
-    place = jnp.arange(mixed.shape[0], dtype=jnp.int32)
-    allowed = (place[None, :] <= place[:, None]) & (place[None, :] >= starts[:, None])
-    raw = jnp.einsum(
-        "qhe,khe->hqk", mixed[:, :, 0], mixed[:, :, 1], preferred_element_type=jnp.float32
-    )
-    return jnp.where(allowed[None], raw * HD ** (-0.5), MASKED)
-
-
-def attend_forward(mixed, starts):
-    scores = score_block(mixed, starts)
-    highest = jnp.max(scores, axis=-1, keepdims=True)
-    weights = jnp.exp(scores - highest)
-    totals = jnp.sum(weights, axis=-1, keepdims=True)
-    probs = (weights / totals).astype(jnp.bfloat16)
-    result = jnp.einsum(
-        "hqk,khe->qhe", probs, mixed[:, :, 2], preferred_element_type=jnp.float32
-    )
-    return (result.astype(jnp.bfloat16), highest[:, :, 0] + jnp.log(totals[:, :, 0]))
-
-
-def attend_backward(mixed, starts, log_rows, upstream):
-    scores = score_block(mixed, starts)
-    probs = jnp.exp(scores - log_rows[:, :, None])
-    dprobs = jnp.einsum(
-        "qhe,khe->hqk", upstream, mixed[:, :, 2], preferred_element_type=jnp.float32
-    )
-    dvalues = jnp.einsum(
-        "hqk,qhe->khe", probs.astype(jnp.bfloat16), upstream, preferred_element_type=jnp.float32
-    )
-    inner = jnp.sum(probs * dprobs, axis=-1, keepdims=True)
-    dscores = (probs * (dprobs - inner)).astype(jnp.bfloat16)
-    dquery = jnp.einsum(
-        "hqk,khe->qhe", dscores, mixed[:, :, 1], preferred_element_type=jnp.float32
-    ) * HD ** (-0.5)
-    dkeys = jnp.einsum(
-        "hqk,qhe->khe", dscores, mixed[:, :, 0], preferred_element_type=jnp.float32
-    ) * HD ** (-0.5)
-    return jnp.stack([dquery, dkeys, dvalues], axis=2).astype(jnp.bfloat16)
 
 
 def local(
@@ -1178,11 +1386,13 @@
     pair_out = own_and_twins(w_out, 0)
     pair_fc = own_and_twins(w_fc, 1)
     pair_proj = own_and_twins(w_proj, 0)
+    piece = rows // chunks_full
+    token = jnp.arange(tokens, dtype=jnp.int32)
     place = (
-        (jnp.arange(size_mp, dtype=jnp.int32) * size_dp)[None, :, None] * rows
-        + (jnp.arange(size_dp, dtype=jnp.int32) * rows)[:, None, None]
-        + jnp.arange(rows, dtype=jnp.int32)[None, None, :]
-    ).reshape(size_dp, tokens)
+        token // piece * (size_dp * piece)
+        + (jnp.arange(size_dp, dtype=jnp.int32) * piece)[:, None]
+        + token % piece
+    )
     local_ids = all_ids - first_row
     inside = (local_ids >= 0) & (local_ids < vocab)
     shift = spots.bit_length()
@@ -1191,52 +1401,37 @@
     keys = jnp.sort(keys.reshape(-1))
     owned = jnp.sum(inside.astype(jnp.int32)).reshape(1)
     found, low_table, table_sq = lookup(keys, owned, embedding, spots, shift)
-    picked_rows, wide_qkv, wide_out, wide_fc = line_call(
-        "rs_lookup",
+    inner_one, stream0, wide_qkv, wide_out, wide_fc, wide_proj = line_call(
+        "lookup_sum",
         1,
         found,
-        [],
-        [jax.ShapeDtypeStruct((size_dp * rows, part_width), bf16)],
-        step_lookup,
+        [norm_params],
+        [jax.ShapeDtypeStruct((rows, width), bf16)],
+        step_first,
         size_dp * rows,
         part_width,
         chunks_full,
         chips,
-        0,
-        50,
-        [("gather", 0, pair_qkv), ("gather", 1, pair_out), ("gather", 0, pair_fc)],
-    )
-    stream0 = lax.all_to_all(
-        picked_rows.reshape(size_dp, rows, part_width), "dp", 0, 0, tiled=False
-    )
-    stream0 = jnp.swapaxes(stream0, 0, 1).reshape(rows, width)
-
-    low_table, picked_rows = lax.optimization_barrier((low_table, picked_rows))
+        near,
+        70,
+        [
+            ("gather", 0, pair_qkv),
+            ("gather", 1, pair_out),
+            ("gather", 0, pair_fc),
+            ("gather", 1, pair_proj),
+        ],
+        "gather",
+        4,
+    )
+    low_table, inner_one = lax.optimization_barrier((low_table, inner_one))
     wide_table = lax.all_gather(low_table, "dp", axis=1, tiled=True)
     row_f32 = jax.ShapeDtypeStruct((rows, width), f32)
     pair_f32 = jax.ShapeDtypeStruct((8, width), f32)
-    (inner_one,) = line_call(
-        "ag_inner1",
-        2,
-        None,
-        [stream0, norm_params],
-        [],
-        step_first,
-        rows,
-        width,
-        chunks_near,
-        0,
-        near,
-        17,
-    )
-    heads = wide_qkv.shape[1] // (3 * HD)
-    my_starts = row_slice(starts, (mp // sharers) * LEN, LEN)
+    my_starts = row_slice(starts, (mp // sharers) * LEN, LEN)[:, None]
     mixed = jnp.dot(inner_one, wide_qkv, preferred_element_type=f32).astype(bf16)
-    mixed = mixed.reshape(LEN, heads, 3, HD)
-    attended, log_sums = attend_forward(mixed, my_starts)
-    attended = attended.reshape(LEN, heads * HD)
+    attended = attend(mixed, my_starts)
     partial = jnp.dot(attended, wide_out, preferred_element_type=f32).astype(bf16)
-    inner_two, stream1, wide_proj = line_call(
+    inner_two, stream1 = line_call(
         "attn_sum",
         3,
         partial,
@@ -1249,7 +1444,6 @@
         near,
         near,
         32,
-        [("gather", 1, pair_proj)],
     )
     before = jnp.dot(inner_two, wide_fc, preferred_element_type=f32)
     hidden = gelu_tanh(before).astype(bf16)
@@ -1330,43 +1524,30 @@
     grad_fc = jnp.einsum("td,tf->df", inner_two, dbefore, preferred_element_type=f32).astype(bf16)
     grad_out = jnp.einsum("tf,td->fd", attended, dbranch1, preferred_element_type=f32).astype(bf16)
     dattended = jnp.einsum("td,fd->tf", dbranch1, wide_out, preferred_element_type=f32)
-    dattended = dattended.astype(bf16).reshape(LEN, heads, HD)
-    dmixed = attend_backward(mixed, my_starts, log_sums, dattended)
-    dmixed = dmixed.reshape(LEN, heads * 3 * HD)
+    dmixed = attend_back(mixed, my_starts, dattended.astype(bf16))
     partial = jnp.einsum("tc,dc->td", dmixed, wide_qkv, preferred_element_type=f32).astype(bf16)
-    dstream0, norm1, grad_proj, grad_out = line_call(
+    grad_qkv = jnp.einsum("td,tc->dc", inner_one, dmixed, preferred_element_type=f32).astype(bf16)
+    drows, norm1, grad_proj, grad_out, grad_fc, grad_qkv = line_call(
         "attn_back",
         8,
         partial,
         [stream0, norm_params, dstream1],
-        [jax.ShapeDtypeStruct((rows, width), bf16), pair_f32],
+        [pair_f32],
         functools.partial(step_backward, 0),
         rows,
         width,
-        chunks_near,
+        chunks_full,
         near,
-        0,
-        28,
-        [("scatter", 1, grad_proj), ("scatter", 1, grad_out)],
-    )
-    grad_qkv = jnp.einsum("td,tc->dc", inner_one, dmixed, preferred_element_type=f32).astype(bf16)
-
-    sent = jnp.swapaxes(dstream0.reshape(rows, size_dp, part_width), 0, 1)
-    sent = lax.all_to_all(sent, "dp", 0, 0, tiled=False).reshape(size_dp * rows, part_width)
-    drows, grad_fc, grad_qkv = line_call(
-        "ag_lookup",
-        9,
-        None,
-        [sent],
-        [],
-        step_pass,
-        size_dp * rows,
-        part_width,
-        chunks_full,
-        0,
         chips,
-        45,
-        [("scatter", 0, grad_fc), ("scatter", 0, grad_qkv)],
+        70,
+        [
+            ("scatter", 1, grad_proj),
+            ("scatter", 1, grad_out),
+            ("scatter", 0, grad_fc),
+            ("scatter", 0, grad_qkv),
+        ],
+        "spread",
+        5,
     )
 
     def to_twins(share, axis):

time: 800 us -> 769 us (0.961)
  matrix products: 82.8 us -> 43.1 us
  Pallas kernels: 553 us -> 579 us
  other arithmetic: 75.1 us -> 56 us
  waiting for transfers between devices: 17 us -> 34.2 us
  local copies, waits for them, and re-layouts: 31.7 us -> 23.5 us
    dot_general x6 -> x0, matrix products: 38.4 us -> none  [the longest x1 15.3 us: attend_backward(): jnp.einsum('qhe,khe->hqk', upstream, mixed[:, :, 2], preferred_element_ty...]
    pallas_call x0 -> x2, Pallas kernels: none -> 26.9 us  [the longest x1 17.4 us: attend_back(): pl.pallas_call(attend_back_kernel, grid=(pairs,), out_shape=jax.ShapeDtyp...]
    ppermute x4, waiting for transfers between devices: 7.24 us -> 18.1 us  [to_twins(): found.append(lax.ppermute(pieces[turn].astype(bf16), 'mp', back))]
    reduce_sum x1 -> x0, other arithmetic: 8.01 us -> none  [attend_forward(): totals = jnp.sum(weights, axis=-1, keepdims=True)]
    pallas_call x8 -> x6, Pallas kernels: 367 us -> 366 us  [line_call(): return list(call(*args))]
  transfers between devices with their start and end apart: 12 -> 10, of which waited for: 4 -> 3; matrix products, arithmetic and copies ran while one was open for 16% -> 8% of each run, Pallas kernels for 42% -> 43%
where the time goes in v4:
time: 769 us; the launch traced here: 763 us
  Pallas kernels  579 us (75%)
  other arithmetic  56 us (7%)
  matrix products  43.1 us (6%)
  waiting for transfers between devices  34.2 us (4%)
  local copies, waits for them, and re-layouts  23.5 us (3%)
  between operations  15.2 us (2%)
  starting transfers between devices  12 us (2%)
    pallas_call x6, Pallas kernels, line_call(): return list(call(*args))  366 us
    pallas_call x1, Pallas kernels, head_back(): pl.pallas_call(functools.partial(head_back_kernel, rows, block, tile), gr...  69.7 us
    pallas_call x1, Pallas kernels, head_stats(): pl.pallas_call(functools.partial(head_stats_kernel, block, tile), grid=(s...  47.1 us
    ppermute x4, waiting for transfers between devices, to_twins(): found.append(lax.ppermute(pieces[turn].astype(bf16), 'mp', back))  18.1 us
    pallas_call x1, Pallas kernels, update_stats(): pl.pallas_call(functools.partial(stats_kernel, full, size_dp, size_mp), o...  18 us
    sub x5, other arithmetic, local(): updated = [weights[n] - factors[n, 0] * steps[n] for n in range(5)]  17.8 us
    pallas_call x1, Pallas kernels, attend_back(): pl.pallas_call(attend_back_kernel, grid=(pairs,), out_shape=jax.ShapeDtyp...  17.4 us
    pallas_call x2, Pallas kernels, small_gather(): pl.pallas_call(functools.partial(small_gather_kernel, axis, count), out_s...  17 us
  transfers between devices with their start and end apart: 10, of which 3 were waited for; matrix products, arithmetic and copies ran while one was open for 8% of the time, Pallas kernels for 43%

profile of v4, /device:TPU:0, one launch (start us, length us, event | category | flops | bytes accessed | tf_op | source)
XLA Modules:
  0.0 762.6 jit_solution(11631890195908367718)
XLA Ops:
  8.6 7.9 %gather_ids.1 = s32[4,32,128]{2,1,0:T(8,128)} custom-call(s32[32,128]{1,0:T(8,128)} %reshape.256.src_ref), custom_call_target="tpu_custom_call" | custom-call | flops 6000000000 | bytes 18000000 | tf_op jit(solution)/shard_map/gather_ids/pallas_call | solution.py:844
  16.5 0.9 reshape.257
  18.1 2.6 collective-permute-start.2
  22.4 2.6 collective-permute-start
  26.5 6.8 sort.14
  33.3 12.2 %lookup.1 = (bf16[8192,256]{1,0:T(8,128)(2,1)}, bf16[6288,256]{1,0:T(8,128)(2,1)}, f32[8,128]{1,0:T(8,128)}) custom-call(s32[1]{0:T(128)} %bitcast.2.count_ref, s32[8192]{0:T(1024)} %get-tuple-element.90.key_ref, f32[6288,256]{1,0:T(8,128)} %table_ref.1), custom_call_target="tpu_custom_call" | custom-call | flops 20000000000 | bytes 60000000 | tf_op jit(solution)/shard_map/lookup/pallas_call | solution.py:1206
  45.6 8.4 %collective-permute-done.1 = bf16[128,256]{1,0:T(8,128)(2,1)S(1)} collective-permute-done((bf16[128,256]{1,0:T(8,128)(2,1)S(1)}, bf16[128,256]{1,0:T(8,128)(2,1)S(1)}, u32[]{:S(2)}, u32[]{:S(2)}) %collective-permute-start.1) | collective-permute-done | bytes 65568 | tf_op jit(solution)/shard_map/ppermute | solution.py:1382
  54.7 0.8 pad_maximum_fusion.2.refs_2_
  55.5 0.9 pad_maximum_fusion.refs_4_
  56.3 0.8 pad_maximum_fusion.1.refs_5_
  57.2 85.9 %lookup_sum.1 = (bf16[1024,1024]{1,0:T(8,128)(2,1)}, bf16[256,1024]{1,0:T(8,128)(2,1)}, bf16[1024,768]{1,0:T(8,128)(2,1)}, bf16[256,1024]{1,0:T(8,128)(2,1)}, bf...) custom-call(bf16[8192,256]{1,0:T(8,128)(2,1)} %get-tuple-element.92.refs_0_, f32[6,1024]{1,0:T(8,128)} %refs_29_.1, ...), custom_call_target="tpu_custom_call" | custom-call | flops 70000001024 | bytes 210000000 | tf_op jit(solution)/shard_map/lookup_sum/pallas_call | solution.py:568
  144.4 3.8 convolution_convert_fusion.7.mixed_ref
  148.3 9.5 %attend.1 = bf16[1024,256]{1,0:T(8,128)(2,1)S(1)} custom-call(bf16[1024,768]{1,0:T(8,128)(2,1)S(1)} %convolution_convert_fusion.7.mixed_ref, s32[1024,1]{1,0:T(8,128)S(1)} %copy.52.starts_ref), custom_call_target="tpu_custom_call" | custom-call | flops 1073741824 | bytes 1572864 | tf_op jit(solution)/shard_map/attend/pallas_call | solution.py:740
  157.8 0.8 copy-done
  158.6 2.0 convolution_convert_fusion.4.refs_0_
  160.7 33.9 %attn_sum.1 = (bf16[1024,1024]{1,0:T(8,128)(2,1)}, f32[256,1024]{1,0:T(8,128)}) custom-call(bf16[1024,1024]{1,0:T(8,128)(2,1)} %convolution_convert_fusion.4.refs_0_, bf16[256,1024]{1,0:T(8,128)(2,1)} %get-tuple-element.102.refs_1_, f32[6,1024]{1,0:T(8,128)} %refs_29_.1), custom_call_target="tpu_custom_call" | custom-call | flops 32000000000 | bytes 96000000 | tf_op jit(solution)/shard_map/attn_sum/pallas_call | solution.py:568
  194.6 4.1 fusion.37
  198.7 4.0 convolution_convert_fusion.3.refs_0_
  202.7 58.2 %mlp_sum.1 = (bf16[2048,1024]{1,0:T(8,128)(2,1)}, f32[256,1024]{1,0:T(8,128)}) custom-call(bf16[1024,1024]{1,0:T(8,128)(2,1)} %convolution_convert_fusion.3.refs_0_, f32[256,1024]{1,0:T(8,128)} %get-tuple-element.106.refs_1_, f32[6,1024]{1,0:T(8,128)} %refs_29_.1), custom_call_target="tpu_custom_call" | custom-call | flops 57999998976 | bytes 174000000 | tf_op jit(solution)/shard_map/mlp_sum/pallas_call | solution.py:568
  260.9 7.6 all-gather.2.cloned.1.call-done.table_ref
  268.5 47.1 %head_stats.1 = (bf16[6400,2048]{1,0:T(8,128)(2,1)}, f32[10,1,2048]{2,1,0:T(1,128)}, f32[10,1,2048]{2,1,0:T(1,128)}, f32[10,1,2048]{2,1,0:T(1,128)}) custom-call(bf16[6288,1024]{1,0:T(8,128)(2,1)} %all-gather.2.cloned.1.call-done.table_ref, bf16[2048,1024]{1,0:T(8,128)(2,1)} %get-tuple-element.107.final_ref, s32[1,2048]{1,0:T(1,128)} %bitcast.153, ...), custom_call_target="tpu_custom_call" | custom-call | flops 26373783552 | bytes 38633472 | tf_op jit(solution)/shard_map/head_stats/pallas_call | solution.py:606
  315.6 1.0 reduce_max.18
  316.5 1.0 fusion.17
  317.5 1.0 reduce_sum.245
  319.1 9.2 %gather_stats.1 = f32[8,48,128]{2,1,0:T(8,128)} custom-call(f32[48,128]{1,0:T(8,128)} %pad_maximum_fusion.4.src_ref), custom_call_target="tpu_custom_call" | custom-call | flops 6000000000 | bytes 18000000 | tf_op jit(solution)/shard_map/gather_stats/pallas_call | solution.py:844
  328.3 1.0 reshape.265
  331.0 69.7 %head_back.1 = (bf16[6288,1024]{1,0:T(8,128)(2,1)}, bf16[2048,1024]{1,0:T(8,128)(2,1)}) custom-call(bf16[6400,2048]{1,0:T(8,128)(2,1)} %get-tuple-element.108.exp_ref, bf16[6288,1024]{1,0:T(8,128)(2,1)} %all-gather.2.cloned.1.call-done.table_ref, bf16[2048,1024]{1,0:T(8,128)(2,1)} %get-tuple-element.107.final_ref, ...), custom_call_target="tpu_custom_call" | custom-call | flops 52747567104 | bytes 51511296 | tf_op jit(solution)/shard_map/head_back/pallas_call | solution.py:674
  402.0 58.6 %final_back.1 = (bf16[1024,1024]{1,0:T(8,128)(2,1)}, f32[256,1024]{1,0:T(8,128)}, f32[8,1024]{1,0:T(8,128)}) custom-call(bf16[2048,1024]{1,0:T(8,128)(2,1)} %get-tuple-element.112.refs_0_, f32[256,1024]{1,0:T(8,128)} %get-tuple-element.113.refs_1_, f32[6,1024]{1,0:T(8,128)} %refs_29_.1), custom_call_target="tpu_custom_call" | custom-call | flops 60000002048 | bytes 180000000 | tf_op jit(solution)/shard_map/final_back/pallas_call | solution.py:568
  460.7 6.9 fusion.8
  467.6 3.8 convolution_convert_fusion.2.refs_0_
  471.3 35.2 %mlp_back.1 = (bf16[1024,1024]{1,0:T(8,128)(2,1)}, f32[256,1024]{1,0:T(8,128)}, f32[8,1024]{1,0:T(8,128)}) custom-call(bf16[1024,1024]{1,0:T(8,128)(2,1)} %convolution_convert_fusion.2.refs_0_, f32[256,1024]{1,0:T(8,128)} %get-tuple-element.106.refs_1_, f32[6,1024]{1,0:T(8,128)} %refs_29_.1, f32[256,1024]{1,0:T(8,128)} %get-tuple-element.115.refs_3_), custom_call_target="tpu_custom_call" | custom-call | flops 33999998976 | bytes 102000000 | tf_op jit(solution)/shard_map/mlp_back/pallas_call | solution.py:568
  506.5 2.9 convolution_convert_fusion.9.upstream_ref
  509.5 17.4 %attend_back.1 = bf16[1024,768]{1,0:T(8,128)(2,1)S(1)} custom-call(bf16[1024,768]{1,0:T(8,128)(2,1)S(1)} %copy-done.3, s32[1024,1]{1,0:T(8,128)S(1)} %copy.52.starts_ref, bf16[1024,256]{1,0:T(8,128)(2,1)S(1)} %convolution_convert_fusion.9.upstream_ref), custom_call_target="tpu_custom_call" | custom-call | flops 2684354560 | bytes 3145728 | tf_op jit(solution)/shard_map/attend_back/pallas_call | solution.py:788
  526.9 1.5 convolution_convert_fusion.8.refs_5_
  528.4 3.1 convolution_convert_fusion.5.refs_0_
  531.6 3.1 convolution_convert_fusion.6.refs_7_
  534.7 3.8 convolution_convert_fusion.refs_6_
  538.5 4.1 convolution_convert_fusion.1.refs_4_
  542.6 93.9 %attn_back.1 = (bf16[8192,256]{1,0:T(8,128)(2,1)}, f32[8,1024]{1,0:T(8,128)}, f32[1024,256]{1,0:T(8,128)}, f32[256,256]{1,0:T(8,128)}, f32[256,1024]{1,0:T(8,128)}, /*index=5*/f32[256,768]{1,0:T(8,128)}) custom-call(bf16[1024,1024]{1,0:T(8,128)(2,1)} %convolution_convert_fusion.5.refs_0_, bf16[256,1024]{1,0:T(8,128)(2,1)} %get-tuple-element.102.refs_1_, ...), custom_call_target="tpu_custom_call" | custom-call | flops 70000001024 | bytes 210000000 | tf_op jit(solution)/shard_map/attn_back/pallas_call | solution.py:568
  636.5 1.1 split.45
  637.6 1.1 split.32
  638.7 1.1 split.44
  639.7 1.1 split.34
  640.8 1.0 split.46
  641.8 1.0 split.28
  643.0 2.9 collective-permute-start.7
  646.0 2.8 collective-permute-start.5
  649.3 11.6 %scatter.1 = f32[6288,256]{1,0:T(8,128)} custom-call(s32[1]{0:T(128)} %bitcast.2.count_ref, s32[8192]{0:T(1024)} %get-tuple-element.90.key_ref, bf16[6288,256]{1,0:T(8,128)(2,1)} %reduce-scatter.2.cloned.1.call-done.head_ref, bf16[8192,256]{1,0:T(8,128)(2,1)} %get-tuple-element.123.rows_in_ref), custom_call_target="tpu_custom_call" | custom-call | flops 23000000512 | bytes 69000000 | tf_op jit(solution)/shard_map/scatter/pallas_call | solution.py:1250
  660.9 18.1 %collective-permute-done.5 = bf16[128,256]{1,0:T(8,128)(2,1)S(1)} collective-permute-done((bf16[128,256]{1,0:T(8,128)(2,1)S(1)}, bf16[128,256]{1,0:T(8,128)(2,1)S(1)}, u32[]{:S(2)}, u32[]{:S(2)}) %collective-permute-start.5) | collective-permute-done | bytes 65568 | tf_op jit(solution)/shard_map/ppermute | solution.py:1558
  679.0 4.4 fusion
  687.0 18.0 %update_stats.1 = (f32[50,128]{1,0:T(8,128)}, f32[2,128]{1,0:T(2,128)}, f32[1,128]{1,0:T(1,128)}, f32[2,128]{1,0:T(2,128)}, f32[4,128]{1,0:T(4,128)}, /*index=5*...) custom-call(f32[50,128]{1,0:T(8,128)} %pad_bitcast_fusion.1.refs_0_,, ...), custom_call_target="tpu_custom_call" | custom-call | flops 12000000000 | bytes 36000000 | tf_op jit(solution)/shard_map/update_stats/pallas_call | solution.py:1095
  705.1 1.4 fusion.35
  706.4 5.5 multiply_reduce_fusion
  711.9 1.4 multiply_reduce_fusion.1
  713.3 1.4 multiply_reduce_fusion.2
  714.8 1.3 multiply_reduce_fusion.7
  716.1 1.4 multiply_reduce_fusion.5
  717.5 10.4 %clip_rates.1 = f32[8,128]{1,0:T(8,128)} custom-call(f32[2,128]{1,0:T(2,128)} %bitcast.175, f32[3,128]{1,0:T(4,128)} %bitcast.162, f32[2,128]{1,0:T(2,128)} %bitcast.172, f32[4,128]{1,0:T(4,128)} %bitcast.161, f32[2,128]{1,0:T(2,128)} %bitcast.171, f32[16,128]{1,0:T(8,128)} %get-tuple-element.140.refs_5_), custom_call_target="tpu_custom_call" | custom-call | flops 8000000000 | bytes 24000000 | tf_op jit(solution)/shard_map/clip_rates/pallas_call | solution.py:1143
  727.9 1.4 fusion.36
  729.3 2.3 multiply_subtract_fusion.1
  731.6 2.3 multiply_subtract_fusion.2
  733.9 2.0 multiply_subtract_fusion.4
  735.9 2.2 multiply_subtract_fusion.3
  738.1 9.1 %multiply_subtract_fusion = f32[6288,256]{1,0:T(8,128)} fusion(f32[6288,256]{1,0:T(8,128)} %table_ref.1, f32[]{:T(128)} %bitcast.58, f32[6288,256]{1,0:T(8,128)} %scatter.1, f32[]{:T(128)} %bitcast.40, f32[256]{0:T(256)S(1)} %bitcast.151, f32[6288]{0:T(1024)S(1)} %bitcast.118), kind=kLoop, calls=%fused_computation | loop fusion | flops 8048640 | bytes 19342920 | tf_op jit(solution)/shard_map/sub | solution.py:1601
  (166 shorter events, 23.4 us)
Async XLA Ops:
  7.2 261.3 %all-gather.2.cloned.1.call-start = ((), (), s32[]{:S(2)}) async-start(), calls=%async_computation.1 | async-start | bytes 16097280 | tf_op jit(solution)/shard_map/all_gather | solution.py:1427
  8.6 8.9 %copy-start.9 = (f32[256,512]{1,0:T(8,128)S(1)}, f32[256,512]{1,0:T(8,128)}, u32[]{:S(2)}) copy-start(f32[256,512]{1,0:T(8,128)} %param.28) | copy-start | bytes 1572868
  8.6 12.1 %copy-start.7 = (f32[512,256]{1,0:T(8,128)S(1)}, f32[512,256]{1,0:T(8,128)}, u32[]{:S(2)}) copy-start(f32[512,256]{1,0:T(8,128)} %param.29) | copy-start | bytes 1572868
  8.6 13.1 %copy-start.12 = (f32[256,384]{1,0:T(8,128)S(1)}, f32[256,384]{1,0:T(8,128)}, u32[]{:S(2)}) copy-start(f32[256,384]{1,0:T(8,128)} %param.26) | copy-start | bytes 1179652
  8.6 16.3 %copy-start.16 = (f32[128,256]{1,0:T(8,128)S(1)}, f32[128,256]{1,0:T(8,128)}, u32[]{:S(2)}) copy-start(f32[128,256]{1,0:T(8,128)} %param.27) | copy-start | bytes 393220
  18.1 37.3 %collective-permute-start.2 = (bf16[256,512]{1,0:T(8,128)(2,1)S(1)}, bf16[256,512]{1,0:T(8,128)(2,1)S(1)}, u32[]{:S(2)}, u32[]{:S(2)}) collective-permute-start(bf16[256,512]{1,0:T(8,128)(2,1)S(1)} %get-tuple-element.175), channel_id=1, source_target_pairs={{0,4},{1,5},{2,6},{3,7},{4,0},{5,1},{6,2},{7,3},{8,12},{9,13},{10,... | collective-permute-start | bytes 786440 | tf_op jit(solution)/shard_map/ppermute | solution.py:1382
  21.4 35.0 %collective-permute-start.3 = (bf16[512,256]{1,0:T(8,128)(2,1)S(1)}, bf16[512,256]{1,0:T(8,128)(2,1)S(1)}, u32[]{:S(2)}, u32[]{:S(2)}) collective-permute-start(bf16[512,256]{1,0:T(8,128)(2,1)S(1)} %get-tuple-element.173), channel_id=1, source_target_pairs={{0,4},{1,5},{2,6},{3,7},{4,0},{5,1},{6,2},{7,3},{8,12},{9,13},{10,... | collective-permute-start | bytes 786440 | tf_op jit(solution)/shard_map/ppermute | solution.py:1382
  22.4 32.3 %collective-permute-start = (bf16[256,384]{1,0:T(8,128)(2,1)S(1)}, bf16[256,384]{1,0:T(8,128)(2,1)S(1)}, u32[]{:S(2)}, u32[]{:S(2)}) collective-permute-start(bf16[256,384]{1,0:T(8,128)(2,1)S(1)} %get-tuple-element.177), channel_id=1, source_target_pairs={{0,4},{1,5},{2,6},{3,7},{4,0},{5,1},{6,2},{7,3},{8,12},{9,13},{10,... | collective-permute-start | bytes 589832 | tf_op jit(solution)/shard_map/ppermute | solution.py:1382
  25.5 28.5 %collective-permute-start.1 = (bf16[128,256]{1,0:T(8,128)(2,1)S(1)}, bf16[128,256]{1,0:T(8,128)(2,1)S(1)}, u32[]{:S(2)}, u32[]{:S(2)}) collective-permute-start(bf16[128,256]{1,0:T(8,128)(2,1)S(1)} %get-tuple-element.181), channel_id=1, source_target_pairs={{0,4},{1,5},{2,6},{3,7},{4,0},{5,1},{6,2},{7,3},{8,12},{9,13},{10,... | collective-permute-start | bytes 196616 | tf_op jit(solution)/shard_map/ppermute | solution.py:1382
  57.2 86.2 %copy-start.38 = (s32[2048]{0:T(1024)S(1)}, s32[2048]{0:T(1024)}, u32[]{:S(2)}) copy-start(s32[2048]{0:T(1024)} %param.23) | copy-start | bytes 24580
  57.2 86.6 %copy-start.36 = (s32[2048]{0:T(1024)S(1)}, s32[2048]{0:T(1024)}, u32[]{:S(2)}) copy-start(s32[2048]{0:T(1024)} %param.22) | copy-start | bytes 24580
  143.1 506.3 %reduce-scatter.2.cloned.1.call-start = ((), (), s32[]{:S(2)}) async-start(), calls=%async_computation.2 | async-start | bytes 16097280 | tf_op jit(solution)/shard_map/reduce_scatter | solution.py:1489
  143.8 4.5 copy-start.39
  148.3 12.4 %copy-start.2 = (bf16[1024,768]{1,0:T(8,128)(2,1)}, bf16[1024,768]{1,0:T(8,128)(2,1)S(1)}, u32[]{:S(2)}) copy-start(bf16[1024,768]{1,0:T(8,128)(2,1)S(1)} %convolution_convert_fusion.7.mixed_ref) | copy-start | bytes 4718596
  148.3 10.4 %copy-start.18 = (bf16[256,1024]{1,0:T(8,128)(2,1)S(1)}, bf16[256,1024]{1,0:T(8,128)(2,1)}, u32[]{:S(2)}) copy-start(bf16[256,1024]{1,0:T(8,128)(2,1)} %get-tuple-element.101) | copy-start | bytes 1572868
  157.8 0.8 copy-start
  160.7 33.9 %copy-start.47 = (bf16[1024,1024]{1,0:T(8,128)(2,1)S(1)}, bf16[1024,1024]{1,0:T(8,128)(2,1)}, u32[]{:S(2)}) copy-start(bf16[1024,1024]{1,0:T(8,128)(2,1)} %get-tuple-element.104) | copy-start | bytes 6291460
  194.6 4.1 copy-start.51
  198.7 4.0 copy-start.42
  319.1 10.5 %copy-start.26 = (s32[2048]{0:T(1024)S(1)}, s32[2048]{0:T(1024)}, u32[]{:S(2)}) copy-start(s32[2048]{0:T(1024)} %param.24) | copy-start | bytes 24580
  319.1 11.1 %copy-start.15 = (f32[10,1,2048]{2,1,0:T(1,128)S(1)}, f32[10,1,2048]{2,1,0:T(1,128)}, u32[]{:S(2)}) copy-start(f32[10,1,2048]{2,1,0:T(1,128)} %get-tuple-element.109) | copy-start | bytes 245764
  330.2 0.7 copy-start.22
  400.6 0.7 copy-start.27
  402.0 58.6 %copy-start.43 = (f32[1024,1024]{1,0:T(8,128)S(1)}, f32[1024,1024]{1,0:T(8,128)}, u32[]{:S(2)}) copy-start(f32[1024,1024]{1,0:T(8,128)} %copy-done.42) | copy-start | bytes 12582916
  460.7 6.9 copy-start.48
  471.3 35.2 %copy-start.19 = (bf16[256,1024]{1,0:T(8,128)(2,1)S(1)}, bf16[256,1024]{1,0:T(8,128)(2,1)}, u32[]{:S(2)}) copy-start(bf16[256,1024]{1,0:T(8,128)(2,1)} %get-tuple-element.101) | copy-start | bytes 1572868
  506.5 2.9 copy-start.3
  509.4 17.4 %copy-start.1 = (bf16[1024,256]{1,0:T(8,128)(2,1)S(1)}, bf16[1024,256]{1,0:T(8,128)(2,1)}, u32[]{:S(2)}) copy-start(bf16[1024,256]{1,0:T(8,128)(2,1)} %copy-done) | copy-start | bytes 1572868
  509.5 17.4 %copy-start.11 = (bf16[1024,1024]{1,0:T(8,128)(2,1)S(1)}, bf16[1024,1024]{1,0:T(8,128)(2,1)}, u32[]{:S(2)}) copy-start(bf16[1024,1024]{1,0:T(8,128)(2,1)} %get-tuple-element.116) | copy-start | bytes 6291460
  509.5 19.0 %copy-start.46 = (bf16[1024,768]{1,0:T(8,128)(2,1)S(1)}, bf16[1024,768]{1,0:T(8,128)(2,1)}, u32[]{:S(2)}) copy-start(bf16[1024,768]{1,0:T(8,128)(2,1)} %get-tuple-element.99) | copy-start | bytes 4718596
  528.4 3.1 copy-start.45
  531.6 3.1 copy-start.49
  534.7 3.8 copy-start.44
  534.7 3.8 copy-start.50
  636.4 6.4 copy-start.21
  636.4 12.4 %copy-start.40 = (f32[4]{0:T(128)S(1)}, f32[4]{0:T(128)}, u32[]{:S(2)}) copy-start(f32[4]{0:T(128)} %get-tuple-element.164) | copy-start | bytes 52
  642.9 36.1 %collective-permute-start.6 = (bf16[256,512]{1,0:T(8,128)(2,1)S(1)}, bf16[256,512]{1,0:T(8,128)(2,1)S(1)}, u32[]{:S(2)}, u32[]{:S(2)}) collective-permute-start(bf16[256,512]{1,0:T(8,128)(2,1)S(1)} %split.45), channel_id=1, source_target_pairs={{0,4},{1,5},{2,6},{3,7},{4,0},{5,1},{6,2},{7,3},{8,12},{9,13},{10,... | collective-permute-start | bytes 786440 | tf_op jit(solution)/shard_map/ppermute | solution.py:1558
  643.0 36.0 %collective-permute-start.7 = (bf16[512,256]{1,0:T(8,128)(2,1)S(1)}, bf16[512,256]{1,0:T(8,128)(2,1)S(1)}, u32[]{:S(2)}, u32[]{:S(2)}) collective-permute-start(bf16[512,256]{1,0:T(8,128)(2,1)S(1)} %split.44), channel_id=1, source_target_pairs={{0,4},{1,5},{2,6},{3,7},{4,0},{5,1},{6,2},{7,3},{8,12},{9,13},{10,... | collective-permute-start | bytes 786440 | tf_op jit(solution)/shard_map/ppermute | solution.py:1558
  645.9 33.1 %collective-permute-start.4 = (bf16[256,384]{1,0:T(8,128)(2,1)S(1)}, bf16[256,384]{1,0:T(8,128)(2,1)S(1)}, u32[]{:S(2)}, u32[]{:S(2)}) collective-permute-start(bf16[256,384]{1,0:T(8,128)(2,1)S(1)} %split.46), channel_id=1, source_target_pairs={{0,4},{1,5},{2,6},{3,7},{4,0},{5,1},{6,2},{7,3},{8,12},{9,13},{10,... | collective-permute-start | bytes 589832 | tf_op jit(solution)/shard_map/ppermute | solution.py:1558
  646.0 33.0 %collective-permute-start.5 = (bf16[128,256]{1,0:T(8,128)(2,1)S(1)}, bf16[128,256]{1,0:T(8,128)(2,1)S(1)}, u32[]{:S(2)}, u32[]{:S(2)}) collective-permute-start(bf16[128,256]{1,0:T(8,128)(2,1)S(1)} %split.47), channel_id=1, source_target_pairs={{0,4},{1,5},{2,6},{3,7},{4,0},{5,1},{6,2},{7,3},{8,12},{9,13},{10,... | collective-permute-start | bytes 196616 | tf_op jit(solution)/shard_map/ppermute | solution.py:1558
  684.8 44.5 %copy-start.4 = (f32[512,256]{1,0:T(8,128)}, f32[512,256]{1,0:T(8,128)S(1)}, u32[]{:S(2)}) copy-start(f32[512,256]{1,0:T(8,128)S(1)} %get-tuple-element.241) | copy-start | bytes 1572868
  685.6 46.0 %copy-start.5 = (f32[256,512]{1,0:T(8,128)}, f32[256,512]{1,0:T(8,128)S(1)}, u32[]{:S(2)}) copy-start(f32[256,512]{1,0:T(8,128)S(1)} %get-tuple-element.237) | copy-start | bytes 1572868
  686.3 47.6 %copy-start.14 = (f32[128,256]{1,0:T(8,128)}, f32[128,256]{1,0:T(8,128)S(1)}, u32[]{:S(2)}) copy-start(f32[128,256]{1,0:T(8,128)S(1)} %get-tuple-element.233) | copy-start | bytes 393220
  687.0 48.9 %copy-start.6 = (f32[256,384]{1,0:T(8,128)}, f32[256,384]{1,0:T(8,128)S(1)}, u32[]{:S(2)}) copy-start(f32[256,384]{1,0:T(8,128)S(1)} %get-tuple-element.229) | copy-start | bytes 1179652
  705.0 7.0 copy-start.28
  705.0 6.9 copy-start.31
  705.0 8.3 %copy-start.29 = (f32[4,128]{1,0:T(4,128)S(1)}, f32[4,128]{1,0:T(4,128)}, u32[]{:S(2)}) copy-start(f32[4,128]{1,0:T(4,128)} %get-tuple-element.146) | copy-start | bytes 6148
  705.0 8.3 %copy-start.32 = (f32[2,128]{1,0:T(2,128)S(1)}, f32[2,128]{1,0:T(2,128)}, u32[]{:S(2)}) copy-start(f32[2,128]{1,0:T(2,128)} %get-tuple-element.145) | copy-start | bytes 3076
  705.0 9.7 %copy-start.33 = (f32[2,128]{1,0:T(2,128)S(1)}, f32[2,128]{1,0:T(2,128)}, u32[]{:S(2)}) copy-start(f32[2,128]{1,0:T(2,128)} %get-tuple-element.144) | copy-start | bytes 3076
  705.0 9.7 %copy-start.37 = (f32[1,128]{1,0:T(1,128)S(1)}, f32[1,128]{1,0:T(1,128)}, u32[]{:S(2)}) copy-start(f32[1,128]{1,0:T(1,128)} %get-tuple-element.143) | copy-start | bytes 1540
  705.0 11.0 %copy-start.30 = (f32[3,128]{1,0:T(4,128)S(1)}, f32[3,128]{1,0:T(4,128)}, u32[]{:S(2)}) copy-start(f32[3,128]{1,0:T(4,128)} %get-tuple-element.142) | copy-start | bytes 4612
  705.0 11.0 %copy-start.34 = (f32[2,128]{1,0:T(2,128)S(1)}, f32[2,128]{1,0:T(2,128)}, u32[]{:S(2)}) copy-start(f32[2,128]{1,0:T(2,128)} %get-tuple-element.141) | copy-start | bytes 3076
  717.5 11.9 %copy-start.8 = (f32[512,256]{1,0:T(8,128)S(1)}, f32[512,256]{1,0:T(8,128)}, u32[]{:S(2)}) copy-start(f32[512,256]{1,0:T(8,128)} %param.29) | copy-start | bytes 1572868
  717.5 14.1 %copy-start.10 = (f32[256,512]{1,0:T(8,128)S(1)}, f32[256,512]{1,0:T(8,128)}, u32[]{:S(2)}) copy-start(f32[256,512]{1,0:T(8,128)} %param.28) | copy-start | bytes 1572868
  717.5 16.4 %copy-start.17 = (f32[128,256]{1,0:T(8,128)S(1)}, f32[128,256]{1,0:T(8,128)}, u32[]{:S(2)}) copy-start(f32[128,256]{1,0:T(8,128)} %param.27) | copy-start | bytes 393220
  717.5 18.4 %copy-start.13 = (f32[256,384]{1,0:T(8,128)S(1)}, f32[256,384]{1,0:T(8,128)}, u32[]{:S(2)}) copy-start(f32[256,384]{1,0:T(8,128)} %param.26) | copy-start | bytes 1179652
  727.9 10.2 %copy-start.20 = (f32[50,128]{1,0:T(8,128)S(1)}, f32[50,128]{1,0:T(8,128)}, u32[]{:S(2)}) copy-start(f32[50,128]{1,0:T(8,128)} %get-tuple-element.138) | copy-start | bytes 76804
  727.9 10.2 %copy-start.35 = (f32[2,128]{1,0:T(2,128)S(1)}, f32[2,128]{1,0:T(2,128)}, u32[]{:S(2)}) copy-start(f32[2,128]{1,0:T(2,128)} %get-tuple-element.139) | copy-start | bytes 3076
  738.1 9.1 %copy-start.41 = (f32[1,128]{1,0:T(1,128)S(1)}, f32[1,128]{1,0:T(1,128)}, u32[]{:S(2)}) copy-start(f32[1,128]{1,0:T(1,128)} %get-tuple-element.137) | copy-start | bytes 1540
  738.1 15.3 %copy-start.25 = (f32[6,1024]{1,0:T(8,128)S(1)}, f32[6,1024]{1,0:T(8,128)}, u32[]{:S(2)}) copy-start(f32[6,1024]{1,0:T(8,128)} %get-tuple-element.245) | copy-start | bytes 73732
  738.1 15.9 %copy-start.24 = (f32[6,1024]{1,0:T(8,128)S(1)}, f32[6,1024]{1,0:T(8,128)}, u32[]{:S(2)}) copy-start(f32[6,1024]{1,0:T(8,128)} %get-tuple-element.246) | copy-start | bytes 73732
  738.1 16.5 %copy-start.23 = (f32[6,1024]{1,0:T(8,128)S(1)}, f32[6,1024]{1,0:T(8,128)}, u32[]{:S(2)}) copy-start(f32[6,1024]{1,0:T(8,128)} %get-tuple-element.247) | copy-start | bytes 73732
Sparse Core Ops, SparseCore 0:
  143.2 125.2 all-gather.1
  400.8 123.9 reduce-scatter.1

commit v5 on v4

--- a/solution.py
+++ b/solution.py
@@ -35,7 +35,7 @@
     return lax.dynamic_slice_in_dim(values, start, count, 0)
 
 
-def line_kernel(nr, ng, chunks, shapes, n_in, n_out, step, sides, turn, relay_tick, *refs):
+def line_kernel(nr, ng, chunks, shapes, n_in, n_out, step, sides, turn, side_ticks, *refs):
     (rows_r, width_r), (rows_g, width_g) = shapes
     part = refs[0] if nr else None
     first = 1 if nr else 0
@@ -163,21 +163,25 @@
                 own = src.at[half_share(axis, length, far_one, height, side)]
                 relays.append((arrives, (own, slots, 4 * side, height), summed))
 
-    def start_sides():
-        for copy in first_copies + more_copies:
-            copy.start()
-
-    def pass_on():
-        for arrives, adding, copy in relays:
-            arrives.wait_recv()
-            if adding is not None:
-                own, slots, at, height = adding
-                both = own[...].astype(jnp.float32) + slots[at].astype(jnp.float32)
-                slots[at + 2] = both.astype(slots.dtype)
-            copy.start()
-
-    if nr == 0:
-        start_sides()
+    def pass_on(arrives, adding, copy):
+        arrives.wait_recv()
+        if adding is not None:
+            own, slots, at, height = adding
+            both = own[...].astype(jnp.float32) + slots[at].astype(jnp.float32)
+            slots[at + 2] = both.astype(slots.dtype)
+        copy.start()
+
+    jobs = [copy.start for copy in first_copies + more_copies]
+    jobs += [functools.partial(pass_on, *one) for one in relays]
+
+    def side_jobs(now):
+        for spot in range(side_ticks if jobs else 0):
+            chosen = jobs[len(jobs) * spot // side_ticks : len(jobs) * (spot + 1) // side_ticks]
+
+            @pl.when(now == spot)
+            def _():
+                for job in chosen:
+                    job()
 
     if nr:
         half, from_left, from_right, going = scratch[:4]
@@ -219,7 +223,6 @@
             return carry
 
         lax.fori_loop(0, chunks, send_halves, 0)
-        start_sides()
 
         def right_copy(dest, k):
             return remote(
@@ -374,6 +377,7 @@
         return jnp.maximum(at, last_r - at)
 
     def tick(now, carry):
+        side_jobs(now)
         if nr:
             k_right = now - zr
             k_left = now - (last_r - zr)
@@ -398,12 +402,6 @@
             @pl.when(inside(k_own - 1))
             def _():
                 turned_rows(k_own - 1)
-
-        if relays:
-
-            @pl.when(now == relay_tick)
-            def _():
-                pass_on()
 
         if ng:
             for block in range(ng):
@@ -502,7 +500,7 @@
     time,
     sides=(),
     turn=None,
-    relay_tick=0,
+    side_ticks=0,
 ):
     piece = rows // chunks
     size_dp = lax.axis_size("dp")
@@ -553,7 +551,7 @@
             step,
             tuple(side[:2] for side in sides),
             turn,
-            relay_tick,
+            side_ticks,
         ),
         out_shape=out_shape,
         in_specs=[vmem] * len(args),
@@ -1360,6 +1358,7 @@
     spots = tokens * size_dp
     chunks_full = max(1, min(8, rows // 32))
     chunks_near = max(1, min(4, rows // 32))
+    chunks_turn = max(1, min(4, rows // 32))
 
     both = jnp.stack([token_ids, sources]).reshape(-1, 128)
     both = small_gather("gather_ids", 0, both, "dp").reshape(size_dp, 2, tokens)
@@ -1386,7 +1385,7 @@
     pair_out = own_and_twins(w_out, 0)
     pair_fc = own_and_twins(w_fc, 1)
     pair_proj = own_and_twins(w_proj, 0)
-    piece = rows // chunks_full
+    piece = rows // chunks_turn
     token = jnp.arange(tokens, dtype=jnp.int32)
     place = (
         token // piece * (size_dp * piece)
@@ -1410,7 +1409,7 @@
         step_first,
         size_dp * rows,
         part_width,
-        chunks_full,
+        chunks_turn,
         chips,
         near,
         70,
@@ -1421,7 +1420,7 @@
             ("gather", 1, pair_proj),
         ],
         "gather",
-        4,
+        8,
     )
     low_table, inner_one = lax.optimization_barrier((low_table, inner_one))
     wide_table = lax.all_gather(low_table, "dp", axis=1, tiled=True)
@@ -1536,7 +1535,7 @@
         functools.partial(step_backward, 0),
         rows,
         width,
-        chunks_full,
+        chunks_turn,
         near,
         chips,
         70,
@@ -1547,7 +1546,7 @@
             ("scatter", 0, grad_qkv),
         ],
         "spread",
-        5,
+        9,
     )
 
     def to_twins(share, axis):

time: 769 us -> 731 us (0.951)
  Pallas kernels: 579 us -> 550 us
  waiting for transfers between devices: 34.2 us -> 24.6 us
    pallas_call x6, Pallas kernels: 366 us -> 330 us  [line_call(): return list(call(*args))]
    ppermute x4, waiting for transfers between devices: 18.1 us -> 10.1 us  [to_twins(): found.append(lax.ppermute(pieces[turn].astype(bf16), 'mp', back))]
  transfers between devices with their start and end apart: 10 -> 10, of which waited for: 3 -> 3; matrix products, arithmetic and copies ran while one was open for 8% -> 9% of each run, Pallas kernels for 43% -> 44%
where the time goes in v5:
time: 731 us; the launch traced here: 724 us
  Pallas kernels  550 us (75%)
  other arithmetic  56 us (8%)
  matrix products  43.1 us (6%)
  waiting for transfers between devices  24.6 us (3%)
  local copies, waits for them, and re-layouts  23.5 us (3%)
  between operations  15.2 us (2%)
  starting transfers between devices  12 us (2%)
    pallas_call x6, Pallas kernels, line_call(): return list(call(*args))  330 us
    pallas_call x1, Pallas kernels, head_back(): pl.pallas_call(functools.partial(head_back_kernel, rows, block, tile), gr...  69.7 us
    pallas_call x1, Pallas kernels, head_stats(): pl.pallas_call(functools.partial(head_stats_kernel, block, tile), grid=(s...  47.1 us
    sub x5, other arithmetic, local(): updated = [weights[n] - factors[n, 0] * steps[n] for n in range(5)]  17.8 us
    pallas_call x1, Pallas kernels, attend_back(): pl.pallas_call(attend_back_kernel, grid=(pairs,), out_shape=jax.ShapeDtyp...  17.4 us
    pallas_call x2, Pallas kernels, small_gather(): pl.pallas_call(functools.partial(small_gather_kernel, axis, count), out_s...  17 us
    pallas_call x1, Pallas kernels, scatter(): pl.pallas_call(functools.partial(scatter_kernel, shift), out_shape=jax.Sh...  16.4 us
    pallas_call x1, Pallas kernels, update_stats(): pl.pallas_call(functools.partial(stats_kernel, full, size_dp, size_mp), o...  16.2 us
  transfers between devices with their start and end apart: 10, of which 3 were waited for; matrix products, arithmetic and copies ran while one was open for 9% of the time, Pallas kernels for 44%

profile of v5, /device:TPU:0, one launch (start us, length us, event | category | flops | bytes accessed | tf_op | source)
XLA Modules:
  0.0 724.0 jit_solution(527411225618989557)
XLA Ops:
  8.6 7.9 %gather_ids.1 = s32[4,32,128]{2,1,0:T(8,128)} custom-call(s32[32,128]{1,0:T(8,128)} %reshape.256.src_ref), custom_call_target="tpu_custom_call" | custom-call | flops 6000000000 | bytes 18000000 | tf_op jit(solution)/shard_map/gather_ids/pallas_call | solution.py:842
  16.5 0.9 reshape.257
  18.1 2.6 collective-permute-start.2
  22.4 2.6 collective-permute-start
  26.5 6.8 sort.14
  33.3 15.3 %lookup.1 = (bf16[8192,256]{1,0:T(8,128)(2,1)}, bf16[6288,256]{1,0:T(8,128)(2,1)}, f32[8,128]{1,0:T(8,128)}) custom-call(s32[1]{0:T(128)} %bitcast.2.count_ref, s32[8192]{0:T(1024)} %get-tuple-element.90.key_ref, f32[6288,256]{1,0:T(8,128)} %table_ref.1), custom_call_target="tpu_custom_call" | custom-call | flops 20000000000 | bytes 60000000 | tf_op jit(solution)/shard_map/lookup/pallas_call | solution.py:1204
  48.6 5.4 collective-permute-done.1
  54.7 0.8 pad_maximum_fusion.2.refs_2_
  55.5 0.9 pad_maximum_fusion.refs_4_
  56.3 0.8 pad_maximum_fusion.1.refs_5_
  57.2 68.8 %lookup_sum.1 = (bf16[1024,1024]{1,0:T(8,128)(2,1)}, bf16[256,1024]{1,0:T(8,128)(2,1)}, bf16[1024,768]{1,0:T(8,128)(2,1)}, bf16[256,1024]{1,0:T(8,128)(2,1)}, bf...) custom-call(bf16[8192,256]{1,0:T(8,128)(2,1)} %get-tuple-element.92.refs_0_, f32[6,1024]{1,0:T(8,128)} %refs_29_.1, ...), custom_call_target="tpu_custom_call" | custom-call | flops 70000001024 | bytes 210000000 | tf_op jit(solution)/shard_map/lookup_sum/pallas_call | solution.py:566
  127.4 3.8 convolution_convert_fusion.7.mixed_ref
  131.2 9.5 %attend.1 = bf16[1024,256]{1,0:T(8,128)(2,1)S(1)} custom-call(bf16[1024,768]{1,0:T(8,128)(2,1)S(1)} %convolution_convert_fusion.7.mixed_ref, s32[1024,1]{1,0:T(8,128)S(1)} %copy.52.starts_ref), custom_call_target="tpu_custom_call" | custom-call | flops 1073741824 | bytes 1572864 | tf_op jit(solution)/shard_map/attend/pallas_call | solution.py:738
  140.8 0.8 copy-done
  141.6 2.0 convolution_convert_fusion.4.refs_0_
  143.6 34.6 %attn_sum.1 = (bf16[1024,1024]{1,0:T(8,128)(2,1)}, f32[256,1024]{1,0:T(8,128)}) custom-call(bf16[1024,1024]{1,0:T(8,128)(2,1)} %convolution_convert_fusion.4.refs_0_, bf16[256,1024]{1,0:T(8,128)(2,1)} %get-tuple-element.102.refs_1_, f32[6,1024]{1,0:T(8,128)} %refs_29_.1), custom_call_target="tpu_custom_call" | custom-call | flops 32000000000 | bytes 96000000 | tf_op jit(solution)/shard_map/attn_sum/pallas_call | solution.py:566
  178.2 4.1 fusion.37
  182.3 4.0 convolution_convert_fusion.3.refs_0_
  186.3 59.3 %mlp_sum.1 = (bf16[2048,1024]{1,0:T(8,128)(2,1)}, f32[256,1024]{1,0:T(8,128)}) custom-call(bf16[1024,1024]{1,0:T(8,128)(2,1)} %convolution_convert_fusion.3.refs_0_, f32[256,1024]{1,0:T(8,128)} %get-tuple-element.106.refs_1_, f32[6,1024]{1,0:T(8,128)} %refs_29_.1), custom_call_target="tpu_custom_call" | custom-call | flops 57999998976 | bytes 174000000 | tf_op jit(solution)/shard_map/mlp_sum/pallas_call | solution.py:566
  245.6 9.1 %all-gather.2.cloned.1.call-done.table_ref = bf16[6288,1024]{1,0:T(8,128)(2,1)} async-done(((bf16[6288,256]{1,0:T(8,128)(2,1)}), bf16[6288,1024]{1,0:T(8,128)(2,1)}) %all-gather.2.cloned.1.call-update) | async-done | bytes 12877840 | tf_op jit(solution)/shard_map/all_gather | solution.py:1426
  254.6 47.1 %head_stats.1 = (bf16[6400,2048]{1,0:T(8,128)(2,1)}, f32[10,1,2048]{2,1,0:T(1,128)}, f32[10,1,2048]{2,1,0:T(1,128)}, f32[10,1,2048]{2,1,0:T(1,128)}) custom-call(bf16[6288,1024]{1,0:T(8,128)(2,1)} %all-gather.2.cloned.1.call-done.table_ref, bf16[2048,1024]{1,0:T(8,128)(2,1)} %get-tuple-element.107.final_ref, s32[1,2048]{1,0:T(1,128)} %bitcast.153, ...), custom_call_target="tpu_custom_call" | custom-call | flops 26373783552 | bytes 38633472 | tf_op jit(solution)/shard_map/head_stats/pallas_call | solution.py:604
  301.7 1.0 reduce_max.18
  302.6 1.0 fusion.17
  303.7 1.0 reduce_sum.245
  305.2 9.1 %gather_stats.1 = f32[8,48,128]{2,1,0:T(8,128)} custom-call(f32[48,128]{1,0:T(8,128)} %pad_maximum_fusion.4.src_ref), custom_call_target="tpu_custom_call" | custom-call | flops 6000000000 | bytes 18000000 | tf_op jit(solution)/shard_map/gather_stats/pallas_call | solution.py:842
  314.4 1.0 reshape.265
  317.1 69.7 %head_back.1 = (bf16[6288,1024]{1,0:T(8,128)(2,1)}, bf16[2048,1024]{1,0:T(8,128)(2,1)}) custom-call(bf16[6400,2048]{1,0:T(8,128)(2,1)} %get-tuple-element.108.exp_ref, bf16[6288,1024]{1,0:T(8,128)(2,1)} %all-gather.2.cloned.1.call-done.table_ref, bf16[2048,1024]{1,0:T(8,128)(2,1)} %get-tuple-element.107.final_ref, ...), custom_call_target="tpu_custom_call" | custom-call | flops 52747567104 | bytes 51511296 | tf_op jit(solution)/shard_map/head_back/pallas_call | solution.py:672
  388.1 58.6 %final_back.1 = (bf16[1024,1024]{1,0:T(8,128)(2,1)}, f32[256,1024]{1,0:T(8,128)}, f32[8,1024]{1,0:T(8,128)}) custom-call(bf16[2048,1024]{1,0:T(8,128)(2,1)} %get-tuple-element.112.refs_0_, f32[256,1024]{1,0:T(8,128)} %get-tuple-element.113.refs_1_, f32[6,1024]{1,0:T(8,128)} %refs_29_.1), custom_call_target="tpu_custom_call" | custom-call | flops 60000002048 | bytes 180000000 | tf_op jit(solution)/shard_map/final_back/pallas_call | solution.py:566
  446.8 6.9 fusion.8
  453.6 3.8 convolution_convert_fusion.2.refs_0_
  457.4 35.2 %mlp_back.1 = (bf16[1024,1024]{1,0:T(8,128)(2,1)}, f32[256,1024]{1,0:T(8,128)}, f32[8,1024]{1,0:T(8,128)}) custom-call(bf16[1024,1024]{1,0:T(8,128)(2,1)} %convolution_convert_fusion.2.refs_0_, f32[256,1024]{1,0:T(8,128)} %get-tuple-element.106.refs_1_, f32[6,1024]{1,0:T(8,128)} %refs_29_.1, f32[256,1024]{1,0:T(8,128)} %get-tuple-element.115.refs_3_), custom_call_target="tpu_custom_call" | custom-call | flops 33999998976 | bytes 102000000 | tf_op jit(solution)/shard_map/mlp_back/pallas_call | solution.py:566
  492.6 2.9 convolution_convert_fusion.9.upstream_ref
  495.6 17.4 %attend_back.1 = bf16[1024,768]{1,0:T(8,128)(2,1)S(1)} custom-call(bf16[1024,768]{1,0:T(8,128)(2,1)S(1)} %copy-done.3, s32[1024,1]{1,0:T(8,128)S(1)} %copy.52.starts_ref, bf16[1024,256]{1,0:T(8,128)(2,1)S(1)} %convolution_convert_fusion.9.upstream_ref), custom_call_target="tpu_custom_call" | custom-call | flops 2684354560 | bytes 3145728 | tf_op jit(solution)/shard_map/attend_back/pallas_call | solution.py:786
  513.0 1.5 convolution_convert_fusion.8.refs_5_
  514.5 3.1 convolution_convert_fusion.5.refs_0_
  517.7 3.1 convolution_convert_fusion.6.refs_7_
  520.7 3.8 convolution_convert_fusion.refs_6_
  524.6 4.1 convolution_convert_fusion.1.refs_4_
  528.6 73.2 %attn_back.1 = (bf16[8192,256]{1,0:T(8,128)(2,1)}, f32[8,1024]{1,0:T(8,128)}, f32[1024,256]{1,0:T(8,128)}, f32[256,256]{1,0:T(8,128)}, f32[256,1024]{1,0:T(8,128)}, /*index=5*/f32[256,768]{1,0:T(8,128)}) custom-call(bf16[1024,1024]{1,0:T(8,128)(2,1)} %convolution_convert_fusion.5.refs_0_, bf16[256,1024]{1,0:T(8,128)(2,1)} %get-tuple-element.102.refs_1_, ...), custom_call_target="tpu_custom_call" | custom-call | flops 70000001024 | bytes 210000000 | tf_op jit(solution)/shard_map/attn_back/pallas_call | solution.py:566
  601.9 1.1 split.45
  603.0 1.1 split.32
  604.1 1.1 split.44
  605.2 1.1 split.34
  606.3 1.0 split.46
  607.3 1.0 split.28
  608.4 2.9 collective-permute-start.7
  611.4 2.8 collective-permute-start.5
  614.8 16.4 %scatter.1 = f32[6288,256]{1,0:T(8,128)} custom-call(s32[1]{0:T(128)} %bitcast.2.count_ref, s32[8192]{0:T(1024)} %get-tuple-element.90.key_ref, bf16[6288,256]{1,0:T(8,128)(2,1)} %reduce-scatter.2.cloned.1.call-done.head_ref, bf16[8192,256]{1,0:T(8,128)(2,1)} %get-tuple-element.123.rows_in_ref), custom_call_target="tpu_custom_call" | custom-call | flops 23000000512 | bytes 69000000 | tf_op jit(solution)/shard_map/scatter/pallas_call | solution.py:1248
  631.2 10.1 %collective-permute-done.5 = bf16[128,256]{1,0:T(8,128)(2,1)S(1)} collective-permute-done((bf16[128,256]{1,0:T(8,128)(2,1)S(1)}, bf16[128,256]{1,0:T(8,128)(2,1)S(1)}, u32[]{:S(2)}, u32[]{:S(2)}) %collective-permute-start.5) | collective-permute-done | bytes 65568 | tf_op jit(solution)/shard_map/ppermute | solution.py:1557
  641.3 4.4 fusion
  649.3 16.2 %update_stats.1 = (f32[50,128]{1,0:T(8,128)}, f32[2,128]{1,0:T(2,128)}, f32[1,128]{1,0:T(1,128)}, f32[2,128]{1,0:T(2,128)}, f32[4,128]{1,0:T(4,128)}, /*index=5*...) custom-call(f32[50,128]{1,0:T(8,128)} %pad_bitcast_fusion.1.refs_0_,, ...), custom_call_target="tpu_custom_call" | custom-call | flops 12000000000 | bytes 36000000 | tf_op jit(solution)/shard_map/update_stats/pallas_call | solution.py:1093
  665.5 1.4 fusion.35
  666.9 5.5 multiply_reduce_fusion
  672.4 1.4 multiply_reduce_fusion.1
  673.8 1.4 multiply_reduce_fusion.2
  675.2 1.3 multiply_reduce_fusion.7
  676.6 1.4 multiply_reduce_fusion.5
  678.0 11.4 %clip_rates.1 = f32[8,128]{1,0:T(8,128)} custom-call(f32[2,128]{1,0:T(2,128)} %bitcast.175, f32[3,128]{1,0:T(4,128)} %bitcast.162, f32[2,128]{1,0:T(2,128)} %bitcast.172, f32[4,128]{1,0:T(4,128)} %bitcast.161, f32[2,128]{1,0:T(2,128)} %bitcast.171, f32[16,128]{1,0:T(8,128)} %get-tuple-element.140.refs_5_), custom_call_target="tpu_custom_call" | custom-call | flops 8000000000 | bytes 24000000 | tf_op jit(solution)/shard_map/clip_rates/pallas_call | solution.py:1141
  689.3 1.4 fusion.36
  690.7 2.3 multiply_subtract_fusion.1
  693.0 2.3 multiply_subtract_fusion.2
  695.3 2.0 multiply_subtract_fusion.4
  697.3 2.2 multiply_subtract_fusion.3
  699.6 9.1 %multiply_subtract_fusion = f32[6288,256]{1,0:T(8,128)} fusion(f32[6288,256]{1,0:T(8,128)} %table_ref.1, f32[]{:T(128)} %bitcast.58, f32[6288,256]{1,0:T(8,128)} %scatter.1, f32[]{:T(128)} %bitcast.40, f32[256]{0:T(256)S(1)} %bitcast.151, f32[6288]{0:T(1024)S(1)} %bitcast.118), kind=kLoop, calls=%fused_computation | loop fusion | flops 8048640 | bytes 19342920 | tf_op jit(solution)/shard_map/sub | solution.py:1600
  (166 shorter events, 23.4 us)
Async XLA Ops:
  7.2 247.4 %all-gather.2.cloned.1.call-start = ((), (), s32[]{:S(2)}) async-start(), calls=%async_computation.1 | async-start | bytes 16097280 | tf_op jit(solution)/shard_map/all_gather | solution.py:1426
  8.6 8.9 %copy-start.9 = (f32[256,512]{1,0:T(8,128)S(1)}, f32[256,512]{1,0:T(8,128)}, u32[]{:S(2)}) copy-start(f32[256,512]{1,0:T(8,128)} %param.28) | copy-start | bytes 1572868
  8.6 12.1 %copy-start.7 = (f32[512,256]{1,0:T(8,128)S(1)}, f32[512,256]{1,0:T(8,128)}, u32[]{:S(2)}) copy-start(f32[512,256]{1,0:T(8,128)} %param.29) | copy-start | bytes 1572868
  8.6 13.1 %copy-start.12 = (f32[256,384]{1,0:T(8,128)S(1)}, f32[256,384]{1,0:T(8,128)}, u32[]{:S(2)}) copy-start(f32[256,384]{1,0:T(8,128)} %param.26) | copy-start | bytes 1179652
  8.6 16.3 %copy-start.16 = (f32[128,256]{1,0:T(8,128)S(1)}, f32[128,256]{1,0:T(8,128)}, u32[]{:S(2)}) copy-start(f32[128,256]{1,0:T(8,128)} %param.27) | copy-start | bytes 393220
  18.1 37.3 %collective-permute-start.2 = (bf16[256,512]{1,0:T(8,128)(2,1)S(1)}, bf16[256,512]{1,0:T(8,128)(2,1)S(1)}, u32[]{:S(2)}, u32[]{:S(2)}) collective-permute-start(bf16[256,512]{1,0:T(8,128)(2,1)S(1)} %get-tuple-element.175), channel_id=1, source_target_pairs={{0,4},{1,5},{2,6},{3,7},{4,0},{5,1},{6,2},{7,3},{8,12},{9,13},{10,... | collective-permute-start | bytes 786440 | tf_op jit(solution)/shard_map/ppermute | solution.py:1381
  21.4 35.0 %collective-permute-start.3 = (bf16[512,256]{1,0:T(8,128)(2,1)S(1)}, bf16[512,256]{1,0:T(8,128)(2,1)S(1)}, u32[]{:S(2)}, u32[]{:S(2)}) collective-permute-start(bf16[512,256]{1,0:T(8,128)(2,1)S(1)} %get-tuple-element.173), channel_id=1, source_target_pairs={{0,4},{1,5},{2,6},{3,7},{4,0},{5,1},{6,2},{7,3},{8,12},{9,13},{10,... | collective-permute-start | bytes 786440 | tf_op jit(solution)/shard_map/ppermute | solution.py:1381
  22.4 32.3 %collective-permute-start = (bf16[256,384]{1,0:T(8,128)(2,1)S(1)}, bf16[256,384]{1,0:T(8,128)(2,1)S(1)}, u32[]{:S(2)}, u32[]{:S(2)}) collective-permute-start(bf16[256,384]{1,0:T(8,128)(2,1)S(1)} %get-tuple-element.177), channel_id=1, source_target_pairs={{0,4},{1,5},{2,6},{3,7},{4,0},{5,1},{6,2},{7,3},{8,12},{9,13},{10,... | collective-permute-start | bytes 589832 | tf_op jit(solution)/shard_map/ppermute | solution.py:1381
  25.5 28.5 %collective-permute-start.1 = (bf16[128,256]{1,0:T(8,128)(2,1)S(1)}, bf16[128,256]{1,0:T(8,128)(2,1)S(1)}, u32[]{:S(2)}, u32[]{:S(2)}) collective-permute-start(bf16[128,256]{1,0:T(8,128)(2,1)S(1)} %get-tuple-element.181), channel_id=1, source_target_pairs={{0,4},{1,5},{2,6},{3,7},{4,0},{5,1},{6,2},{7,3},{8,12},{9,13},{10,... | collective-permute-start | bytes 196616 | tf_op jit(solution)/shard_map/ppermute | solution.py:1381
  57.2 69.1 %copy-start.38 = (s32[2048]{0:T(1024)S(1)}, s32[2048]{0:T(1024)}, u32[]{:S(2)}) copy-start(s32[2048]{0:T(1024)} %param.23) | copy-start | bytes 24580
  57.2 69.6 %copy-start.36 = (s32[2048]{0:T(1024)S(1)}, s32[2048]{0:T(1024)}, u32[]{:S(2)}) copy-start(s32[2048]{0:T(1024)} %param.22) | copy-start | bytes 24580
  126.0 488.8 %reduce-scatter.2.cloned.1.call-start = ((), (), s32[]{:S(2)}) async-start(), calls=%async_computation.2 | async-start | bytes 16097280 | tf_op jit(solution)/shard_map/reduce_scatter | solution.py:1488
  126.7 4.5 copy-start.39
  131.2 12.4 %copy-start.2 = (bf16[1024,768]{1,0:T(8,128)(2,1)}, bf16[1024,768]{1,0:T(8,128)(2,1)S(1)}, u32[]{:S(2)}) copy-start(bf16[1024,768]{1,0:T(8,128)(2,1)S(1)} %convolution_convert_fusion.7.mixed_ref) | copy-start | bytes 4718596
  131.2 10.3 %copy-start.18 = (bf16[256,1024]{1,0:T(8,128)(2,1)S(1)}, bf16[256,1024]{1,0:T(8,128)(2,1)}, u32[]{:S(2)}) copy-start(bf16[256,1024]{1,0:T(8,128)(2,1)} %get-tuple-element.101) | copy-start | bytes 1572868
  140.8 0.8 copy-start
  143.6 34.6 %copy-start.47 = (bf16[1024,1024]{1,0:T(8,128)(2,1)S(1)}, bf16[1024,1024]{1,0:T(8,128)(2,1)}, u32[]{:S(2)}) copy-start(bf16[1024,1024]{1,0:T(8,128)(2,1)} %get-tuple-element.104) | copy-start | bytes 6291460
  178.2 4.1 copy-start.51
  182.2 4.0 copy-start.42
  305.2 10.4 %copy-start.26 = (s32[2048]{0:T(1024)S(1)}, s32[2048]{0:T(1024)}, u32[]{:S(2)}) copy-start(s32[2048]{0:T(1024)} %param.24) | copy-start | bytes 24580
  305.2 11.1 %copy-start.15 = (f32[10,1,2048]{2,1,0:T(1,128)S(1)}, f32[10,1,2048]{2,1,0:T(1,128)}, u32[]{:S(2)}) copy-start(f32[10,1,2048]{2,1,0:T(1,128)} %get-tuple-element.109) | copy-start | bytes 245764
  316.3 0.7 copy-start.22
  386.7 0.7 copy-start.27
  388.1 58.6 %copy-start.43 = (f32[1024,1024]{1,0:T(8,128)S(1)}, f32[1024,1024]{1,0:T(8,128)}, u32[]{:S(2)}) copy-start(f32[1024,1024]{1,0:T(8,128)} %copy-done.42) | copy-start | bytes 12582916
  446.7 6.9 copy-start.48
  457.4 35.2 %copy-start.19 = (bf16[256,1024]{1,0:T(8,128)(2,1)S(1)}, bf16[256,1024]{1,0:T(8,128)(2,1)}, u32[]{:S(2)}) copy-start(bf16[256,1024]{1,0:T(8,128)(2,1)} %get-tuple-element.101) | copy-start | bytes 1572868
  492.6 2.9 copy-start.3
  495.5 17.4 %copy-start.1 = (bf16[1024,256]{1,0:T(8,128)(2,1)S(1)}, bf16[1024,256]{1,0:T(8,128)(2,1)}, u32[]{:S(2)}) copy-start(bf16[1024,256]{1,0:T(8,128)(2,1)} %copy-done) | copy-start | bytes 1572868
  495.5 17.4 %copy-start.11 = (bf16[1024,1024]{1,0:T(8,128)(2,1)S(1)}, bf16[1024,1024]{1,0:T(8,128)(2,1)}, u32[]{:S(2)}) copy-start(bf16[1024,1024]{1,0:T(8,128)(2,1)} %get-tuple-element.116) | copy-start | bytes 6291460
  495.6 19.0 %copy-start.46 = (bf16[1024,768]{1,0:T(8,128)(2,1)S(1)}, bf16[1024,768]{1,0:T(8,128)(2,1)}, u32[]{:S(2)}) copy-start(bf16[1024,768]{1,0:T(8,128)(2,1)} %get-tuple-element.99) | copy-start | bytes 4718596
  514.5 3.1 copy-start.45
  517.7 3.1 copy-start.49
  520.7 3.8 copy-start.44
  520.7 3.8 copy-start.50
  601.9 6.4 copy-start.21
  601.9 12.4 %copy-start.40 = (f32[4]{0:T(128)S(1)}, f32[4]{0:T(128)}, u32[]{:S(2)}) copy-start(f32[4]{0:T(128)} %get-tuple-element.164) | copy-start | bytes 52
  608.4 32.9 %collective-permute-start.6 = (bf16[256,512]{1,0:T(8,128)(2,1)S(1)}, bf16[256,512]{1,0:T(8,128)(2,1)S(1)}, u32[]{:S(2)}, u32[]{:S(2)}) collective-permute-start(bf16[256,512]{1,0:T(8,128)(2,1)S(1)} %split.45), channel_id=1, source_target_pairs={{0,4},{1,5},{2,6},{3,7},{4,0},{5,1},{6,2},{7,3},{8,12},{9,13},{10,... | collective-permute-start | bytes 786440 | tf_op jit(solution)/shard_map/ppermute | solution.py:1557
  608.4 32.8 %collective-permute-start.7 = (bf16[512,256]{1,0:T(8,128)(2,1)S(1)}, bf16[512,256]{1,0:T(8,128)(2,1)S(1)}, u32[]{:S(2)}, u32[]{:S(2)}) collective-permute-start(bf16[512,256]{1,0:T(8,128)(2,1)S(1)} %split.44), channel_id=1, source_target_pairs={{0,4},{1,5},{2,6},{3,7},{4,0},{5,1},{6,2},{7,3},{8,12},{9,13},{10,... | collective-permute-start | bytes 786440 | tf_op jit(solution)/shard_map/ppermute | solution.py:1557
  611.4 29.9 %collective-permute-start.4 = (bf16[256,384]{1,0:T(8,128)(2,1)S(1)}, bf16[256,384]{1,0:T(8,128)(2,1)S(1)}, u32[]{:S(2)}, u32[]{:S(2)}) collective-permute-start(bf16[256,384]{1,0:T(8,128)(2,1)S(1)} %split.46), channel_id=1, source_target_pairs={{0,4},{1,5},{2,6},{3,7},{4,0},{5,1},{6,2},{7,3},{8,12},{9,13},{10,... | collective-permute-start | bytes 589832 | tf_op jit(solution)/shard_map/ppermute | solution.py:1557
  611.4 29.8 %collective-permute-start.5 = (bf16[128,256]{1,0:T(8,128)(2,1)S(1)}, bf16[128,256]{1,0:T(8,128)(2,1)S(1)}, u32[]{:S(2)}, u32[]{:S(2)}) collective-permute-start(bf16[128,256]{1,0:T(8,128)(2,1)S(1)} %split.47), channel_id=1, source_target_pairs={{0,4},{1,5},{2,6},{3,7},{4,0},{5,1},{6,2},{7,3},{8,12},{9,13},{10,... | collective-permute-start | bytes 196616 | tf_op jit(solution)/shard_map/ppermute | solution.py:1557
  647.1 43.6 %copy-start.4 = (f32[512,256]{1,0:T(8,128)}, f32[512,256]{1,0:T(8,128)S(1)}, u32[]{:S(2)}) copy-start(f32[512,256]{1,0:T(8,128)S(1)} %get-tuple-element.241) | copy-start | bytes 1572868
  647.9 45.2 %copy-start.5 = (f32[256,512]{1,0:T(8,128)}, f32[256,512]{1,0:T(8,128)S(1)}, u32[]{:S(2)}) copy-start(f32[256,512]{1,0:T(8,128)S(1)} %get-tuple-element.237) | copy-start | bytes 1572868
  648.5 46.7 %copy-start.14 = (f32[128,256]{1,0:T(8,128)}, f32[128,256]{1,0:T(8,128)S(1)}, u32[]{:S(2)}) copy-start(f32[128,256]{1,0:T(8,128)S(1)} %get-tuple-element.233) | copy-start | bytes 393220
  649.3 48.1 %copy-start.6 = (f32[256,384]{1,0:T(8,128)}, f32[256,384]{1,0:T(8,128)S(1)}, u32[]{:S(2)}) copy-start(f32[256,384]{1,0:T(8,128)S(1)} %get-tuple-element.229) | copy-start | bytes 1179652
  665.5 7.0 copy-start.28
  665.5 6.9 copy-start.31
  665.5 8.3 %copy-start.29 = (f32[4,128]{1,0:T(4,128)S(1)}, f32[4,128]{1,0:T(4,128)}, u32[]{:S(2)}) copy-start(f32[4,128]{1,0:T(4,128)} %get-tuple-element.146) | copy-start | bytes 6148
  665.5 8.3 %copy-start.32 = (f32[2,128]{1,0:T(2,128)S(1)}, f32[2,128]{1,0:T(2,128)}, u32[]{:S(2)}) copy-start(f32[2,128]{1,0:T(2,128)} %get-tuple-element.145) | copy-start | bytes 3076
  665.5 9.7 %copy-start.33 = (f32[2,128]{1,0:T(2,128)S(1)}, f32[2,128]{1,0:T(2,128)}, u32[]{:S(2)}) copy-start(f32[2,128]{1,0:T(2,128)} %get-tuple-element.144) | copy-start | bytes 3076
  665.5 9.7 %copy-start.37 = (f32[1,128]{1,0:T(1,128)S(1)}, f32[1,128]{1,0:T(1,128)}, u32[]{:S(2)}) copy-start(f32[1,128]{1,0:T(1,128)} %get-tuple-element.143) | copy-start | bytes 1540
  665.5 11.0 %copy-start.30 = (f32[3,128]{1,0:T(4,128)S(1)}, f32[3,128]{1,0:T(4,128)}, u32[]{:S(2)}) copy-start(f32[3,128]{1,0:T(4,128)} %get-tuple-element.142) | copy-start | bytes 4612
  665.5 11.0 %copy-start.34 = (f32[2,128]{1,0:T(2,128)S(1)}, f32[2,128]{1,0:T(2,128)}, u32[]{:S(2)}) copy-start(f32[2,128]{1,0:T(2,128)} %get-tuple-element.141) | copy-start | bytes 3076
  677.9 12.8 %copy-start.8 = (f32[512,256]{1,0:T(8,128)S(1)}, f32[512,256]{1,0:T(8,128)}, u32[]{:S(2)}) copy-start(f32[512,256]{1,0:T(8,128)} %param.29) | copy-start | bytes 1572868
  678.0 15.1 %copy-start.10 = (f32[256,512]{1,0:T(8,128)S(1)}, f32[256,512]{1,0:T(8,128)}, u32[]{:S(2)}) copy-start(f32[256,512]{1,0:T(8,128)} %param.28) | copy-start | bytes 1572868
  678.0 17.3 %copy-start.17 = (f32[128,256]{1,0:T(8,128)S(1)}, f32[128,256]{1,0:T(8,128)}, u32[]{:S(2)}) copy-start(f32[128,256]{1,0:T(8,128)} %param.27) | copy-start | bytes 393220
  678.0 19.4 %copy-start.13 = (f32[256,384]{1,0:T(8,128)S(1)}, f32[256,384]{1,0:T(8,128)}, u32[]{:S(2)}) copy-start(f32[256,384]{1,0:T(8,128)} %param.26) | copy-start | bytes 1179652
  689.3 10.2 %copy-start.20 = (f32[50,128]{1,0:T(8,128)S(1)}, f32[50,128]{1,0:T(8,128)}, u32[]{:S(2)}) copy-start(f32[50,128]{1,0:T(8,128)} %get-tuple-element.138) | copy-start | bytes 76804
  689.3 10.2 %copy-start.35 = (f32[2,128]{1,0:T(2,128)S(1)}, f32[2,128]{1,0:T(2,128)}, u32[]{:S(2)}) copy-start(f32[2,128]{1,0:T(2,128)} %get-tuple-element.139) | copy-start | bytes 3076
  699.5 9.1 %copy-start.41 = (f32[1,128]{1,0:T(1,128)S(1)}, f32[1,128]{1,0:T(1,128)}, u32[]{:S(2)}) copy-start(f32[1,128]{1,0:T(1,128)} %get-tuple-element.137) | copy-start | bytes 1540
  699.5 15.3 %copy-start.25 = (f32[6,1024]{1,0:T(8,128)S(1)}, f32[6,1024]{1,0:T(8,128)}, u32[]{:S(2)}) copy-start(f32[6,1024]{1,0:T(8,128)} %get-tuple-element.245) | copy-start | bytes 73732
  699.5 15.9 %copy-start.24 = (f32[6,1024]{1,0:T(8,128)S(1)}, f32[6,1024]{1,0:T(8,128)}, u32[]{:S(2)}) copy-start(f32[6,1024]{1,0:T(8,128)} %get-tuple-element.246) | copy-start | bytes 73732
  699.5 16.5 %copy-start.23 = (f32[6,1024]{1,0:T(8,128)S(1)}, f32[6,1024]{1,0:T(8,128)}, u32[]{:S(2)}) copy-start(f32[6,1024]{1,0:T(8,128)} %get-tuple-element.247) | copy-start | bytes 73732
Sparse Core Ops, SparseCore 0:
  126.1 128.4 all-gather.1
  386.9 124.0 reduce-scatter.1

commit v6 on v5

--- a/solution.py
+++ b/solution.py
@@ -21,6 +21,7 @@
 RHO = 0.5
 MASKED = -1e30
 QUERIES = 256
+HEAD_BLOCK = 640
 MESH = pl.DeviceIdType.MESH
 VMEM_CAP = 56 * 2**20
 
@@ -35,10 +36,16 @@
     return lax.dynamic_slice_in_dim(values, start, count, 0)
 
 
-def line_kernel(nr, ng, chunks, shapes, n_in, n_out, step, sides, turn, side_ticks, *refs):
+def line_kernel(
+    nr, ng, chunks, shapes, n_in, n_out, step, sides, turn, side_ticks, product, chunk_major, *refs
+):
     (rows_r, width_r), (rows_g, width_g) = shapes
-    part = refs[0] if nr else None
-    first = 1 if nr else 0
+    if product:
+        dl, table = refs[:2]
+        first = 2
+    else:
+        part = refs[0] if nr else None
+        first = 1 if nr else 0
     ins = refs[first : first + n_in]
     refs = refs[first + n_in :]
     side_ins, refs = refs[: len(sides)], refs[len(sides) :]
@@ -50,6 +57,8 @@
     side_scratch, scratch = scratch[: 3 * len(sides)], scratch[3 * len(sides) :]
     if turn:
         cast, turn_send, turn_recv = scratch[-3:]
+    if product:
+        part, dl_buf, total_ref, dl_sem = scratch[-4:]
     size_dp = lax.axis_size("dp")
     dp = lax.axis_index("dp")
     mp = lax.axis_index("mp")
@@ -60,6 +69,7 @@
     piece_g = rows_g // chunks
     small = min(piece_r, piece_g)
     late = 1 if turn else 0
+    ahead = 1 if product else 0
     most = max(nr, ng)
     zb = lax.rem(z, most)
     if nr:
@@ -194,6 +204,9 @@
         return pl.ds(pl.multiple_of(block * rows_r + k * piece_r, piece_r), piece_r)
 
     def whole_rows(block, k):
+        if chunk_major:
+            start = k * (2 * ng * piece_g) + block * piece_g
+            return pl.ds(pl.multiple_of(start, piece_g), piece_g)
         return pl.ds(pl.multiple_of(block * rows_g + k * piece_g, piece_g), piece_g)
 
     def remote(src, dst, send, recv, target):
@@ -222,7 +235,8 @@
                 half_copy(dest, k).start()
             return carry
 
-        lax.fori_loop(0, chunks, send_halves, 0)
+        if not product:
+            lax.fori_loop(0, chunks, send_halves, 0)
 
         def right_copy(dest, k):
             return remote(
@@ -374,13 +388,59 @@
         if not nr:
             return 0
         at = lax.rem(chip, nr)
-        return jnp.maximum(at, last_r - at)
+        return jnp.maximum(at, last_r - at) + ahead
+
+    def dl_copy(k):
+        columns = dl_buf.shape[2]
+        return pltpu.make_async_copy(
+            dl.at[:, pl.ds(pl.multiple_of(k * columns, columns), columns)],
+            dl_buf.at[lax.rem(k, 2)],
+            dl_sem.at[lax.rem(k, 2)],
+        )
+
+    def make_part(k):
+        dl_copy(k).wait()
+
+        @pl.when(k + 1 < chunks)
+        def _():
+            dl_copy(k + 1).start()
+
+        slot = lax.rem(k, 2)
+
+        def add(i, carry):
+            at = pl.ds(pl.multiple_of(i * HEAD_BLOCK, HEAD_BLOCK), HEAD_BLOCK)
+            found = lax.dot_general(
+                dl_buf[slot, at, :],
+                table[at, :],
+                (((0,), (0,)), ((), ())),
+                preferred_element_type=jnp.float32,
+            )
+
+            @pl.when(i == 0)
+            def _():
+                total_ref[...] = found
+
+            @pl.when(i > 0)
+            def _():
+                total_ref[...] += found
+
+            return carry
+
+        lax.fori_loop(0, table.shape[0] // HEAD_BLOCK, add, 0)
+        for block in range(2 * nr):
+            part[part_rows(block, k), :] = total_ref[
+                block * piece_r : block * piece_r + piece_r, :
+            ].astype(jnp.bfloat16)
+        send_halves(k, 0)
+
+    if product:
+        dl_copy(0).start()
 
     def tick(now, carry):
         side_jobs(now)
         if nr:
-            k_right = now - zr
-            k_left = now - (last_r - zr)
+            k_right = now - zr - ahead
+            k_left = now - (last_r - zr) - ahead
             for far in range(last_r):
 
                 @pl.when(inside(k_right) & (last_r - far > zr))
@@ -425,9 +485,15 @@
                     def _():
                         ag_left_copy(block, k).start()
 
+        if product:
+
+            @pl.when(now < chunks)
+            def _():
+                make_part(now)
+
         return carry
 
-    ticks = chunks + (nr - 1 if nr else 0) + (ng - 1 if ng else 0) + late
+    ticks = ahead + chunks + (nr - 1 if nr else 0) + (ng - 1 if ng else 0) + late
     lax.fori_loop(0, ticks, tick, 0)
 
     def finish(k, carry):
@@ -501,6 +567,8 @@
     sides=(),
     turn=None,
     side_ticks=0,
+    product=False,
+    chunk_major=False,
 ):
     piece = rows // chunks
     size_dp = lax.axis_size("dp")
@@ -537,7 +605,19 @@
     if turn:
         scratch.append(pltpu.VMEM((chunks, piece, width), jnp.bfloat16))
         scratch += [dma((size_dp, chunks))] * 2
-    args = ([partial] if nr else []) + list(ins) + [side[2] for side in sides]
+    if product:
+        dl, table = partial
+        columns = dl.shape[1] // chunks
+        scratch += [
+            pltpu.VMEM((2 * nr * rows, width), jnp.bfloat16),
+            pltpu.VMEM((2, dl.shape[0], columns), jnp.bfloat16),
+            pltpu.VMEM((columns, width), jnp.float32),
+            dma((2,)),
+        ]
+        partial = [dl, table]
+    else:
+        partial = [partial] if nr else []
+    args = partial + list(ins) + [side[2] for side in sides]
     vmem = pl.BlockSpec(memory_space=pltpu.VMEM)
     call = pl.pallas_call(
         functools.partial(
@@ -552,9 +632,11 @@
             tuple(side[:2] for side in sides),
             turn,
             side_ticks,
+            product,
+            chunk_major,
         ),
         out_shape=out_shape,
-        in_specs=[vmem] * len(args),
+        in_specs=[pl.BlockSpec(memory_space=pl.ANY) if product and n == 0 else vmem for n in range(len(args))],
         out_specs=[vmem] * len(out_shape),
         scratch_shapes=scratch,
         compiler_params=pltpu.CompilerParams(
@@ -598,7 +680,7 @@
 def head_stats(table, final, wanted, edge, block, tile=512):
     rows, width = table.shape
     tokens = final.shape[0]
-    steps = pl.cdiv(rows, block)
+    steps = rows // block
     row = jax.ShapeDtypeStruct((steps, 1, tokens), jnp.float32)
     row_spec = pl.BlockSpec((1, 1, tokens), lambda j: (j, 0, 0))
     return pl.pallas_call(
@@ -622,84 +704,52 @@
     )(table, final, wanted, edge)
 
 
-def head_back_kernel(rows, block, tile, exp_ref, table_ref, final_ref, scale_ref, weight_ref, wanted_ref, grad_ref, dfinal_ref, dl_ref, sum_ref):
+def head_back_kernel(block, tile, exp_ref, final_ref, scale_ref, weight_ref, wanted_ref, dl_ref, grad_ref):
     j = pl.program_id(0)
     tokens = final_ref.shape[0]
     place = j * block + lax.broadcasted_iota(jnp.int32, (block, 1), 0)
-
-    @pl.when(j == 0)
-    def _():
-        sum_ref[...] = jnp.zeros_like(sum_ref)
-
-    table = jnp.where(place < rows, table_ref[...], jnp.zeros_like(table_ref))
-
-    def one(i, carry):
-        at = pl.ds(i * tile, tile)
-        weight = weight_ref[:, at]
+    for start in range(0, tokens, tile):
+        at = pl.ds(start, tile)
         dl = exp_ref[:, at].astype(jnp.float32) * scale_ref[0, :, at]
-        dl = dl - jnp.where(place == wanted_ref[:, at], weight, 0.0)
-        dl = dl.astype(jnp.bfloat16)
-        dl_ref[:, at] = dl
-        sum_ref[at, :] += lax.dot_general(
-            dl, table, (((0,), (0,)), ((), ())), preferred_element_type=jnp.float32
-        )
-        return carry
-
-    for i in range(tokens // tile):
-        one(i, 0)
-
+        dl = dl - jnp.where(place == wanted_ref[:, at], weight_ref[:, at], 0.0)
+        dl_ref[:, at] = dl.astype(jnp.bfloat16)
     strip = block // max(1, block // 256)
-
-    def two(i, carry):
-        at = pl.ds(i * strip, strip)
+    for start in range(0, block, strip):
+        at = pl.ds(start, strip)
         grad_ref[at, :] = jnp.dot(
             dl_ref[at, :], final_ref[...], preferred_element_type=jnp.float32
         ).astype(jnp.bfloat16)
-        return carry
-
-    for i in range(block // strip):
-        two(i, 0)
-
-    @pl.when(j == pl.num_programs(0) - 1)
-    def _():
-        dfinal_ref[...] = sum_ref[...].astype(jnp.bfloat16)
-
-
-def head_back(exps, table, final, scale, weight, wanted, block, tile=256):
-    rows, width = table.shape
-    tokens = final.shape[0]
-    steps = pl.cdiv(rows, block)
+
+
+def head_back(exps, final, scale, weight, wanted, block, tile=256):
+    rows, tokens = exps.shape
+    width = final.shape[1]
     return pl.pallas_call(
-        functools.partial(head_back_kernel, rows, block, tile),
-        grid=(steps,),
+        functools.partial(head_back_kernel, block, tile),
+        grid=(rows // block,),
         out_shape=[
+            jax.ShapeDtypeStruct((rows, tokens), jnp.bfloat16),
             jax.ShapeDtypeStruct((rows, width), jnp.bfloat16),
-            jax.ShapeDtypeStruct((tokens, width), jnp.bfloat16),
         ],
         in_specs=[
             pl.BlockSpec((block, tokens), lambda j: (j, 0)),
-            pl.BlockSpec((block, width), lambda j: (j, 0)),
             pl.BlockSpec((tokens, width), lambda j: (0, 0)),
             pl.BlockSpec((1, 1, tokens), lambda j: (j, 0, 0)),
             pl.BlockSpec((1, tokens), lambda j: (0, 0)),
             pl.BlockSpec((1, tokens), lambda j: (0, 0)),
         ],
         out_specs=[
+            pl.BlockSpec((block, tokens), lambda j: (j, 0)),
             pl.BlockSpec((block, width), lambda j: (j, 0)),
-            pl.BlockSpec((tokens, width), lambda j: (0, 0)),
         ],
-        scratch_shapes=[
-            pltpu.VMEM((block, tokens), jnp.bfloat16),
-            pltpu.VMEM((tokens, width), jnp.float32),
-        ],
-        compiler_params=pltpu.CompilerParams(vmem_limit_bytes=60 * 2**20),
+        compiler_params=pltpu.CompilerParams(vmem_limit_bytes=56 * 2**20),
         cost_estimate=pl.CostEstimate(
-            flops=4 * rows * width * tokens,
-            bytes_accessed=2 * rows * (2 * width + tokens),
+            flops=2 * rows * width * tokens,
+            bytes_accessed=2 * rows * (width + 2 * tokens),
             transcendentals=0,
         ),
         name="head_back",
-    )(exps, table, final, scale, weight, wanted)
+    )(exps, final, scale, weight, wanted)
 
 
 def head_weights(mixed_ref, starts_ref, base, at, seen):
@@ -1179,18 +1229,29 @@
         return carry
 
     lax.fori_loop(0, spots // 256, narrow, 0)
-    strip = 48 if vocab % 48 == 0 else 8
+    strip = 48
+    rest = vocab % strip
+    done = vocab - rest
+    low_ref[done:, :] = jnp.zeros((low_ref.shape[0] - done, width), jnp.bfloat16)
+
+    def squares(values, total):
+        for row in range(0, values.shape[0], 8):
+            piece = values[row : row + 8, :]
+            total = total + piece * piece
+        return total
 
     def lower(i, total):
         at = pl.ds(pl.multiple_of(i * strip, strip), strip)
         values = table_ref[at, :]
         low_ref[at, :] = values.astype(jnp.bfloat16)
-        for row in range(0, strip, 8):
-            piece = values[row : row + 8, :]
-            total = total + piece * piece
-        return total
-
-    total = lax.fori_loop(0, vocab // strip, lower, jnp.zeros((8, width), jnp.float32))
+        return squares(values, total)
+
+    total = lax.fori_loop(0, done // strip, lower, jnp.zeros((8, width), jnp.float32))
+    if rest:
+        values = table_ref[done:, :]
+        total = squares(values, total)
+        values = jnp.concatenate([values, jnp.zeros((strip - rest, width), jnp.float32)])
+        low_ref[done : done + strip, :] = values.astype(jnp.bfloat16)
     folded = total[:, 0:128]
     for start in range(128, width, 128):
         folded = folded + total[:, start : start + 128]
@@ -1205,7 +1266,7 @@
         functools.partial(lookup_kernel, shift),
         out_shape=[
             jax.ShapeDtypeStruct((spots, width), jnp.bfloat16),
-            jax.ShapeDtypeStruct((vocab, width), jnp.bfloat16),
+            jax.ShapeDtypeStruct((vocab + -vocab % HEAD_BLOCK, width), jnp.bfloat16),
             jax.ShapeDtypeStruct((8, 128), jnp.float32),
         ],
         in_specs=[smem, smem, vmem],
@@ -1228,7 +1289,7 @@
 
     lax.fori_loop(0, spots // 256, widen, 0)
     rows_ref[spots:, :] = jnp.zeros((8, width), jnp.float32)
-    grad_ref[...] = head_ref[...].astype(jnp.float32)
+    grad_ref[...] = head_ref[...].astype(jnp.float32)[: grad_ref.shape[0]]
 
     def some(i, carry):
         for j in range(UNROLL):
@@ -1240,9 +1301,8 @@
     lax.fori_loop(0, (count_ref[0] + UNROLL - 1) // UNROLL, some, 0)
 
 
-def scatter(keys, count, head_grad, rows, shift):
+def scatter(keys, count, head_grad, rows, vocab, shift):
     spots, width = rows.shape
-    vocab = head_grad.shape[0]
     smem = pl.BlockSpec(memory_space=pltpu.SMEM)
     vmem = pl.BlockSpec(memory_space=pltpu.VMEM)
     return pl.pallas_call(
@@ -1460,12 +1520,18 @@
         near,
         chips,
         58,
+        chunk_major=True,
     )
 
     edge = jnp.clip(VREAL - first_row, 0, vocab).astype(jnp.int32).reshape(1)
-    wanted = targets - first_row
+
+    def by_chunk(values):
+        return values.reshape(size_mp, chunks_full, -1).swapaxes(0, 1).reshape(tokens)
+
+    sources = by_chunk(sources)
+    wanted = by_chunk(targets) - first_row
     wanted = jnp.where((wanted >= 0) & (wanted < vocab), wanted, -1).reshape(1, tokens)
-    block = 640
+    block = HEAD_BLOCK
     exps, tops, sums, picks = head_stats(wide_table, final, wanted, edge, block)
     tops = tops[:, 0]
     top = jnp.max(tops, axis=0)
@@ -1482,15 +1548,15 @@
     loss_part = jnp.sum(member * token_loss[:, None], axis=0)
     weight = jnp.sum(member / (NSRC * jnp.maximum(counts, 1.0))[None, :], axis=1)
     scale = jnp.exp(tops - log_total[None, :]) * weight[None, :]
-    table_grad, dfinal = head_back(
-        exps, wide_table, final, scale[:, None, :], weight[None, :], wanted, block
+    dlogits, table_grad = head_back(
+        exps, final, scale[:, None, :], weight[None, :], wanted, block
     )
     head_grad = lax.psum_scatter(table_grad, "dp", scatter_dimension=1, tiled=True)
 
     dbranch2, dstream2, norm3 = line_call(
         "final_back",
         6,
-        dfinal,
+        (dlogits, wide_table),
         [stream2, norm_params],
         [row_f32, pair_f32],
         functools.partial(step_backward, 4),
@@ -1499,7 +1565,8 @@
         chunks_full,
         chips,
         near,
-        60,
+        65,
+        product=True,
     )
     grad_proj = jnp.einsum("tf,td->fd", hidden, dbranch2, preferred_element_type=f32).astype(bf16)
     dhidden = jnp.einsum("td,fd->tf", dbranch2, wide_proj, preferred_element_type=f32)
@@ -1563,7 +1630,7 @@
         to_twins(grad_fc, 1),
         to_twins(grad_proj, 0),
     ]
-    grad_table = scatter(keys, owned, head_grad, drows, shift)
+    grad_table = scatter(keys, owned, head_grad, drows, vocab, shift)
     shares, grad_table = lax.optimization_barrier((shares, grad_table))
     grad_qkv, grad_out, grad_fc, grad_proj = [
         sum((piece.astype(f32) for piece in found), mine) for mine, found in shares

time: 731 us -> 732 us (level)
    pallas_call x6, Pallas kernels: 330 us -> 366 us  [line_call(): return list(call(*args))]
    pallas_call x1, Pallas kernels: 69.7 us -> 33.8 us  [head_back(): pl.pallas_call(functools.partial(head_back_kernel, block, tile), grid=(ro...]
  transfers between devices with their start and end apart: 10 -> 10, of which waited for: 3 -> 3; matrix products, arithmetic and copies ran while one was open for 9% -> 9% of each run, Pallas kernels for 44% -> 49%
where the time goes in v6:
time: 732 us; the launch traced here: 725 us
  Pallas kernels  550 us (75%)
  other arithmetic  56 us (8%)
  matrix products  42 us (6%)
  waiting for transfers between devices  26.1 us (4%)
  local copies, waits for them, and re-layouts  23.8 us (3%)
  between operations  15 us (2%)
  starting transfers between devices  12 us (2%)
    pallas_call x6, Pallas kernels, line_call(): return list(call(*args))  366 us
    pallas_call x1, Pallas kernels, head_stats(): pl.pallas_call(functools.partial(head_stats_kernel, block, tile), grid=(s...  46.9 us
    pallas_call x1, Pallas kernels, head_back(): pl.pallas_call(functools.partial(head_back_kernel, block, tile), grid=(ro...  33.8 us
    sub x5, other arithmetic, local(): updated = [weights[n] - factors[n, 0] * steps[n] for n in range(5)]  17.8 us
    pallas_call x1, Pallas kernels, update_stats(): pl.pallas_call(functools.partial(stats_kernel, full, size_dp, size_mp), o...  17.4 us
    pallas_call x1, Pallas kernels, attend_back(): pl.pallas_call(attend_back_kernel, grid=(pairs,), out_shape=jax.ShapeDtyp...  17.4 us
    pallas_call x2, Pallas kernels, small_gather(): pl.pallas_call(functools.partial(small_gather_kernel, axis, count), out_s...  17 us
    pallas_call x1, Pallas kernels, scatter(): pl.pallas_call(functools.partial(scatter_kernel, shift), out_shape=jax.Sh...  16.4 us
  transfers between devices with their start and end apart: 10, of which 3 were waited for; matrix products, arithmetic and copies ran while one was open for 9% of the time, Pallas kernels for 49%

profile of v6, /device:TPU:0, one launch (start us, length us, event | category | flops | bytes accessed | tf_op | source)
XLA Modules:
  0.0 725.3 jit_solution(857626706898724519)
XLA Ops:
  8.6 7.9 %gather_ids.1 = s32[4,32,128]{2,1,0:T(8,128)} custom-call(s32[32,128]{1,0:T(8,128)} %reshape.285.src_ref), custom_call_target="tpu_custom_call" | custom-call | flops 6000000000 | bytes 18000000 | tf_op jit(solution)/shard_map/gather_ids/pallas_call | solution.py:892
  16.5 0.9 reshape.286
  18.1 2.6 collective-permute-start.2
  22.4 2.6 collective-permute-start
  26.5 6.8 sort.14
  33.3 15.3 %lookup.1 = (bf16[8192,256]{1,0:T(8,128)(2,1)}, bf16[6400,256]{1,0:T(8,128)(2,1)}, f32[8,128]{1,0:T(8,128)}) custom-call(s32[1]{0:T(128)} %bitcast.2.count_ref, s32[8192]{0:T(1024)} %get-tuple-element.90.key_ref, f32[6288,256]{1,0:T(8,128)} %table_ref.1), custom_call_target="tpu_custom_call" | custom-call | flops 20000000000 | bytes 60000000 | tf_op jit(solution)/shard_map/lookup/pallas_call | solution.py:1265
  48.7 5.3 collective-permute-done.1
  54.7 0.8 pad_maximum_fusion.2.refs_2_
  55.5 0.9 pad_maximum_fusion.refs_4_
  56.3 0.8 pad_maximum_fusion.1.refs_5_
  57.2 68.8 %lookup_sum.1 = (bf16[1024,1024]{1,0:T(8,128)(2,1)}, bf16[256,1024]{1,0:T(8,128)(2,1)}, bf16[1024,768]{1,0:T(8,128)(2,1)}, bf16[256,1024]{1,0:T(8,128)(2,1)}, bf...) custom-call(bf16[8192,256]{1,0:T(8,128)(2,1)} %get-tuple-element.92.refs_0_, f32[6,1024]{1,0:T(8,128)} %refs_29_.1, ...), custom_call_target="tpu_custom_call" | custom-call | flops 70000001024 | bytes 210000000 | tf_op jit(solution)/shard_map/lookup_sum/pallas_call | solution.py:648
  127.7 3.2 convolution_convert_fusion.7.mixed_ref
  130.9 9.5 %attend.1 = bf16[1024,256]{1,0:T(8,128)(2,1)S(1)} custom-call(bf16[1024,768]{1,0:T(8,128)(2,1)S(1)} %convolution_convert_fusion.7.mixed_ref, s32[1024,1]{1,0:T(8,128)S(1)} %copy.60.starts_ref), custom_call_target="tpu_custom_call" | custom-call | flops 1073741824 | bytes 1572864 | tf_op jit(solution)/shard_map/attend/pallas_call | solution.py:788
  140.5 0.8 copy-done
  141.3 2.0 convolution_convert_fusion.4.refs_0_
  143.3 34.5 %attn_sum.1 = (bf16[1024,1024]{1,0:T(8,128)(2,1)}, f32[256,1024]{1,0:T(8,128)}) custom-call(bf16[1024,1024]{1,0:T(8,128)(2,1)} %convolution_convert_fusion.4.refs_0_, bf16[256,1024]{1,0:T(8,128)(2,1)} %get-tuple-element.102.refs_1_, f32[6,1024]{1,0:T(8,128)} %refs_29_.1), custom_call_target="tpu_custom_call" | custom-call | flops 32000000000 | bytes 96000000 | tf_op jit(solution)/shard_map/attn_sum/pallas_call | solution.py:648
  177.8 4.1 fusion.37
  181.9 4.0 convolution_convert_fusion.3.refs_0_
  186.0 59.6 %mlp_sum.1 = (bf16[2048,1024]{1,0:T(8,128)(2,1)}, f32[256,1024]{1,0:T(8,128)}) custom-call(bf16[1024,1024]{1,0:T(8,128)(2,1)} %convolution_convert_fusion.3.refs_0_, f32[256,1024]{1,0:T(8,128)} %get-tuple-element.106.refs_1_, f32[6,1024]{1,0:T(8,128)} %refs_29_.1), custom_call_target="tpu_custom_call" | custom-call | flops 57999998976 | bytes 174000000 | tf_op jit(solution)/shard_map/mlp_sum/pallas_call | solution.py:648
  245.5 11.0 %all-gather.2.cloned.1.call-done.table_ref.refs_1_ = bf16[6400,1024]{1,0:T(8,128)(2,1)} async-done(((bf16[6400,256]{1,0:T(8,128)(2,1)}), bf16[6400,1024]{1,0:T(8,128)(2,1)}) %all-gather.2.cloned.1.call-update) | async-done | bytes 13107216 | tf_op jit(solution)/shard_map/all_gather | solution.py:1486
  256.5 46.9 %head_stats.1 = (bf16[6400,2048]{1,0:T(8,128)(2,1)}, f32[10,1,2048]{2,1,0:T(1,128)}, f32[10,1,2048]{2,1,0:T(1,128)}, f32[10,1,2048]{2,1,0:T(1,128)}) custom-call(bf16[6400,1024]{1,0:T(8,128)(2,1)} %all-gather.2.cloned.1.call-done.table_ref.refs_1_, bf16[2048,1024]{1,0:T(8,128)(2,1)} %get-tuple-element.107.final_ref, s32[1,2048]{1,0:T(1,128)} %and_select_fusion.wanted_ref, ...), custom_call_target="tpu_custom_call" | custom-call | flops 26843545600 | bytes 39321600 | tf_op jit(solution)/shard_map/head_stats/pallas_call | solution.py:686
  303.5 1.0 reduce_max.18
  304.4 1.0 fusion.17
  305.4 1.0 reduce_sum.245
  307.0 9.1 %gather_stats.1 = f32[8,48,128]{2,1,0:T(8,128)} custom-call(f32[48,128]{1,0:T(8,128)} %pad_maximum_fusion.4.src_ref), custom_call_target="tpu_custom_call" | custom-call | flops 6000000000 | bytes 18000000 | tf_op jit(solution)/shard_map/gather_stats/pallas_call | solution.py:892
  316.1 1.0 reshape.293
  318.8 33.8 %head_back.1 = (bf16[6400,2048]{1,0:T(8,128)(2,1)}, bf16[6400,1024]{1,0:T(8,128)(2,1)}) custom-call(bf16[6400,2048]{1,0:T(8,128)(2,1)} %get-tuple-element.108.exp_ref, bf16[2048,1024]{1,0:T(8,128)(2,1)} %get-tuple-element.107.final_ref, f32[10,1,2048]{2,1,0:T(1,128)} %exponential_multiply_fusion.scale_ref, f32[1,2048]{1,0:T(1,128)} %bitcast.127, ...), custom_call_target="tpu_custom_call" | custom-call | flops 26843545600 | bytes 65536000 | tf_op jit(solution)/shard_map/head_back/pallas_call | solution.py:727
  353.9 95.3 %final_back.1 = (bf16[1024,1024]{1,0:T(8,128)(2,1)}, f32[256,1024]{1,0:T(8,128)}, f32[8,1024]{1,0:T(8,128)}) custom-call(bf16[6400,2048]{1,0:T(8,128)(2,1)} %get-tuple-element.112.refs_0_, bf16[6400,1024]{1,0:T(8,128)(2,1)} %all-gather.2.cloned.1.call-done.table_ref.refs_1_, f32[256,1024]{1,0:T(8,128)} %get-tuple-element.113.refs_2_, f32[6,1024]{1,0:T(8,128)} %refs_29_.1), custom_call_target="tpu_custom_call" | custom-call | flops 65000001536 | bytes 195000000 | tf_op jit(solution)/shard_map/final_back/pallas_call | solution.py:648
  449.2 6.9 fusion.8
  456.1 3.8 convolution_convert_fusion.2.refs_0_
  459.9 34.7 %mlp_back.1 = (bf16[1024,1024]{1,0:T(8,128)(2,1)}, f32[256,1024]{1,0:T(8,128)}, f32[8,1024]{1,0:T(8,128)}) custom-call(bf16[1024,1024]{1,0:T(8,128)(2,1)} %convolution_convert_fusion.2.refs_0_, f32[256,1024]{1,0:T(8,128)} %get-tuple-element.106.refs_1_, f32[6,1024]{1,0:T(8,128)} %refs_29_.1, f32[256,1024]{1,0:T(8,128)} %get-tuple-element.115.refs_3_), custom_call_target="tpu_custom_call" | custom-call | flops 33999998976 | bytes 102000000 | tf_op jit(solution)/shard_map/mlp_back/pallas_call | solution.py:648
  494.7 2.4 convolution_convert_fusion.9.upstream_ref
  497.2 17.4 %attend_back.1 = bf16[1024,768]{1,0:T(8,128)(2,1)S(1)} custom-call(bf16[1024,768]{1,0:T(8,128)(2,1)S(1)} %copy-done.3, s32[1024,1]{1,0:T(8,128)S(1)} %copy.60.starts_ref, bf16[1024,256]{1,0:T(8,128)(2,1)S(1)} %convolution_convert_fusion.9.upstream_ref), custom_call_target="tpu_custom_call" | custom-call | flops 2684354560 | bytes 3145728 | tf_op jit(solution)/shard_map/attend_back/pallas_call | solution.py:836
  514.6 1.5 convolution_convert_fusion.8.refs_5_
  516.1 3.1 convolution_convert_fusion.5.refs_0_
  519.2 3.1 convolution_convert_fusion.6.refs_7_
  522.3 3.8 convolution_convert_fusion.refs_6_
  526.1 4.1 convolution_convert_fusion.1.refs_4_
  530.2 73.5 %attn_back.1 = (bf16[8192,256]{1,0:T(8,128)(2,1)}, f32[8,1024]{1,0:T(8,128)}, f32[1024,256]{1,0:T(8,128)}, f32[256,256]{1,0:T(8,128)}, f32[256,1024]{1,0:T(8,128)}, /*index=5*/f32[256,768]{1,0:T(8,128)}) custom-call(bf16[1024,1024]{1,0:T(8,128)(2,1)} %convolution_convert_fusion.5.refs_0_, bf16[256,1024]{1,0:T(8,128)(2,1)} %get-tuple-element.102.refs_1_, ...), custom_call_target="tpu_custom_call" | custom-call | flops 70000001024 | bytes 210000000 | tf_op jit(solution)/shard_map/attn_back/pallas_call | solution.py:648
  603.7 1.1 split.45
  604.8 1.1 split.32
  605.9 1.1 split.44
  607.0 1.1 split.34
  608.0 1.0 split.46
  609.1 1.0 split.28
  610.2 2.9 collective-permute-start.7
  613.2 2.8 collective-permute-start.5
  616.6 16.4 %scatter.1 = f32[6288,256]{1,0:T(8,128)} custom-call(s32[1]{0:T(128)} %bitcast.2.count_ref, s32[8192]{0:T(1024)} %get-tuple-element.90.key_ref, bf16[6400,256]{1,0:T(8,128)(2,1)} %reduce-scatter.2.cloned.1.call-done.head_ref, bf16[8192,256]{1,0:T(8,128)(2,1)} %get-tuple-element.123.rows_in_ref), custom_call_target="tpu_custom_call" | custom-call | flops 23000000512 | bytes 69000000 | tf_op jit(solution)/shard_map/scatter/pallas_call | solution.py:1308
  633.0 9.7 %collective-permute-done.5 = bf16[128,256]{1,0:T(8,128)(2,1)S(1)} collective-permute-done((bf16[128,256]{1,0:T(8,128)(2,1)S(1)}, bf16[128,256]{1,0:T(8,128)(2,1)S(1)}, u32[]{:S(2)}, u32[]{:S(2)}) %collective-permute-start.5) | collective-permute-done | bytes 65568 | tf_op jit(solution)/shard_map/ppermute | solution.py:1624
  642.7 4.4 fusion
  650.6 17.4 %update_stats.1 = (f32[50,128]{1,0:T(8,128)}, f32[2,128]{1,0:T(2,128)}, f32[1,128]{1,0:T(1,128)}, f32[2,128]{1,0:T(2,128)}, f32[4,128]{1,0:T(4,128)}, /*index=5*...) custom-call(f32[50,128]{1,0:T(8,128)} %pad_bitcast_fusion.1.refs_0_,, ...), custom_call_target="tpu_custom_call" | custom-call | flops 12000000000 | bytes 36000000 | tf_op jit(solution)/shard_map/update_stats/pallas_call | solution.py:1143
  668.1 1.4 fusion.35
  669.5 5.5 multiply_reduce_fusion
  675.0 1.4 multiply_reduce_fusion.1
  676.4 1.4 multiply_reduce_fusion.2
  677.8 1.3 multiply_reduce_fusion.7
  679.1 1.4 multiply_reduce_fusion.5
  680.5 10.3 %clip_rates.1 = f32[8,128]{1,0:T(8,128)} custom-call(f32[2,128]{1,0:T(2,128)} %bitcast.176, f32[3,128]{1,0:T(4,128)} %bitcast.163, f32[2,128]{1,0:T(2,128)} %bitcast.173, f32[4,128]{1,0:T(4,128)} %bitcast.162, f32[2,128]{1,0:T(2,128)} %bitcast.172, f32[16,128]{1,0:T(8,128)} %get-tuple-element.140.refs_5_), custom_call_target="tpu_custom_call" | custom-call | flops 8000000000 | bytes 24000000 | tf_op jit(solution)/shard_map/clip_rates/pallas_call | solution.py:1191
  690.9 1.4 fusion.36
  692.3 2.3 multiply_subtract_fusion.1
  694.5 2.3 multiply_subtract_fusion.2
  696.8 2.0 multiply_subtract_fusion.4
  698.9 2.2 multiply_subtract_fusion.3
  701.1 9.1 %multiply_subtract_fusion = f32[6288,256]{1,0:T(8,128)} fusion(f32[6288,256]{1,0:T(8,128)} %table_ref.1, f32[]{:T(128)} %bitcast.59, f32[6288,256]{1,0:T(8,128)} %scatter.1, f32[]{:T(128)} %bitcast.41, f32[256]{0:T(256)S(1)} %bitcast.154, f32[6288]{0:T(1024)S(1)} %bitcast.119), kind=kLoop, calls=%fused_computation | loop fusion | flops 8048640 | bytes 19342920 | tf_op jit(solution)/shard_map/sub | solution.py:1667
  (175 shorter events, 23.6 us)
Async XLA Ops:
  7.2 249.3 %all-gather.2.cloned.1.call-start = ((), (), s32[]{:S(2)}) async-start(), calls=%async_computation.1 | async-start | bytes 16384000 | tf_op jit(solution)/shard_map/all_gather | solution.py:1486
  8.6 8.9 %copy-start.9 = (f32[256,512]{1,0:T(8,128)S(1)}, f32[256,512]{1,0:T(8,128)}, u32[]{:S(2)}) copy-start(f32[256,512]{1,0:T(8,128)} %param.28) | copy-start | bytes 1572868
  8.6 12.1 %copy-start.7 = (f32[512,256]{1,0:T(8,128)S(1)}, f32[512,256]{1,0:T(8,128)}, u32[]{:S(2)}) copy-start(f32[512,256]{1,0:T(8,128)} %param.29) | copy-start | bytes 1572868
  8.6 13.1 %copy-start.12 = (f32[256,384]{1,0:T(8,128)S(1)}, f32[256,384]{1,0:T(8,128)}, u32[]{:S(2)}) copy-start(f32[256,384]{1,0:T(8,128)} %param.26) | copy-start | bytes 1179652
  8.6 16.3 %copy-start.16 = (f32[128,256]{1,0:T(8,128)S(1)}, f32[128,256]{1,0:T(8,128)}, u32[]{:S(2)}) copy-start(f32[128,256]{1,0:T(8,128)} %param.27) | copy-start | bytes 393220
  18.1 37.3 %collective-permute-start.2 = (bf16[256,512]{1,0:T(8,128)(2,1)S(1)}, bf16[256,512]{1,0:T(8,128)(2,1)S(1)}, u32[]{:S(2)}, u32[]{:S(2)}) collective-permute-start(bf16[256,512]{1,0:T(8,128)(2,1)S(1)} %get-tuple-element.175), channel_id=1, source_target_pairs={{0,4},{1,5},{2,6},{3,7},{4,0},{5,1},{6,2},{7,3},{8,12},{9,13},{10,... | collective-permute-start | bytes 786440 | tf_op jit(solution)/shard_map/ppermute | solution.py:1441
  21.4 35.0 %collective-permute-start.3 = (bf16[512,256]{1,0:T(8,128)(2,1)S(1)}, bf16[512,256]{1,0:T(8,128)(2,1)S(1)}, u32[]{:S(2)}, u32[]{:S(2)}) collective-permute-start(bf16[512,256]{1,0:T(8,128)(2,1)S(1)} %get-tuple-element.173), channel_id=1, source_target_pairs={{0,4},{1,5},{2,6},{3,7},{4,0},{5,1},{6,2},{7,3},{8,12},{9,13},{10,... | collective-permute-start | bytes 786440 | tf_op jit(solution)/shard_map/ppermute | solution.py:1441
  22.4 32.3 %collective-permute-start = (bf16[256,384]{1,0:T(8,128)(2,1)S(1)}, bf16[256,384]{1,0:T(8,128)(2,1)S(1)}, u32[]{:S(2)}, u32[]{:S(2)}) collective-permute-start(bf16[256,384]{1,0:T(8,128)(2,1)S(1)} %get-tuple-element.177), channel_id=1, source_target_pairs={{0,4},{1,5},{2,6},{3,7},{4,0},{5,1},{6,2},{7,3},{8,12},{9,13},{10,... | collective-permute-start | bytes 589832 | tf_op jit(solution)/shard_map/ppermute | solution.py:1441
  25.5 28.5 %collective-permute-start.1 = (bf16[128,256]{1,0:T(8,128)(2,1)S(1)}, bf16[128,256]{1,0:T(8,128)(2,1)S(1)}, u32[]{:S(2)}, u32[]{:S(2)}) collective-permute-start(bf16[128,256]{1,0:T(8,128)(2,1)S(1)} %get-tuple-element.181), channel_id=1, source_target_pairs={{0,4},{1,5},{2,6},{3,7},{4,0},{5,1},{6,2},{7,3},{8,12},{9,13},{10,... | collective-permute-start | bytes 196616 | tf_op jit(solution)/shard_map/ppermute | solution.py:1441
  57.2 69.1 %copy-start.26 = (s32[2048]{0:T(1024)S(1)}, s32[2048]{0:T(1024)}, u32[]{:S(2)}) copy-start(s32[2048]{0:T(1024)} %param.24) | copy-start | bytes 24580
  57.2 69.2 %copy-start.38 = (s32[2048]{0:T(1024)S(1)}, s32[2048]{0:T(1024)}, u32[]{:S(2)}) copy-start(s32[2048]{0:T(1024)} %param.23) | copy-start | bytes 24580
  57.2 69.4 %copy-start.36 = (s32[2048]{0:T(1024)S(1)}, s32[2048]{0:T(1024)}, u32[]{:S(2)}) copy-start(s32[2048]{0:T(1024)} %param.22) | copy-start | bytes 24580
  126.0 1.7 copy-start.45
  126.0 490.5 %reduce-scatter.2.cloned.1.call-start = ((), (), s32[]{:S(2)}) async-start(), calls=%async_computation.2 | async-start | bytes 16384000 | tf_op jit(solution)/shard_map/reduce_scatter | solution.py:1554
  127.0 3.8 copy-start.39
  130.9 12.4 %copy-start.2 = (bf16[1024,768]{1,0:T(8,128)(2,1)}, bf16[1024,768]{1,0:T(8,128)(2,1)S(1)}, u32[]{:S(2)}) copy-start(bf16[1024,768]{1,0:T(8,128)(2,1)S(1)} %convolution_convert_fusion.7.mixed_ref) | copy-start | bytes 4718596
  130.9 10.4 %copy-start.18 = (bf16[256,1024]{1,0:T(8,128)(2,1)S(1)}, bf16[256,1024]{1,0:T(8,128)(2,1)}, u32[]{:S(2)}) copy-start(bf16[256,1024]{1,0:T(8,128)(2,1)} %get-tuple-element.101) | copy-start | bytes 1572868
  140.5 0.8 copy-start
  143.3 34.5 %copy-start.48 = (bf16[1024,1024]{1,0:T(8,128)(2,1)S(1)}, bf16[1024,1024]{1,0:T(8,128)(2,1)}, u32[]{:S(2)}) copy-start(bf16[1024,1024]{1,0:T(8,128)(2,1)} %get-tuple-element.104) | copy-start | bytes 6291460
  177.8 4.1 copy-start.52
  181.9 4.0 copy-start.42
  307.0 11.1 %copy-start.15 = (f32[10,1,2048]{2,1,0:T(1,128)S(1)}, f32[10,1,2048]{2,1,0:T(1,128)}, u32[]{:S(2)}) copy-start(f32[10,1,2048]{2,1,0:T(1,128)} %get-tuple-element.109) | copy-start | bytes 245764
  318.1 0.7 copy-start.22
  352.6 0.7 copy-start.27
  353.9 95.3 %copy-start.43 = (f32[1024,1024]{1,0:T(8,128)S(1)}, f32[1024,1024]{1,0:T(8,128)}, u32[]{:S(2)}) copy-start(f32[1024,1024]{1,0:T(8,128)} %copy-done.42) | copy-start | bytes 12582916
  449.2 6.9 copy-start.49
  459.9 34.8 %copy-start.19 = (bf16[256,1024]{1,0:T(8,128)(2,1)S(1)}, bf16[256,1024]{1,0:T(8,128)(2,1)}, u32[]{:S(2)}) copy-start(bf16[256,1024]{1,0:T(8,128)(2,1)} %get-tuple-element.101) | copy-start | bytes 1572868
  494.7 2.5 copy-start.3
  497.1 17.4 %copy-start.1 = (bf16[1024,256]{1,0:T(8,128)(2,1)S(1)}, bf16[1024,256]{1,0:T(8,128)(2,1)}, u32[]{:S(2)}) copy-start(bf16[1024,256]{1,0:T(8,128)(2,1)} %copy-done) | copy-start | bytes 1572868
  497.2 17.4 %copy-start.11 = (bf16[1024,1024]{1,0:T(8,128)(2,1)S(1)}, bf16[1024,1024]{1,0:T(8,128)(2,1)}, u32[]{:S(2)}) copy-start(bf16[1024,1024]{1,0:T(8,128)(2,1)} %get-tuple-element.116) | copy-start | bytes 6291460
  497.2 18.9 %copy-start.47 = (bf16[1024,768]{1,0:T(8,128)(2,1)S(1)}, bf16[1024,768]{1,0:T(8,128)(2,1)}, u32[]{:S(2)}) copy-start(bf16[1024,768]{1,0:T(8,128)(2,1)} %get-tuple-element.99) | copy-start | bytes 4718596
  516.1 3.1 copy-start.46
  519.2 3.1 copy-start.50
  522.3 3.8 copy-start.44
  522.3 3.8 copy-start.51
  603.7 6.4 copy-start.21
  603.7 12.4 %copy-start.40 = (f32[4]{0:T(128)S(1)}, f32[4]{0:T(128)}, u32[]{:S(2)}) copy-start(f32[4]{0:T(128)} %get-tuple-element.164) | copy-start | bytes 52
  610.1 32.5 %collective-permute-start.6 = (bf16[256,512]{1,0:T(8,128)(2,1)S(1)}, bf16[256,512]{1,0:T(8,128)(2,1)S(1)}, u32[]{:S(2)}, u32[]{:S(2)}) collective-permute-start(bf16[256,512]{1,0:T(8,128)(2,1)S(1)} %split.45), channel_id=1, source_target_pairs={{0,4},{1,5},{2,6},{3,7},{4,0},{5,1},{6,2},{7,3},{8,12},{9,13},{10,... | collective-permute-start | bytes 786440 | tf_op jit(solution)/shard_map/ppermute | solution.py:1624
  610.2 32.4 %collective-permute-start.7 = (bf16[512,256]{1,0:T(8,128)(2,1)S(1)}, bf16[512,256]{1,0:T(8,128)(2,1)S(1)}, u32[]{:S(2)}, u32[]{:S(2)}) collective-permute-start(bf16[512,256]{1,0:T(8,128)(2,1)S(1)} %split.44), channel_id=1, source_target_pairs={{0,4},{1,5},{2,6},{3,7},{4,0},{5,1},{6,2},{7,3},{8,12},{9,13},{10,... | collective-permute-start | bytes 786440 | tf_op jit(solution)/shard_map/ppermute | solution.py:1624
  613.1 29.5 %collective-permute-start.4 = (bf16[256,384]{1,0:T(8,128)(2,1)S(1)}, bf16[256,384]{1,0:T(8,128)(2,1)S(1)}, u32[]{:S(2)}, u32[]{:S(2)}) collective-permute-start(bf16[256,384]{1,0:T(8,128)(2,1)S(1)} %split.46), channel_id=1, source_target_pairs={{0,4},{1,5},{2,6},{3,7},{4,0},{5,1},{6,2},{7,3},{8,12},{9,13},{10,... | collective-permute-start | bytes 589832 | tf_op jit(solution)/shard_map/ppermute | solution.py:1624
  613.2 29.4 %collective-permute-start.5 = (bf16[128,256]{1,0:T(8,128)(2,1)S(1)}, bf16[128,256]{1,0:T(8,128)(2,1)S(1)}, u32[]{:S(2)}, u32[]{:S(2)}) collective-permute-start(bf16[128,256]{1,0:T(8,128)(2,1)S(1)} %split.47), channel_id=1, source_target_pairs={{0,4},{1,5},{2,6},{3,7},{4,0},{5,1},{6,2},{7,3},{8,12},{9,13},{10,... | collective-permute-start | bytes 196616 | tf_op jit(solution)/shard_map/ppermute | solution.py:1624
  648.5 43.8 %copy-start.4 = (f32[512,256]{1,0:T(8,128)}, f32[512,256]{1,0:T(8,128)S(1)}, u32[]{:S(2)}) copy-start(f32[512,256]{1,0:T(8,128)S(1)} %get-tuple-element.241) | copy-start | bytes 1572868
  649.2 45.3 %copy-start.5 = (f32[256,512]{1,0:T(8,128)}, f32[256,512]{1,0:T(8,128)S(1)}, u32[]{:S(2)}) copy-start(f32[256,512]{1,0:T(8,128)S(1)} %get-tuple-element.237) | copy-start | bytes 1572868
  649.9 46.9 %copy-start.14 = (f32[128,256]{1,0:T(8,128)}, f32[128,256]{1,0:T(8,128)S(1)}, u32[]{:S(2)}) copy-start(f32[128,256]{1,0:T(8,128)S(1)} %get-tuple-element.233) | copy-start | bytes 393220
  650.6 48.2 %copy-start.6 = (f32[256,384]{1,0:T(8,128)}, f32[256,384]{1,0:T(8,128)S(1)}, u32[]{:S(2)}) copy-start(f32[256,384]{1,0:T(8,128)S(1)} %get-tuple-element.229) | copy-start | bytes 1179652
  668.0 7.0 copy-start.28
  668.1 6.9 copy-start.31
  668.1 8.3 %copy-start.29 = (f32[4,128]{1,0:T(4,128)S(1)}, f32[4,128]{1,0:T(4,128)}, u32[]{:S(2)}) copy-start(f32[4,128]{1,0:T(4,128)} %get-tuple-element.146) | copy-start | bytes 6148
  668.1 8.3 %copy-start.32 = (f32[2,128]{1,0:T(2,128)S(1)}, f32[2,128]{1,0:T(2,128)}, u32[]{:S(2)}) copy-start(f32[2,128]{1,0:T(2,128)} %get-tuple-element.145) | copy-start | bytes 3076
  668.1 9.7 %copy-start.33 = (f32[2,128]{1,0:T(2,128)S(1)}, f32[2,128]{1,0:T(2,128)}, u32[]{:S(2)}) copy-start(f32[2,128]{1,0:T(2,128)} %get-tuple-element.144) | copy-start | bytes 3076
  668.1 9.7 %copy-start.37 = (f32[1,128]{1,0:T(1,128)S(1)}, f32[1,128]{1,0:T(1,128)}, u32[]{:S(2)}) copy-start(f32[1,128]{1,0:T(1,128)} %get-tuple-element.143) | copy-start | bytes 1540
  668.1 11.0 %copy-start.30 = (f32[3,128]{1,0:T(4,128)S(1)}, f32[3,128]{1,0:T(4,128)}, u32[]{:S(2)}) copy-start(f32[3,128]{1,0:T(4,128)} %get-tuple-element.142) | copy-start | bytes 4612
  668.1 11.0 %copy-start.34 = (f32[2,128]{1,0:T(2,128)S(1)}, f32[2,128]{1,0:T(2,128)}, u32[]{:S(2)}) copy-start(f32[2,128]{1,0:T(2,128)} %get-tuple-element.141) | copy-start | bytes 3076
  680.5 11.7 %copy-start.8 = (f32[512,256]{1,0:T(8,128)S(1)}, f32[512,256]{1,0:T(8,128)}, u32[]{:S(2)}) copy-start(f32[512,256]{1,0:T(8,128)} %param.29) | copy-start | bytes 1572868
  680.5 14.0 %copy-start.10 = (f32[256,512]{1,0:T(8,128)S(1)}, f32[256,512]{1,0:T(8,128)}, u32[]{:S(2)}) copy-start(f32[256,512]{1,0:T(8,128)} %param.28) | copy-start | bytes 1572868
  680.5 16.3 %copy-start.17 = (f32[128,256]{1,0:T(8,128)S(1)}, f32[128,256]{1,0:T(8,128)}, u32[]{:S(2)}) copy-start(f32[128,256]{1,0:T(8,128)} %param.27) | copy-start | bytes 393220
  680.5 18.3 %copy-start.13 = (f32[256,384]{1,0:T(8,128)S(1)}, f32[256,384]{1,0:T(8,128)}, u32[]{:S(2)}) copy-start(f32[256,384]{1,0:T(8,128)} %param.26) | copy-start | bytes 1179652
  690.8 10.2 %copy-start.20 = (f32[50,128]{1,0:T(8,128)S(1)}, f32[50,128]{1,0:T(8,128)}, u32[]{:S(2)}) copy-start(f32[50,128]{1,0:T(8,128)} %get-tuple-element.138) | copy-start | bytes 76804
  690.9 10.2 %copy-start.35 = (f32[2,128]{1,0:T(2,128)S(1)}, f32[2,128]{1,0:T(2,128)}, u32[]{:S(2)}) copy-start(f32[2,128]{1,0:T(2,128)} %get-tuple-element.139) | copy-start | bytes 3076
  701.1 9.1 %copy-start.41 = (f32[1,128]{1,0:T(1,128)S(1)}, f32[1,128]{1,0:T(1,128)}, u32[]{:S(2)}) copy-start(f32[1,128]{1,0:T(1,128)} %get-tuple-element.137) | copy-start | bytes 1540
  701.1 15.3 %copy-start.25 = (f32[6,1024]{1,0:T(8,128)S(1)}, f32[6,1024]{1,0:T(8,128)}, u32[]{:S(2)}) copy-start(f32[6,1024]{1,0:T(8,128)} %get-tuple-element.245) | copy-start | bytes 73732
  701.1 15.9 %copy-start.24 = (f32[6,1024]{1,0:T(8,128)S(1)}, f32[6,1024]{1,0:T(8,128)}, u32[]{:S(2)}) copy-start(f32[6,1024]{1,0:T(8,128)} %get-tuple-element.246) | copy-start | bytes 73732
  701.1 16.5 %copy-start.23 = (f32[6,1024]{1,0:T(8,128)S(1)}, f32[6,1024]{1,0:T(8,128)}, u32[]{:S(2)}) copy-start(f32[6,1024]{1,0:T(8,128)} %get-tuple-element.247) | copy-start | bytes 73732
Sparse Core Ops, SparseCore 0:
  126.1 130.3 all-gather.1
  352.7 125.1 reduce-scatter.1

commit v7 on v6

--- a/solution.py
+++ b/solution.py
@@ -41,8 +41,8 @@
 ):
     (rows_r, width_r), (rows_g, width_g) = shapes
     if product:
-        dl, table = refs[:2]
-        first = 2
+        dl, *tables = refs[:3]
+        first = 3
     else:
         part = refs[0] if nr else None
         first = 1 if nr else 0
@@ -53,7 +53,9 @@
         whole, refs = refs[0], refs[1:]
     outs = refs[:n_out]
     refs = refs[n_out:]
-    side_outs, scratch = refs[: len(sides)], refs[len(sides) :]
+    scatters = [index for index, (kind, unused) in enumerate(sides) if kind == "scatter"]
+    side_outs, refs = refs[: len(sides)], refs[len(sides) :]
+    twin_outs, scratch = (refs[:2], refs[2:]) if scatters else ([], refs)
     side_scratch, scratch = scratch[: 3 * len(sides)], scratch[3 * len(sides) :]
     if turn:
         cast, turn_send, turn_recv = scratch[-3:]
@@ -130,8 +132,11 @@
     for index, (kind, axis) in enumerate(sides):
         src, dst = side_ins[index], side_outs[index]
         send, recv, slots = side_scratch[3 * index : 3 * index + 3]
-        shard = src if kind == "gather" else dst
-        length, height = shard.shape[axis], shard.shape[0] // 2
+        if kind == "gather":
+            length, height = src.shape[axis], src.shape[0] // 2
+        else:
+            length = src.shape[axis] // size_dp
+            height = (length if axis == 0 else src.shape[0]) // 2
         if not relay:
             for hop in range(1, size_dp):
                 peer = lax.rem(dp + hop, size_dp)
@@ -407,26 +412,19 @@
 
         slot = lax.rem(k, 2)
 
-        def add(i, carry):
-            at = pl.ds(pl.multiple_of(i * HEAD_BLOCK, HEAD_BLOCK), HEAD_BLOCK)
+        start = 0
+        for piece in tables:
             found = lax.dot_general(
-                dl_buf[slot, at, :],
-                table[at, :],
+                dl_buf[slot, start : start + piece.shape[0], :],
+                piece[...],
                 (((0,), (0,)), ((), ())),
                 preferred_element_type=jnp.float32,
             )
-
-            @pl.when(i == 0)
-            def _():
+            if start:
+                total_ref[...] += found
+            else:
                 total_ref[...] = found
-
-            @pl.when(i > 0)
-            def _():
-                total_ref[...] += found
-
-            return carry
-
-        lax.fori_loop(0, table.shape[0] // HEAD_BLOCK, add, 0)
+            start += piece.shape[0]
         for block in range(2 * nr):
             part[part_rows(block, k), :] = total_ref[
                 block * piece_r : block * piece_r + piece_r, :
@@ -533,22 +531,38 @@
         copy.wait()
     for unused, unused, copy in relays:
         copy.wait()
-    for index, (kind, axis) in enumerate(sides):
-        if kind == "scatter":
-            src, dst = side_ins[index], side_outs[index]
-            slots = side_scratch[3 * index + 2]
-            length, height = dst.shape[axis], dst.shape[0] // 2
-            if relay:
-                for side in range(2):
-                    total = src[half_share(axis, length, dp, height, side)].astype(jnp.float32)
-                    total += slots[4 * side + 1].astype(jnp.float32)
-                    total += slots[4 * side + 3].astype(jnp.float32)
-                    dst[pl.ds(side * height, height), :] = total
-            else:
-                total = src[share(axis, length, dp)].astype(jnp.float32)
-                for hop in range(1, size_dp):
-                    total += slots[hop].astype(jnp.float32)
-                dst[...] = total
+    placed = [0, 0]
+    for index in scatters:
+        axis = sides[index][1]
+        src, dst = side_ins[index], side_outs[index]
+        slots = side_scratch[3 * index + 2]
+        length = src.shape[axis] // size_dp
+        height = (length if axis == 0 else src.shape[0]) // 2
+        if relay:
+            total = []
+            for side in range(2):
+                one = src[half_share(axis, length, dp, height, side)].astype(jnp.float32)
+                one += slots[4 * side + 1].astype(jnp.float32)
+                one += slots[4 * side + 3].astype(jnp.float32)
+                total.append(one)
+            total = jnp.concatenate(total)
+        else:
+            total = src[share(axis, length, dp)].astype(jnp.float32)
+            for hop in range(1, size_dp):
+                total += slots[hop].astype(jnp.float32)
+        twins = twin_outs[axis]
+        at = placed[axis]
+        if axis == 0:
+            own = dst.shape[1]
+            dst[...] = total[:, :own]
+            more = total.shape[1] - own
+            twins[:, at : at + more] = total[:, own:].astype(twins.dtype)
+        else:
+            own = dst.shape[0]
+            dst[...] = total[:own, :]
+            more = total.shape[0] - own
+            twins[at : at + more, :] = total[own:, :].astype(twins.dtype)
+        placed[axis] += more
 
 
 def line_call(
@@ -569,6 +583,7 @@
     side_ticks=0,
     product=False,
     chunk_major=False,
+    seqs=1,
 ):
     piece = rows // chunks
     size_dp = lax.axis_size("dp")
@@ -585,6 +600,7 @@
     out_shape += out_types
     dma = pltpu.SemaphoreType.DMA
     scratch = []
+    twin_shapes = [[0, 0], [0, 0]]
     for kind, axis, values in sides:
         shape = list(values.shape)
         scratch += [dma((max(size_dp, 6),)), dma((max(size_dp, 6),))]
@@ -594,9 +610,15 @@
             scratch.append(pltpu.VMEM((16, 128), values.dtype))
         else:
             shape[axis] //= size_dp
-            out_shape.append(jax.ShapeDtypeStruct(tuple(shape), jnp.float32))
+            own = list(shape)
+            own[1 - axis] //= seqs
+            out_shape.append(jax.ShapeDtypeStruct(tuple(own), jnp.float32))
+            twin_shapes[axis][axis] = shape[axis]
+            twin_shapes[axis][1 - axis] += shape[1 - axis] - own[1 - axis]
             slots = (8, shape[0] // 2, shape[1]) if size_dp == 4 else (size_dp, *shape)
             scratch.append(pltpu.VMEM(slots, values.dtype))
+    if any(side[0] == "scatter" for side in sides):
+        out_shape += [jax.ShapeDtypeStruct(tuple(shape), jnp.bfloat16) for shape in twin_shapes]
     if nr:
         scratch += [pltpu.VMEM((nr, chunks, piece, width), jnp.bfloat16)] * 4
         scratch += [dma((nr, chunks))] * 5
@@ -606,7 +628,7 @@
         scratch.append(pltpu.VMEM((chunks, piece, width), jnp.bfloat16))
         scratch += [dma((size_dp, chunks))] * 2
     if product:
-        dl, table = partial
+        dl = partial[0]
         columns = dl.shape[1] // chunks
         scratch += [
             pltpu.VMEM((2 * nr * rows, width), jnp.bfloat16),
@@ -614,7 +636,7 @@
             pltpu.VMEM((columns, width), jnp.float32),
             dma((2,)),
         ]
-        partial = [dl, table]
+        partial = list(partial)
     else:
         partial = [partial] if nr else []
     args = partial + list(ins) + [side[2] for side in sides]
@@ -648,16 +670,17 @@
     return list(call(*args))
 
 
-def head_stats_kernel(block, tile, table_ref, final_ref, wanted_ref, edge_ref, exp_ref, top_ref, sum_ref, pick_ref):
+def head_stats_kernel(block, tile, early, early_ref, late_ref, final_ref, wanted_ref, edge_ref, exp_ref, top_ref, sum_ref, pick_ref):
     j = pl.program_id(0)
     tokens = final_ref.shape[0]
     place = j * block + lax.broadcasted_iota(jnp.int32, (block, 1), 0)
     valid = place < edge_ref[0]
+    table = jnp.where(j < early, early_ref[...], late_ref[...])
 
     def one(i, carry):
         at = pl.ds(i * tile, tile)
         logits = lax.dot_general(
-            table_ref[...],
+            table,
             final_ref[at, :],
             (((1,), (1,)), ((), ())),
             preferred_element_type=jnp.float32,
@@ -677,18 +700,21 @@
         one(i, 0)
 
 
-def head_stats(table, final, wanted, edge, block, tile=512):
-    rows, width = table.shape
+def head_stats(tables, final, wanted, edge, block, tile=512):
+    early = tables[0].shape[0] // block
+    rows = sum(table.shape[0] for table in tables)
+    width = tables[0].shape[1]
     tokens = final.shape[0]
     steps = rows // block
     row = jax.ShapeDtypeStruct((steps, 1, tokens), jnp.float32)
     row_spec = pl.BlockSpec((1, 1, tokens), lambda j: (j, 0, 0))
     return pl.pallas_call(
-        functools.partial(head_stats_kernel, block, tile),
+        functools.partial(head_stats_kernel, block, tile, early),
         grid=(steps,),
         out_shape=[jax.ShapeDtypeStruct((steps * block, tokens), jnp.bfloat16), row, row, row],
         in_specs=[
-            pl.BlockSpec((block, width), lambda j: (j, 0)),
+            pl.BlockSpec((block, width), lambda j: (jnp.minimum(j, early - 1), 0)),
+            pl.BlockSpec((block, width), lambda j: (jnp.maximum(j - early, 0), 0)),
             pl.BlockSpec((tokens, width), lambda j: (0, 0)),
             pl.BlockSpec((1, tokens), lambda j: (0, 0)),
             pl.BlockSpec(memory_space=pltpu.SMEM),
@@ -701,7 +727,7 @@
             transcendentals=rows * tokens,
         ),
         name="head_stats",
-    )(table, final, wanted, edge)
+    )(*tables, final, wanted, edge)
 
 
 def head_back_kernel(block, tile, exp_ref, final_ref, scale_ref, weight_ref, wanted_ref, dl_ref, grad_ref):
@@ -1209,7 +1235,7 @@
 UNROLL = 8
 
 
-def lookup_kernel(shift, count_ref, key_ref, table_ref, out_ref, low_ref, square_ref, rows_ref):
+def lookup_kernel(shift, early, count_ref, key_ref, table_ref, out_ref, low_ref, square_ref, rows_ref):
     spots = out_ref.shape[0]
     vocab, width = table_ref.shape
     rows_ref[...] = jnp.zeros_like(rows_ref)
@@ -1232,7 +1258,9 @@
     strip = 48
     rest = vocab % strip
     done = vocab - rest
-    low_ref[done:, :] = jnp.zeros((low_ref.shape[0] - done, width), jnp.bfloat16)
+    low_ref[done - early :, :] = jnp.zeros(
+        (low_ref.shape[0] - done + early, width), jnp.bfloat16
+    )
 
     def squares(values, total):
         for row in range(0, values.shape[0], 8):
@@ -1243,7 +1271,12 @@
     def lower(i, total):
         at = pl.ds(pl.multiple_of(i * strip, strip), strip)
         values = table_ref[at, :]
-        low_ref[at, :] = values.astype(jnp.bfloat16)
+
+        @pl.when(i >= early // strip)
+        def _():
+            start = pl.multiple_of(i * strip - early, 16)
+            low_ref[pl.ds(start, strip), :] = values.astype(jnp.bfloat16)
+
         return squares(values, total)
 
     total = lax.fori_loop(0, done // strip, lower, jnp.zeros((8, width), jnp.float32))
@@ -1251,22 +1284,22 @@
         values = table_ref[done:, :]
         total = squares(values, total)
         values = jnp.concatenate([values, jnp.zeros((strip - rest, width), jnp.float32)])
-        low_ref[done : done + strip, :] = values.astype(jnp.bfloat16)
+        low_ref[done - early : done - early + strip, :] = values.astype(jnp.bfloat16)
     folded = total[:, 0:128]
     for start in range(128, width, 128):
         folded = folded + total[:, start : start + 128]
     square_ref[...] = folded
 
 
-def lookup(keys, count, table, spots, shift):
+def lookup(keys, count, table, spots, shift, early):
     vocab, width = table.shape
     smem = pl.BlockSpec(memory_space=pltpu.SMEM)
     vmem = pl.BlockSpec(memory_space=pltpu.VMEM)
     return pl.pallas_call(
-        functools.partial(lookup_kernel, shift),
+        functools.partial(lookup_kernel, shift, early),
         out_shape=[
             jax.ShapeDtypeStruct((spots, width), jnp.bfloat16),
-            jax.ShapeDtypeStruct((vocab + -vocab % HEAD_BLOCK, width), jnp.bfloat16),
+            jax.ShapeDtypeStruct((vocab + -vocab % HEAD_BLOCK - early, width), jnp.bfloat16),
             jax.ShapeDtypeStruct((8, 128), jnp.float32),
         ],
         in_specs=[smem, smem, vmem],
@@ -1420,6 +1453,9 @@
     chunks_near = max(1, min(4, rows // 32))
     chunks_turn = max(1, min(4, rows // 32))
 
+    early = (vocab + -vocab % HEAD_BLOCK) * 3 // (10 * HEAD_BLOCK) * HEAD_BLOCK
+    early_table = lax.all_gather(embedding[:early].astype(bf16), "dp", axis=1, tiled=True)
+
     both = jnp.stack([token_ids, sources]).reshape(-1, 128)
     both = small_gather("gather_ids", 0, both, "dp").reshape(size_dp, 2, tokens)
     all_ids = both[:, 0]
@@ -1459,7 +1495,8 @@
     keys = jnp.where(inside, (local_ids << shift) + place, idle)
     keys = jnp.sort(keys.reshape(-1))
     owned = jnp.sum(inside.astype(jnp.int32)).reshape(1)
-    found, low_table, table_sq = lookup(keys, owned, embedding, spots, shift)
+    found, low_table, table_sq = lookup(keys, owned, embedding, spots, shift, early)
+    found, early_table = lax.optimization_barrier((found, early_table))
     inner_one, stream0, wide_qkv, wide_out, wide_fc, wide_proj = line_call(
         "lookup_sum",
         1,
@@ -1483,7 +1520,7 @@
         8,
     )
     low_table, inner_one = lax.optimization_barrier((low_table, inner_one))
-    wide_table = lax.all_gather(low_table, "dp", axis=1, tiled=True)
+    wide_table = (early_table, lax.all_gather(low_table, "dp", axis=1, tiled=True))
     row_f32 = jax.ShapeDtypeStruct((rows, width), f32)
     pair_f32 = jax.ShapeDtypeStruct((8, width), f32)
     my_starts = row_slice(starts, (mp // sharers) * LEN, LEN)[:, None]
@@ -1556,7 +1593,7 @@
     dbranch2, dstream2, norm3 = line_call(
         "final_back",
         6,
-        (dlogits, wide_table),
+        (dlogits, *wide_table),
         [stream2, norm_params],
         [row_f32, pair_f32],
         functools.partial(step_backward, 4),
@@ -1593,7 +1630,7 @@
     dmixed = attend_back(mixed, my_starts, dattended.astype(bf16))
     partial = jnp.einsum("tc,dc->td", dmixed, wide_qkv, preferred_element_type=f32).astype(bf16)
     grad_qkv = jnp.einsum("td,tc->dc", inner_one, dmixed, preferred_element_type=f32).astype(bf16)
-    drows, norm1, grad_proj, grad_out, grad_fc, grad_qkv = line_call(
+    drows, norm1, grad_proj, grad_out, grad_fc, grad_qkv, twins_wide, twins_tall = line_call(
         "attn_back",
         8,
         partial,
@@ -1614,27 +1651,35 @@
         ],
         "spread",
         9,
-    )
-
-    def to_twins(share, axis):
-        pieces = jnp.split(share, seqs, axis=axis)
+        seqs=seqs,
+    )
+
+    def from_twins(values, axis, sizes):
+        starts = [(seqs - 1) * sum(sizes[:n]) for n in range(len(sizes))]
         found = []
         for turn in range(1, seqs):
+            pieces = [
+                lax.slice_in_dim(values, at + (turn - 1) * size, at + turn * size, axis=axis)
+                for at, size in zip(starts, sizes)
+            ]
             back = [(i, (i - turn * sharers) % size_mp) for i in range(size_mp)]
-            found.append(lax.ppermute(pieces[turn].astype(bf16), "mp", back))
-        return pieces[0], found
-
-    shares = [
-        to_twins(grad_qkv, 1),
-        to_twins(grad_out, 0),
-        to_twins(grad_fc, 1),
-        to_twins(grad_proj, 0),
-    ]
+            found.append(lax.ppermute(jnp.concatenate(pieces, axis=axis), "mp", back))
+        return found
+
+    tall = [grad_proj.shape[0], grad_out.shape[0]]
+    wide = [grad_fc.shape[1], grad_qkv.shape[1]]
+    found_tall = from_twins(twins_tall, 0, tall)
+    found_wide = from_twins(twins_wide, 1, wide)
     grad_table = scatter(keys, owned, head_grad, drows, vocab, shift)
-    shares, grad_table = lax.optimization_barrier((shares, grad_table))
-    grad_qkv, grad_out, grad_fc, grad_proj = [
-        sum((piece.astype(f32) for piece in found), mine) for mine, found in shares
-    ]
+    found_tall, found_wide, grad_table = lax.optimization_barrier(
+        (found_tall, found_wide, grad_table)
+    )
+    for values in found_tall:
+        grad_proj += values[: tall[0]].astype(f32)
+        grad_out += values[tall[0] :].astype(f32)
+    for values in found_wide:
+        grad_fc += values[:, : wide[0]].astype(f32)
+        grad_qkv += values[:, wide[0] :].astype(f32)
 
     weights = (embedding, w_qkv, w_out, w_fc, w_proj)
     grads = (grad_table, grad_qkv, grad_out, grad_fc, grad_proj)

time: 732 us -> 694 us (0.948)
  Pallas kernels: 550 us -> 516 us
    pallas_call x6, Pallas kernels: 366 us -> 340 us  [line_call(): return list(call(*args))]
    all_gather x1 -> x2, waiting for transfers between devices: 11 us -> 3.3 us  [the longest x1 3.28 us: local(): lax.all_gather(embedding[:early].astype(bf16), 'dp', axis=1, tiled=True)]
    ppermute x4 -> x2, waiting for transfers between devices: 9.7 us -> 17.2 us  [from_twins(): found.append(lax.ppermute(jnp.concatenate(pieces, axis=axis), 'mp', back))]
  transfers between devices with their start and end apart: 10 -> 9, of which waited for: 3 -> 3; matrix products, arithmetic and copies ran while one was open for 9% -> 9% of each run, Pallas kernels for 49% -> 48%
where the time goes in v7:
time: 694 us; the launch traced here: 687 us
  Pallas kernels  516 us (74%)
  other arithmetic  56.2 us (8%)
  matrix products  42.7 us (6%)
  waiting for transfers between devices  29.1 us (4%)
  local copies, waits for them, and re-layouts  20 us (3%)
  between operations  14.6 us (2%)
  starting transfers between devices  9.25 us (1%)
    pallas_call x6, Pallas kernels, line_call(): return list(call(*args))  340 us
    pallas_call x1, Pallas kernels, head_stats(): pl.pallas_call(functools.partial(head_stats_kernel, block, tile, early),...  46.1 us
    pallas_call x1, Pallas kernels, head_back(): pl.pallas_call(functools.partial(head_back_kernel, block, tile), grid=(ro...  33.8 us
    pallas_call x1, Pallas kernels, update_stats(): pl.pallas_call(functools.partial(stats_kernel, full, size_dp, size_mp), o...  17.9 us
    sub x5, other arithmetic, local(): updated = [weights[n] - factors[n, 0] * steps[n] for n in range(5)]  17.8 us
    pallas_call x1, Pallas kernels, attend_back(): pl.pallas_call(attend_back_kernel, grid=(pairs,), out_shape=jax.ShapeDtyp...  17.6 us
    ppermute x2, waiting for transfers between devices, from_twins(): found.append(lax.ppermute(jnp.concatenate(pieces, axis=axis), 'mp', back))  17.2 us
    pallas_call x2, Pallas kernels, small_gather(): pl.pallas_call(functools.partial(small_gather_kernel, axis, count), out_s...  16.2 us
  transfers between devices with their start and end apart: 9, of which 3 were waited for; matrix products, arithmetic and copies ran while one was open for 9% of the time, Pallas kernels for 48%

profile of v7, /device:TPU:0, one launch (start us, length us, event | category | flops | bytes accessed | tf_op | source)
XLA Modules:
  0.0 687.3 jit_solution(14339877876746386609)
XLA Ops:
  7.2 2.6 slice.111
  9.9 0.7 pad_add_fusion
  11.3 7.9 %gather_ids.1 = s32[4,32,128]{2,1,0:T(8,128)} custom-call(s32[32,128]{1,0:T(8,128)} %reshape.285.src_ref), custom_call_target="tpu_custom_call" | custom-call | flops 6000000000 | bytes 18000000 | tf_op jit(solution)/shard_map/gather_ids/pallas_call | solution.py:918
  19.2 0.9 reshape.286
  20.8 2.6 collective-permute-start.2
  25.0 2.6 collective-permute-start
  29.2 6.8 sort.14
  36.0 12.2 %lookup.1 = (bf16[8192,256]{1,0:T(8,128)(2,1)}, bf16[4480,256]{1,0:T(8,128)(2,1)}, f32[8,128]{1,0:T(8,128)}) custom-call(s32[1]{0:T(128)} %bitcast.2.count_ref, s32[8192]{0:T(1024)} %get-tuple-element.88.key_ref, f32[6288,256]{1,0:T(8,128)} %table_ref.1), custom_call_target="tpu_custom_call" | custom-call | flops 20000000000 | bytes 60000000 | tf_op jit(solution)/shard_map/lookup/pallas_call | solution.py:1298
  48.2 8.5 %collective-permute-done.1 = bf16[128,256]{1,0:T(8,128)(2,1)S(1)} collective-permute-done((bf16[128,256]{1,0:T(8,128)(2,1)S(1)}, bf16[128,256]{1,0:T(8,128)(2,1)S(1)}, u32[]{:S(2)}, u32[]{:S(2)}) %collective-permute-start.1) | collective-permute-done | bytes 65568 | tf_op jit(solution)/shard_map/ppermute | solution.py:1477
  57.4 0.8 pad_maximum_fusion.2.refs_2_
  58.1 0.9 pad_maximum_fusion.refs_4_
  59.0 0.8 pad_maximum_fusion.1.refs_5_
  59.8 3.3 all-gather.3.cloned.1.call-done.early_ref.refs_1_
  63.1 69.6 %lookup_sum.1 = (bf16[1024,1024]{1,0:T(8,128)(2,1)}, bf16[256,1024]{1,0:T(8,128)(2,1)}, bf16[1024,768]{1,0:T(8,128)(2,1)}, bf16[256,1024]{1,0:T(8,128)(2,1)}, bf...) custom-call(bf16[8192,256]{1,0:T(8,128)(2,1)} %get-tuple-element.91.refs_0_, f32[6,1024]{1,0:T(8,128)} %refs_29_.1, ...), custom_call_target="tpu_custom_call" | custom-call | flops 70000001024 | bytes 210000000 | tf_op jit(solution)/shard_map/lookup_sum/pallas_call | solution.py:670
  134.5 3.8 convolution_convert_fusion.7.mixed_ref
  138.4 9.5 %attend.1 = bf16[1024,256]{1,0:T(8,128)(2,1)S(1)} custom-call(bf16[1024,768]{1,0:T(8,128)(2,1)S(1)} %convolution_convert_fusion.7.mixed_ref, s32[1024,1]{1,0:T(8,128)S(1)} %copy.60.starts_ref), custom_call_target="tpu_custom_call" | custom-call | flops 1073741824 | bytes 1572864 | tf_op jit(solution)/shard_map/attend/pallas_call | solution.py:814
  147.9 0.8 copy-done
  148.7 2.0 convolution_convert_fusion.4.refs_0_
  150.8 35.1 %attn_sum.1 = (bf16[1024,1024]{1,0:T(8,128)(2,1)}, f32[256,1024]{1,0:T(8,128)}) custom-call(bf16[1024,1024]{1,0:T(8,128)(2,1)} %convolution_convert_fusion.4.refs_0_, bf16[256,1024]{1,0:T(8,128)(2,1)} %get-tuple-element.102.refs_1_, f32[6,1024]{1,0:T(8,128)} %refs_29_.1), custom_call_target="tpu_custom_call" | custom-call | flops 32000000000 | bytes 96000000 | tf_op jit(solution)/shard_map/attn_sum/pallas_call | solution.py:670
  185.9 4.2 fusion.37
  190.1 4.0 convolution_convert_fusion.3.refs_0_
  194.1 57.9 %mlp_sum.1 = (bf16[2048,1024]{1,0:T(8,128)(2,1)}, f32[256,1024]{1,0:T(8,128)}) custom-call(bf16[1024,1024]{1,0:T(8,128)(2,1)} %convolution_convert_fusion.3.refs_0_, f32[256,1024]{1,0:T(8,128)} %get-tuple-element.106.refs_1_, f32[6,1024]{1,0:T(8,128)} %refs_29_.1), custom_call_target="tpu_custom_call" | custom-call | flops 57999998976 | bytes 174000000 | tf_op jit(solution)/shard_map/mlp_sum/pallas_call | solution.py:670
  252.1 46.1 %head_stats.1 = (bf16[6400,2048]{1,0:T(8,128)(2,1)}, f32[10,1,2048]{2,1,0:T(1,128)}, f32[10,1,2048]{2,1,0:T(1,128)}, f32[10,1,2048]{2,1,0:T(1,128)}) custom-call(bf16[1920,1024]{1,0:T(8,128)(2,1)} %all-gather.3.cloned.1.call-done.early_ref.refs_1_, bf16[4480,1024]{1,0:T(8,128)(2,1)} %all-gather.5.cloned.1.call-done.late_ref.refs_2_, ...), custom_call_target="tpu_custom_call" | custom-call | flops 26843545600 | bytes 39321600 | tf_op jit(solution)/shard_map/head_stats/pallas_call | solution.py:711
  298.2 1.0 reduce_max.18
  299.1 1.0 fusion.17
  300.1 1.0 reduce_sum.245
  301.7 8.3 %gather_stats.1 = f32[8,48,128]{2,1,0:T(8,128)} custom-call(f32[48,128]{1,0:T(8,128)} %pad_maximum_fusion.4.src_ref), custom_call_target="tpu_custom_call" | custom-call | flops 6000000000 | bytes 18000000 | tf_op jit(solution)/shard_map/gather_stats/pallas_call | solution.py:918
  310.0 1.0 reshape.293
  312.0 0.7 exponential_multiply_fusion.scale_ref
  312.7 33.8 %head_back.1 = (bf16[6400,2048]{1,0:T(8,128)(2,1)}, bf16[6400,1024]{1,0:T(8,128)(2,1)}) custom-call(bf16[6400,2048]{1,0:T(8,128)(2,1)} %get-tuple-element.108.exp_ref, bf16[2048,1024]{1,0:T(8,128)(2,1)} %get-tuple-element.107.final_ref, f32[10,1,2048]{2,1,0:T(1,128)} %exponential_multiply_fusion.scale_ref, f32[1,2048]{1,0:T(1,128)} %bitcast.127, ...), custom_call_target="tpu_custom_call" | custom-call | flops 26843545600 | bytes 65536000 | tf_op jit(solution)/shard_map/head_back/pallas_call | solution.py:753
  346.5 0.7 copy-done.30
  347.8 70.2 %final_back.1 = (bf16[1024,1024]{1,0:T(8,128)(2,1)}, f32[256,1024]{1,0:T(8,128)}, f32[8,1024]{1,0:T(8,128)}) custom-call(bf16[6400,2048]{1,0:T(8,128)(2,1)} %get-tuple-element.112.refs_0_, bf16[1920,1024]{1,0:T(8,128)(2,1)} %all-gather.3.cloned.1.call-done.early_ref.refs_1_, bf16[4480,1024]{1,0:T(8,128)(2,1)} %all-gather.5.cloned.1.call-done.late_ref.refs_2_, ...), custom_call_target="tpu_custom_call" | custom-call | flops 65000001536 | bytes 195000000 | tf_op jit(solution)/shard_map/final_back/pallas_call | solution.py:670
  418.1 6.9 %fusion.8 = bf16[1024,1024]{1,0:T(8,128)(2,1)S(1)} fusion(f32[1024,1024]{1,0:T(8,128)S(1)} %copy-done.46, bf16[1024,1024]{1,0:T(8,128)(2,1)} %get-tuple-element.114, bf16[1024,1024]{1,0:T(8,128)(2,1)} %get-tuple-element.105), kind=kOutput, calls=%fused_computation.14 | convolution fusion | flops 2168455168 | bytes 10485760 | tf_op jit(solution)/shard_map/td,fd->tf/dot_general | solution.py:1609
  425.0 3.8 convolution_convert_fusion.2.refs_0_
  428.7 35.1 %mlp_back.1 = (bf16[1024,1024]{1,0:T(8,128)(2,1)}, f32[256,1024]{1,0:T(8,128)}, f32[8,1024]{1,0:T(8,128)}) custom-call(bf16[1024,1024]{1,0:T(8,128)(2,1)} %convolution_convert_fusion.2.refs_0_, f32[256,1024]{1,0:T(8,128)} %get-tuple-element.106.refs_1_, f32[6,1024]{1,0:T(8,128)} %refs_29_.1, f32[256,1024]{1,0:T(8,128)} %get-tuple-element.115.refs_3_), custom_call_target="tpu_custom_call" | custom-call | flops 33999998976 | bytes 102000000 | tf_op jit(solution)/shard_map/mlp_back/pallas_call | solution.py:670
  463.8 2.5 convolution_convert_fusion.9.upstream_ref
  466.3 17.6 %attend_back.1 = bf16[1024,768]{1,0:T(8,128)(2,1)S(1)} custom-call(bf16[1024,768]{1,0:T(8,128)(2,1)S(1)} %copy-done.3, s32[1024,1]{1,0:T(8,128)S(1)} %copy.60.starts_ref, bf16[1024,256]{1,0:T(8,128)(2,1)S(1)} %convolution_convert_fusion.9.upstream_ref), custom_call_target="tpu_custom_call" | custom-call | flops 2684354560 | bytes 3145728 | tf_op jit(solution)/shard_map/attend_back/pallas_call | solution.py:862
  483.9 1.5 convolution_convert_fusion.8.refs_5_
  485.4 3.1 convolution_convert_fusion.5.refs_0_
  488.6 3.1 convolution_convert_fusion.6.refs_7_
  491.6 3.8 convolution_convert_fusion.refs_6_
  495.4 4.1 convolution_convert_fusion.1.refs_4_
  499.5 72.5 %attn_back.1 = (bf16[8192,256]{1,0:T(8,128)(2,1)}, f32[8,1024]{1,0:T(8,128)}, f32[512,256]{1,0:T(8,128)}, f32[128,256]{1,0:T(8,128)}, f32[256,512]{1,0:T(8,128)}...) custom-call(bf16[1024,1024]{1,0:T(8,128)(2,1)} %convolution_convert_fusion.5.refs_0_, ...), custom_call_target="tpu_custom_call" | custom-call | flops 70000001024 | bytes 210000000 | tf_op jit(solution)/shard_map/attn_back/pallas_call | solution.py:670
  572.1 2.9 collective-permute-start.4
  575.6 11.4 %scatter.1 = f32[6288,256]{1,0:T(8,128)} custom-call(s32[1]{0:T(128)} %bitcast.2.count_ref, s32[8192]{0:T(1024)} %get-tuple-element.88.key_ref, bf16[6400,256]{1,0:T(8,128)(2,1)} %reduce-scatter.2.cloned.1.call-done.head_ref, bf16[8192,256]{1,0:T(8,128)(2,1)} %get-tuple-element.121.rows_in_ref), custom_call_target="tpu_custom_call" | custom-call | flops 23000000512 | bytes 69000000 | tf_op jit(solution)/shard_map/scatter/pallas_call | solution.py:1341
  587.0 17.2 %collective-permute-done.4 = bf16[640,256]{1,0:T(8,128)(2,1)S(1)} collective-permute-done((bf16[640,256]{1,0:T(8,128)(2,1)}, bf16[640,256]{1,0:T(8,128)(2,1)S(1)}, u32[]{:S(2)}, u32[]{:S(2)}) %collective-permute-start.4) | collective-permute-done | bytes 327712 | tf_op jit(solution)/shard_map/ppermute | solution.py:1666
  604.2 0.8 fusion.11
  605.7 0.8 fusion.9
  606.4 0.7 fusion.13
  607.2 4.6 fusion
  612.3 17.9 %update_stats.1 = (f32[50,128]{1,0:T(8,128)}, f32[2,128]{1,0:T(2,128)}, f32[1,128]{1,0:T(1,128)}, f32[2,128]{1,0:T(2,128)}, f32[4,128]{1,0:T(4,128)}, /*index=5*...) custom-call(f32[50,128]{1,0:T(8,128)} %pad_bitcast_fusion.1.refs_0_,, ...), custom_call_target="tpu_custom_call" | custom-call | flops 12000000000 | bytes 36000000 | tf_op jit(solution)/shard_map/update_stats/pallas_call | solution.py:1169
  630.3 1.4 fusion.35
  631.7 5.5 multiply_reduce_fusion
  637.2 1.4 multiply_reduce_fusion.1
  638.6 1.4 multiply_reduce_fusion.2
  640.0 1.3 multiply_reduce_fusion.7
  641.3 1.4 multiply_reduce_fusion.5
  642.7 10.5 %clip_rates.1 = f32[8,128]{1,0:T(8,128)} custom-call(f32[2,128]{1,0:T(2,128)} %bitcast.176, f32[3,128]{1,0:T(4,128)} %bitcast.163, f32[2,128]{1,0:T(2,128)} %bitcast.173, f32[4,128]{1,0:T(4,128)} %bitcast.162, f32[2,128]{1,0:T(2,128)} %bitcast.172, f32[16,128]{1,0:T(8,128)} %get-tuple-element.136.refs_5_), custom_call_target="tpu_custom_call" | custom-call | flops 8000000000 | bytes 24000000 | tf_op jit(solution)/shard_map/clip_rates/pallas_call | solution.py:1217
  653.3 1.4 fusion.36
  654.7 2.3 multiply_subtract_fusion.1
  657.0 2.3 multiply_subtract_fusion.2
  659.2 2.0 multiply_subtract_fusion.4
  661.3 2.2 multiply_subtract_fusion.3
  663.5 9.1 %multiply_subtract_fusion = f32[6288,256]{1,0:T(8,128)} fusion(f32[6288,256]{1,0:T(8,128)} %table_ref.1, f32[]{:T(128)} %bitcast.59, f32[6288,256]{1,0:T(8,128)} %scatter.1, f32[]{:T(128)} %bitcast.41, f32[256]{0:T(256)S(1)} %bitcast.154, f32[6288]{0:T(1024)S(1)} %bitcast.119), kind=kLoop, calls=%fused_computation | loop fusion | flops 8048640 | bytes 19342920 | tf_op jit(solution)/shard_map/sub | solution.py:1712
  (171 shorter events, 19.3 us)
Async XLA Ops:
  7.2 55.9 %all-gather.3.cloned.1.call-start = ((), (), s32[]{:S(2)}) async-start(), calls=%async_computation.1 | async-start | bytes 4915200 | tf_op jit(solution)/shard_map/all_gather | solution.py:1457
  9.9 242.2 %all-gather.5.cloned.1.call-start = ((), (), s32[]{:S(2)}) async-start(), calls=%async_computation.2 | async-start | bytes 11468800 | tf_op jit(solution)/shard_map/all_gather | solution.py:1523
  11.3 8.9 %copy-start.9 = (f32[256,512]{1,0:T(8,128)S(1)}, f32[256,512]{1,0:T(8,128)}, u32[]{:S(2)}) copy-start(f32[256,512]{1,0:T(8,128)} %param.28) | copy-start | bytes 1572868
  11.3 12.1 %copy-start.7 = (f32[512,256]{1,0:T(8,128)S(1)}, f32[512,256]{1,0:T(8,128)}, u32[]{:S(2)}) copy-start(f32[512,256]{1,0:T(8,128)} %param.29) | copy-start | bytes 1572868
  11.3 13.1 %copy-start.12 = (f32[256,384]{1,0:T(8,128)S(1)}, f32[256,384]{1,0:T(8,128)}, u32[]{:S(2)}) copy-start(f32[256,384]{1,0:T(8,128)} %param.26) | copy-start | bytes 1179652
  11.3 16.4 %copy-start.18 = (f32[128,256]{1,0:T(8,128)S(1)}, f32[128,256]{1,0:T(8,128)}, u32[]{:S(2)}) copy-start(f32[128,256]{1,0:T(8,128)} %param.27) | copy-start | bytes 393220
  20.8 37.3 %collective-permute-start.2 = (bf16[256,512]{1,0:T(8,128)(2,1)S(1)}, bf16[256,512]{1,0:T(8,128)(2,1)S(1)}, u32[]{:S(2)}, u32[]{:S(2)}) collective-permute-start(bf16[256,512]{1,0:T(8,128)(2,1)S(1)} %get-tuple-element.171), channel_id=1, source_target_pairs={{0,4},{1,5},{2,6},{3,7},{4,0},{5,1},{6,2},{7,3},{8,12},{9,13},{10,... | collective-permute-start | bytes 786440 | tf_op jit(solution)/shard_map/ppermute | solution.py:1477
  24.1 34.9 %collective-permute-start.3 = (bf16[512,256]{1,0:T(8,128)(2,1)S(1)}, bf16[512,256]{1,0:T(8,128)(2,1)S(1)}, u32[]{:S(2)}, u32[]{:S(2)}) collective-permute-start(bf16[512,256]{1,0:T(8,128)(2,1)S(1)} %get-tuple-element.169), channel_id=1, source_target_pairs={{0,4},{1,5},{2,6},{3,7},{4,0},{5,1},{6,2},{7,3},{8,12},{9,13},{10,... | collective-permute-start | bytes 786440 | tf_op jit(solution)/shard_map/ppermute | solution.py:1477
  25.0 32.3 %collective-permute-start = (bf16[256,384]{1,0:T(8,128)(2,1)S(1)}, bf16[256,384]{1,0:T(8,128)(2,1)S(1)}, u32[]{:S(2)}, u32[]{:S(2)}) collective-permute-start(bf16[256,384]{1,0:T(8,128)(2,1)S(1)} %get-tuple-element.173), channel_id=1, source_target_pairs={{0,4},{1,5},{2,6},{3,7},{4,0},{5,1},{6,2},{7,3},{8,12},{9,13},{10,... | collective-permute-start | bytes 589832 | tf_op jit(solution)/shard_map/ppermute | solution.py:1477
  28.2 28.5 %collective-permute-start.1 = (bf16[128,256]{1,0:T(8,128)(2,1)S(1)}, bf16[128,256]{1,0:T(8,128)(2,1)S(1)}, u32[]{:S(2)}, u32[]{:S(2)}) collective-permute-start(bf16[128,256]{1,0:T(8,128)(2,1)S(1)} %get-tuple-element.177), channel_id=1, source_target_pairs={{0,4},{1,5},{2,6},{3,7},{4,0},{5,1},{6,2},{7,3},{8,12},{9,13},{10,... | collective-permute-start | bytes 196616 | tf_op jit(solution)/shard_map/ppermute | solution.py:1477
  63.1 70.0 %copy-start.29 = (s32[2048]{0:T(1024)S(1)}, s32[2048]{0:T(1024)}, u32[]{:S(2)}) copy-start(s32[2048]{0:T(1024)} %param.24) | copy-start | bytes 24580
  63.1 70.1 %copy-start.41 = (s32[2048]{0:T(1024)S(1)}, s32[2048]{0:T(1024)}, u32[]{:S(2)}) copy-start(s32[2048]{0:T(1024)} %param.23) | copy-start | bytes 24580
  63.1 70.3 %copy-start.39 = (s32[2048]{0:T(1024)S(1)}, s32[2048]{0:T(1024)}, u32[]{:S(2)}) copy-start(s32[2048]{0:T(1024)} %param.22) | copy-start | bytes 24580
  132.8 442.8 %reduce-scatter.2.cloned.1.call-start = ((), (), s32[]{:S(2)}) async-start(), calls=%async_computation.3 | async-start | bytes 16384000 | tf_op jit(solution)/shard_map/reduce_scatter | solution.py:1591
  133.9 4.5 copy-start.42
  138.4 12.4 %copy-start.2 = (bf16[1024,768]{1,0:T(8,128)(2,1)}, bf16[1024,768]{1,0:T(8,128)(2,1)S(1)}, u32[]{:S(2)}) copy-start(bf16[1024,768]{1,0:T(8,128)(2,1)S(1)} %convolution_convert_fusion.7.mixed_ref) | copy-start | bytes 4718596
  138.4 10.3 %copy-start.20 = (bf16[256,1024]{1,0:T(8,128)(2,1)S(1)}, bf16[256,1024]{1,0:T(8,128)(2,1)}, u32[]{:S(2)}) copy-start(bf16[256,1024]{1,0:T(8,128)(2,1)} %get-tuple-element.101) | copy-start | bytes 1572868
  147.9 0.8 copy-start
  150.8 35.1 %copy-start.50 = (bf16[1024,1024]{1,0:T(8,128)(2,1)S(1)}, bf16[1024,1024]{1,0:T(8,128)(2,1)}, u32[]{:S(2)}) copy-start(bf16[1024,1024]{1,0:T(8,128)(2,1)} %get-tuple-element.104) | copy-start | bytes 6291460
  185.9 4.2 copy-start.54
  190.0 4.1 copy-start.45
  301.7 10.3 %copy-start.15 = (f32[10,1,2048]{2,1,0:T(1,128)S(1)}, f32[10,1,2048]{2,1,0:T(1,128)}, u32[]{:S(2)}) copy-start(f32[10,1,2048]{2,1,0:T(1,128)} %get-tuple-element.109) | copy-start | bytes 245764
  312.0 0.7 copy-start.25
  346.5 0.7 copy-start.30
  347.8 70.2 %copy-start.46 = (f32[1024,1024]{1,0:T(8,128)S(1)}, f32[1024,1024]{1,0:T(8,128)}, u32[]{:S(2)}) copy-start(f32[1024,1024]{1,0:T(8,128)} %copy-done.45) | copy-start | bytes 12582916
  418.1 6.9 %copy-start.51 = (bf16[1024,1024]{1,0:T(8,128)(2,1)S(1)}, bf16[1024,1024]{1,0:T(8,128)(2,1)}, u32[]{:S(2)}) copy-start(bf16[1024,1024]{1,0:T(8,128)(2,1)} %get-tuple-element.104) | copy-start | bytes 6291460
  428.7 35.1 %copy-start.21 = (bf16[256,1024]{1,0:T(8,128)(2,1)S(1)}, bf16[256,1024]{1,0:T(8,128)(2,1)}, u32[]{:S(2)}) copy-start(bf16[256,1024]{1,0:T(8,128)(2,1)} %get-tuple-element.101) | copy-start | bytes 1572868
  463.8 2.5 copy-start.3
  466.3 17.6 %copy-start.1 = (bf16[1024,256]{1,0:T(8,128)(2,1)S(1)}, bf16[1024,256]{1,0:T(8,128)(2,1)}, u32[]{:S(2)}) copy-start(bf16[1024,256]{1,0:T(8,128)(2,1)} %copy-done) | copy-start | bytes 1572868
  466.3 17.6 %copy-start.11 = (bf16[1024,1024]{1,0:T(8,128)(2,1)S(1)}, bf16[1024,1024]{1,0:T(8,128)(2,1)}, u32[]{:S(2)}) copy-start(bf16[1024,1024]{1,0:T(8,128)(2,1)} %get-tuple-element.116) | copy-start | bytes 6291460
  466.3 19.1 %copy-start.49 = (bf16[1024,768]{1,0:T(8,128)(2,1)S(1)}, bf16[1024,768]{1,0:T(8,128)(2,1)}, u32[]{:S(2)}) copy-start(bf16[1024,768]{1,0:T(8,128)(2,1)} %get-tuple-element.98) | copy-start | bytes 4718596
  485.4 3.1 copy-start.48
  488.6 3.1 copy-start.52
  491.6 3.8 copy-start.47
  491.6 3.8 copy-start.53
  499.5 75.5 %copy-start.43 = (f32[4]{0:T(128)S(1)}, f32[4]{0:T(128)}, u32[]{:S(2)}) copy-start(f32[4]{0:T(128)} %get-tuple-element.160) | copy-start | bytes 52
  572.0 32.2 %collective-permute-start.5 = (bf16[256,896]{1,0:T(8,128)(2,1)}, bf16[256,896]{1,0:T(8,128)(2,1)S(1)}, u32[]{:S(2)}, u32[]{:S(2)}) collective-permute-start(bf16[256,896]{1,0:T(8,128)(2,1)} %get-tuple-element.119), channel_id=1, source_target_pairs={{0,4},{1,5},{2,6},{3,7},{4,0},{5,1},{6,2},{7,3},{8,12},{9,13},{10,... | collective-permute-start | bytes 1376264 | tf_op jit(solution)/shard_map/ppermute | solution.py:1666
  572.1 32.1 %collective-permute-start.4 = (bf16[640,256]{1,0:T(8,128)(2,1)}, bf16[640,256]{1,0:T(8,128)(2,1)S(1)}, u32[]{:S(2)}, u32[]{:S(2)}) collective-permute-start(bf16[640,256]{1,0:T(8,128)(2,1)} %get-tuple-element.118), channel_id=1, source_target_pairs={{0,4},{1,5},{2,6},{3,7},{4,0},{5,1},{6,2},{7,3},{8,12},{9,13},{10,... | collective-permute-start | bytes 983048 | tf_op jit(solution)/shard_map/ppermute | solution.py:1666
  575.5 28.7 %copy-start.17 = (f32[512,256]{1,0:T(8,128)S(1)}, f32[512,256]{1,0:T(8,128)}, u32[]{:S(2)}) copy-start(f32[512,256]{1,0:T(8,128)} %get-tuple-element.128) | copy-start | bytes 1572868
  575.5 29.4 %copy-start.24 = (f32[128,256]{1,0:T(8,128)S(1)}, f32[128,256]{1,0:T(8,128)}, u32[]{:S(2)}) copy-start(f32[128,256]{1,0:T(8,128)} %get-tuple-element.125) | copy-start | bytes 393220
  575.5 30.1 %copy-start.16 = (f32[256,512]{1,0:T(8,128)S(1)}, f32[256,512]{1,0:T(8,128)}, u32[]{:S(2)}) copy-start(f32[256,512]{1,0:T(8,128)} %get-tuple-element.127) | copy-start | bytes 1572868
  575.5 30.9 %copy-start.22 = (f32[256,384]{1,0:T(8,128)S(1)}, f32[256,384]{1,0:T(8,128)}, u32[]{:S(2)}) copy-start(f32[256,384]{1,0:T(8,128)} %get-tuple-element.123) | copy-start | bytes 1179652
  605.0 49.7 %copy-start.4 = (f32[512,256]{1,0:T(8,128)}, f32[512,256]{1,0:T(8,128)S(1)}, u32[]{:S(2)}) copy-start(f32[512,256]{1,0:T(8,128)S(1)} %get-tuple-element.237) | copy-start | bytes 1572868
  605.6 53.6 %copy-start.14 = (f32[128,256]{1,0:T(8,128)}, f32[128,256]{1,0:T(8,128)S(1)}, u32[]{:S(2)}) copy-start(f32[128,256]{1,0:T(8,128)S(1)} %get-tuple-element.229) | copy-start | bytes 393220
  606.4 50.6 %copy-start.5 = (f32[256,512]{1,0:T(8,128)}, f32[256,512]{1,0:T(8,128)S(1)}, u32[]{:S(2)}) copy-start(f32[256,512]{1,0:T(8,128)S(1)} %get-tuple-element.233) | copy-start | bytes 1572868
  607.2 54.1 %copy-start.6 = (f32[256,384]{1,0:T(8,128)}, f32[256,384]{1,0:T(8,128)S(1)}, u32[]{:S(2)}) copy-start(f32[256,384]{1,0:T(8,128)S(1)} %get-tuple-element.225) | copy-start | bytes 1179652
  630.2 7.0 %copy-start.31 = (f32[4,128]{1,0:T(4,128)S(1)}, f32[4,128]{1,0:T(4,128)}, u32[]{:S(2)}) copy-start(f32[4,128]{1,0:T(4,128)} %get-tuple-element.143) | copy-start | bytes 6148
  630.2 6.9 %copy-start.34 = (f32[2,128]{1,0:T(2,128)S(1)}, f32[2,128]{1,0:T(2,128)}, u32[]{:S(2)}) copy-start(f32[2,128]{1,0:T(2,128)} %get-tuple-element.144) | copy-start | bytes 3076
  630.3 8.3 %copy-start.32 = (f32[4,128]{1,0:T(4,128)S(1)}, f32[4,128]{1,0:T(4,128)}, u32[]{:S(2)}) copy-start(f32[4,128]{1,0:T(4,128)} %get-tuple-element.142) | copy-start | bytes 6148
  630.3 8.3 %copy-start.35 = (f32[2,128]{1,0:T(2,128)S(1)}, f32[2,128]{1,0:T(2,128)}, u32[]{:S(2)}) copy-start(f32[2,128]{1,0:T(2,128)} %get-tuple-element.141) | copy-start | bytes 3076
  630.3 9.7 %copy-start.36 = (f32[2,128]{1,0:T(2,128)S(1)}, f32[2,128]{1,0:T(2,128)}, u32[]{:S(2)}) copy-start(f32[2,128]{1,0:T(2,128)} %get-tuple-element.140) | copy-start | bytes 3076
  630.3 9.7 %copy-start.40 = (f32[1,128]{1,0:T(1,128)S(1)}, f32[1,128]{1,0:T(1,128)}, u32[]{:S(2)}) copy-start(f32[1,128]{1,0:T(1,128)} %get-tuple-element.139) | copy-start | bytes 1540
  630.3 11.0 %copy-start.33 = (f32[3,128]{1,0:T(4,128)S(1)}, f32[3,128]{1,0:T(4,128)}, u32[]{:S(2)}) copy-start(f32[3,128]{1,0:T(4,128)} %get-tuple-element.138) | copy-start | bytes 4612
  630.3 11.0 %copy-start.37 = (f32[2,128]{1,0:T(2,128)S(1)}, f32[2,128]{1,0:T(2,128)}, u32[]{:S(2)}) copy-start(f32[2,128]{1,0:T(2,128)} %get-tuple-element.137) | copy-start | bytes 3076
  642.7 12.0 %copy-start.8 = (f32[512,256]{1,0:T(8,128)S(1)}, f32[512,256]{1,0:T(8,128)}, u32[]{:S(2)}) copy-start(f32[512,256]{1,0:T(8,128)} %param.29) | copy-start | bytes 1572868
  642.7 14.2 %copy-start.10 = (f32[256,512]{1,0:T(8,128)S(1)}, f32[256,512]{1,0:T(8,128)}, u32[]{:S(2)}) copy-start(f32[256,512]{1,0:T(8,128)} %param.28) | copy-start | bytes 1572868
  642.7 16.5 %copy-start.19 = (f32[128,256]{1,0:T(8,128)S(1)}, f32[128,256]{1,0:T(8,128)}, u32[]{:S(2)}) copy-start(f32[128,256]{1,0:T(8,128)} %param.27) | copy-start | bytes 393220
  642.7 18.6 %copy-start.13 = (f32[256,384]{1,0:T(8,128)S(1)}, f32[256,384]{1,0:T(8,128)}, u32[]{:S(2)}) copy-start(f32[256,384]{1,0:T(8,128)} %param.26) | copy-start | bytes 1179652
  653.3 10.2 %copy-start.23 = (f32[50,128]{1,0:T(8,128)S(1)}, f32[50,128]{1,0:T(8,128)}, u32[]{:S(2)}) copy-start(f32[50,128]{1,0:T(8,128)} %get-tuple-element.134) | copy-start | bytes 76804
  653.3 10.2 %copy-start.38 = (f32[2,128]{1,0:T(2,128)S(1)}, f32[2,128]{1,0:T(2,128)}, u32[]{:S(2)}) copy-start(f32[2,128]{1,0:T(2,128)} %get-tuple-element.135) | copy-start | bytes 3076
  663.5 9.1 %copy-start.44 = (f32[1,128]{1,0:T(1,128)S(1)}, f32[1,128]{1,0:T(1,128)}, u32[]{:S(2)}) copy-start(f32[1,128]{1,0:T(1,128)} %get-tuple-element.133) | copy-start | bytes 1540
  663.5 15.3 %copy-start.28 = (f32[6,1024]{1,0:T(8,128)S(1)}, f32[6,1024]{1,0:T(8,128)}, u32[]{:S(2)}) copy-start(f32[6,1024]{1,0:T(8,128)} %get-tuple-element.241) | copy-start | bytes 73732
  663.5 15.9 %copy-start.27 = (f32[6,1024]{1,0:T(8,128)S(1)}, f32[6,1024]{1,0:T(8,128)}, u32[]{:S(2)}) copy-start(f32[6,1024]{1,0:T(8,128)} %get-tuple-element.242) | copy-start | bytes 73732
  663.5 16.5 %copy-start.26 = (f32[6,1024]{1,0:T(8,128)S(1)}, f32[6,1024]{1,0:T(8,128)}, u32[]{:S(2)}) copy-start(f32[6,1024]{1,0:T(8,128)} %get-tuple-element.243) | copy-start | bytes 73732
Sparse Core Ops, SparseCore 0:
  10.0 53.0 all-gather.2
  132.9 96.2 all-gather.4
  346.6 124.4 reduce-scatter.1

commit v8 on v7

--- a/solution.py
+++ b/solution.py
@@ -1255,7 +1255,7 @@
         return carry
 
     lax.fori_loop(0, spots // 256, narrow, 0)
-    strip = 48
+    strip = 64
     rest = vocab % strip
     done = vocab - rest
     low_ref[done - early :, :] = jnp.zeros(
@@ -1453,7 +1453,24 @@
     chunks_near = max(1, min(4, rows // 32))
     chunks_turn = max(1, min(4, rows // 32))
 
-    early = (vocab + -vocab % HEAD_BLOCK) * 3 // (10 * HEAD_BLOCK) * HEAD_BLOCK
+    def own_and_twins(weights, axis):
+        low = [weight.astype(bf16) for weight in weights]
+        found = [[weight] for weight in low]
+        sent = jnp.concatenate(low, axis=axis)
+        for turn in range(1, seqs):
+            shift = [(i, (i + turn * sharers) % size_mp) for i in range(size_mp)]
+            arrived = lax.ppermute(sent, "mp", shift)
+            start = 0
+            for index, weight in enumerate(low):
+                size = weight.shape[axis]
+                found[index].append(lax.slice_in_dim(arrived, start, start + size, axis=axis))
+                start += size
+        return [jnp.concatenate(pieces, axis=axis) for pieces in found]
+
+    pair_fc, pair_qkv = own_and_twins((w_fc, w_qkv), 1)
+    pair_proj, pair_out = own_and_twins((w_proj, w_out), 0)
+
+    early = (vocab + -vocab % HEAD_BLOCK) * 2 // (10 * HEAD_BLOCK) * HEAD_BLOCK
     early_table = lax.all_gather(embedding[:early].astype(bf16), "dp", axis=1, tiled=True)
 
     both = jnp.stack([token_ids, sources]).reshape(-1, 128)
@@ -1464,23 +1481,6 @@
         (all_sources[:, None] == jnp.arange(NSRC, dtype=jnp.int32)[None, :]).astype(f32), axis=0
     )
 
-    w_qkv, w_out, w_fc, w_proj, all_ids = lax.optimization_barrier(
-        (w_qkv, w_out, w_fc, w_proj, all_ids)
-    )
-
-
-    def own_and_twins(weight, axis):
-        weight = weight.astype(bf16)
-        found = [weight]
-        for turn in range(1, seqs):
-            shift = [(i, (i + turn * sharers) % size_mp) for i in range(size_mp)]
-            found.append(lax.ppermute(weight, "mp", shift))
-        return jnp.concatenate(found, axis=axis) if seqs > 1 else weight
-
-    pair_qkv = own_and_twins(w_qkv, 1)
-    pair_out = own_and_twins(w_out, 0)
-    pair_fc = own_and_twins(w_fc, 1)
-    pair_proj = own_and_twins(w_proj, 0)
     piece = rows // chunks_turn
     token = jnp.arange(tokens, dtype=jnp.int32)
     place = (
@@ -1606,6 +1606,8 @@
         product=True,
     )
     grad_proj = jnp.einsum("tf,td->fd", hidden, dbranch2, preferred_element_type=f32).astype(bf16)
+    grad_proj, head_grad = lax.optimization_barrier((grad_proj, head_grad))
+    grad_proj = lax.psum_scatter(grad_proj, "dp", scatter_dimension=1, tiled=True)
     dhidden = jnp.einsum("td,fd->tf", dbranch2, wide_proj, preferred_element_type=f32)
     unused, gelu_pull = jax.vjp(gelu_tanh, before)
     dbefore = gelu_pull(dhidden)[0].astype(bf16)
@@ -1630,7 +1632,7 @@
     dmixed = attend_back(mixed, my_starts, dattended.astype(bf16))
     partial = jnp.einsum("tc,dc->td", dmixed, wide_qkv, preferred_element_type=f32).astype(bf16)
     grad_qkv = jnp.einsum("td,tc->dc", inner_one, dmixed, preferred_element_type=f32).astype(bf16)
-    drows, norm1, grad_proj, grad_out, grad_fc, grad_qkv, twins_wide, twins_tall = line_call(
+    drows, norm1, grad_out, grad_fc, grad_qkv, twins_wide, twins_out = line_call(
         "attn_back",
         8,
         partial,
@@ -1644,7 +1646,6 @@
         chips,
         70,
         [
-            ("scatter", 1, grad_proj),
             ("scatter", 1, grad_out),
             ("scatter", 0, grad_fc),
             ("scatter", 0, grad_qkv),
@@ -1666,17 +1667,20 @@
             found.append(lax.ppermute(jnp.concatenate(pieces, axis=axis), "mp", back))
         return found
 
-    tall = [grad_proj.shape[0], grad_out.shape[0]]
+    proj_rows = w_proj.shape[0]
     wide = [grad_fc.shape[1], grad_qkv.shape[1]]
-    found_tall = from_twins(twins_tall, 0, tall)
+    found_proj = from_twins(grad_proj[proj_rows:], 0, [proj_rows])
+    found_out = from_twins(twins_out, 0, [w_out.shape[0]])
     found_wide = from_twins(twins_wide, 1, wide)
     grad_table = scatter(keys, owned, head_grad, drows, vocab, shift)
-    found_tall, found_wide, grad_table = lax.optimization_barrier(
-        (found_tall, found_wide, grad_table)
-    )
-    for values in found_tall:
-        grad_proj += values[: tall[0]].astype(f32)
-        grad_out += values[tall[0] :].astype(f32)
+    found_proj, found_out, found_wide, grad_table = lax.optimization_barrier(
+        (found_proj, found_out, found_wide, grad_table)
+    )
+    grad_proj = grad_proj[:proj_rows].astype(f32)
+    for values in found_proj:
+        grad_proj += values.astype(f32)
+    for values in found_out:
+        grad_out += values.astype(f32)
     for values in found_wide:
         grad_fc += values[:, : wide[0]].astype(f32)
         grad_qkv += values[:, wide[0] :].astype(f32)

time: 694 us -> 688 us (level)
  waiting for transfers between devices: 29.1 us -> 21.9 us
    ppermute x2 -> x3, waiting for transfers between devices: 17.2 us -> 18 us  [from_twins(): found.append(lax.ppermute(jnp.concatenate(pieces, axis=axis), 'mp', back))]
where the time goes in v8:
time: 688 us; the launch traced here: 682 us
  Pallas kernels  516 us (75%)
  other arithmetic  57.9 us (8%)
  matrix products  42.9 us (6%)
  waiting for transfers between devices  21.9 us (3%)
  local copies, waits for them, and re-layouts  20.6 us (3%)
  between operations  14.7 us (2%)
  starting transfers between devices  7.77 us (1%)
    pallas_call x6, Pallas kernels, line_call(): return list(call(*args))  340 us
    pallas_call x1, Pallas kernels, head_stats(): pl.pallas_call(functools.partial(head_stats_kernel, block, tile, early),...  46.1 us
    pallas_call x1, Pallas kernels, head_back(): pl.pallas_call(functools.partial(head_back_kernel, block, tile), grid=(ro...  33.7 us
    ppermute x3, waiting for transfers between devices, from_twins(): found.append(lax.ppermute(jnp.concatenate(pieces, axis=axis), 'mp', back))  18 us
    sub x5, other arithmetic, local(): updated = [weights[n] - factors[n, 0] * steps[n] for n in range(5)]  17.8 us
    pallas_call x1, Pallas kernels, attend_back(): pl.pallas_call(attend_back_kernel, grid=(pairs,), out_shape=jax.ShapeDtyp...  17.6 us
    pallas_call x1, Pallas kernels, update_stats(): pl.pallas_call(functools.partial(stats_kernel, full, size_dp, size_mp), o...  17.3 us
    pallas_call x2, Pallas kernels, small_gather(): pl.pallas_call(functools.partial(small_gather_kernel, axis, count), out_s...  15.9 us
  transfers between devices with their start and end apart: 9, of which 3 were waited for; matrix products, arithmetic and copies ran while one was open for 9% of the time, Pallas kernels for 48%

profile of v8, /device:TPU:0, one launch (start us, length us, event | category | flops | bytes accessed | tf_op | source)
XLA Modules:
  0.0 681.6 jit_solution(13106808115372234606)
XLA Ops:
  7.3 2.3 slice.129
  9.6 1.9 multiply_reduce_fusion.4
  11.5 1.8 multiply_reduce_fusion.6
  13.3 4.1 collective-permute-start
  19.4 7.3 %gather_ids.1 = s32[4,32,128]{2,1,0:T(8,128)} custom-call(s32[32,128]{1,0:T(8,128)} %reshape.306.src_ref), custom_call_target="tpu_custom_call" | custom-call | flops 6000000000 | bytes 18000000 | tf_op jit(solution)/shard_map/gather_ids/pallas_call | solution.py:918
  26.7 0.9 reshape.307
  28.5 6.8 sort.14
  35.2 12.8 %lookup.1 = (bf16[8192,256]{1,0:T(8,128)(2,1)}, bf16[5120,256]{1,0:T(8,128)(2,1)}, f32[8,128]{1,0:T(8,128)}) custom-call(s32[1]{0:T(128)} %bitcast.2.count_ref, s32[8192]{0:T(1024)} %get-tuple-element.84.key_ref, f32[6288,256]{1,0:T(8,128)} %table_ref.1), custom_call_target="tpu_custom_call" | custom-call | flops 20000000000 | bytes 60000000 | tf_op jit(solution)/shard_map/lookup/pallas_call | solution.py:1298
  48.0 3.8 collective-permute-done.1
  52.5 0.8 pad_maximum_fusion.1.refs_5_
  53.4 0.8 pad_maximum_fusion.3.refs_2_
  54.2 0.9 pad_maximum_fusion.refs_4_
  55.0 69.1 %lookup_sum.1 = (bf16[1024,1024]{1,0:T(8,128)(2,1)}, bf16[256,1024]{1,0:T(8,128)(2,1)}, bf16[1024,768]{1,0:T(8,128)(2,1)}, bf16[256,1024]{1,0:T(8,128)(2,1)}, bf...) custom-call(bf16[8192,256]{1,0:T(8,128)(2,1)} %get-tuple-element.87.refs_0_, f32[6,1024]{1,0:T(8,128)} %refs_29_.1, ...), custom_call_target="tpu_custom_call" | custom-call | flops 70000001024 | bytes 210000000 | tf_op jit(solution)/shard_map/lookup_sum/pallas_call | solution.py:670
  125.9 3.8 convolution_convert_fusion.7.mixed_ref
  129.7 9.5 %attend.1 = bf16[1024,256]{1,0:T(8,128)(2,1)S(1)} custom-call(bf16[1024,768]{1,0:T(8,128)(2,1)S(1)} %convolution_convert_fusion.7.mixed_ref, s32[1024,1]{1,0:T(8,128)S(1)} %copy.59.starts_ref), custom_call_target="tpu_custom_call" | custom-call | flops 1073741824 | bytes 1572864 | tf_op jit(solution)/shard_map/attend/pallas_call | solution.py:814
  139.3 0.8 copy-done
  140.1 2.0 convolution_convert_fusion.4.refs_0_
  142.1 34.2 %attn_sum.1 = (bf16[1024,1024]{1,0:T(8,128)(2,1)}, f32[256,1024]{1,0:T(8,128)}) custom-call(bf16[1024,1024]{1,0:T(8,128)(2,1)} %convolution_convert_fusion.4.refs_0_, bf16[256,1024]{1,0:T(8,128)(2,1)} %get-tuple-element.92.refs_1_, f32[6,1024]{1,0:T(8,128)} %refs_29_.1), custom_call_target="tpu_custom_call" | custom-call | flops 32000000000 | bytes 96000000 | tf_op jit(solution)/shard_map/attn_sum/pallas_call | solution.py:670
  176.4 4.2 fusion.37
  180.6 4.0 convolution_convert_fusion.3.refs_0_
  184.6 60.1 %mlp_sum.1 = (bf16[2048,1024]{1,0:T(8,128)(2,1)}, f32[256,1024]{1,0:T(8,128)}) custom-call(bf16[1024,1024]{1,0:T(8,128)(2,1)} %convolution_convert_fusion.3.refs_0_, f32[256,1024]{1,0:T(8,128)} %get-tuple-element.98.refs_1_, f32[6,1024]{1,0:T(8,128)} %refs_29_.1), custom_call_target="tpu_custom_call" | custom-call | flops 57999998976 | bytes 174000000 | tf_op jit(solution)/shard_map/mlp_sum/pallas_call | solution.py:670
  244.8 46.1 %head_stats.1 = (bf16[6400,2048]{1,0:T(8,128)(2,1)}, f32[10,1,2048]{2,1,0:T(1,128)}, f32[10,1,2048]{2,1,0:T(1,128)}, f32[10,1,2048]{2,1,0:T(1,128)}) custom-call(bf16[1280,1024]{1,0:T(8,128)(2,1)} %all-gather.3.cloned.1.call-done.early_ref.refs_1_, bf16[5120,1024]{1,0:T(8,128)(2,1)} %all-gather.5.cloned.1.call-done.late_ref.refs_2_, ...), custom_call_target="tpu_custom_call" | custom-call | flops 26843545600 | bytes 39321600 | tf_op jit(solution)/shard_map/head_stats/pallas_call | solution.py:711
  290.9 1.0 reduce_max.18
  291.8 1.0 fusion.17
  292.8 1.0 reduce_sum.245
  294.4 8.6 %gather_stats.1 = f32[8,48,128]{2,1,0:T(8,128)} custom-call(f32[48,128]{1,0:T(8,128)} %pad_maximum_fusion.6.src_ref), custom_call_target="tpu_custom_call" | custom-call | flops 6000000000 | bytes 18000000 | tf_op jit(solution)/shard_map/gather_stats/pallas_call | solution.py:918
  303.0 1.0 reshape.313
  305.0 0.7 exponential_multiply_fusion.scale_ref
  305.7 33.7 %head_back.1 = (bf16[6400,2048]{1,0:T(8,128)(2,1)}, bf16[6400,1024]{1,0:T(8,128)(2,1)}) custom-call(bf16[6400,2048]{1,0:T(8,128)(2,1)} %get-tuple-element.100.exp_ref, bf16[2048,1024]{1,0:T(8,128)(2,1)} %get-tuple-element.99.final_ref, f32[10,1,2048]{2,1,0:T(1,128)} %exponential_multiply_fusion.scale_ref, f32[1,2048]{1,0:T(1,128)} %bitcast.131, ...), custom_call_target="tpu_custom_call" | custom-call | flops 26843545600 | bytes 65536000 | tf_op jit(solution)/shard_map/head_back/pallas_call | solution.py:753
  340.8 69.4 %final_back.1 = (bf16[1024,1024]{1,0:T(8,128)(2,1)}, f32[256,1024]{1,0:T(8,128)}, f32[8,1024]{1,0:T(8,128)}) custom-call(bf16[6400,2048]{1,0:T(8,128)(2,1)} %get-tuple-element.104.refs_0_, bf16[1280,1024]{1,0:T(8,128)(2,1)} %all-gather.3.cloned.1.call-done.early_ref.refs_1_, bf16[5120,1024]{1,0:T(8,128)(2,1)} %all-gather.5.cloned.1.call-done.late_ref.refs_2_, ...), custom_call_target="tpu_custom_call" | custom-call | flops 65000001536 | bytes 195000000 | tf_op jit(solution)/shard_map/final_back/pallas_call | solution.py:670
  410.3 7.0 %fusion.8 = bf16[1024,1024]{1,0:T(8,128)(2,1)S(1)} fusion(f32[1024,1024]{1,0:T(8,128)S(1)} %copy-done.45, bf16[1024,1024]{1,0:T(8,128)(2,1)} %get-tuple-element.106, bf16[1024,1024]{1,0:T(8,128)(2,1)} %get-tuple-element.97), kind=kOutput, calls=%fused_computation.14 | convolution fusion | flops 2168455168 | bytes 10485760 | tf_op jit(solution)/shard_map/td,fd->tf/dot_general | solution.py:1611
  417.3 3.8 convolution_convert_fusion.1.refs_0_
  421.1 34.2 %mlp_back.1 = (bf16[1024,1024]{1,0:T(8,128)(2,1)}, f32[256,1024]{1,0:T(8,128)}, f32[8,1024]{1,0:T(8,128)}) custom-call(bf16[1024,1024]{1,0:T(8,128)(2,1)} %convolution_convert_fusion.1.refs_0_, f32[256,1024]{1,0:T(8,128)} %get-tuple-element.98.refs_1_, f32[6,1024]{1,0:T(8,128)} %refs_29_.1, f32[256,1024]{1,0:T(8,128)} %get-tuple-element.109.refs_3_), custom_call_target="tpu_custom_call" | custom-call | flops 33999998976 | bytes 102000000 | tf_op jit(solution)/shard_map/mlp_back/pallas_call | solution.py:670
  455.4 2.5 convolution_convert_fusion.9.upstream_ref
  457.9 17.6 %attend_back.1 = bf16[1024,768]{1,0:T(8,128)(2,1)S(1)} custom-call(bf16[1024,768]{1,0:T(8,128)(2,1)S(1)} %copy-done.3, s32[1024,1]{1,0:T(8,128)S(1)} %copy.59.starts_ref, bf16[1024,256]{1,0:T(8,128)(2,1)S(1)} %convolution_convert_fusion.9.upstream_ref), custom_call_target="tpu_custom_call" | custom-call | flops 2684354560 | bytes 3145728 | tf_op jit(solution)/shard_map/attend_back/pallas_call | solution.py:862
  475.5 1.5 convolution_convert_fusion.8.refs_4_
  477.0 3.1 convolution_convert_fusion.5.refs_0_
  480.2 3.1 convolution_convert_fusion.6.refs_6_
  483.2 3.8 convolution_convert_fusion.refs_5_
  487.0 4.1 convolution_convert_fusion.2
  491.1 72.9 %attn_back.1 = (bf16[8192,256]{1,0:T(8,128)(2,1)}, f32[8,1024]{1,0:T(8,128)}, f32[128,256]{1,0:T(8,128)}, f32[256,512]{1,0:T(8,128)}, f32[256,384]{1,0:T(8,128)}...) custom-call(bf16[1024,1024]{1,0:T(8,128)(2,1)} %convolution_convert_fusion.5.refs_0_, ...), custom_call_target="tpu_custom_call" | custom-call | flops 70000001024 | bytes 210000000 | tf_op jit(solution)/shard_map/attn_back/pallas_call | solution.py:670
  564.1 2.9 collective-permute-start.3
  567.6 1.0 slice.118
  568.7 12.0 %scatter.1 = f32[6288,256]{1,0:T(8,128)} custom-call(s32[1]{0:T(128)} %bitcast.2.count_ref, s32[8192]{0:T(1024)} %get-tuple-element.84.key_ref, bf16[6400,256]{1,0:T(8,128)(2,1)} %reduce-scatter.3.cloned.1.call-done.head_ref, bf16[8192,256]{1,0:T(8,128)(2,1)} %get-tuple-element.115.rows_in_ref), custom_call_target="tpu_custom_call" | custom-call | flops 23000000512 | bytes 69000000 | tf_op jit(solution)/shard_map/scatter/pallas_call | solution.py:1341
  580.6 12.5 %collective-permute-done.3 = bf16[128,256]{1,0:T(8,128)(2,1)S(1)} collective-permute-done((bf16[128,256]{1,0:T(8,128)(2,1)}, bf16[128,256]{1,0:T(8,128)(2,1)S(1)}, u32[]{:S(2)}, u32[]{:S(2)}) %collective-permute-start.3) | collective-permute-done | bytes 65568 | tf_op jit(solution)/shard_map/ppermute | solution.py:1667
  593.2 5.5 collective-permute-done.2
  598.7 0.8 fusion.9
  599.5 0.7 fusion.13
  600.2 4.6 fusion
  606.0 0.8 fusion.11
  606.8 17.3 %update_stats.1 = (f32[50,128]{1,0:T(8,128)}, f32[2,128]{1,0:T(2,128)}, f32[1,128]{1,0:T(1,128)}, f32[2,128]{1,0:T(2,128)}, f32[4,128]{1,0:T(4,128)}, /*index=5*...) custom-call(f32[50,128]{1,0:T(8,128)} %pad_bitcast_fusion.1.refs_0_,, ...), custom_call_target="tpu_custom_call" | custom-call | flops 12000000000 | bytes 36000000 | tf_op jit(solution)/shard_map/update_stats/pallas_call | solution.py:1169
  624.1 1.4 fusion.35
  625.5 5.5 multiply_reduce_fusion
  631.0 1.4 multiply_reduce_fusion.1
  632.4 1.4 multiply_reduce_fusion.2
  633.8 1.3 multiply_reduce_fusion.7
  635.2 1.4 multiply_reduce_fusion.5
  636.6 11.0 %clip_rates.1 = f32[8,128]{1,0:T(8,128)} custom-call(f32[2,128]{1,0:T(2,128)} %bitcast.182, f32[3,128]{1,0:T(4,128)} %bitcast.169, f32[2,128]{1,0:T(2,128)} %bitcast.180, f32[4,128]{1,0:T(4,128)} %bitcast.168, f32[2,128]{1,0:T(2,128)} %bitcast.179, f32[16,128]{1,0:T(8,128)} %get-tuple-element.130.refs_5_), custom_call_target="tpu_custom_call" | custom-call | flops 8000000000 | bytes 24000000 | tf_op jit(solution)/shard_map/clip_rates/pallas_call | solution.py:1217
  647.6 1.4 fusion.36
  649.0 2.3 multiply_subtract_fusion.1
  651.3 2.3 multiply_subtract_fusion.2
  653.5 2.0 multiply_subtract_fusion.4
  655.6 2.2 multiply_subtract_fusion.3
  657.8 9.1 %multiply_subtract_fusion = f32[6288,256]{1,0:T(8,128)} fusion(f32[6288,256]{1,0:T(8,128)} %table_ref.1, f32[]{:T(128)} %bitcast.59, f32[6288,256]{1,0:T(8,128)} %scatter.1, f32[]{:T(128)} %bitcast.41, f32[256]{0:T(256)S(1)} %bitcast.160, f32[6288]{0:T(1024)S(1)} %bitcast.123), kind=kLoop, calls=%fused_computation | loop fusion | flops 8048640 | bytes 19342920 | tf_op jit(solution)/shard_map/sub | solution.py:1716
  (180 shorter events, 18.5 us)
Async XLA Ops:
  7.2 10.2 %copy-start.7 = (f32[512,256]{1,0:T(8,128)S(1)}, f32[512,256]{1,0:T(8,128)}, u32[]{:S(2)}) copy-start(f32[512,256]{1,0:T(8,128)} %param.29) | copy-start | bytes 1572868
  7.2 10.8 %copy-start.16 = (f32[128,256]{1,0:T(8,128)S(1)}, f32[128,256]{1,0:T(8,128)}, u32[]{:S(2)}) copy-start(f32[128,256]{1,0:T(8,128)} %param.27) | copy-start | bytes 393220
  7.2 11.5 %copy-start.38 = (s32[2048]{0:T(1024)S(1)}, s32[2048]{0:T(1024)}, u32[]{:S(2)}) copy-start(s32[2048]{0:T(1024)} %param.21) | copy-start | bytes 24580
  7.2 11.5 %copy-start.27 = (s32[2048]{0:T(1024)S(1)}, s32[2048]{0:T(1024)}, u32[]{:S(2)}) copy-start(s32[2048]{0:T(1024)} %param.24) | copy-start | bytes 24580
  7.2 47.8 %all-gather.3.cloned.1.call-start = ((), (), s32[]{:S(2)}) async-start(), calls=%async_computation.2 | async-start | bytes 3276800 | tf_op jit(solution)/shard_map/all_gather | solution.py:1474
  9.6 235.2 %all-gather.5.cloned.1.call-start = ((), (), s32[]{:S(2)}) async-start(), calls=%async_computation.3 | async-start | bytes 13107200 | tf_op jit(solution)/shard_map/all_gather | solution.py:1523
  13.3 40.0 %collective-permute-start = (bf16[256,896]{1,0:T(8,128)(2,1)S(1)}, bf16[256,896]{1,0:T(8,128)(2,1)S(1)}, u32[]{:S(2)}, u32[]{:S(2)}) collective-permute-start(bf16[256,896]{1,0:T(8,128)(2,1)S(1)} %pad_maximum_fusion.2), channel_id=1, source_target_pairs={{0,4},{1,5},{2,6},{3,7},{4,0},{5,1},{6,2},{7,3},{8,12},{9,13},{10,... | collective-permute-start | bytes 1376264 | tf_op jit(solution)/shard_map/ppermute | solution.py:1462
  18.7 33.1 %collective-permute-start.1 = (bf16[640,256]{1,0:T(8,128)(2,1)S(1)}, bf16[640,256]{1,0:T(8,128)(2,1)S(1)}, u32[]{:S(2)}, u32[]{:S(2)}) collective-permute-start(bf16[640,256]{1,0:T(8,128)(2,1)S(1)} %pad_maximum_fusion.4), channel_id=1, source_target_pairs={{0,4},{1,5},{2,6},{3,7},{4,0},{5,1},{6,2},{7,3},{8,12},{9,13},{10,... | collective-permute-start | bytes 983048 | tf_op jit(solution)/shard_map/ppermute | solution.py:1462
  55.0 69.5 %copy-start.40 = (s32[2048]{0:T(1024)S(1)}, s32[2048]{0:T(1024)}, u32[]{:S(2)}) copy-start(s32[2048]{0:T(1024)} %param.23) | copy-start | bytes 24580
  55.0 69.8 %copy-start.37 = (s32[2048]{0:T(1024)S(1)}, s32[2048]{0:T(1024)}, u32[]{:S(2)}) copy-start(s32[2048]{0:T(1024)} %param.22) | copy-start | bytes 24580
  124.1 367.0 %reduce-scatter.3.cloned.1.call-start = ((), (), s32[]{:S(2)}) async-start(), calls=%async_computation.4 | async-start | bytes 16384000 | tf_op jit(solution)/shard_map/reduce_scatter | solution.py:1591
  125.3 4.5 copy-start.41
  129.7 12.4 %copy-start.2 = (bf16[1024,768]{1,0:T(8,128)(2,1)}, bf16[1024,768]{1,0:T(8,128)(2,1)S(1)}, u32[]{:S(2)}) copy-start(bf16[1024,768]{1,0:T(8,128)(2,1)S(1)} %convolution_convert_fusion.7.mixed_ref) | copy-start | bytes 4718596
  129.7 10.3 %copy-start.18 = (bf16[256,1024]{1,0:T(8,128)(2,1)S(1)}, bf16[256,1024]{1,0:T(8,128)(2,1)}, u32[]{:S(2)}) copy-start(bf16[256,1024]{1,0:T(8,128)(2,1)} %get-tuple-element.91) | copy-start | bytes 1572868
  139.3 0.8 copy-start
  142.1 34.3 %copy-start.49 = (bf16[1024,1024]{1,0:T(8,128)(2,1)S(1)}, bf16[1024,1024]{1,0:T(8,128)(2,1)}, u32[]{:S(2)}) copy-start(bf16[1024,1024]{1,0:T(8,128)(2,1)} %get-tuple-element.94) | copy-start | bytes 6291460
  176.4 4.2 copy-start.53
  180.6 4.1 copy-start.44
  294.4 10.6 %copy-start.13 = (f32[10,1,2048]{2,1,0:T(1,128)S(1)}, f32[10,1,2048]{2,1,0:T(1,128)}, u32[]{:S(2)}) copy-start(f32[10,1,2048]{2,1,0:T(1,128)} %get-tuple-element.101) | copy-start | bytes 245764
  305.0 0.7 copy-start.23
  339.5 0.7 copy-start.28
  339.5 228.1 %reduce-scatter.5.cloned.1.call-start = ((), (), s32[]{:S(2)}) async-start(), calls=%async_computation.5 | async-start | bytes 2621440 | tf_op jit(solution)/shard_map/reduce_scatter | solution.py:1610
  340.8 69.5 %copy-start.45 = (f32[1024,1024]{1,0:T(8,128)S(1)}, f32[1024,1024]{1,0:T(8,128)}, u32[]{:S(2)}) copy-start(f32[1024,1024]{1,0:T(8,128)} %copy-done.44) | copy-start | bytes 12582916
  410.3 7.0 %copy-start.50 = (bf16[1024,1024]{1,0:T(8,128)(2,1)S(1)}, bf16[1024,1024]{1,0:T(8,128)(2,1)}, u32[]{:S(2)}) copy-start(bf16[1024,1024]{1,0:T(8,128)(2,1)} %get-tuple-element.94) | copy-start | bytes 6291460
  421.1 34.2 %copy-start.19 = (bf16[256,1024]{1,0:T(8,128)(2,1)S(1)}, bf16[256,1024]{1,0:T(8,128)(2,1)}, u32[]{:S(2)}) copy-start(bf16[256,1024]{1,0:T(8,128)(2,1)} %get-tuple-element.91) | copy-start | bytes 1572868
  455.3 2.5 copy-start.3
  457.9 17.6 %copy-start.1 = (bf16[1024,256]{1,0:T(8,128)(2,1)S(1)}, bf16[1024,256]{1,0:T(8,128)(2,1)}, u32[]{:S(2)}) copy-start(bf16[1024,256]{1,0:T(8,128)(2,1)} %copy-done) | copy-start | bytes 1572868
  457.9 17.6 %copy-start.10 = (bf16[1024,1024]{1,0:T(8,128)(2,1)S(1)}, bf16[1024,1024]{1,0:T(8,128)(2,1)}, u32[]{:S(2)}) copy-start(bf16[1024,1024]{1,0:T(8,128)(2,1)} %get-tuple-element.110) | copy-start | bytes 6291460
  457.9 19.1 %copy-start.48 = (bf16[1024,768]{1,0:T(8,128)(2,1)S(1)}, bf16[1024,768]{1,0:T(8,128)(2,1)}, u32[]{:S(2)}) copy-start(bf16[1024,768]{1,0:T(8,128)(2,1)} %get-tuple-element.90) | copy-start | bytes 4718596
  477.0 3.1 copy-start.47
  480.2 3.1 copy-start.51
  483.2 3.8 copy-start.46
  483.2 3.8 copy-start.52
  491.1 75.9 %copy-start.42 = (f32[4]{0:T(128)S(1)}, f32[4]{0:T(128)}, u32[]{:S(2)}) copy-start(f32[4]{0:T(128)} %get-tuple-element.154) | copy-start | bytes 52
  564.1 29.1 %collective-permute-start.4 = (bf16[256,896]{1,0:T(8,128)(2,1)}, bf16[256,896]{1,0:T(8,128)(2,1)S(1)}, u32[]{:S(2)}, u32[]{:S(2)}) collective-permute-start(bf16[256,896]{1,0:T(8,128)(2,1)} %get-tuple-element.113), channel_id=1, source_target_pairs={{0,4},{1,5},{2,6},{3,7},{4,0},{5,1},{6,2},{7,3},{8,12},{9,13},{10,... | collective-permute-start | bytes 1376264 | tf_op jit(solution)/shard_map/ppermute | solution.py:1667
  564.1 29.0 %collective-permute-start.3 = (bf16[128,256]{1,0:T(8,128)(2,1)}, bf16[128,256]{1,0:T(8,128)(2,1)S(1)}, u32[]{:S(2)}, u32[]{:S(2)}) collective-permute-start(bf16[128,256]{1,0:T(8,128)(2,1)} %get-tuple-element.112), channel_id=1, source_target_pairs={{0,4},{1,5},{2,6},{3,7},{4,0},{5,1},{6,2},{7,3},{8,12},{9,13},{10,... | collective-permute-start | bytes 196616 | tf_op jit(solution)/shard_map/ppermute | solution.py:1667
  568.5 30.1 %collective-permute-start.2 = (bf16[512,256]{1,0:T(8,128)(2,1)S(1)}, bf16[512,256]{1,0:T(8,128)(2,1)S(1)}, u32[]{:S(2)}, u32[]{:S(2)}) collective-permute-start(bf16[512,256]{1,0:T(8,128)(2,1)S(1)} %slice.118), channel_id=1, source_target_pairs={{0,4},{1,5},{2,6},{3,7},{4,0},{5,1},{6,2},{7,3},{8,12},{9,13},{10,... | collective-permute-start | bytes 786440 | tf_op jit(solution)/shard_map/ppermute | solution.py:1667
  568.7 30.0 %copy-start.15 = (f32[256,512]{1,0:T(8,128)S(1)}, f32[256,512]{1,0:T(8,128)}, u32[]{:S(2)}) copy-start(f32[256,512]{1,0:T(8,128)} %get-tuple-element.121) | copy-start | bytes 1572868
  568.7 30.8 %copy-start.20 = (f32[256,384]{1,0:T(8,128)S(1)}, f32[256,384]{1,0:T(8,128)}, u32[]{:S(2)}) copy-start(f32[256,384]{1,0:T(8,128)} %get-tuple-element.117) | copy-start | bytes 1179652
  598.7 6.7 copy-start.22
  599.4 51.8 %copy-start.5 = (f32[256,512]{1,0:T(8,128)}, f32[256,512]{1,0:T(8,128)S(1)}, u32[]{:S(2)}) copy-start(f32[256,512]{1,0:T(8,128)S(1)} %get-tuple-element.228) | copy-start | bytes 1572868
  599.5 6.6 copy-start.14
  600.2 55.4 %copy-start.6 = (f32[256,384]{1,0:T(8,128)}, f32[256,384]{1,0:T(8,128)S(1)}, u32[]{:S(2)}) copy-start(f32[256,384]{1,0:T(8,128)S(1)} %get-tuple-element.220) | copy-start | bytes 1179652
  606.0 47.5 %copy-start.12 = (f32[128,256]{1,0:T(8,128)}, f32[128,256]{1,0:T(8,128)S(1)}, u32[]{:S(2)}) copy-start(f32[128,256]{1,0:T(8,128)S(1)} %get-tuple-element.224) | copy-start | bytes 393220
  606.8 42.2 %copy-start.4 = (f32[512,256]{1,0:T(8,128)}, f32[512,256]{1,0:T(8,128)S(1)}, u32[]{:S(2)}) copy-start(f32[512,256]{1,0:T(8,128)S(1)} %get-tuple-element.232) | copy-start | bytes 1572868
  624.1 7.0 %copy-start.29 = (f32[4,128]{1,0:T(4,128)S(1)}, f32[4,128]{1,0:T(4,128)}, u32[]{:S(2)}) copy-start(f32[4,128]{1,0:T(4,128)} %get-tuple-element.137) | copy-start | bytes 6148
  624.1 6.9 %copy-start.32 = (f32[2,128]{1,0:T(2,128)S(1)}, f32[2,128]{1,0:T(2,128)}, u32[]{:S(2)}) copy-start(f32[2,128]{1,0:T(2,128)} %get-tuple-element.138) | copy-start | bytes 3076
  624.1 8.3 %copy-start.30 = (f32[4,128]{1,0:T(4,128)S(1)}, f32[4,128]{1,0:T(4,128)}, u32[]{:S(2)}) copy-start(f32[4,128]{1,0:T(4,128)} %get-tuple-element.136) | copy-start | bytes 6148
  624.1 8.3 %copy-start.33 = (f32[2,128]{1,0:T(2,128)S(1)}, f32[2,128]{1,0:T(2,128)}, u32[]{:S(2)}) copy-start(f32[2,128]{1,0:T(2,128)} %get-tuple-element.135) | copy-start | bytes 3076
  624.1 9.7 %copy-start.34 = (f32[2,128]{1,0:T(2,128)S(1)}, f32[2,128]{1,0:T(2,128)}, u32[]{:S(2)}) copy-start(f32[2,128]{1,0:T(2,128)} %get-tuple-element.134) | copy-start | bytes 3076
  624.1 9.7 %copy-start.39 = (f32[1,128]{1,0:T(1,128)S(1)}, f32[1,128]{1,0:T(1,128)}, u32[]{:S(2)}) copy-start(f32[1,128]{1,0:T(1,128)} %get-tuple-element.133) | copy-start | bytes 1540
  624.1 11.0 %copy-start.31 = (f32[3,128]{1,0:T(4,128)S(1)}, f32[3,128]{1,0:T(4,128)}, u32[]{:S(2)}) copy-start(f32[3,128]{1,0:T(4,128)} %get-tuple-element.132) | copy-start | bytes 4612
  624.1 11.0 %copy-start.35 = (f32[2,128]{1,0:T(2,128)S(1)}, f32[2,128]{1,0:T(2,128)}, u32[]{:S(2)}) copy-start(f32[2,128]{1,0:T(2,128)} %get-tuple-element.131) | copy-start | bytes 3076
  636.5 12.4 %copy-start.8 = (f32[512,256]{1,0:T(8,128)S(1)}, f32[512,256]{1,0:T(8,128)}, u32[]{:S(2)}) copy-start(f32[512,256]{1,0:T(8,128)} %param.29) | copy-start | bytes 1572868
  636.6 14.7 %copy-start.9 = (f32[256,512]{1,0:T(8,128)S(1)}, f32[256,512]{1,0:T(8,128)}, u32[]{:S(2)}) copy-start(f32[256,512]{1,0:T(8,128)} %param.28) | copy-start | bytes 1572868
  636.6 17.0 %copy-start.17 = (f32[128,256]{1,0:T(8,128)S(1)}, f32[128,256]{1,0:T(8,128)}, u32[]{:S(2)}) copy-start(f32[128,256]{1,0:T(8,128)} %param.27) | copy-start | bytes 393220
  636.6 19.0 %copy-start.11 = (f32[256,384]{1,0:T(8,128)S(1)}, f32[256,384]{1,0:T(8,128)}, u32[]{:S(2)}) copy-start(f32[256,384]{1,0:T(8,128)} %param.26) | copy-start | bytes 1179652
  647.6 10.2 %copy-start.21 = (f32[50,128]{1,0:T(8,128)S(1)}, f32[50,128]{1,0:T(8,128)}, u32[]{:S(2)}) copy-start(f32[50,128]{1,0:T(8,128)} %get-tuple-element.128) | copy-start | bytes 76804
  647.6 10.2 %copy-start.36 = (f32[2,128]{1,0:T(2,128)S(1)}, f32[2,128]{1,0:T(2,128)}, u32[]{:S(2)}) copy-start(f32[2,128]{1,0:T(2,128)} %get-tuple-element.129) | copy-start | bytes 3076
  657.8 9.1 %copy-start.43 = (f32[1,128]{1,0:T(1,128)S(1)}, f32[1,128]{1,0:T(1,128)}, u32[]{:S(2)}) copy-start(f32[1,128]{1,0:T(1,128)} %get-tuple-element.127) | copy-start | bytes 1540
  657.8 15.3 %copy-start.26 = (f32[6,1024]{1,0:T(8,128)S(1)}, f32[6,1024]{1,0:T(8,128)}, u32[]{:S(2)}) copy-start(f32[6,1024]{1,0:T(8,128)} %get-tuple-element.236) | copy-start | bytes 73732
  657.8 15.9 %copy-start.25 = (f32[6,1024]{1,0:T(8,128)S(1)}, f32[6,1024]{1,0:T(8,128)}, u32[]{:S(2)}) copy-start(f32[6,1024]{1,0:T(8,128)} %get-tuple-element.237) | copy-start | bytes 73732
  657.8 16.5 %copy-start.24 = (f32[6,1024]{1,0:T(8,128)S(1)}, f32[6,1024]{1,0:T(8,128)}, u32[]{:S(2)}) copy-start(f32[6,1024]{1,0:T(8,128)} %get-tuple-element.238) | copy-start | bytes 73732
Sparse Core Ops, SparseCore 0:
  9.9 43.5 all-gather.2
  124.2 108.9 all-gather.4
  339.6 124.8 reduce-scatter.2
  491.2 51.8 reduce-scatter.4

commit v9 on v8

--- a/solution.py
+++ b/solution.py
@@ -677,27 +677,35 @@
     valid = place < edge_ref[0]
     table = jnp.where(j < early, early_ref[...], late_ref[...])
 
-    def one(i, carry):
-        at = pl.ds(i * tile, tile)
-        logits = lax.dot_general(
-            table,
-            final_ref[at, :],
-            (((1,), (1,)), ((), ())),
-            preferred_element_type=jnp.float32,
-        )
-        logits = jnp.where(valid, logits, MASKED)
-        top = jnp.max(logits, axis=0, keepdims=True)
-        weights = jnp.exp(logits - top)
-        exp_ref[:, at] = weights.astype(jnp.bfloat16)
-        top_ref[0, :, at] = top
-        sum_ref[0, :, at] = jnp.sum(weights, axis=0, keepdims=True)
-        pick_ref[0, :, at] = jnp.sum(
-            jnp.where(place == wanted_ref[:, at], logits, 0.0), axis=0, keepdims=True
-        )
-        return carry
-
-    for i in range(tokens // tile):
-        one(i, 0)
+    def weigh(masked):
+        for start in range(0, tokens, tile):
+            at = pl.ds(start, tile)
+            logits = lax.dot_general(
+                table,
+                final_ref[at, :],
+                (((1,), (1,)), ((), ())),
+                preferred_element_type=jnp.float32,
+            )
+            if masked:
+                logits = jnp.where(valid, logits, MASKED)
+            top = jnp.max(logits, axis=0, keepdims=True)
+            weights = jnp.exp(logits - top)
+            exp_ref[:, at] = weights.astype(jnp.bfloat16)
+            top_ref[0, :, at] = top
+            sum_ref[0, :, at] = jnp.sum(weights, axis=0, keepdims=True)
+            pick_ref[0, :, at] = jnp.sum(
+                jnp.where(place == wanted_ref[:, at], logits, 0.0), axis=0, keepdims=True
+            )
+
+    whole = (j + 1) * block <= edge_ref[0]
+
+    @pl.when(whole)
+    def _():
+        weigh(False)
+
+    @pl.when(jnp.logical_not(whole))
+    def _():
+        weigh(True)
 
 
 def head_stats(tables, final, wanted, edge, block, tile=512):
@@ -1271,15 +1279,17 @@
     def lower(i, total):
         at = pl.ds(pl.multiple_of(i * strip, strip), strip)
         values = table_ref[at, :]
-
-        @pl.when(i >= early // strip)
-        def _():
-            start = pl.multiple_of(i * strip - early, 16)
-            low_ref[pl.ds(start, strip), :] = values.astype(jnp.bfloat16)
-
+        start = pl.multiple_of(i * strip - early, strip)
+        low_ref[pl.ds(start, strip), :] = values.astype(jnp.bfloat16)
         return squares(values, total)
 
-    total = lax.fori_loop(0, done // strip, lower, jnp.zeros((8, width), jnp.float32))
+    def square(i, total):
+        at = pl.ds(pl.multiple_of(i * strip, strip), strip)
+        return squares(table_ref[at, :], total)
+
+    total = jnp.zeros((8, width), jnp.float32)
+    total = lax.fori_loop(0, early // strip, square, total)
+    total = lax.fori_loop(early // strip, done // strip, lower, total)
     if rest:
         values = table_ref[done:, :]
         total = squares(values, total)
@@ -1606,12 +1616,11 @@
         product=True,
     )
     grad_proj = jnp.einsum("tf,td->fd", hidden, dbranch2, preferred_element_type=f32).astype(bf16)
-    grad_proj, head_grad = lax.optimization_barrier((grad_proj, head_grad))
-    grad_proj = lax.psum_scatter(grad_proj, "dp", scatter_dimension=1, tiled=True)
     dhidden = jnp.einsum("td,fd->tf", dbranch2, wide_proj, preferred_element_type=f32)
     unused, gelu_pull = jax.vjp(gelu_tanh, before)
     dbefore = gelu_pull(dhidden)[0].astype(bf16)
     partial = jnp.einsum("tf,df->td", dbefore, wide_fc, preferred_element_type=f32).astype(bf16)
+    partial, grad_proj = lax.optimization_barrier((partial, grad_proj))
     dbranch1, dstream1, norm2 = line_call(
         "mlp_back",
         7,
@@ -1626,6 +1635,8 @@
         near,
         34,
     )
+    grad_proj, head_grad = lax.optimization_barrier((grad_proj, head_grad))
+    grad_proj = lax.psum_scatter(grad_proj, "dp", scatter_dimension=1, tiled=True)
     grad_fc = jnp.einsum("td,tf->df", inner_two, dbefore, preferred_element_type=f32).astype(bf16)
     grad_out = jnp.einsum("tf,td->fd", attended, dbranch1, preferred_element_type=f32).astype(bf16)
     dattended = jnp.einsum("td,fd->tf", dbranch1, wide_out, preferred_element_type=f32)

time: 688 us -> 689 us (level)
  transfers between devices with their start and end apart: 9 -> 9, of which waited for: 3 -> 3; matrix products, arithmetic and copies ran while one was open for 9% -> 9% of each run, Pallas kernels for 48% -> 49%
where the time goes in v9:
time: 689 us; the launch traced here: 682 us
  Pallas kernels  518 us (75%)
  other arithmetic  58.1 us (8%)
  matrix products  43 us (6%)
  local copies, waits for them, and re-layouts  20.6 us (3%)
  waiting for transfers between devices  20.3 us (3%)
  between operations  14.7 us (2%)
  starting transfers between devices  7.77 us (1%)
    pallas_call x6, Pallas kernels, line_call(): return list(call(*args))  339 us
    pallas_call x1, Pallas kernels, head_stats(): pl.pallas_call(functools.partial(head_stats_kernel, block, tile, early),...  46.9 us
    pallas_call x1, Pallas kernels, head_back(): pl.pallas_call(functools.partial(head_back_kernel, block, tile), grid=(ro...  33.7 us
    sub x5, other arithmetic, local(): updated = [weights[n] - factors[n, 0] * steps[n] for n in range(5)]  17.8 us
    pallas_call x1, Pallas kernels, attend_back(): pl.pallas_call(attend_back_kernel, grid=(pairs,), out_shape=jax.ShapeDtyp...  17.6 us
    pallas_call x1, Pallas kernels, update_stats(): pl.pallas_call(functools.partial(stats_kernel, full, size_dp, size_mp), o...  17.1 us
    ppermute x3, waiting for transfers between devices, from_twins(): found.append(lax.ppermute(jnp.concatenate(pieces, axis=axis), 'mp', back))  17.1 us
    pallas_call x2, Pallas kernels, small_gather(): pl.pallas_call(functools.partial(small_gather_kernel, axis, count), out_s...  15.9 us
  transfers between devices with their start and end apart: 9, of which 3 were waited for; matrix products, arithmetic and copies ran while one was open for 9% of the time, Pallas kernels for 49%

profile of v9, /device:TPU:0, one launch (start us, length us, event | category | flops | bytes accessed | tf_op | source)
XLA Modules:
  0.0 682.3 jit_solution(14269609811770968678)
XLA Ops:
  7.3 2.3 slice.129
  9.6 1.9 multiply_reduce_fusion.4
  11.5 1.8 multiply_reduce_fusion.6
  13.3 4.1 collective-permute-start
  19.4 7.3 %gather_ids.1 = s32[4,32,128]{2,1,0:T(8,128)} custom-call(s32[32,128]{1,0:T(8,128)} %reshape.306.src_ref), custom_call_target="tpu_custom_call" | custom-call | flops 6000000000 | bytes 18000000 | tf_op jit(solution)/shard_map/gather_ids/pallas_call | solution.py:926
  26.7 0.9 reshape.307
  28.5 6.8 sort.14
  35.2 13.4 %lookup.1 = (bf16[8192,256]{1,0:T(8,128)(2,1)}, bf16[5120,256]{1,0:T(8,128)(2,1)}, f32[8,128]{1,0:T(8,128)}) custom-call(s32[1]{0:T(128)} %bitcast.2.count_ref, s32[8192]{0:T(1024)} %get-tuple-element.86.key_ref, f32[6288,256]{1,0:T(8,128)} %table_ref.1), custom_call_target="tpu_custom_call" | custom-call | flops 20000000000 | bytes 60000000 | tf_op jit(solution)/shard_map/lookup/pallas_call | solution.py:1308
  48.7 3.1 collective-permute-done.1
  52.5 0.8 pad_maximum_fusion.1.refs_5_
  53.4 0.8 pad_maximum_fusion.3.refs_2_
  54.2 0.9 pad_maximum_fusion.refs_4_
  55.0 69.1 %lookup_sum.1 = (bf16[1024,1024]{1,0:T(8,128)(2,1)}, bf16[256,1024]{1,0:T(8,128)(2,1)}, bf16[1024,768]{1,0:T(8,128)(2,1)}, bf16[256,1024]{1,0:T(8,128)(2,1)}, bf...) custom-call(bf16[8192,256]{1,0:T(8,128)(2,1)} %get-tuple-element.90.refs_0_, f32[6,1024]{1,0:T(8,128)} %refs_29_.1, ...), custom_call_target="tpu_custom_call" | custom-call | flops 70000001024 | bytes 210000000 | tf_op jit(solution)/shard_map/lookup_sum/pallas_call | solution.py:670
  125.9 3.8 convolution_convert_fusion.7.mixed_ref
  129.7 9.5 %attend.1 = bf16[1024,256]{1,0:T(8,128)(2,1)S(1)} custom-call(bf16[1024,768]{1,0:T(8,128)(2,1)S(1)} %convolution_convert_fusion.7.mixed_ref, s32[1024,1]{1,0:T(8,128)S(1)} %copy.59.starts_ref), custom_call_target="tpu_custom_call" | custom-call | flops 1073741824 | bytes 1572864 | tf_op jit(solution)/shard_map/attend/pallas_call | solution.py:822
  139.3 0.8 copy-done
  140.1 2.0 convolution_convert_fusion.4.refs_0_
  142.1 34.2 %attn_sum.1 = (bf16[1024,1024]{1,0:T(8,128)(2,1)}, f32[256,1024]{1,0:T(8,128)}) custom-call(bf16[1024,1024]{1,0:T(8,128)(2,1)} %convolution_convert_fusion.4.refs_0_, bf16[256,1024]{1,0:T(8,128)(2,1)} %get-tuple-element.96.refs_1_, f32[6,1024]{1,0:T(8,128)} %refs_29_.1), custom_call_target="tpu_custom_call" | custom-call | flops 32000000000 | bytes 96000000 | tf_op jit(solution)/shard_map/attn_sum/pallas_call | solution.py:670
  176.3 4.2 fusion.37
  180.5 4.0 convolution_convert_fusion.3.refs_0_
  184.6 59.5 %mlp_sum.1 = (bf16[2048,1024]{1,0:T(8,128)(2,1)}, f32[256,1024]{1,0:T(8,128)}) custom-call(bf16[1024,1024]{1,0:T(8,128)(2,1)} %convolution_convert_fusion.3.refs_0_, f32[256,1024]{1,0:T(8,128)} %get-tuple-element.100.refs_1_, f32[6,1024]{1,0:T(8,128)} %refs_29_.1), custom_call_target="tpu_custom_call" | custom-call | flops 57999998976 | bytes 174000000 | tf_op jit(solution)/shard_map/mlp_sum/pallas_call | solution.py:670
  244.1 46.9 %head_stats.1 = (bf16[6400,2048]{1,0:T(8,128)(2,1)}, f32[10,1,2048]{2,1,0:T(1,128)}, f32[10,1,2048]{2,1,0:T(1,128)}, f32[10,1,2048]{2,1,0:T(1,128)}) custom-call(bf16[1280,1024]{1,0:T(8,128)(2,1)} %all-gather.3.cloned.1.call-done.early_ref.refs_1_, bf16[5120,1024]{1,0:T(8,128)(2,1)} %all-gather.5.cloned.1.call-done.late_ref.refs_2_, ...), custom_call_target="tpu_custom_call" | custom-call | flops 26843545600 | bytes 39321600 | tf_op jit(solution)/shard_map/head_stats/pallas_call | solution.py:719
  291.0 1.0 reduce_max.18
  291.9 1.0 fusion.17
  293.0 1.0 reduce_sum.245
  294.5 8.7 %gather_stats.1 = f32[8,48,128]{2,1,0:T(8,128)} custom-call(f32[48,128]{1,0:T(8,128)} %pad_maximum_fusion.6.src_ref), custom_call_target="tpu_custom_call" | custom-call | flops 6000000000 | bytes 18000000 | tf_op jit(solution)/shard_map/gather_stats/pallas_call | solution.py:926
  303.2 1.0 reshape.313
  305.1 0.7 exponential_multiply_fusion.scale_ref
  305.9 33.7 %head_back.1 = (bf16[6400,2048]{1,0:T(8,128)(2,1)}, bf16[6400,1024]{1,0:T(8,128)(2,1)}) custom-call(bf16[6400,2048]{1,0:T(8,128)(2,1)} %get-tuple-element.102.exp_ref, bf16[2048,1024]{1,0:T(8,128)(2,1)} %get-tuple-element.101.final_ref, f32[10,1,2048]{2,1,0:T(1,128)} %exponential_multiply_fusion.scale_ref, f32[1,2048]{1,0:T(1,128)} %bitcast.131, ...), custom_call_target="tpu_custom_call" | custom-call | flops 26843545600 | bytes 65536000 | tf_op jit(solution)/shard_map/head_back/pallas_call | solution.py:761
  341.0 69.3 %final_back.1 = (bf16[1024,1024]{1,0:T(8,128)(2,1)}, f32[256,1024]{1,0:T(8,128)}, f32[8,1024]{1,0:T(8,128)}) custom-call(bf16[6400,2048]{1,0:T(8,128)(2,1)} %get-tuple-element.106.refs_0_, bf16[1280,1024]{1,0:T(8,128)(2,1)} %all-gather.3.cloned.1.call-done.early_ref.refs_1_, bf16[5120,1024]{1,0:T(8,128)(2,1)} %all-gather.5.cloned.1.call-done.late_ref.refs_2_, ...), custom_call_target="tpu_custom_call" | custom-call | flops 65000001536 | bytes 195000000 | tf_op jit(solution)/shard_map/final_back/pallas_call | solution.py:670
  410.3 7.0 %fusion.8 = bf16[1024,1024]{1,0:T(8,128)(2,1)S(1)} fusion(f32[1024,1024]{1,0:T(8,128)S(1)} %copy-done.45, bf16[1024,1024]{1,0:T(8,128)(2,1)} %get-tuple-element.108, bf16[1024,1024]{1,0:T(8,128)(2,1)} %get-tuple-element.99), kind=kOutput, calls=%fused_computation.14 | convolution fusion | flops 2168455168 | bytes 10485760 | tf_op jit(solution)/shard_map/td,fd->tf/dot_general | solution.py:1619
  417.4 3.8 convolution_convert_fusion.2.refs_0_
  421.1 4.1 convolution_convert_fusion.1
  425.2 34.5 %mlp_back.1 = (bf16[1024,1024]{1,0:T(8,128)(2,1)}, f32[256,1024]{1,0:T(8,128)}, f32[8,1024]{1,0:T(8,128)}) custom-call(bf16[1024,1024]{1,0:T(8,128)(2,1)} %convolution_convert_fusion.2.refs_0_, f32[256,1024]{1,0:T(8,128)} %get-tuple-element.100.refs_1_, f32[6,1024]{1,0:T(8,128)} %refs_29_.1, f32[256,1024]{1,0:T(8,128)} %get-tuple-element.113.refs_3_), custom_call_target="tpu_custom_call" | custom-call | flops 33999998976 | bytes 102000000 | tf_op jit(solution)/shard_map/mlp_back/pallas_call | solution.py:670
  459.8 2.5 convolution_convert_fusion.9.upstream_ref
  462.4 17.6 %attend_back.1 = bf16[1024,768]{1,0:T(8,128)(2,1)S(1)} custom-call(bf16[1024,768]{1,0:T(8,128)(2,1)S(1)} %copy-done.3, s32[1024,1]{1,0:T(8,128)S(1)} %copy.59.starts_ref, bf16[1024,256]{1,0:T(8,128)(2,1)S(1)} %convolution_convert_fusion.9.upstream_ref), custom_call_target="tpu_custom_call" | custom-call | flops 2684354560 | bytes 3145728 | tf_op jit(solution)/shard_map/attend_back/pallas_call | solution.py:870
  479.9 1.5 convolution_convert_fusion.8.refs_4_
  481.5 3.1 convolution_convert_fusion.5.refs_0_
  484.6 3.1 convolution_convert_fusion.6.refs_6_
  487.7 3.8 convolution_convert_fusion.refs_5_
  491.5 72.6 %attn_back.1 = (bf16[8192,256]{1,0:T(8,128)(2,1)}, f32[8,1024]{1,0:T(8,128)}, f32[128,256]{1,0:T(8,128)}, f32[256,512]{1,0:T(8,128)}, f32[256,384]{1,0:T(8,128)}...) custom-call(bf16[1024,1024]{1,0:T(8,128)(2,1)} %convolution_convert_fusion.5.refs_0_, ...), custom_call_target="tpu_custom_call" | custom-call | flops 70000001024 | bytes 210000000 | tf_op jit(solution)/shard_map/attn_back/pallas_call | solution.py:670
  564.2 2.9 collective-permute-start.3
  567.7 1.0 slice.118
  568.8 13.5 %scatter.1 = f32[6288,256]{1,0:T(8,128)} custom-call(s32[1]{0:T(128)} %bitcast.2.count_ref, s32[8192]{0:T(1024)} %get-tuple-element.86.key_ref, bf16[6400,256]{1,0:T(8,128)(2,1)} %reduce-scatter.3.cloned.1.call-done.head_ref, bf16[8192,256]{1,0:T(8,128)(2,1)} %get-tuple-element.119.rows_in_ref), custom_call_target="tpu_custom_call" | custom-call | flops 23000000512 | bytes 69000000 | tf_op jit(solution)/shard_map/scatter/pallas_call | solution.py:1351
  582.3 11.5 %collective-permute-done.3 = bf16[128,256]{1,0:T(8,128)(2,1)S(1)} collective-permute-done((bf16[128,256]{1,0:T(8,128)(2,1)}, bf16[128,256]{1,0:T(8,128)(2,1)S(1)}, u32[]{:S(2)}, u32[]{:S(2)}) %collective-permute-start.3) | collective-permute-done | bytes 65568 | tf_op jit(solution)/shard_map/ppermute | solution.py:1678
  593.8 5.5 collective-permute-done.2
  599.3 0.8 fusion.9
  600.1 0.7 fusion.13
  600.8 4.6 fusion
  606.7 0.8 fusion.11
  607.4 17.1 %update_stats.1 = (f32[50,128]{1,0:T(8,128)}, f32[2,128]{1,0:T(2,128)}, f32[1,128]{1,0:T(1,128)}, f32[2,128]{1,0:T(2,128)}, f32[4,128]{1,0:T(4,128)}, /*index=5*...) custom-call(f32[50,128]{1,0:T(8,128)} %pad_bitcast_fusion.1.refs_0_,, ...), custom_call_target="tpu_custom_call" | custom-call | flops 12000000000 | bytes 36000000 | tf_op jit(solution)/shard_map/update_stats/pallas_call | solution.py:1177
  624.7 1.4 fusion.35
  626.0 5.7 multiply_reduce_fusion
  631.7 1.4 multiply_reduce_fusion.1
  633.1 1.4 multiply_reduce_fusion.2
  634.5 1.3 multiply_reduce_fusion.7
  635.9 1.4 multiply_reduce_fusion.5
  637.2 11.0 %clip_rates.1 = f32[8,128]{1,0:T(8,128)} custom-call(f32[2,128]{1,0:T(2,128)} %bitcast.182, f32[3,128]{1,0:T(4,128)} %bitcast.169, f32[2,128]{1,0:T(2,128)} %bitcast.180, f32[4,128]{1,0:T(4,128)} %bitcast.168, f32[2,128]{1,0:T(2,128)} %bitcast.179, f32[16,128]{1,0:T(8,128)} %get-tuple-element.134.refs_5_), custom_call_target="tpu_custom_call" | custom-call | flops 8000000000 | bytes 24000000 | tf_op jit(solution)/shard_map/clip_rates/pallas_call | solution.py:1225
  648.3 1.4 fusion.36
  649.7 2.3 multiply_subtract_fusion.1
  651.9 2.3 multiply_subtract_fusion.2
  654.2 2.0 multiply_subtract_fusion.4
  656.3 2.2 multiply_subtract_fusion.3
  658.5 9.1 %multiply_subtract_fusion = f32[6288,256]{1,0:T(8,128)} fusion(f32[6288,256]{1,0:T(8,128)} %table_ref.1, f32[]{:T(128)} %bitcast.59, f32[6288,256]{1,0:T(8,128)} %scatter.1, f32[]{:T(128)} %bitcast.41, f32[256]{0:T(256)S(1)} %bitcast.160, f32[6288]{0:T(1024)S(1)} %bitcast.123), kind=kLoop, calls=%fused_computation | loop fusion | flops 8048640 | bytes 19342920 | tf_op jit(solution)/shard_map/sub | solution.py:1727
  (178 shorter events, 18.5 us)
Async XLA Ops:
  7.2 10.2 %copy-start.7 = (f32[512,256]{1,0:T(8,128)S(1)}, f32[512,256]{1,0:T(8,128)}, u32[]{:S(2)}) copy-start(f32[512,256]{1,0:T(8,128)} %param.29) | copy-start | bytes 1572868
  7.2 10.8 %copy-start.16 = (f32[128,256]{1,0:T(8,128)S(1)}, f32[128,256]{1,0:T(8,128)}, u32[]{:S(2)}) copy-start(f32[128,256]{1,0:T(8,128)} %param.27) | copy-start | bytes 393220
  7.2 11.5 %copy-start.38 = (s32[2048]{0:T(1024)S(1)}, s32[2048]{0:T(1024)}, u32[]{:S(2)}) copy-start(s32[2048]{0:T(1024)} %param.21) | copy-start | bytes 24580
  7.2 11.5 %copy-start.27 = (s32[2048]{0:T(1024)S(1)}, s32[2048]{0:T(1024)}, u32[]{:S(2)}) copy-start(s32[2048]{0:T(1024)} %param.24) | copy-start | bytes 24580
  7.2 47.8 %all-gather.3.cloned.1.call-start = ((), (), s32[]{:S(2)}) async-start(), calls=%async_computation.2 | async-start | bytes 3276800 | tf_op jit(solution)/shard_map/all_gather | solution.py:1484
  9.6 234.5 %all-gather.5.cloned.1.call-start = ((), (), s32[]{:S(2)}) async-start(), calls=%async_computation.3 | async-start | bytes 13107200 | tf_op jit(solution)/shard_map/all_gather | solution.py:1533
  13.3 40.0 %collective-permute-start = (bf16[256,896]{1,0:T(8,128)(2,1)S(1)}, bf16[256,896]{1,0:T(8,128)(2,1)S(1)}, u32[]{:S(2)}, u32[]{:S(2)}) collective-permute-start(bf16[256,896]{1,0:T(8,128)(2,1)S(1)} %pad_maximum_fusion.2), channel_id=1, source_target_pairs={{0,4},{1,5},{2,6},{3,7},{4,0},{5,1},{6,2},{7,3},{8,12},{9,13},{10,... | collective-permute-start | bytes 1376264 | tf_op jit(solution)/shard_map/ppermute | solution.py:1472
  18.7 33.1 %collective-permute-start.1 = (bf16[640,256]{1,0:T(8,128)(2,1)S(1)}, bf16[640,256]{1,0:T(8,128)(2,1)S(1)}, u32[]{:S(2)}, u32[]{:S(2)}) collective-permute-start(bf16[640,256]{1,0:T(8,128)(2,1)S(1)} %pad_maximum_fusion.4), channel_id=1, source_target_pairs={{0,4},{1,5},{2,6},{3,7},{4,0},{5,1},{6,2},{7,3},{8,12},{9,13},{10,... | collective-permute-start | bytes 983048 | tf_op jit(solution)/shard_map/ppermute | solution.py:1472
  55.0 69.5 %copy-start.40 = (s32[2048]{0:T(1024)S(1)}, s32[2048]{0:T(1024)}, u32[]{:S(2)}) copy-start(s32[2048]{0:T(1024)} %param.23) | copy-start | bytes 24580
  55.0 69.8 %copy-start.37 = (s32[2048]{0:T(1024)S(1)}, s32[2048]{0:T(1024)}, u32[]{:S(2)}) copy-start(s32[2048]{0:T(1024)} %param.22) | copy-start | bytes 24580
  124.1 367.3 %reduce-scatter.3.cloned.1.call-start = ((), (), s32[]{:S(2)}) async-start(), calls=%async_computation.4 | async-start | bytes 16384000 | tf_op jit(solution)/shard_map/reduce_scatter | solution.py:1601
  125.3 4.5 copy-start.41
  129.7 12.4 %copy-start.2 = (bf16[1024,768]{1,0:T(8,128)(2,1)}, bf16[1024,768]{1,0:T(8,128)(2,1)S(1)}, u32[]{:S(2)}) copy-start(bf16[1024,768]{1,0:T(8,128)(2,1)S(1)} %convolution_convert_fusion.7.mixed_ref) | copy-start | bytes 4718596
  129.7 10.3 %copy-start.18 = (bf16[256,1024]{1,0:T(8,128)(2,1)S(1)}, bf16[256,1024]{1,0:T(8,128)(2,1)}, u32[]{:S(2)}) copy-start(bf16[256,1024]{1,0:T(8,128)(2,1)} %get-tuple-element.95) | copy-start | bytes 1572868
  139.3 0.8 copy-start
  142.1 34.2 %copy-start.48 = (bf16[1024,1024]{1,0:T(8,128)(2,1)S(1)}, bf16[1024,1024]{1,0:T(8,128)(2,1)}, u32[]{:S(2)}) copy-start(bf16[1024,1024]{1,0:T(8,128)(2,1)} %get-tuple-element.98) | copy-start | bytes 6291460
  176.3 4.2 copy-start.52
  180.5 4.1 copy-start.44
  294.5 10.6 %copy-start.13 = (f32[10,1,2048]{2,1,0:T(1,128)S(1)}, f32[10,1,2048]{2,1,0:T(1,128)}, u32[]{:S(2)}) copy-start(f32[10,1,2048]{2,1,0:T(1,128)} %get-tuple-element.103) | copy-start | bytes 245764
  305.1 0.7 copy-start.23
  339.6 0.7 copy-start.28
  339.6 228.0 %reduce-scatter.5.cloned.1.call-start = ((), (), s32[]{:S(2)}) async-start(), calls=%async_computation.5 | async-start | bytes 2621440 | tf_op jit(solution)/shard_map/reduce_scatter | solution.py:1639
  341.0 69.3 %copy-start.45 = (f32[1024,1024]{1,0:T(8,128)S(1)}, f32[1024,1024]{1,0:T(8,128)}, u32[]{:S(2)}) copy-start(f32[1024,1024]{1,0:T(8,128)} %copy-done.44) | copy-start | bytes 12582916
  410.3 7.0 %copy-start.49 = (bf16[1024,1024]{1,0:T(8,128)(2,1)S(1)}, bf16[1024,1024]{1,0:T(8,128)(2,1)}, u32[]{:S(2)}) copy-start(bf16[1024,1024]{1,0:T(8,128)(2,1)} %get-tuple-element.98) | copy-start | bytes 6291460
  417.3 3.8 copy-start.51
  425.2 34.6 %copy-start.19 = (bf16[256,1024]{1,0:T(8,128)(2,1)S(1)}, bf16[256,1024]{1,0:T(8,128)(2,1)}, u32[]{:S(2)}) copy-start(bf16[256,1024]{1,0:T(8,128)(2,1)} %get-tuple-element.95) | copy-start | bytes 1572868
  459.8 2.5 copy-start.3
  462.3 17.6 %copy-start.1 = (bf16[1024,256]{1,0:T(8,128)(2,1)S(1)}, bf16[1024,256]{1,0:T(8,128)(2,1)}, u32[]{:S(2)}) copy-start(bf16[1024,256]{1,0:T(8,128)(2,1)} %copy-done) | copy-start | bytes 1572868
  462.3 17.6 %copy-start.10 = (bf16[1024,1024]{1,0:T(8,128)(2,1)S(1)}, bf16[1024,1024]{1,0:T(8,128)(2,1)}, u32[]{:S(2)}) copy-start(bf16[1024,1024]{1,0:T(8,128)(2,1)} %get-tuple-element.114) | copy-start | bytes 6291460
  462.4 19.1 %copy-start.47 = (bf16[1024,768]{1,0:T(8,128)(2,1)S(1)}, bf16[1024,768]{1,0:T(8,128)(2,1)}, u32[]{:S(2)}) copy-start(bf16[1024,768]{1,0:T(8,128)(2,1)} %get-tuple-element.94) | copy-start | bytes 4718596
  481.5 3.1 copy-start.46
  484.6 3.1 copy-start.50
  491.5 75.7 %copy-start.42 = (f32[4]{0:T(128)S(1)}, f32[4]{0:T(128)}, u32[]{:S(2)}) copy-start(f32[4]{0:T(128)} %get-tuple-element.158) | copy-start | bytes 52
  564.1 29.7 %collective-permute-start.4 = (bf16[256,896]{1,0:T(8,128)(2,1)}, bf16[256,896]{1,0:T(8,128)(2,1)S(1)}, u32[]{:S(2)}, u32[]{:S(2)}) collective-permute-start(bf16[256,896]{1,0:T(8,128)(2,1)} %get-tuple-element.117), channel_id=1, source_target_pairs={{0,4},{1,5},{2,6},{3,7},{4,0},{5,1},{6,2},{7,3},{8,12},{9,13},{10,... | collective-permute-start | bytes 1376264 | tf_op jit(solution)/shard_map/ppermute | solution.py:1678
  564.2 29.6 %collective-permute-start.3 = (bf16[128,256]{1,0:T(8,128)(2,1)}, bf16[128,256]{1,0:T(8,128)(2,1)S(1)}, u32[]{:S(2)}, u32[]{:S(2)}) collective-permute-start(bf16[128,256]{1,0:T(8,128)(2,1)} %get-tuple-element.116), channel_id=1, source_target_pairs={{0,4},{1,5},{2,6},{3,7},{4,0},{5,1},{6,2},{7,3},{8,12},{9,13},{10,... | collective-permute-start | bytes 196616 | tf_op jit(solution)/shard_map/ppermute | solution.py:1678
  568.6 30.7 %collective-permute-start.2 = (bf16[512,256]{1,0:T(8,128)(2,1)S(1)}, bf16[512,256]{1,0:T(8,128)(2,1)S(1)}, u32[]{:S(2)}, u32[]{:S(2)}) collective-permute-start(bf16[512,256]{1,0:T(8,128)(2,1)S(1)} %slice.118), channel_id=1, source_target_pairs={{0,4},{1,5},{2,6},{3,7},{4,0},{5,1},{6,2},{7,3},{8,12},{9,13},{10,... | collective-permute-start | bytes 786440 | tf_op jit(solution)/shard_map/ppermute | solution.py:1678
  568.8 30.6 %copy-start.15 = (f32[256,512]{1,0:T(8,128)S(1)}, f32[256,512]{1,0:T(8,128)}, u32[]{:S(2)}) copy-start(f32[256,512]{1,0:T(8,128)} %get-tuple-element.125) | copy-start | bytes 1572868
  568.8 31.3 %copy-start.20 = (f32[256,384]{1,0:T(8,128)S(1)}, f32[256,384]{1,0:T(8,128)}, u32[]{:S(2)}) copy-start(f32[256,384]{1,0:T(8,128)} %get-tuple-element.121) | copy-start | bytes 1179652
  599.3 6.7 copy-start.22
  600.1 51.8 %copy-start.5 = (f32[256,512]{1,0:T(8,128)}, f32[256,512]{1,0:T(8,128)S(1)}, u32[]{:S(2)}) copy-start(f32[256,512]{1,0:T(8,128)S(1)} %get-tuple-element.232) | copy-start | bytes 1572868
  600.1 6.6 copy-start.14
  600.8 55.4 %copy-start.6 = (f32[256,384]{1,0:T(8,128)}, f32[256,384]{1,0:T(8,128)S(1)}, u32[]{:S(2)}) copy-start(f32[256,384]{1,0:T(8,128)S(1)} %get-tuple-element.224) | copy-start | bytes 1179652
  606.7 47.5 %copy-start.12 = (f32[128,256]{1,0:T(8,128)}, f32[128,256]{1,0:T(8,128)S(1)}, u32[]{:S(2)}) copy-start(f32[128,256]{1,0:T(8,128)S(1)} %get-tuple-element.228) | copy-start | bytes 393220
  607.4 42.2 %copy-start.4 = (f32[512,256]{1,0:T(8,128)}, f32[512,256]{1,0:T(8,128)S(1)}, u32[]{:S(2)}) copy-start(f32[512,256]{1,0:T(8,128)S(1)} %get-tuple-element.236) | copy-start | bytes 1572868
  624.6 7.1 %copy-start.29 = (f32[4,128]{1,0:T(4,128)S(1)}, f32[4,128]{1,0:T(4,128)}, u32[]{:S(2)}) copy-start(f32[4,128]{1,0:T(4,128)} %get-tuple-element.141) | copy-start | bytes 6148
  624.6 7.1 %copy-start.32 = (f32[2,128]{1,0:T(2,128)S(1)}, f32[2,128]{1,0:T(2,128)}, u32[]{:S(2)}) copy-start(f32[2,128]{1,0:T(2,128)} %get-tuple-element.142) | copy-start | bytes 3076
  624.6 8.5 %copy-start.30 = (f32[4,128]{1,0:T(4,128)S(1)}, f32[4,128]{1,0:T(4,128)}, u32[]{:S(2)}) copy-start(f32[4,128]{1,0:T(4,128)} %get-tuple-element.140) | copy-start | bytes 6148
  624.6 8.5 %copy-start.33 = (f32[2,128]{1,0:T(2,128)S(1)}, f32[2,128]{1,0:T(2,128)}, u32[]{:S(2)}) copy-start(f32[2,128]{1,0:T(2,128)} %get-tuple-element.139) | copy-start | bytes 3076
  624.6 9.9 %copy-start.34 = (f32[2,128]{1,0:T(2,128)S(1)}, f32[2,128]{1,0:T(2,128)}, u32[]{:S(2)}) copy-start(f32[2,128]{1,0:T(2,128)} %get-tuple-element.138) | copy-start | bytes 3076
  624.6 9.9 %copy-start.39 = (f32[1,128]{1,0:T(1,128)S(1)}, f32[1,128]{1,0:T(1,128)}, u32[]{:S(2)}) copy-start(f32[1,128]{1,0:T(1,128)} %get-tuple-element.137) | copy-start | bytes 1540
  624.6 11.2 %copy-start.31 = (f32[3,128]{1,0:T(4,128)S(1)}, f32[3,128]{1,0:T(4,128)}, u32[]{:S(2)}) copy-start(f32[3,128]{1,0:T(4,128)} %get-tuple-element.136) | copy-start | bytes 4612
  624.6 11.2 %copy-start.35 = (f32[2,128]{1,0:T(2,128)S(1)}, f32[2,128]{1,0:T(2,128)}, u32[]{:S(2)}) copy-start(f32[2,128]{1,0:T(2,128)} %get-tuple-element.135) | copy-start | bytes 3076
  637.2 12.4 %copy-start.8 = (f32[512,256]{1,0:T(8,128)S(1)}, f32[512,256]{1,0:T(8,128)}, u32[]{:S(2)}) copy-start(f32[512,256]{1,0:T(8,128)} %param.29) | copy-start | bytes 1572868
  637.2 14.7 %copy-start.9 = (f32[256,512]{1,0:T(8,128)S(1)}, f32[256,512]{1,0:T(8,128)}, u32[]{:S(2)}) copy-start(f32[256,512]{1,0:T(8,128)} %param.28) | copy-start | bytes 1572868
  637.2 17.0 %copy-start.17 = (f32[128,256]{1,0:T(8,128)S(1)}, f32[128,256]{1,0:T(8,128)}, u32[]{:S(2)}) copy-start(f32[128,256]{1,0:T(8,128)} %param.27) | copy-start | bytes 393220
  637.2 19.0 %copy-start.11 = (f32[256,384]{1,0:T(8,128)S(1)}, f32[256,384]{1,0:T(8,128)}, u32[]{:S(2)}) copy-start(f32[256,384]{1,0:T(8,128)} %param.26) | copy-start | bytes 1179652
  648.2 10.2 %copy-start.21 = (f32[50,128]{1,0:T(8,128)S(1)}, f32[50,128]{1,0:T(8,128)}, u32[]{:S(2)}) copy-start(f32[50,128]{1,0:T(8,128)} %get-tuple-element.132) | copy-start | bytes 76804
  648.3 10.2 %copy-start.36 = (f32[2,128]{1,0:T(2,128)S(1)}, f32[2,128]{1,0:T(2,128)}, u32[]{:S(2)}) copy-start(f32[2,128]{1,0:T(2,128)} %get-tuple-element.133) | copy-start | bytes 3076
  658.5 9.1 %copy-start.43 = (f32[1,128]{1,0:T(1,128)S(1)}, f32[1,128]{1,0:T(1,128)}, u32[]{:S(2)}) copy-start(f32[1,128]{1,0:T(1,128)} %get-tuple-element.131) | copy-start | bytes 1540
  658.5 15.3 %copy-start.26 = (f32[6,1024]{1,0:T(8,128)S(1)}, f32[6,1024]{1,0:T(8,128)}, u32[]{:S(2)}) copy-start(f32[6,1024]{1,0:T(8,128)} %get-tuple-element.240) | copy-start | bytes 73732
  658.5 15.9 %copy-start.25 = (f32[6,1024]{1,0:T(8,128)S(1)}, f32[6,1024]{1,0:T(8,128)}, u32[]{:S(2)}) copy-start(f32[6,1024]{1,0:T(8,128)} %get-tuple-element.241) | copy-start | bytes 73732
  658.5 16.5 %copy-start.24 = (f32[6,1024]{1,0:T(8,128)S(1)}, f32[6,1024]{1,0:T(8,128)}, u32[]{:S(2)}) copy-start(f32[6,1024]{1,0:T(8,128)} %get-tuple-element.242) | copy-start | bytes 73732
Sparse Core Ops, SparseCore 0:
  9.9 43.5 all-gather.2
  124.2 108.4 all-gather.4
  339.8 124.9 reduce-scatter.2
  491.6 52.0 reduce-scatter.4

commit v10 on v9

--- a/solution.py
+++ b/solution.py
@@ -1459,7 +1459,7 @@
     width = part_width * size_dp
     first_row = mp * vocab
     spots = tokens * size_dp
-    chunks_full = max(1, min(8, rows // 32))
+    chunks_full = max(1, min(4, rows // 32))
     chunks_near = max(1, min(4, rows // 32))
     chunks_turn = max(1, min(4, rows // 32))
 
@@ -1620,7 +1620,6 @@
     unused, gelu_pull = jax.vjp(gelu_tanh, before)
     dbefore = gelu_pull(dhidden)[0].astype(bf16)
     partial = jnp.einsum("tf,df->td", dbefore, wide_fc, preferred_element_type=f32).astype(bf16)
-    partial, grad_proj = lax.optimization_barrier((partial, grad_proj))
     dbranch1, dstream1, norm2 = line_call(
         "mlp_back",
         7,
@@ -1635,15 +1634,13 @@
         near,
         34,
     )
-    grad_proj, head_grad = lax.optimization_barrier((grad_proj, head_grad))
-    grad_proj = lax.psum_scatter(grad_proj, "dp", scatter_dimension=1, tiled=True)
     grad_fc = jnp.einsum("td,tf->df", inner_two, dbefore, preferred_element_type=f32).astype(bf16)
     grad_out = jnp.einsum("tf,td->fd", attended, dbranch1, preferred_element_type=f32).astype(bf16)
     dattended = jnp.einsum("td,fd->tf", dbranch1, wide_out, preferred_element_type=f32)
     dmixed = attend_back(mixed, my_starts, dattended.astype(bf16))
     partial = jnp.einsum("tc,dc->td", dmixed, wide_qkv, preferred_element_type=f32).astype(bf16)
     grad_qkv = jnp.einsum("td,tc->dc", inner_one, dmixed, preferred_element_type=f32).astype(bf16)
-    drows, norm1, grad_out, grad_fc, grad_qkv, twins_wide, twins_out = line_call(
+    drows, norm1, grad_proj, grad_out, grad_fc, grad_qkv, twins_wide, twins_tall = line_call(
         "attn_back",
         8,
         partial,
@@ -1657,6 +1654,7 @@
         chips,
         70,
         [
+            ("scatter", 1, grad_proj),
             ("scatter", 1, grad_out),
             ("scatter", 0, grad_fc),
             ("scatter", 0, grad_qkv),
@@ -1678,20 +1676,20 @@
             found.append(lax.ppermute(jnp.concatenate(pieces, axis=axis), "mp", back))
         return found
 
-    proj_rows = w_proj.shape[0]
+    tall = [grad_proj.shape[0], grad_out.shape[0]]
     wide = [grad_fc.shape[1], grad_qkv.shape[1]]
-    found_proj = from_twins(grad_proj[proj_rows:], 0, [proj_rows])
-    found_out = from_twins(twins_out, 0, [w_out.shape[0]])
+    found_tall = from_twins(twins_tall, 0, tall)
     found_wide = from_twins(twins_wide, 1, wide)
     grad_table = scatter(keys, owned, head_grad, drows, vocab, shift)
-    found_proj, found_out, found_wide, grad_table = lax.optimization_barrier(
-        (found_proj, found_out, found_wide, grad_table)
-    )
-    grad_proj = grad_proj[:proj_rows].astype(f32)
-    for values in found_proj:
-        grad_proj += values.astype(f32)
-    for values in found_out:
-        grad_out += values.astype(f32)
+    table_squares = grad_table * grad_table + EPS_ONE
+    table_rows = jnp.sum(table_squares, axis=1)
+    table_cols = jnp.sum(table_squares, axis=0)
+    found_tall, found_wide, table_rows = lax.optimization_barrier(
+        (found_tall, found_wide, table_rows)
+    )
+    for values in found_tall:
+        grad_proj += values[: tall[0]].astype(f32)
+        grad_out += values[tall[0] :].astype(f32)
     for values in found_wide:
         grad_fc += values[:, : wide[0]].astype(f32)
         grad_qkv += values[:, wide[0] :].astype(f32)
@@ -1703,12 +1701,12 @@
     full = tuple(
         (g.shape[0] * r, g.shape[1] * c) for g, r, c in zip(grads, row_span, col_span)
     )
-    squares = [gradient * gradient + EPS_ONE for gradient in grads]
+    squares = [gradient * gradient + EPS_ONE for gradient in grads[1:]]
     rows_new, cols_new, loss_sums, grad_norms, second_new, norms_new, rates = update_stats(
         10,
-        [jnp.sum(square, axis=1) for square in squares],
+        [table_rows] + [jnp.sum(square, axis=1) for square in squares],
         (rows_table, rows_qkv, rows_out, rows_fc, rows_proj),
-        [jnp.sum(square, axis=0) for square in squares],
+        [table_cols] + [jnp.sum(square, axis=0) for square in squares],
         (cols_table, cols_qkv, cols_out, cols_fc, cols_proj),
         [table_sq] + [jnp.sum(value * value, axis=0) for value in weights[1:]],
         loss_part,

time: 689 us -> 681 us (0.988)
    ppermute x3 -> x2, waiting for transfers between devices: 17.1 us -> 12.1 us  [from_twins(): found.append(lax.ppermute(jnp.concatenate(pieces, axis=axis), 'mp', back))]
  transfers between devices with their start and end apart: 9 -> 7, of which waited for: 3 -> 2; matrix products, arithmetic and copies ran while one was open for 9% -> 10% of each run, Pallas kernels for 49% -> 49%
where the time goes in v10:
time: 681 us; the launch traced here: 675 us
  Pallas kernels  516 us (76%)
  other arithmetic  57.9 us (9%)
  matrix products  42.7 us (6%)
  local copies, waits for them, and re-layouts  19.8 us (3%)
  waiting for transfers between devices  15.8 us (2%)
  between operations  14.7 us (2%)
  starting transfers between devices  7.46 us (1%)
    pallas_call x6, Pallas kernels, line_call(): return list(call(*args))  339 us
    pallas_call x1, Pallas kernels, head_stats(): pl.pallas_call(functools.partial(head_stats_kernel, block, tile, early),...  46.9 us
    pallas_call x1, Pallas kernels, head_back(): pl.pallas_call(functools.partial(head_back_kernel, block, tile), grid=(ro...  33.7 us
    sub x5, other arithmetic, local(): updated = [weights[n] - factors[n, 0] * steps[n] for n in range(5)]  17.8 us
    pallas_call x1, Pallas kernels, update_stats(): pl.pallas_call(functools.partial(stats_kernel, full, size_dp, size_mp), o...  17.7 us
    pallas_call x1, Pallas kernels, attend_back(): pl.pallas_call(attend_back_kernel, grid=(pairs,), out_shape=jax.ShapeDtyp...  17.4 us
    pallas_call x2, Pallas kernels, small_gather(): pl.pallas_call(functools.partial(small_gather_kernel, axis, count), out_s...  15.5 us
  transfers between devices with their start and end apart: 7, of which 2 were waited for; matrix products, arithmetic and copies ran while one was open for 10% of the time, Pallas kernels for 49%

profile of v10, /device:TPU:0, one launch (start us, length us, event | category | flops | bytes accessed | tf_op | source)
XLA Modules:
  0.0 674.8 jit_solution(9535905294388316260)
XLA Ops:
  7.3 2.3 slice.131
  9.6 1.9 multiply_reduce_fusion.4
  11.5 1.8 multiply_reduce_fusion.6
  13.3 4.1 collective-permute-start
  19.4 7.3 %gather_ids.1 = s32[4,32,128]{2,1,0:T(8,128)} custom-call(s32[32,128]{1,0:T(8,128)} %reshape.306.src_ref), custom_call_target="tpu_custom_call" | custom-call | flops 6000000000 | bytes 18000000 | tf_op jit(solution)/shard_map/gather_ids/pallas_call | solution.py:926
  26.7 0.9 reshape.307
  28.5 6.8 %sort.14 = (s32[8192]{0:T(1024)}, s32[8192]{0:T(1024)}) sort(s32[8192]{0:T(1024)S(1)} %add_select_fusion, s32[8192]{0:T(1024)S(1)} %iota.23), dimensions={0}, to_apply=%region_1.2 | sort | flops 106496 | bytes 131072 | tf_op jit(solution)/shard_map/jit(sort)/sort | solution.py:1506
  35.2 13.0 %lookup.1 = (bf16[8192,256]{1,0:T(8,128)(2,1)}, bf16[5120,256]{1,0:T(8,128)(2,1)}, f32[8,128]{1,0:T(8,128)}) custom-call(s32[1]{0:T(128)} %bitcast.2.count_ref, s32[8192]{0:T(1024)} %get-tuple-element.82.key_ref, f32[6288,256]{1,0:T(8,128)} %table_ref.1), custom_call_target="tpu_custom_call" | custom-call | flops 20000000000 | bytes 60000000 | tf_op jit(solution)/shard_map/lookup/pallas_call | solution.py:1308
  48.2 3.6 collective-permute-done.1
  52.5 0.8 pad_maximum_fusion.1.refs_5_
  53.4 0.8 pad_maximum_fusion.3.refs_2_
  54.2 0.9 pad_maximum_fusion.refs_4_
  55.0 69.1 %lookup_sum.1 = (bf16[1024,1024]{1,0:T(8,128)(2,1)}, bf16[256,1024]{1,0:T(8,128)(2,1)}, bf16[1024,768]{1,0:T(8,128)(2,1)}, bf16[256,1024]{1,0:T(8,128)(2,1)}, bf...) custom-call(bf16[8192,256]{1,0:T(8,128)(2,1)} %get-tuple-element.85.refs_0_, f32[6,1024]{1,0:T(8,128)} %refs_29_.1, ...), custom_call_target="tpu_custom_call" | custom-call | flops 70000001024 | bytes 210000000 | tf_op jit(solution)/shard_map/lookup_sum/pallas_call | solution.py:670
  125.8 3.8 convolution_convert_fusion.7.mixed_ref
  129.6 9.5 %attend.1 = bf16[1024,256]{1,0:T(8,128)(2,1)S(1)} custom-call(bf16[1024,768]{1,0:T(8,128)(2,1)S(1)} %convolution_convert_fusion.7.mixed_ref, s32[1024,1]{1,0:T(8,128)S(1)} %copy.63.starts_ref), custom_call_target="tpu_custom_call" | custom-call | flops 1073741824 | bytes 1572864 | tf_op jit(solution)/shard_map/attend/pallas_call | solution.py:822
  139.2 0.8 copy-done
  140.0 2.0 convolution_convert_fusion.4.refs_0_
  142.0 34.2 %attn_sum.1 = (bf16[1024,1024]{1,0:T(8,128)(2,1)}, f32[256,1024]{1,0:T(8,128)}) custom-call(bf16[1024,1024]{1,0:T(8,128)(2,1)} %convolution_convert_fusion.4.refs_0_, bf16[256,1024]{1,0:T(8,128)(2,1)} %get-tuple-element.92.refs_1_, f32[6,1024]{1,0:T(8,128)} %refs_29_.1), custom_call_target="tpu_custom_call" | custom-call | flops 32000000000 | bytes 96000000 | tf_op jit(solution)/shard_map/attn_sum/pallas_call | solution.py:670
  176.2 4.2 fusion.37
  180.4 4.0 convolution_convert_fusion.3.refs_0_
  184.4 58.5 %mlp_sum.1 = (bf16[2048,1024]{1,0:T(8,128)(2,1)}, f32[256,1024]{1,0:T(8,128)}) custom-call(bf16[1024,1024]{1,0:T(8,128)(2,1)} %convolution_convert_fusion.3.refs_0_, f32[256,1024]{1,0:T(8,128)} %get-tuple-element.96.refs_1_, f32[6,1024]{1,0:T(8,128)} %refs_29_.1), custom_call_target="tpu_custom_call" | custom-call | flops 57999998976 | bytes 174000000 | tf_op jit(solution)/shard_map/mlp_sum/pallas_call | solution.py:670
  243.0 46.9 %head_stats.1 = (bf16[6400,2048]{1,0:T(8,128)(2,1)}, f32[10,1,2048]{2,1,0:T(1,128)}, f32[10,1,2048]{2,1,0:T(1,128)}, f32[10,1,2048]{2,1,0:T(1,128)}) custom-call(bf16[1280,1024]{1,0:T(8,128)(2,1)} %all-gather.3.cloned.1.call-done.early_ref.refs_1_, bf16[5120,1024]{1,0:T(8,128)(2,1)} %all-gather.5.cloned.1.call-done.late_ref.refs_2_, ...), custom_call_target="tpu_custom_call" | custom-call | flops 26843545600 | bytes 39321600 | tf_op jit(solution)/shard_map/head_stats/pallas_call | solution.py:719
  289.9 1.0 reduce_max.18
  290.8 1.0 fusion.17
  291.8 1.0 reduce_sum.245
  293.4 8.2 %gather_stats.1 = f32[8,48,128]{2,1,0:T(8,128)} custom-call(f32[48,128]{1,0:T(8,128)} %pad_maximum_fusion.6.src_ref), custom_call_target="tpu_custom_call" | custom-call | flops 6000000000 | bytes 18000000 | tf_op jit(solution)/shard_map/gather_stats/pallas_call | solution.py:926
  301.6 1.0 reshape.313
  303.6 0.7 exponential_multiply_fusion.scale_ref
  304.3 33.7 %head_back.1 = (bf16[6400,2048]{1,0:T(8,128)(2,1)}, bf16[6400,1024]{1,0:T(8,128)(2,1)}) custom-call(bf16[6400,2048]{1,0:T(8,128)(2,1)} %get-tuple-element.98.exp_ref, bf16[2048,1024]{1,0:T(8,128)(2,1)} %get-tuple-element.97.final_ref, f32[10,1,2048]{2,1,0:T(1,128)} %exponential_multiply_fusion.scale_ref, f32[1,2048]{1,0:T(1,128)} %bitcast.131, ...), custom_call_target="tpu_custom_call" | custom-call | flops 26843545600 | bytes 65536000 | tf_op jit(solution)/shard_map/head_back/pallas_call | solution.py:761
  338.1 0.7 copy-done.28
  339.4 70.1 %final_back.1 = (bf16[1024,1024]{1,0:T(8,128)(2,1)}, f32[256,1024]{1,0:T(8,128)}, f32[8,1024]{1,0:T(8,128)}) custom-call(bf16[6400,2048]{1,0:T(8,128)(2,1)} %get-tuple-element.102.refs_0_, bf16[1280,1024]{1,0:T(8,128)(2,1)} %all-gather.3.cloned.1.call-done.early_ref.refs_1_, bf16[5120,1024]{1,0:T(8,128)(2,1)} %all-gather.5.cloned.1.call-done.late_ref.refs_2_, ...), custom_call_target="tpu_custom_call" | custom-call | flops 65000001536 | bytes 195000000 | tf_op jit(solution)/shard_map/final_back/pallas_call | solution.py:670
  409.5 6.9 %fusion.8 = bf16[1024,1024]{1,0:T(8,128)(2,1)S(1)} fusion(f32[1024,1024]{1,0:T(8,128)S(1)} %copy-done.45, bf16[1024,1024]{1,0:T(8,128)(2,1)} %get-tuple-element.104, bf16[1024,1024]{1,0:T(8,128)(2,1)} %get-tuple-element.95), kind=kOutput, calls=%fused_computation.14 | convolution fusion | flops 2168455168 | bytes 10485760 | tf_op jit(solution)/shard_map/td,fd->tf/dot_general | solution.py:1619
  416.4 3.7 convolution_convert_fusion.2.refs_0_
  420.1 34.7 %mlp_back.1 = (bf16[1024,1024]{1,0:T(8,128)(2,1)}, f32[256,1024]{1,0:T(8,128)}, f32[8,1024]{1,0:T(8,128)}) custom-call(bf16[1024,1024]{1,0:T(8,128)(2,1)} %convolution_convert_fusion.2.refs_0_, f32[256,1024]{1,0:T(8,128)} %get-tuple-element.96.refs_1_, f32[6,1024]{1,0:T(8,128)} %refs_29_.1, f32[256,1024]{1,0:T(8,128)} %get-tuple-element.105.refs_3_), custom_call_target="tpu_custom_call" | custom-call | flops 33999998976 | bytes 102000000 | tf_op jit(solution)/shard_map/mlp_back/pallas_call | solution.py:670
  454.9 2.5 convolution_convert_fusion.9.upstream_ref
  457.4 17.4 %attend_back.1 = bf16[1024,768]{1,0:T(8,128)(2,1)S(1)} custom-call(bf16[1024,768]{1,0:T(8,128)(2,1)S(1)} %copy-done.3, s32[1024,1]{1,0:T(8,128)S(1)} %copy.63.starts_ref, bf16[1024,256]{1,0:T(8,128)(2,1)S(1)} %convolution_convert_fusion.9.upstream_ref), custom_call_target="tpu_custom_call" | custom-call | flops 2684354560 | bytes 3145728 | tf_op jit(solution)/shard_map/attend_back/pallas_call | solution.py:870
  474.8 1.5 convolution_convert_fusion.8.refs_5_
  476.3 3.1 convolution_convert_fusion.5.refs_0_
  479.5 3.1 convolution_convert_fusion.6.refs_7_
  482.6 3.8 convolution_convert_fusion.refs_6_
  486.4 4.1 convolution_convert_fusion.1.refs_4_
  490.4 72.7 %attn_back.1 = (bf16[8192,256]{1,0:T(8,128)(2,1)}, f32[8,1024]{1,0:T(8,128)}, f32[512,256]{1,0:T(8,128)}, f32[128,256]{1,0:T(8,128)}, f32[256,512]{1,0:T(8,128)}...) custom-call(bf16[1024,1024]{1,0:T(8,128)(2,1)} %convolution_convert_fusion.5.refs_0_, ...), custom_call_target="tpu_custom_call" | custom-call | flops 70000001024 | bytes 210000000 | tf_op jit(solution)/shard_map/attn_back/pallas_call | solution.py:670
  563.2 2.9 collective-permute-start.2
  566.6 13.0 %scatter.1 = f32[6288,256]{1,0:T(8,128)} custom-call(s32[1]{0:T(128)} %bitcast.2.count_ref, s32[8192]{0:T(1024)} %get-tuple-element.82.key_ref, bf16[6400,256]{1,0:T(8,128)(2,1)} %reduce-scatter.2.cloned.1.call-done.head_ref, bf16[8192,256]{1,0:T(8,128)(2,1)} %get-tuple-element.111.rows_in_ref), custom_call_target="tpu_custom_call" | custom-call | flops 23000000512 | bytes 69000000 | tf_op jit(solution)/shard_map/scatter/pallas_call | solution.py:1351
  579.6 4.6 fusion
  584.2 12.1 %collective-permute-done.2 = bf16[640,256]{1,0:T(8,128)(2,1)S(1)} collective-permute-done((bf16[640,256]{1,0:T(8,128)(2,1)}, bf16[640,256]{1,0:T(8,128)(2,1)S(1)}, u32[]{:S(2)}, u32[]{:S(2)}) %collective-permute-start.2) | collective-permute-done | bytes 327712 | tf_op jit(solution)/shard_map/ppermute | solution.py:1676
  596.3 0.8 fusion.11
  597.1 0.7 fusion.18
  597.8 0.8 fusion.9
  598.5 0.7 fusion.13
  599.9 17.7 %update_stats.1 = (f32[50,128]{1,0:T(8,128)}, f32[2,128]{1,0:T(2,128)}, f32[1,128]{1,0:T(1,128)}, f32[2,128]{1,0:T(2,128)}, f32[4,128]{1,0:T(4,128)}, /*index=5*...) custom-call(f32[50,128]{1,0:T(8,128)} %pad_bitcast_fusion.1.refs_0_,, ...), custom_call_target="tpu_custom_call" | custom-call | flops 12000000000 | bytes 36000000 | tf_op jit(solution)/shard_map/update_stats/pallas_call | solution.py:1177
  617.7 1.4 fusion.35
  619.1 5.5 multiply_reduce_fusion
  624.6 1.4 multiply_reduce_fusion.1
  626.0 1.4 multiply_reduce_fusion.2
  627.4 1.3 multiply_reduce_fusion.7
  628.7 1.4 multiply_reduce_fusion.5
  630.1 10.5 %clip_rates.1 = f32[8,128]{1,0:T(8,128)} custom-call(f32[2,128]{1,0:T(2,128)} %bitcast.182, f32[3,128]{1,0:T(4,128)} %bitcast.169, f32[2,128]{1,0:T(2,128)} %bitcast.179, f32[4,128]{1,0:T(4,128)} %bitcast.168, f32[2,128]{1,0:T(2,128)} %bitcast.178, f32[16,128]{1,0:T(8,128)} %get-tuple-element.126.refs_5_), custom_call_target="tpu_custom_call" | custom-call | flops 8000000000 | bytes 24000000 | tf_op jit(solution)/shard_map/clip_rates/pallas_call | solution.py:1225
  640.7 1.4 fusion.36
  642.1 2.3 multiply_subtract_fusion.1
  644.4 2.3 multiply_subtract_fusion.2
  646.6 2.0 multiply_subtract_fusion.4
  648.7 2.2 multiply_subtract_fusion.3
  650.9 9.1 %multiply_subtract_fusion = f32[6288,256]{1,0:T(8,128)} fusion(f32[6288,256]{1,0:T(8,128)} %table_ref.1, f32[]{:T(128)} %bitcast.59, f32[6288,256]{1,0:T(8,128)} %scatter.1, f32[]{:T(128)} %bitcast.41, f32[256]{0:T(256)S(1)} %bitcast.160, f32[6288]{0:T(1024)S(1)} %bitcast.123), kind=kLoop, calls=%fused_computation | loop fusion | flops 8048640 | bytes 19342920 | tf_op jit(solution)/shard_map/sub | solution.py:1725
  (174 shorter events, 16.9 us)
Async XLA Ops:
  7.2 10.2 %copy-start.7 = (f32[512,256]{1,0:T(8,128)S(1)}, f32[512,256]{1,0:T(8,128)}, u32[]{:S(2)}) copy-start(f32[512,256]{1,0:T(8,128)} %param.29) | copy-start | bytes 1572868
  7.2 10.8 %copy-start.16 = (f32[128,256]{1,0:T(8,128)S(1)}, f32[128,256]{1,0:T(8,128)}, u32[]{:S(2)}) copy-start(f32[128,256]{1,0:T(8,128)} %param.27) | copy-start | bytes 393220
  7.2 11.5 %copy-start.38 = (s32[2048]{0:T(1024)S(1)}, s32[2048]{0:T(1024)}, u32[]{:S(2)}) copy-start(s32[2048]{0:T(1024)} %param.21) | copy-start | bytes 24580
  7.2 11.5 %copy-start.27 = (s32[2048]{0:T(1024)S(1)}, s32[2048]{0:T(1024)}, u32[]{:S(2)}) copy-start(s32[2048]{0:T(1024)} %param.24) | copy-start | bytes 24580
  7.2 47.8 %all-gather.3.cloned.1.call-start = ((), (), s32[]{:S(2)}) async-start(), calls=%async_computation.1 | async-start | bytes 3276800 | tf_op jit(solution)/shard_map/all_gather | solution.py:1484
  9.6 233.4 %all-gather.5.cloned.1.call-start = ((), (), s32[]{:S(2)}) async-start(), calls=%async_computation.2 | async-start | bytes 13107200 | tf_op jit(solution)/shard_map/all_gather | solution.py:1533
  13.3 40.0 %collective-permute-start = (bf16[256,896]{1,0:T(8,128)(2,1)S(1)}, bf16[256,896]{1,0:T(8,128)(2,1)S(1)}, u32[]{:S(2)}, u32[]{:S(2)}) collective-permute-start(bf16[256,896]{1,0:T(8,128)(2,1)S(1)} %pad_maximum_fusion.2), channel_id=1, source_target_pairs={{0,4},{1,5},{2,6},{3,7},{4,0},{5,1},{6,2},{7,3},{8,12},{9,13},{10,... | collective-permute-start | bytes 1376264 | tf_op jit(solution)/shard_map/ppermute | solution.py:1472
  18.7 33.1 %collective-permute-start.1 = (bf16[640,256]{1,0:T(8,128)(2,1)S(1)}, bf16[640,256]{1,0:T(8,128)(2,1)S(1)}, u32[]{:S(2)}, u32[]{:S(2)}) collective-permute-start(bf16[640,256]{1,0:T(8,128)(2,1)S(1)} %pad_maximum_fusion.4), channel_id=1, source_target_pairs={{0,4},{1,5},{2,6},{3,7},{4,0},{5,1},{6,2},{7,3},{8,12},{9,13},{10,... | collective-permute-start | bytes 983048 | tf_op jit(solution)/shard_map/ppermute | solution.py:1472
  55.0 69.4 %copy-start.40 = (s32[2048]{0:T(1024)S(1)}, s32[2048]{0:T(1024)}, u32[]{:S(2)}) copy-start(s32[2048]{0:T(1024)} %param.23) | copy-start | bytes 24580
  55.0 69.7 %copy-start.37 = (s32[2048]{0:T(1024)S(1)}, s32[2048]{0:T(1024)}, u32[]{:S(2)}) copy-start(s32[2048]{0:T(1024)} %param.22) | copy-start | bytes 24580
  124.1 442.5 %reduce-scatter.2.cloned.1.call-start = ((), (), s32[]{:S(2)}) async-start(), calls=%async_computation.3 | async-start | bytes 16384000 | tf_op jit(solution)/shard_map/reduce_scatter | solution.py:1601
  125.1 0.6 copy-start.41
  129.6 12.4 %copy-start.2 = (bf16[1024,768]{1,0:T(8,128)(2,1)}, bf16[1024,768]{1,0:T(8,128)(2,1)S(1)}, u32[]{:S(2)}) copy-start(bf16[1024,768]{1,0:T(8,128)(2,1)S(1)} %convolution_convert_fusion.7.mixed_ref) | copy-start | bytes 4718596
  129.6 10.3 %copy-start.18 = (bf16[256,1024]{1,0:T(8,128)(2,1)S(1)}, bf16[256,1024]{1,0:T(8,128)(2,1)}, u32[]{:S(2)}) copy-start(bf16[256,1024]{1,0:T(8,128)(2,1)} %get-tuple-element.91) | copy-start | bytes 1572868
  139.2 0.8 copy-start
  142.0 34.2 %copy-start.49 = (bf16[1024,1024]{1,0:T(8,128)(2,1)S(1)}, bf16[1024,1024]{1,0:T(8,128)(2,1)}, u32[]{:S(2)}) copy-start(bf16[1024,1024]{1,0:T(8,128)(2,1)} %get-tuple-element.94) | copy-start | bytes 6291460
  176.2 4.2 copy-start.53
  180.4 4.1 copy-start.44
  293.4 10.2 %copy-start.13 = (f32[10,1,2048]{2,1,0:T(1,128)S(1)}, f32[10,1,2048]{2,1,0:T(1,128)}, u32[]{:S(2)}) copy-start(f32[10,1,2048]{2,1,0:T(1,128)} %get-tuple-element.99) | copy-start | bytes 245764
  303.6 0.7 copy-start.23
  338.0 0.7 copy-start.28
  339.4 70.1 %copy-start.45 = (f32[1024,1024]{1,0:T(8,128)S(1)}, f32[1024,1024]{1,0:T(8,128)}, u32[]{:S(2)}) copy-start(f32[1024,1024]{1,0:T(8,128)} %copy-done.44) | copy-start | bytes 12582916
  409.5 6.9 %copy-start.50 = (bf16[1024,1024]{1,0:T(8,128)(2,1)S(1)}, bf16[1024,1024]{1,0:T(8,128)(2,1)}, u32[]{:S(2)}) copy-start(bf16[1024,1024]{1,0:T(8,128)(2,1)} %get-tuple-element.94) | copy-start | bytes 6291460
  420.1 34.8 %copy-start.19 = (bf16[256,1024]{1,0:T(8,128)(2,1)S(1)}, bf16[256,1024]{1,0:T(8,128)(2,1)}, u32[]{:S(2)}) copy-start(bf16[256,1024]{1,0:T(8,128)(2,1)} %get-tuple-element.91) | copy-start | bytes 1572868
  454.9 2.5 copy-start.3
  457.4 17.4 %copy-start.1 = (bf16[1024,256]{1,0:T(8,128)(2,1)S(1)}, bf16[1024,256]{1,0:T(8,128)(2,1)}, u32[]{:S(2)}) copy-start(bf16[1024,256]{1,0:T(8,128)(2,1)} %copy-done) | copy-start | bytes 1572868
  457.4 17.4 %copy-start.10 = (bf16[1024,1024]{1,0:T(8,128)(2,1)S(1)}, bf16[1024,1024]{1,0:T(8,128)(2,1)}, u32[]{:S(2)}) copy-start(bf16[1024,1024]{1,0:T(8,128)(2,1)} %get-tuple-element.106) | copy-start | bytes 6291460
  457.4 18.9 %copy-start.48 = (bf16[1024,768]{1,0:T(8,128)(2,1)S(1)}, bf16[1024,768]{1,0:T(8,128)(2,1)}, u32[]{:S(2)}) copy-start(bf16[1024,768]{1,0:T(8,128)(2,1)} %get-tuple-element.88) | copy-start | bytes 4718596
  476.3 3.1 copy-start.47
  479.5 3.1 copy-start.51
  482.6 3.8 copy-start.46
  482.6 3.8 copy-start.52
  490.4 75.7 %copy-start.42 = (f32[4]{0:T(128)S(1)}, f32[4]{0:T(128)}, u32[]{:S(2)}) copy-start(f32[4]{0:T(128)} %get-tuple-element.150) | copy-start | bytes 52
  563.1 33.2 %collective-permute-start.3 = (bf16[256,896]{1,0:T(8,128)(2,1)}, bf16[256,896]{1,0:T(8,128)(2,1)S(1)}, u32[]{:S(2)}, u32[]{:S(2)}) collective-permute-start(bf16[256,896]{1,0:T(8,128)(2,1)} %get-tuple-element.109), channel_id=1, source_target_pairs={{0,4},{1,5},{2,6},{3,7},{4,0},{5,1},{6,2},{7,3},{8,12},{9,13},{10,... | collective-permute-start | bytes 1376264 | tf_op jit(solution)/shard_map/ppermute | solution.py:1676
  563.2 33.1 %collective-permute-start.2 = (bf16[640,256]{1,0:T(8,128)(2,1)}, bf16[640,256]{1,0:T(8,128)(2,1)S(1)}, u32[]{:S(2)}, u32[]{:S(2)}) collective-permute-start(bf16[640,256]{1,0:T(8,128)(2,1)} %get-tuple-element.108), channel_id=1, source_target_pairs={{0,4},{1,5},{2,6},{3,7},{4,0},{5,1},{6,2},{7,3},{8,12},{9,13},{10,... | collective-permute-start | bytes 983048 | tf_op jit(solution)/shard_map/ppermute | solution.py:1676
  579.6 16.7 %copy-start.15 = (f32[512,256]{1,0:T(8,128)S(1)}, f32[512,256]{1,0:T(8,128)}, u32[]{:S(2)}) copy-start(f32[512,256]{1,0:T(8,128)} %get-tuple-element.118) | copy-start | bytes 1572868
  579.6 17.5 %copy-start.22 = (f32[128,256]{1,0:T(8,128)S(1)}, f32[128,256]{1,0:T(8,128)}, u32[]{:S(2)}) copy-start(f32[128,256]{1,0:T(8,128)} %get-tuple-element.115) | copy-start | bytes 393220
  579.6 18.2 %copy-start.14 = (f32[256,512]{1,0:T(8,128)S(1)}, f32[256,512]{1,0:T(8,128)}, u32[]{:S(2)}) copy-start(f32[256,512]{1,0:T(8,128)} %get-tuple-element.117) | copy-start | bytes 1572868
  579.6 18.9 %copy-start.20 = (f32[256,384]{1,0:T(8,128)S(1)}, f32[256,384]{1,0:T(8,128)}, u32[]{:S(2)}) copy-start(f32[256,384]{1,0:T(8,128)} %get-tuple-element.113) | copy-start | bytes 1179652
  597.1 45.0 %copy-start.4 = (f32[512,256]{1,0:T(8,128)}, f32[512,256]{1,0:T(8,128)S(1)}, u32[]{:S(2)}) copy-start(f32[512,256]{1,0:T(8,128)S(1)} %get-tuple-element.228) | copy-start | bytes 1572868
  597.8 48.9 %copy-start.12 = (f32[128,256]{1,0:T(8,128)}, f32[128,256]{1,0:T(8,128)S(1)}, u32[]{:S(2)}) copy-start(f32[128,256]{1,0:T(8,128)S(1)} %get-tuple-element.220) | copy-start | bytes 393220
  598.5 45.8 %copy-start.5 = (f32[256,512]{1,0:T(8,128)}, f32[256,512]{1,0:T(8,128)S(1)}, u32[]{:S(2)}) copy-start(f32[256,512]{1,0:T(8,128)S(1)} %get-tuple-element.224) | copy-start | bytes 1572868
  599.3 49.4 %copy-start.6 = (f32[256,384]{1,0:T(8,128)}, f32[256,384]{1,0:T(8,128)S(1)}, u32[]{:S(2)}) copy-start(f32[256,384]{1,0:T(8,128)S(1)} %get-tuple-element.216) | copy-start | bytes 1179652
  617.6 7.0 %copy-start.29 = (f32[4,128]{1,0:T(4,128)S(1)}, f32[4,128]{1,0:T(4,128)}, u32[]{:S(2)}) copy-start(f32[4,128]{1,0:T(4,128)} %get-tuple-element.133) | copy-start | bytes 6148
  617.6 6.9 %copy-start.32 = (f32[2,128]{1,0:T(2,128)S(1)}, f32[2,128]{1,0:T(2,128)}, u32[]{:S(2)}) copy-start(f32[2,128]{1,0:T(2,128)} %get-tuple-element.134) | copy-start | bytes 3076
  617.6 8.3 %copy-start.30 = (f32[4,128]{1,0:T(4,128)S(1)}, f32[4,128]{1,0:T(4,128)}, u32[]{:S(2)}) copy-start(f32[4,128]{1,0:T(4,128)} %get-tuple-element.132) | copy-start | bytes 6148
  617.6 8.3 %copy-start.33 = (f32[2,128]{1,0:T(2,128)S(1)}, f32[2,128]{1,0:T(2,128)}, u32[]{:S(2)}) copy-start(f32[2,128]{1,0:T(2,128)} %get-tuple-element.131) | copy-start | bytes 3076
  617.7 9.7 %copy-start.34 = (f32[2,128]{1,0:T(2,128)S(1)}, f32[2,128]{1,0:T(2,128)}, u32[]{:S(2)}) copy-start(f32[2,128]{1,0:T(2,128)} %get-tuple-element.130) | copy-start | bytes 3076
  617.7 9.7 %copy-start.39 = (f32[1,128]{1,0:T(1,128)S(1)}, f32[1,128]{1,0:T(1,128)}, u32[]{:S(2)}) copy-start(f32[1,128]{1,0:T(1,128)} %get-tuple-element.129) | copy-start | bytes 1540
  617.7 11.0 %copy-start.31 = (f32[3,128]{1,0:T(4,128)S(1)}, f32[3,128]{1,0:T(4,128)}, u32[]{:S(2)}) copy-start(f32[3,128]{1,0:T(4,128)} %get-tuple-element.128) | copy-start | bytes 4612
  617.7 11.0 %copy-start.35 = (f32[2,128]{1,0:T(2,128)S(1)}, f32[2,128]{1,0:T(2,128)}, u32[]{:S(2)}) copy-start(f32[2,128]{1,0:T(2,128)} %get-tuple-element.127) | copy-start | bytes 3076
  630.1 12.0 %copy-start.8 = (f32[512,256]{1,0:T(8,128)S(1)}, f32[512,256]{1,0:T(8,128)}, u32[]{:S(2)}) copy-start(f32[512,256]{1,0:T(8,128)} %param.29) | copy-start | bytes 1572868
  630.1 14.3 %copy-start.9 = (f32[256,512]{1,0:T(8,128)S(1)}, f32[256,512]{1,0:T(8,128)}, u32[]{:S(2)}) copy-start(f32[256,512]{1,0:T(8,128)} %param.28) | copy-start | bytes 1572868
  630.1 16.5 %copy-start.17 = (f32[128,256]{1,0:T(8,128)S(1)}, f32[128,256]{1,0:T(8,128)}, u32[]{:S(2)}) copy-start(f32[128,256]{1,0:T(8,128)} %param.27) | copy-start | bytes 393220
  630.1 18.6 %copy-start.11 = (f32[256,384]{1,0:T(8,128)S(1)}, f32[256,384]{1,0:T(8,128)}, u32[]{:S(2)}) copy-start(f32[256,384]{1,0:T(8,128)} %param.26) | copy-start | bytes 1179652
  640.7 10.2 %copy-start.21 = (f32[50,128]{1,0:T(8,128)S(1)}, f32[50,128]{1,0:T(8,128)}, u32[]{:S(2)}) copy-start(f32[50,128]{1,0:T(8,128)} %get-tuple-element.124) | copy-start | bytes 76804
  640.7 10.2 %copy-start.36 = (f32[2,128]{1,0:T(2,128)S(1)}, f32[2,128]{1,0:T(2,128)}, u32[]{:S(2)}) copy-start(f32[2,128]{1,0:T(2,128)} %get-tuple-element.125) | copy-start | bytes 3076
  650.9 9.1 %copy-start.43 = (f32[1,128]{1,0:T(1,128)S(1)}, f32[1,128]{1,0:T(1,128)}, u32[]{:S(2)}) copy-start(f32[1,128]{1,0:T(1,128)} %get-tuple-element.123) | copy-start | bytes 1540
  650.9 15.3 %copy-start.26 = (f32[6,1024]{1,0:T(8,128)S(1)}, f32[6,1024]{1,0:T(8,128)}, u32[]{:S(2)}) copy-start(f32[6,1024]{1,0:T(8,128)} %get-tuple-element.232) | copy-start | bytes 73732
  650.9 15.9 %copy-start.25 = (f32[6,1024]{1,0:T(8,128)S(1)}, f32[6,1024]{1,0:T(8,128)}, u32[]{:S(2)}) copy-start(f32[6,1024]{1,0:T(8,128)} %get-tuple-element.233) | copy-start | bytes 73732
  650.9 16.5 %copy-start.24 = (f32[6,1024]{1,0:T(8,128)S(1)}, f32[6,1024]{1,0:T(8,128)}, u32[]{:S(2)}) copy-start(f32[6,1024]{1,0:T(8,128)} %get-tuple-element.234) | copy-start | bytes 73732
Sparse Core Ops, SparseCore 0:
  9.9 43.5 all-gather.2
  124.2 108.4 all-gather.4
  338.2 124.7 reduce-scatter.1

commit v11 on v10

--- a/solution.py
+++ b/solution.py
@@ -983,16 +983,16 @@
 
 def stats_kernel(full, size_dp, size_mp, *refs):
     row_part, row_old, col_part, col_old, weight_sq = (refs[5 * n : 5 * n + 5] for n in range(5))
-    loss_part, norm_one, norm_two, norm_three, norms, second_old = refs[25:31]
-    refs = refs[31:]
+    loss_part, norm_one, norm_two, norm_three = refs[25:29]
+    refs = refs[29:]
     row_out, col_out = refs[0:5], refs[5:10]
-    loss_out, grads_out, second_out, norms_out, rate_out = refs[10:15]
-    send_dp, slots_dp, send_mp, slots_mp, parts, part_slots, whole, send, recv = refs[15:]
+    loss_out, part_out, rate_out = refs[10:13]
+    send_dp, slots_dp, send_mp, slots_mp, parts, part_slots, send, recv = refs[13:]
     dp = lax.axis_index("dp")
     mp = lax.axis_index("mp")
     greet_all(dp, mp, size_dp, size_mp)
     beta = 1.0 - STEP ** (-0.8)
-    width = norms.shape[1]
+    width = norm_one.shape[1]
 
     at = 0
     marks = []
@@ -1024,7 +1024,7 @@
         send_dp[at:, :] = jnp.zeros((send_dp.shape[0] - at, 128), jnp.float32)
     over_dp = exchange("dp", dp, mp, send_dp, slots_dp, send, recv, 0)
     taken = [over_dp[start : start + rows] for start, rows in marks]
-    loss_out[...] = taken[5]
+    loss_row = taken[5]
     row_full = {0: taken[0], 2: taken[1], 4: taken[2]}
     col_full = {1: taken[3], 3: taken[4]}
     old_total = {1: taken[6], 3: taken[7]}
@@ -1050,6 +1050,7 @@
         put_mp(fold(row_old[index][...]))
     for index in range(5):
         put_mp(weight_rows[index])
+    put_mp(loss_row)
     if at < send_mp.shape[0]:
         send_mp[at:, :] = jnp.zeros((send_mp.shape[0] - at, 128), jnp.float32)
     each = count_norm // size_mp
@@ -1076,22 +1077,7 @@
     summed = part_slots[0]
     for index in range(1, size_mp):
         summed = summed + part_slots[index]
-    whole[mp] = summed
-    first += size_mp
-    copies = []
-    for hop in range(1, size_mp):
-        peer = lax.rem(mp + hop, size_mp)
-        copy = pltpu.make_async_remote_copy(
-            src_ref=whole.at[mp],
-            dst_ref=whole.at[mp],
-            send_sem=send.at[first + hop],
-            recv_sem=recv.at[first + hop],
-            device_id=(dp, peer),
-            device_id_type=MESH,
-        )
-        copies.append(copy)
-    for copy in copies:
-        copy.start()
+    part_out[...] = summed
     taken = [over_mp[start : start + rows] for start, rows in marks]
     for slot, index in enumerate((0, 2, 4)):
         col_full[index] = taken[slot]
@@ -1100,6 +1086,7 @@
         row_full[index] = taken[3 + slot]
     square_total = taken[5:10]
     weight_total = taken[13:18]
+    loss_out[...] = taken[18]
     for index in range(5):
         full_rows, full_cols = full[index]
         row_new = beta * row_old[index][...] + (1.0 - beta) * row_full[index] / full_cols
@@ -1115,31 +1102,9 @@
         )
         rate_out[index : index + 1, :] = jnp.broadcast_to(mean, (1, 128))
         rate_out[8 + index : 9 + index, :] = jnp.broadcast_to(rate, (1, 128))
-    for copy in copies:
-        copy.wait()
-    for row in range(6):
-        for piece in range(norm_rows):
-            place = row * norm_rows + piece
-            grads_out[row : row + 1, piece * 128 : piece * 128 + 128] = whole[
-                place // each, place % each : place % each + 1, :
-            ]
-    grad = grads_out[...]
-    second = beta * second_old[...] + (1.0 - beta) * (grad * grad + EPS_ONE)
-    second_out[...] = second
-    step = grad * lax.rsqrt(second)
-    entries = step.size
-
-    def mean_square(values):
-        return jnp.sum(jnp.sum(values * values, axis=0, keepdims=True), axis=1, keepdims=True) / (
-            entries
-        )
-
-    step = step / jnp.maximum(1.0, jnp.sqrt(mean_square(step)) / CLIP)
-    old = norms[...]
-    norms_out[...] = old - RHO * jnp.sqrt(mean_square(old)) * step
-
-
-def update_stats(cid, row_parts, rows_old, col_parts, cols_old, weight_sq, loss, norm_parts, norms, second, full):
+
+
+def update_stats(cid, row_parts, rows_old, col_parts, cols_old, weight_sq, loss, norm_parts, full):
     size_dp = lax.axis_size("dp")
     size_mp = lax.axis_size("mp")
     f32 = jnp.float32
@@ -1153,26 +1118,23 @@
         + [v if v.ndim == 2 else lane_rows(v) for v in weight_sq]
         + [lane_rows(loss)]
         + list(norm_parts)
-        + [norms, second]
-    )
-    width = norms.shape[1]
+    )
+    width = norm_parts[0].shape[1]
     count_norm = 6 * width // 128
     size_a = count_norm + sum(rows_old2[n].shape[0] for n in (0, 2, 4))
     size_a += sum(cols_old2[n].shape[0] for n in (1, 3)) + 8
     size_a += -size_a % 8
     size_b = sum(cols_old2[n].shape[0] for n in (0, 2, 4))
-    size_b += sum(rows_old2[n].shape[0] for n in (1, 3)) + 13
+    size_b += sum(rows_old2[n].shape[0] for n in (1, 3)) + 14
     size_b += -size_b % 8
     each = count_norm // size_mp
     out_shape = [jax.ShapeDtypeStruct(v.shape, f32) for v in rows_old2 + cols_old2]
     out_shape += [
         jax.ShapeDtypeStruct((1, 128), f32),
-        jax.ShapeDtypeStruct(norms.shape, f32),
-        jax.ShapeDtypeStruct(norms.shape, f32),
-        jax.ShapeDtypeStruct(norms.shape, f32),
+        jax.ShapeDtypeStruct((each, 128), f32),
         jax.ShapeDtypeStruct((16, 128), f32),
     ]
-    sems = size_dp + 3 * size_mp
+    sems = size_dp + 2 * size_mp
     vmem = pl.BlockSpec(memory_space=pltpu.VMEM)
     found = pl.pallas_call(
         functools.partial(stats_kernel, full, size_dp, size_mp),
@@ -1186,7 +1148,6 @@
             pltpu.VMEM((size_mp, size_b, 128), f32),
             pltpu.VMEM((size_mp, each, 128), f32),
             pltpu.VMEM((size_mp, each, 128), f32),
-            pltpu.VMEM((size_mp, each, 128), f32),
             pltpu.SemaphoreType.DMA((sems,)),
             pltpu.SemaphoreType.DMA((sems,)),
         ],
@@ -1197,47 +1158,90 @@
     rows_new = [found[n].reshape(-1)[: rows_old[n].size] for n in range(5)]
     cols_new = [found[5 + n].reshape(-1)[: cols_old[n].size] for n in range(5)]
     loss_sums = found[10][0, :NSRC]
-    return rows_new, cols_new, loss_sums, found[11], found[12], found[13], found[14]
+    return rows_new, cols_new, loss_sums, found[11], found[12]
 
 
 def clip_kernel(entries, size_dp, size_mp, *refs):
-    parts, rate = refs[:5], refs[5]
-    out, mine, slots_dp, slots_mp, send, recv = refs[6:]
+    parts, rate, part, norms, second_old = refs[:5], *refs[5:9]
+    out, grads_out, second_out, norms_out = refs[9:13]
+    mine, slots_dp, slots_mp, whole, send, recv = refs[13:]
     dp = lax.axis_index("dp")
     mp = lax.axis_index("mp")
     greet_all(dp, mp, size_dp, size_mp)
+    first = size_dp + size_mp
+    copies = []
+    for hop in range(1, size_mp):
+        copy = pltpu.make_async_remote_copy(
+            src_ref=part,
+            dst_ref=whole.at[mp],
+            send_sem=send.at[first + hop],
+            recv_sem=recv.at[first + hop],
+            device_id=(dp, lax.rem(mp + hop, size_mp)),
+            device_id_type=MESH,
+        )
+        copy.start()
+        copies.append(copy)
+    whole[mp] = part[...]
     mine[...] = jnp.zeros_like(mine)
     for index in range(5):
         mine[index : index + 1, :] = fold(parts[index][...])
-    mine[...] = exchange("dp", dp, mp, mine, slots_dp, send, recv, 0)
+    over_dp = exchange("dp", dp, mp, mine, slots_dp, send, recv, 0)
+    mine[...] = over_dp
     total = exchange("mp", mp, dp, mine, slots_mp, send, recv, size_dp)
     total = jnp.sum(total, axis=1, keepdims=True)
     for index in range(5):
         clip = jnp.maximum(1.0, jnp.sqrt(total[index : index + 1] / entries[index]) / CLIP)
         out[index : index + 1, :] = rate[8 + index : 9 + index, :] / clip
-
-
-def clip_rates(cid, step_parts, rate, entries):
+    for copy in copies:
+        copy.wait()
+    beta = 1.0 - STEP ** (-0.8)
+    each = part.shape[0]
+    norm_rows = norms.shape[1] // 128
+    for row in range(6):
+        for piece in range(norm_rows):
+            place = row * norm_rows + piece
+            grads_out[row : row + 1, piece * 128 : piece * 128 + 128] = whole[
+                place // each, place % each : place % each + 1, :
+            ]
+    grad = grads_out[...]
+    second = beta * second_old[...] + (1.0 - beta) * (grad * grad + EPS_ONE)
+    second_out[...] = second
+    step = grad * lax.rsqrt(second)
+    entries = step.size
+
+    def mean_square(values):
+        return jnp.sum(jnp.sum(values * values, axis=0, keepdims=True), axis=1, keepdims=True) / (
+            entries
+        )
+
+    step = step / jnp.maximum(1.0, jnp.sqrt(mean_square(step)) / CLIP)
+    old = norms[...]
+    norms_out[...] = old - RHO * jnp.sqrt(mean_square(old)) * step
+
+
+def clip_rates(cid, step_parts, rate, part, norms, second, entries):
     size_dp = lax.axis_size("dp")
     size_mp = lax.axis_size("mp")
     vmem = pl.BlockSpec(memory_space=pltpu.VMEM)
-    sems = size_dp + size_mp
+    sems = size_dp + 2 * size_mp
+    norm_type = jax.ShapeDtypeStruct(norms.shape, jnp.float32)
     return pl.pallas_call(
         functools.partial(clip_kernel, entries, size_dp, size_mp),
-        out_shape=jax.ShapeDtypeStruct((8, 128), jnp.float32),
-        in_specs=[vmem] * 6,
-        out_specs=vmem,
+        out_shape=[jax.ShapeDtypeStruct((8, 128), jnp.float32)] + [norm_type] * 3,
+        in_specs=[vmem] * 9,
+        out_specs=[vmem] * 4,
         scratch_shapes=[
             pltpu.VMEM((8, 128), jnp.float32),
             pltpu.VMEM((size_dp, 8, 128), jnp.float32),
             pltpu.VMEM((size_mp, 8, 128), jnp.float32),
+            pltpu.VMEM((size_mp, *part.shape), jnp.float32),
             pltpu.SemaphoreType.DMA((sems,)),
             pltpu.SemaphoreType.DMA((sems,)),
         ],
         compiler_params=pltpu.CompilerParams(collective_id=cid, has_side_effects=True),
         cost_estimate=cost_of(8),
         name="clip_rates",
-    )(*[lane_rows(v) for v in step_parts], rate)
+    )(*[lane_rows(v) for v in step_parts], rate, part, norms, second)
 
 
 UNROLL = 8
@@ -1584,13 +1588,13 @@
     top = jnp.max(tops, axis=0)
     total = jnp.sum(sums[:, 0] * jnp.exp(tops - top[None, :]), axis=0)
     pick = jnp.sum(picks[:, 0], axis=0)
-    stats = jnp.concatenate([v.reshape(-1, 128) for v in (top, total, pick)])
-    stats = small_gather("gather_stats", 5, stats, "mp").reshape(size_mp, 3, tokens)
+    stats = jnp.concatenate([v.reshape(-1, 128) for v in (top, total)])
+    stats = small_gather("gather_stats", 5, stats, "mp").reshape(size_mp, 2, tokens)
     highest = jnp.max(stats[:, 0], axis=0)
     log_total = highest + jnp.log(
         jnp.sum(stats[:, 1] * jnp.exp(stats[:, 0] - highest[None, :]), axis=0)
     )
-    token_loss = log_total - jnp.sum(stats[:, 2], axis=0)
+    token_loss = jnp.where(mp == 0, log_total, 0.0) - pick
     member = (sources[:, None] == jnp.arange(NSRC, dtype=jnp.int32)[None, :]).astype(f32)
     loss_part = jnp.sum(member * token_loss[:, None], axis=0)
     weight = jnp.sum(member / (NSRC * jnp.maximum(counts, 1.0))[None, :], axis=1)
@@ -1702,7 +1706,7 @@
         (g.shape[0] * r, g.shape[1] * c) for g, r, c in zip(grads, row_span, col_span)
     )
     squares = [gradient * gradient + EPS_ONE for gradient in grads[1:]]
-    rows_new, cols_new, loss_sums, grad_norms, second_new, norms_new, rates = update_stats(
+    rows_new, cols_new, loss_sums, norm_part, rates = update_stats(
         10,
         [table_rows] + [jnp.sum(square, axis=1) for square in squares],
         (rows_table, rows_qkv, rows_out, rows_fc, rows_proj),
@@ -1711,16 +1715,20 @@
         [table_sq] + [jnp.sum(value * value, axis=0) for value in weights[1:]],
         loss_part,
         (norm1, norm2, norm3),
-        norm_params,
-        second_norms,
         full,
     )
     steps = [
         grads[n] * lax.rsqrt(rows_new[n][:, None] * cols_new[n][None, :] / rates[n, 0])
         for n in range(5)
     ]
-    factors = clip_rates(
-        11, [jnp.sum(step * step, axis=0) for step in steps], rates, [r * c for r, c in full]
+    factors, grad_norms, second_new, norms_new = clip_rates(
+        11,
+        [jnp.sum(step * step, axis=0) for step in steps],
+        rates,
+        norm_part,
+        norm_params,
+        second_norms,
+        [r * c for r, c in full],
     )
     updated = [weights[n] - factors[n, 0] * steps[n] for n in range(5)]
     return (

time: 681 us -> 674 us (0.990)
  no operation moved by 1% of the time
where the time goes in v11:
time: 674 us; the launch traced here: 668 us
  Pallas kernels  511 us (76%)
  other arithmetic  57 us (8%)
  matrix products  42.8 us (6%)
  local copies, waits for them, and re-layouts  19.7 us (3%)
  waiting for transfers between devices  15.3 us (2%)
  between operations  14.7 us (2%)
  starting transfers between devices  7.46 us (1%)
    pallas_call x6, Pallas kernels, line_call(): return list(call(*args))  338 us
    pallas_call x1, Pallas kernels, head_stats(): pl.pallas_call(functools.partial(head_stats_kernel, block, tile, early),...  46.9 us
    pallas_call x1, Pallas kernels, head_back(): pl.pallas_call(functools.partial(head_back_kernel, block, tile), grid=(ro...  33.7 us
    sub x5, other arithmetic, local(): updated = [weights[n] - factors[n, 0] * steps[n] for n in range(5)]  17.8 us
    pallas_call x1, Pallas kernels, attend_back(): pl.pallas_call(attend_back_kernel, grid=(pairs,), out_shape=jax.ShapeDtyp...  17.4 us
    pallas_call x2, Pallas kernels, small_gather(): pl.pallas_call(functools.partial(small_gather_kernel, axis, count), out_s...  14.6 us
  transfers between devices with their start and end apart: 7, of which 2 were waited for; matrix products, arithmetic and copies ran while one was open for 10% of the time, Pallas kernels for 49%

profile of v11, /device:TPU:0, one launch (start us, length us, event | category | flops | bytes accessed | tf_op | source)
XLA Modules:
  0.0 667.6 jit_solution(15087351642676815596)
XLA Ops:
  7.3 2.3 slice.125
  9.6 1.9 multiply_reduce_fusion.4
  11.5 1.8 multiply_reduce_fusion.6
  13.3 4.1 collective-permute-start
  19.4 7.3 %gather_ids.1 = s32[4,32,128]{2,1,0:T(8,128)} custom-call(s32[32,128]{1,0:T(8,128)} %reshape.304.src_ref), custom_call_target="tpu_custom_call" | custom-call | flops 6000000000 | bytes 18000000 | tf_op jit(solution)/shard_map/gather_ids/pallas_call | solution.py:926
  26.7 0.9 reshape.305
  28.5 6.8 %sort.14 = (s32[8192]{0:T(1024)}, s32[8192]{0:T(1024)}) sort(s32[8192]{0:T(1024)S(1)} %add_select_fusion, s32[8192]{0:T(1024)S(1)} %iota.23), dimensions={0}, to_apply=%region_1.2 | sort | flops 106496 | bytes 131072 | tf_op jit(solution)/shard_map/jit(sort)/sort | solution.py:1510
  35.3 13.1 %lookup.1 = (bf16[8192,256]{1,0:T(8,128)(2,1)}, bf16[5120,256]{1,0:T(8,128)(2,1)}, f32[8,128]{1,0:T(8,128)}) custom-call(s32[1]{0:T(128)} %bitcast.2.count_ref, s32[8192]{0:T(1024)} %get-tuple-element.84.key_ref, f32[6288,256]{1,0:T(8,128)} %table_ref.1), custom_call_target="tpu_custom_call" | custom-call | flops 20000000000 | bytes 60000000 | tf_op jit(solution)/shard_map/lookup/pallas_call | solution.py:1312
  48.3 3.5 collective-permute-done.1
  51.8 0.7 pad_maximum_fusion.5.refs_3_
  52.5 0.8 pad_maximum_fusion.1.refs_5_
  53.4 0.8 pad_maximum_fusion.3.refs_2_
  54.2 0.9 pad_maximum_fusion.refs_4_
  55.0 70.0 %lookup_sum.1 = (bf16[1024,1024]{1,0:T(8,128)(2,1)}, bf16[256,1024]{1,0:T(8,128)(2,1)}, bf16[1024,768]{1,0:T(8,128)(2,1)}, bf16[256,1024]{1,0:T(8,128)(2,1)}, bf...) custom-call(bf16[8192,256]{1,0:T(8,128)(2,1)} %get-tuple-element.87.refs_0_, f32[6,1024]{1,0:T(8,128)} %refs_7_.1, ...), custom_call_target="tpu_custom_call" | custom-call | flops 70000001024 | bytes 210000000 | tf_op jit(solution)/shard_map/lookup_sum/pallas_call | solution.py:670
  126.7 3.8 convolution_convert_fusion.7.mixed_ref
  130.6 9.5 %attend.1 = bf16[1024,256]{1,0:T(8,128)(2,1)S(1)} custom-call(bf16[1024,768]{1,0:T(8,128)(2,1)S(1)} %convolution_convert_fusion.7.mixed_ref, s32[1024,1]{1,0:T(8,128)S(1)} %copy.63.starts_ref), custom_call_target="tpu_custom_call" | custom-call | flops 1073741824 | bytes 1572864 | tf_op jit(solution)/shard_map/attend/pallas_call | solution.py:822
  140.1 0.8 copy-done
  140.9 2.0 convolution_convert_fusion.4.refs_0_
  143.0 33.2 %attn_sum.1 = (bf16[1024,1024]{1,0:T(8,128)(2,1)}, f32[256,1024]{1,0:T(8,128)}) custom-call(bf16[1024,1024]{1,0:T(8,128)(2,1)} %convolution_convert_fusion.4.refs_0_, bf16[256,1024]{1,0:T(8,128)(2,1)} %get-tuple-element.94.refs_1_, f32[6,1024]{1,0:T(8,128)} %refs_7_.1), custom_call_target="tpu_custom_call" | custom-call | flops 32000000000 | bytes 96000000 | tf_op jit(solution)/shard_map/attn_sum/pallas_call | solution.py:670
  176.2 4.2 fusion.37
  180.4 4.0 convolution_convert_fusion.3.refs_0_
  184.4 58.5 %mlp_sum.1 = (bf16[2048,1024]{1,0:T(8,128)(2,1)}, f32[256,1024]{1,0:T(8,128)}) custom-call(bf16[1024,1024]{1,0:T(8,128)(2,1)} %convolution_convert_fusion.3.refs_0_, f32[256,1024]{1,0:T(8,128)} %get-tuple-element.98.refs_1_, f32[6,1024]{1,0:T(8,128)} %refs_7_.1), custom_call_target="tpu_custom_call" | custom-call | flops 57999998976 | bytes 174000000 | tf_op jit(solution)/shard_map/mlp_sum/pallas_call | solution.py:670
  243.0 46.9 %head_stats.1 = (bf16[6400,2048]{1,0:T(8,128)(2,1)}, f32[10,1,2048]{2,1,0:T(1,128)}, f32[10,1,2048]{2,1,0:T(1,128)}, f32[10,1,2048]{2,1,0:T(1,128)}) custom-call(bf16[1280,1024]{1,0:T(8,128)(2,1)} %all-gather.3.cloned.1.call-done.early_ref.refs_1_, bf16[5120,1024]{1,0:T(8,128)(2,1)} %all-gather.5.cloned.1.call-done.late_ref.refs_2_, ...), custom_call_target="tpu_custom_call" | custom-call | flops 26843545600 | bytes 39321600 | tf_op jit(solution)/shard_map/head_stats/pallas_call | solution.py:719
  289.9 1.0 reduce_max.18
  290.8 1.0 fusion.17
  292.4 7.3 %gather_stats.1 = f32[8,32,128]{2,1,0:T(8,128)} custom-call(f32[32,128]{1,0:T(8,128)} %pad_maximum_fusion.6.src_ref), custom_call_target="tpu_custom_call" | custom-call | flops 6000000000 | bytes 18000000 | tf_op jit(solution)/shard_map/gather_stats/pallas_call | solution.py:926
  299.8 1.0 reshape.310
  301.7 0.7 exponential_multiply_fusion.scale_ref
  302.4 33.7 %head_back.1 = (bf16[6400,2048]{1,0:T(8,128)(2,1)}, bf16[6400,1024]{1,0:T(8,128)(2,1)}) custom-call(bf16[6400,2048]{1,0:T(8,128)(2,1)} %get-tuple-element.100.exp_ref, bf16[2048,1024]{1,0:T(8,128)(2,1)} %get-tuple-element.99.final_ref, f32[10,1,2048]{2,1,0:T(1,128)} %exponential_multiply_fusion.scale_ref, f32[1,2048]{1,0:T(1,128)} %bitcast.130, ...), custom_call_target="tpu_custom_call" | custom-call | flops 26843545600 | bytes 65536000 | tf_op jit(solution)/shard_map/head_back/pallas_call | solution.py:761
  336.2 0.7 copy-done.29
  337.5 69.3 %final_back.1 = (bf16[1024,1024]{1,0:T(8,128)(2,1)}, f32[256,1024]{1,0:T(8,128)}, f32[8,1024]{1,0:T(8,128)}) custom-call(bf16[6400,2048]{1,0:T(8,128)(2,1)} %get-tuple-element.103.refs_0_, bf16[1280,1024]{1,0:T(8,128)(2,1)} %all-gather.3.cloned.1.call-done.early_ref.refs_1_, bf16[5120,1024]{1,0:T(8,128)(2,1)} %all-gather.5.cloned.1.call-done.late_ref.refs_2_, ...), custom_call_target="tpu_custom_call" | custom-call | flops 65000001536 | bytes 195000000 | tf_op jit(solution)/shard_map/final_back/pallas_call | solution.py:670
  406.9 7.0 %fusion.8 = bf16[1024,1024]{1,0:T(8,128)(2,1)S(1)} fusion(f32[1024,1024]{1,0:T(8,128)S(1)} %copy-done.46, bf16[1024,1024]{1,0:T(8,128)(2,1)} %get-tuple-element.105, bf16[1024,1024]{1,0:T(8,128)(2,1)} %get-tuple-element.97), kind=kOutput, calls=%fused_computation.14 | convolution fusion | flops 2168455168 | bytes 10485760 | tf_op jit(solution)/shard_map/td,fd->tf/dot_general | solution.py:1623
  413.9 3.7 convolution_convert_fusion.2.refs_0_
  417.6 34.4 %mlp_back.1 = (bf16[1024,1024]{1,0:T(8,128)(2,1)}, f32[256,1024]{1,0:T(8,128)}, f32[8,1024]{1,0:T(8,128)}) custom-call(bf16[1024,1024]{1,0:T(8,128)(2,1)} %convolution_convert_fusion.2.refs_0_, f32[256,1024]{1,0:T(8,128)} %get-tuple-element.98.refs_1_, f32[6,1024]{1,0:T(8,128)} %refs_7_.1, f32[256,1024]{1,0:T(8,128)} %get-tuple-element.106.refs_3_), custom_call_target="tpu_custom_call" | custom-call | flops 33999998976 | bytes 102000000 | tf_op jit(solution)/shard_map/mlp_back/pallas_call | solution.py:670
  452.1 2.5 convolution_convert_fusion.9.upstream_ref
  454.6 17.4 %attend_back.1 = bf16[1024,768]{1,0:T(8,128)(2,1)S(1)} custom-call(bf16[1024,768]{1,0:T(8,128)(2,1)S(1)} %copy-done.3, s32[1024,1]{1,0:T(8,128)S(1)} %copy.63.starts_ref, bf16[1024,256]{1,0:T(8,128)(2,1)S(1)} %convolution_convert_fusion.9.upstream_ref), custom_call_target="tpu_custom_call" | custom-call | flops 2684354560 | bytes 3145728 | tf_op jit(solution)/shard_map/attend_back/pallas_call | solution.py:870
  472.0 1.5 convolution_convert_fusion.8.refs_5_
  473.5 3.1 convolution_convert_fusion.5.refs_0_
  476.7 3.1 convolution_convert_fusion.6.refs_7_
  479.8 3.8 convolution_convert_fusion.refs_6_
  483.5 4.1 convolution_convert_fusion.1.refs_4_
  487.6 72.8 %attn_back.1 = (bf16[8192,256]{1,0:T(8,128)(2,1)}, f32[8,1024]{1,0:T(8,128)}, f32[512,256]{1,0:T(8,128)}, f32[128,256]{1,0:T(8,128)}, f32[256,512]{1,0:T(8,128)}...) custom-call(bf16[1024,1024]{1,0:T(8,128)(2,1)} %convolution_convert_fusion.5.refs_0_, ...), custom_call_target="tpu_custom_call" | custom-call | flops 70000001024 | bytes 210000000 | tf_op jit(solution)/shard_map/attn_back/pallas_call | solution.py:670
  560.5 2.9 collective-permute-start.2
  564.0 13.2 %scatter.1 = f32[6288,256]{1,0:T(8,128)} custom-call(s32[1]{0:T(128)} %bitcast.2.count_ref, s32[8192]{0:T(1024)} %get-tuple-element.84.key_ref, bf16[6400,256]{1,0:T(8,128)(2,1)} %reduce-scatter.2.cloned.1.call-done.head_ref, bf16[8192,256]{1,0:T(8,128)(2,1)} %get-tuple-element.112.rows_in_ref), custom_call_target="tpu_custom_call" | custom-call | flops 23000000512 | bytes 69000000 | tf_op jit(solution)/shard_map/scatter/pallas_call | solution.py:1355
  577.2 4.6 fusion
  581.8 11.8 %collective-permute-done.2 = bf16[640,256]{1,0:T(8,128)(2,1)S(1)} collective-permute-done((bf16[640,256]{1,0:T(8,128)(2,1)}, bf16[640,256]{1,0:T(8,128)(2,1)S(1)}, u32[]{:S(2)}, u32[]{:S(2)}) %collective-permute-start.2) | collective-permute-done | bytes 327712 | tf_op jit(solution)/shard_map/ppermute | solution.py:1680
  593.5 0.8 fusion.11
  594.3 0.7 fusion.18
  595.0 0.8 fusion.9
  595.7 0.7 fusion.13
  597.1 12.8 %update_stats.1 = (f32[50,128]{1,0:T(8,128)}, f32[2,128]{1,0:T(2,128)}, f32[1,128]{1,0:T(1,128)}, f32[2,128]{1,0:T(2,128)}, f32[4,128]{1,0:T(4,128)}, /*index=5*...) custom-call(f32[50,128]{1,0:T(8,128)} %pad_bitcast_fusion.1.refs_0_,, ...), custom_call_target="tpu_custom_call" | custom-call | flops 12000000000 | bytes 36000000 | tf_op jit(solution)/shard_map/update_stats/pallas_call | solution.py:1139
  610.0 1.4 fusion.35
  611.4 5.5 multiply_reduce_fusion
  616.8 1.4 multiply_reduce_fusion.1
  618.3 1.4 multiply_reduce_fusion.2
  619.7 1.3 multiply_reduce_fusion.7
  621.0 1.4 multiply_reduce_fusion.5
  622.4 11.1 %clip_rates.1 = (f32[8,128]{1,0:T(8,128)}, f32[6,1024]{1,0:T(8,128)}, f32[6,1024]{1,0:T(8,128)}, f32[6,1024]{1,0:T(8,128)}) custom-call(f32[2,128]{1,0:T(2,128)} %bitcast.180, f32[3,128]{1,0:T(4,128)} %bitcast.167, f32[2,128]{1,0:T(2,128)} %bitcast.177, f32[4,128]{1,0:T(4,128)} %bitcast.166, f32[2,128]{1,0:T(2,128)} %bitcast.176, ...), custom_call_target="tpu_custom_call" | custom-call | flops 8000000000 | bytes 24000000 | tf_op jit(solution)/shard_map/clip_rates/pallas_call | solution.py:1228
  633.5 1.4 fusion.36
  634.9 2.3 multiply_subtract_fusion.1
  637.2 2.3 multiply_subtract_fusion.2
  639.4 2.0 multiply_subtract_fusion.4
  641.5 2.2 multiply_subtract_fusion.3
  643.7 9.1 %multiply_subtract_fusion = f32[6288,256]{1,0:T(8,128)} fusion(f32[6288,256]{1,0:T(8,128)} %table_ref.1, f32[]{:T(128)} %bitcast.58, f32[6288,256]{1,0:T(8,128)} %scatter.1, f32[]{:T(128)} %bitcast.40, f32[256]{0:T(256)S(1)} %bitcast.158, f32[6288]{0:T(1024)S(1)} %bitcast.122), kind=kLoop, calls=%fused_computation | loop fusion | flops 8048640 | bytes 19342920 | tf_op jit(solution)/shard_map/sub | solution.py:1733
  (176 shorter events, 16.2 us)
Async XLA Ops:
  7.2 10.2 %copy-start.7 = (f32[512,256]{1,0:T(8,128)S(1)}, f32[512,256]{1,0:T(8,128)}, u32[]{:S(2)}) copy-start(f32[512,256]{1,0:T(8,128)} %param.29) | copy-start | bytes 1572868
  7.2 10.9 %copy-start.16 = (f32[128,256]{1,0:T(8,128)S(1)}, f32[128,256]{1,0:T(8,128)}, u32[]{:S(2)}) copy-start(f32[128,256]{1,0:T(8,128)} %param.27) | copy-start | bytes 393220
  7.2 11.6 %copy-start.39 = (s32[2048]{0:T(1024)S(1)}, s32[2048]{0:T(1024)}, u32[]{:S(2)}) copy-start(s32[2048]{0:T(1024)} %param.21) | copy-start | bytes 24580
  7.2 11.5 %copy-start.28 = (s32[2048]{0:T(1024)S(1)}, s32[2048]{0:T(1024)}, u32[]{:S(2)}) copy-start(s32[2048]{0:T(1024)} %param.24) | copy-start | bytes 24580
  7.2 47.8 %all-gather.3.cloned.1.call-start = ((), (), s32[]{:S(2)}) async-start(), calls=%async_computation.1 | async-start | bytes 3276800 | tf_op jit(solution)/shard_map/all_gather | solution.py:1488
  9.6 233.4 %all-gather.5.cloned.1.call-start = ((), (), s32[]{:S(2)}) async-start(), calls=%async_computation.2 | async-start | bytes 13107200 | tf_op jit(solution)/shard_map/all_gather | solution.py:1537
  13.3 40.0 %collective-permute-start = (bf16[256,896]{1,0:T(8,128)(2,1)S(1)}, bf16[256,896]{1,0:T(8,128)(2,1)S(1)}, u32[]{:S(2)}, u32[]{:S(2)}) collective-permute-start(bf16[256,896]{1,0:T(8,128)(2,1)S(1)} %pad_maximum_fusion.2), channel_id=1, source_target_pairs={{0,4},{1,5},{2,6},{3,7},{4,0},{5,1},{6,2},{7,3},{8,12},{9,13},{10,... | collective-permute-start | bytes 1376264 | tf_op jit(solution)/shard_map/ppermute | solution.py:1476
  18.7 33.1 %collective-permute-start.1 = (bf16[640,256]{1,0:T(8,128)(2,1)S(1)}, bf16[640,256]{1,0:T(8,128)(2,1)S(1)}, u32[]{:S(2)}, u32[]{:S(2)}) collective-permute-start(bf16[640,256]{1,0:T(8,128)(2,1)S(1)} %pad_maximum_fusion.4), channel_id=1, source_target_pairs={{0,4},{1,5},{2,6},{3,7},{4,0},{5,1},{6,2},{7,3},{8,12},{9,13},{10,... | collective-permute-start | bytes 983048 | tf_op jit(solution)/shard_map/ppermute | solution.py:1476
  55.0 70.4 %copy-start.41 = (s32[2048]{0:T(1024)S(1)}, s32[2048]{0:T(1024)}, u32[]{:S(2)}) copy-start(s32[2048]{0:T(1024)} %param.23) | copy-start | bytes 24580
  55.0 70.6 %copy-start.38 = (s32[2048]{0:T(1024)S(1)}, s32[2048]{0:T(1024)}, u32[]{:S(2)}) copy-start(s32[2048]{0:T(1024)} %param.22) | copy-start | bytes 24580
  125.1 438.9 %reduce-scatter.2.cloned.1.call-start = ((), (), s32[]{:S(2)}) async-start(), calls=%async_computation.3 | async-start | bytes 16384000 | tf_op jit(solution)/shard_map/reduce_scatter | solution.py:1605
  126.1 4.5 copy-start.42
  130.6 12.4 %copy-start.2 = (bf16[1024,768]{1,0:T(8,128)(2,1)}, bf16[1024,768]{1,0:T(8,128)(2,1)S(1)}, u32[]{:S(2)}) copy-start(bf16[1024,768]{1,0:T(8,128)(2,1)S(1)} %convolution_convert_fusion.7.mixed_ref) | copy-start | bytes 4718596
  130.6 10.3 %copy-start.18 = (bf16[256,1024]{1,0:T(8,128)(2,1)S(1)}, bf16[256,1024]{1,0:T(8,128)(2,1)}, u32[]{:S(2)}) copy-start(bf16[256,1024]{1,0:T(8,128)(2,1)} %get-tuple-element.93) | copy-start | bytes 1572868
  140.1 0.8 copy-start
  143.0 33.3 %copy-start.50 = (bf16[1024,1024]{1,0:T(8,128)(2,1)S(1)}, bf16[1024,1024]{1,0:T(8,128)(2,1)}, u32[]{:S(2)}) copy-start(bf16[1024,1024]{1,0:T(8,128)(2,1)} %get-tuple-element.96) | copy-start | bytes 6291460
  176.2 4.2 copy-start.54
  180.4 4.0 copy-start.45
  292.4 8.4 %copy-start.23 = (f32[10,1,2048]{2,1,0:T(1,128)S(1)}, f32[10,1,2048]{2,1,0:T(1,128)}, u32[]{:S(2)}) copy-start(f32[10,1,2048]{2,1,0:T(1,128)} %get-tuple-element.121) | copy-start | bytes 245764
  292.4 9.3 %copy-start.13 = (f32[10,1,2048]{2,1,0:T(1,128)S(1)}, f32[10,1,2048]{2,1,0:T(1,128)}, u32[]{:S(2)}) copy-start(f32[10,1,2048]{2,1,0:T(1,128)} %get-tuple-element.101) | copy-start | bytes 245764
  301.7 0.7 copy-start.24
  336.2 0.7 copy-start.29
  337.5 69.4 %copy-start.46 = (f32[1024,1024]{1,0:T(8,128)S(1)}, f32[1024,1024]{1,0:T(8,128)}, u32[]{:S(2)}) copy-start(f32[1024,1024]{1,0:T(8,128)} %copy-done.45) | copy-start | bytes 12582916
  406.9 7.0 %copy-start.51 = (bf16[1024,1024]{1,0:T(8,128)(2,1)S(1)}, bf16[1024,1024]{1,0:T(8,128)(2,1)}, u32[]{:S(2)}) copy-start(bf16[1024,1024]{1,0:T(8,128)(2,1)} %get-tuple-element.96) | copy-start | bytes 6291460
  417.6 34.4 %copy-start.19 = (bf16[256,1024]{1,0:T(8,128)(2,1)S(1)}, bf16[256,1024]{1,0:T(8,128)(2,1)}, u32[]{:S(2)}) copy-start(bf16[256,1024]{1,0:T(8,128)(2,1)} %get-tuple-element.93) | copy-start | bytes 1572868
  452.1 2.5 copy-start.3
  454.5 17.4 %copy-start.1 = (bf16[1024,256]{1,0:T(8,128)(2,1)S(1)}, bf16[1024,256]{1,0:T(8,128)(2,1)}, u32[]{:S(2)}) copy-start(bf16[1024,256]{1,0:T(8,128)(2,1)} %copy-done) | copy-start | bytes 1572868
  454.6 17.4 %copy-start.10 = (bf16[1024,1024]{1,0:T(8,128)(2,1)S(1)}, bf16[1024,1024]{1,0:T(8,128)(2,1)}, u32[]{:S(2)}) copy-start(bf16[1024,1024]{1,0:T(8,128)(2,1)} %get-tuple-element.107) | copy-start | bytes 6291460
  454.6 18.9 %copy-start.49 = (bf16[1024,768]{1,0:T(8,128)(2,1)S(1)}, bf16[1024,768]{1,0:T(8,128)(2,1)}, u32[]{:S(2)}) copy-start(bf16[1024,768]{1,0:T(8,128)(2,1)} %get-tuple-element.90) | copy-start | bytes 4718596
  473.5 3.1 copy-start.48
  476.7 3.1 copy-start.52
  479.8 3.8 copy-start.47
  479.8 3.8 copy-start.53
  487.6 75.8 %copy-start.43 = (f32[4]{0:T(128)S(1)}, f32[4]{0:T(128)}, u32[]{:S(2)}) copy-start(f32[4]{0:T(128)} %get-tuple-element.152) | copy-start | bytes 52
  560.5 33.1 %collective-permute-start.3 = (bf16[256,896]{1,0:T(8,128)(2,1)}, bf16[256,896]{1,0:T(8,128)(2,1)S(1)}, u32[]{:S(2)}, u32[]{:S(2)}) collective-permute-start(bf16[256,896]{1,0:T(8,128)(2,1)} %get-tuple-element.110), channel_id=1, source_target_pairs={{0,4},{1,5},{2,6},{3,7},{4,0},{5,1},{6,2},{7,3},{8,12},{9,13},{10,... | collective-permute-start | bytes 1376264 | tf_op jit(solution)/shard_map/ppermute | solution.py:1680
  560.5 33.0 %collective-permute-start.2 = (bf16[640,256]{1,0:T(8,128)(2,1)}, bf16[640,256]{1,0:T(8,128)(2,1)S(1)}, u32[]{:S(2)}, u32[]{:S(2)}) collective-permute-start(bf16[640,256]{1,0:T(8,128)(2,1)} %get-tuple-element.109), channel_id=1, source_target_pairs={{0,4},{1,5},{2,6},{3,7},{4,0},{5,1},{6,2},{7,3},{8,12},{9,13},{10,... | collective-permute-start | bytes 983048 | tf_op jit(solution)/shard_map/ppermute | solution.py:1680
  577.2 16.3 %copy-start.15 = (f32[512,256]{1,0:T(8,128)S(1)}, f32[512,256]{1,0:T(8,128)}, u32[]{:S(2)}) copy-start(f32[512,256]{1,0:T(8,128)} %get-tuple-element.119) | copy-start | bytes 1572868
  577.2 17.1 %copy-start.22 = (f32[128,256]{1,0:T(8,128)S(1)}, f32[128,256]{1,0:T(8,128)}, u32[]{:S(2)}) copy-start(f32[128,256]{1,0:T(8,128)} %get-tuple-element.116) | copy-start | bytes 393220
  577.2 17.8 %copy-start.14 = (f32[256,512]{1,0:T(8,128)S(1)}, f32[256,512]{1,0:T(8,128)}, u32[]{:S(2)}) copy-start(f32[256,512]{1,0:T(8,128)} %get-tuple-element.118) | copy-start | bytes 1572868
  577.2 18.5 %copy-start.20 = (f32[256,384]{1,0:T(8,128)S(1)}, f32[256,384]{1,0:T(8,128)}, u32[]{:S(2)}) copy-start(f32[256,384]{1,0:T(8,128)} %get-tuple-element.114) | copy-start | bytes 1179652
  594.3 40.6 %copy-start.4 = (f32[512,256]{1,0:T(8,128)}, f32[512,256]{1,0:T(8,128)S(1)}, u32[]{:S(2)}) copy-start(f32[512,256]{1,0:T(8,128)S(1)} %get-tuple-element.231) | copy-start | bytes 1572868
  595.0 44.4 %copy-start.12 = (f32[128,256]{1,0:T(8,128)}, f32[128,256]{1,0:T(8,128)S(1)}, u32[]{:S(2)}) copy-start(f32[128,256]{1,0:T(8,128)S(1)} %get-tuple-element.223) | copy-start | bytes 393220
  595.7 41.4 %copy-start.5 = (f32[256,512]{1,0:T(8,128)}, f32[256,512]{1,0:T(8,128)S(1)}, u32[]{:S(2)}) copy-start(f32[256,512]{1,0:T(8,128)S(1)} %get-tuple-element.227) | copy-start | bytes 1572868
  596.5 45.0 %copy-start.6 = (f32[256,384]{1,0:T(8,128)}, f32[256,384]{1,0:T(8,128)S(1)}, u32[]{:S(2)}) copy-start(f32[256,384]{1,0:T(8,128)S(1)} %get-tuple-element.219) | copy-start | bytes 1179652
  609.9 7.0 %copy-start.30 = (f32[4,128]{1,0:T(4,128)S(1)}, f32[4,128]{1,0:T(4,128)}, u32[]{:S(2)}) copy-start(f32[4,128]{1,0:T(4,128)} %get-tuple-element.135) | copy-start | bytes 6148
  609.9 6.9 %copy-start.33 = (f32[2,128]{1,0:T(2,128)S(1)}, f32[2,128]{1,0:T(2,128)}, u32[]{:S(2)}) copy-start(f32[2,128]{1,0:T(2,128)} %get-tuple-element.136) | copy-start | bytes 3076
  609.9 8.3 %copy-start.31 = (f32[4,128]{1,0:T(4,128)S(1)}, f32[4,128]{1,0:T(4,128)}, u32[]{:S(2)}) copy-start(f32[4,128]{1,0:T(4,128)} %get-tuple-element.134) | copy-start | bytes 6148
  609.9 8.3 %copy-start.34 = (f32[2,128]{1,0:T(2,128)S(1)}, f32[2,128]{1,0:T(2,128)}, u32[]{:S(2)}) copy-start(f32[2,128]{1,0:T(2,128)} %get-tuple-element.133) | copy-start | bytes 3076
  609.9 9.7 %copy-start.35 = (f32[2,128]{1,0:T(2,128)S(1)}, f32[2,128]{1,0:T(2,128)}, u32[]{:S(2)}) copy-start(f32[2,128]{1,0:T(2,128)} %get-tuple-element.132) | copy-start | bytes 3076
  609.9 9.7 %copy-start.40 = (f32[1,128]{1,0:T(1,128)S(1)}, f32[1,128]{1,0:T(1,128)}, u32[]{:S(2)}) copy-start(f32[1,128]{1,0:T(1,128)} %get-tuple-element.131) | copy-start | bytes 1540
  610.0 11.0 %copy-start.32 = (f32[3,128]{1,0:T(4,128)S(1)}, f32[3,128]{1,0:T(4,128)}, u32[]{:S(2)}) copy-start(f32[3,128]{1,0:T(4,128)} %get-tuple-element.130) | copy-start | bytes 4612
  610.0 11.0 %copy-start.36 = (f32[2,128]{1,0:T(2,128)S(1)}, f32[2,128]{1,0:T(2,128)}, u32[]{:S(2)}) copy-start(f32[2,128]{1,0:T(2,128)} %get-tuple-element.129) | copy-start | bytes 3076
  622.4 12.5 %copy-start.8 = (f32[512,256]{1,0:T(8,128)S(1)}, f32[512,256]{1,0:T(8,128)}, u32[]{:S(2)}) copy-start(f32[512,256]{1,0:T(8,128)} %param.29) | copy-start | bytes 1572868
  622.4 14.8 %copy-start.9 = (f32[256,512]{1,0:T(8,128)S(1)}, f32[256,512]{1,0:T(8,128)}, u32[]{:S(2)}) copy-start(f32[256,512]{1,0:T(8,128)} %param.28) | copy-start | bytes 1572868
  622.4 17.0 %copy-start.17 = (f32[128,256]{1,0:T(8,128)S(1)}, f32[128,256]{1,0:T(8,128)}, u32[]{:S(2)}) copy-start(f32[128,256]{1,0:T(8,128)} %param.27) | copy-start | bytes 393220
  622.4 19.1 %copy-start.11 = (f32[256,384]{1,0:T(8,128)S(1)}, f32[256,384]{1,0:T(8,128)}, u32[]{:S(2)}) copy-start(f32[256,384]{1,0:T(8,128)} %param.26) | copy-start | bytes 1179652
  633.5 10.2 %copy-start.21 = (f32[50,128]{1,0:T(8,128)S(1)}, f32[50,128]{1,0:T(8,128)}, u32[]{:S(2)}) copy-start(f32[50,128]{1,0:T(8,128)} %get-tuple-element.126) | copy-start | bytes 76804
  633.5 10.2 %copy-start.37 = (f32[2,128]{1,0:T(2,128)S(1)}, f32[2,128]{1,0:T(2,128)}, u32[]{:S(2)}) copy-start(f32[2,128]{1,0:T(2,128)} %get-tuple-element.127) | copy-start | bytes 3076
  643.7 9.1 %copy-start.44 = (f32[1,128]{1,0:T(1,128)S(1)}, f32[1,128]{1,0:T(1,128)}, u32[]{:S(2)}) copy-start(f32[1,128]{1,0:T(1,128)} %get-tuple-element.125) | copy-start | bytes 1540
  643.7 15.3 %copy-start.27 = (f32[6,1024]{1,0:T(8,128)S(1)}, f32[6,1024]{1,0:T(8,128)}, u32[]{:S(2)}) copy-start(f32[6,1024]{1,0:T(8,128)} %get-tuple-element.235) | copy-start | bytes 73732
  643.7 15.9 %copy-start.26 = (f32[6,1024]{1,0:T(8,128)S(1)}, f32[6,1024]{1,0:T(8,128)}, u32[]{:S(2)}) copy-start(f32[6,1024]{1,0:T(8,128)} %get-tuple-element.236) | copy-start | bytes 73732
  643.7 16.5 %copy-start.25 = (f32[6,1024]{1,0:T(8,128)S(1)}, f32[6,1024]{1,0:T(8,128)}, u32[]{:S(2)}) copy-start(f32[6,1024]{1,0:T(8,128)} %get-tuple-element.237) | copy-start | bytes 73732
Sparse Core Ops, SparseCore 0:
  9.9 43.5 all-gather.2
  125.2 107.4 all-gather.4
  336.3 124.5 reduce-scatter.1

commit v12 on v11

--- a/solution.py
+++ b/solution.py
@@ -1244,7 +1244,7 @@
     )(*[lane_rows(v) for v in step_parts], rate, part, norms, second)
 
 
-UNROLL = 8
+UNROLL = 16
 
 
 def lookup_kernel(shift, early, count_ref, key_ref, table_ref, out_ref, low_ref, square_ref, rows_ref):

time: 674 us -> 674 us (level)
  no operation moved by 1% of the time
where the time goes in v12:
time: 674 us; the launch traced here: 668 us
  Pallas kernels  511 us (76%)
  other arithmetic  57 us (8%)
  matrix products  42.8 us (6%)
  local copies, waits for them, and re-layouts  19.7 us (3%)
  waiting for transfers between devices  15.1 us (2%)
  between operations  14.7 us (2%)
  starting transfers between devices  7.46 us (1%)
    pallas_call x6, Pallas kernels, line_call(): return list(call(*args))  338 us
    pallas_call x1, Pallas kernels, head_stats(): pl.pallas_call(functools.partial(head_stats_kernel, block, tile, early),...  46.9 us
    pallas_call x1, Pallas kernels, head_back(): pl.pallas_call(functools.partial(head_back_kernel, block, tile), grid=(ro...  33.7 us
    sub x5, other arithmetic, local(): updated = [weights[n] - factors[n, 0] * steps[n] for n in range(5)]  17.8 us
    pallas_call x1, Pallas kernels, attend_back(): pl.pallas_call(attend_back_kernel, grid=(pairs,), out_shape=jax.ShapeDtyp...  17.4 us
    pallas_call x2, Pallas kernels, small_gather(): pl.pallas_call(functools.partial(small_gather_kernel, axis, count), out_s...  14.6 us
    pallas_call x1, Pallas kernels, scatter(): pl.pallas_call(functools.partial(scatter_kernel, shift), out_shape=jax.Sh...  13.6 us
  transfers between devices with their start and end apart: 7, of which 2 were waited for; matrix products, arithmetic and copies ran while one was open for 10% of the time, Pallas kernels for 49%

profile of v12, /device:TPU:0, one launch (start us, length us, event | category | flops | bytes accessed | tf_op | source)
XLA Modules:
  0.0 667.6 jit_solution(9764856249278049078)
XLA Ops:
  7.3 2.3 slice.125
  9.6 1.9 multiply_reduce_fusion.4
  11.5 1.8 multiply_reduce_fusion.6
  13.3 4.1 collective-permute-start
  19.4 7.3 %gather_ids.1 = s32[4,32,128]{2,1,0:T(8,128)} custom-call(s32[32,128]{1,0:T(8,128)} %reshape.304.src_ref), custom_call_target="tpu_custom_call" | custom-call | flops 6000000000 | bytes 18000000 | tf_op jit(solution)/shard_map/gather_ids/pallas_call | solution.py:926
  26.7 0.9 reshape.305
  28.5 6.8 %sort.14 = (s32[8192]{0:T(1024)}, s32[8192]{0:T(1024)}) sort(s32[8192]{0:T(1024)S(1)} %add_select_fusion, s32[8192]{0:T(1024)S(1)} %iota.23), dimensions={0}, to_apply=%region_1.2 | sort | flops 106496 | bytes 131072 | tf_op jit(solution)/shard_map/jit(sort)/sort | solution.py:1510
  35.3 13.0 %lookup.1 = (bf16[8192,256]{1,0:T(8,128)(2,1)}, bf16[5120,256]{1,0:T(8,128)(2,1)}, f32[8,128]{1,0:T(8,128)}) custom-call(s32[1]{0:T(128)} %bitcast.2.count_ref, s32[8192]{0:T(1024)} %get-tuple-element.84.key_ref, f32[6288,256]{1,0:T(8,128)} %table_ref.1), custom_call_target="tpu_custom_call" | custom-call | flops 20000000000 | bytes 60000000 | tf_op jit(solution)/shard_map/lookup/pallas_call | solution.py:1312
  48.2 3.6 collective-permute-done.1
  51.8 0.7 pad_maximum_fusion.5.refs_3_
  52.5 0.8 pad_maximum_fusion.1.refs_5_
  53.4 0.8 pad_maximum_fusion.3.refs_2_
  54.2 0.9 pad_maximum_fusion.refs_4_
  55.0 69.1 %lookup_sum.1 = (bf16[1024,1024]{1,0:T(8,128)(2,1)}, bf16[256,1024]{1,0:T(8,128)(2,1)}, bf16[1024,768]{1,0:T(8,128)(2,1)}, bf16[256,1024]{1,0:T(8,128)(2,1)}, bf...) custom-call(bf16[8192,256]{1,0:T(8,128)(2,1)} %get-tuple-element.87.refs_0_, f32[6,1024]{1,0:T(8,128)} %refs_7_.1, ...), custom_call_target="tpu_custom_call" | custom-call | flops 70000001024 | bytes 210000000 | tf_op jit(solution)/shard_map/lookup_sum/pallas_call | solution.py:670
  125.8 3.8 convolution_convert_fusion.7.mixed_ref
  129.6 9.5 %attend.1 = bf16[1024,256]{1,0:T(8,128)(2,1)S(1)} custom-call(bf16[1024,768]{1,0:T(8,128)(2,1)S(1)} %convolution_convert_fusion.7.mixed_ref, s32[1024,1]{1,0:T(8,128)S(1)} %copy.63.starts_ref), custom_call_target="tpu_custom_call" | custom-call | flops 1073741824 | bytes 1572864 | tf_op jit(solution)/shard_map/attend/pallas_call | solution.py:822
  139.2 0.8 copy-done
  140.0 2.0 convolution_convert_fusion.4.refs_0_
  142.0 34.2 %attn_sum.1 = (bf16[1024,1024]{1,0:T(8,128)(2,1)}, f32[256,1024]{1,0:T(8,128)}) custom-call(bf16[1024,1024]{1,0:T(8,128)(2,1)} %convolution_convert_fusion.4.refs_0_, bf16[256,1024]{1,0:T(8,128)(2,1)} %get-tuple-element.94.refs_1_, f32[6,1024]{1,0:T(8,128)} %refs_7_.1), custom_call_target="tpu_custom_call" | custom-call | flops 32000000000 | bytes 96000000 | tf_op jit(solution)/shard_map/attn_sum/pallas_call | solution.py:670
  176.2 4.2 fusion.37
  180.4 4.0 convolution_convert_fusion.3.refs_0_
  184.5 58.5 %mlp_sum.1 = (bf16[2048,1024]{1,0:T(8,128)(2,1)}, f32[256,1024]{1,0:T(8,128)}) custom-call(bf16[1024,1024]{1,0:T(8,128)(2,1)} %convolution_convert_fusion.3.refs_0_, f32[256,1024]{1,0:T(8,128)} %get-tuple-element.98.refs_1_, f32[6,1024]{1,0:T(8,128)} %refs_7_.1), custom_call_target="tpu_custom_call" | custom-call | flops 57999998976 | bytes 174000000 | tf_op jit(solution)/shard_map/mlp_sum/pallas_call | solution.py:670
  243.0 46.9 %head_stats.1 = (bf16[6400,2048]{1,0:T(8,128)(2,1)}, f32[10,1,2048]{2,1,0:T(1,128)}, f32[10,1,2048]{2,1,0:T(1,128)}, f32[10,1,2048]{2,1,0:T(1,128)}) custom-call(bf16[1280,1024]{1,0:T(8,128)(2,1)} %all-gather.3.cloned.1.call-done.early_ref.refs_1_, bf16[5120,1024]{1,0:T(8,128)(2,1)} %all-gather.5.cloned.1.call-done.late_ref.refs_2_, ...), custom_call_target="tpu_custom_call" | custom-call | flops 26843545600 | bytes 39321600 | tf_op jit(solution)/shard_map/head_stats/pallas_call | solution.py:719
  289.9 1.0 reduce_max.18
  290.8 1.0 fusion.17
  292.4 7.3 %gather_stats.1 = f32[8,32,128]{2,1,0:T(8,128)} custom-call(f32[32,128]{1,0:T(8,128)} %pad_maximum_fusion.6.src_ref), custom_call_target="tpu_custom_call" | custom-call | flops 6000000000 | bytes 18000000 | tf_op jit(solution)/shard_map/gather_stats/pallas_call | solution.py:926
  299.8 1.0 reshape.310
  301.7 0.7 exponential_multiply_fusion.scale_ref
  302.4 33.7 %head_back.1 = (bf16[6400,2048]{1,0:T(8,128)(2,1)}, bf16[6400,1024]{1,0:T(8,128)(2,1)}) custom-call(bf16[6400,2048]{1,0:T(8,128)(2,1)} %get-tuple-element.100.exp_ref, bf16[2048,1024]{1,0:T(8,128)(2,1)} %get-tuple-element.99.final_ref, f32[10,1,2048]{2,1,0:T(1,128)} %exponential_multiply_fusion.scale_ref, f32[1,2048]{1,0:T(1,128)} %bitcast.130, ...), custom_call_target="tpu_custom_call" | custom-call | flops 26843545600 | bytes 65536000 | tf_op jit(solution)/shard_map/head_back/pallas_call | solution.py:761
  336.2 0.7 copy-done.29
  337.5 69.3 %final_back.1 = (bf16[1024,1024]{1,0:T(8,128)(2,1)}, f32[256,1024]{1,0:T(8,128)}, f32[8,1024]{1,0:T(8,128)}) custom-call(bf16[6400,2048]{1,0:T(8,128)(2,1)} %get-tuple-element.103.refs_0_, bf16[1280,1024]{1,0:T(8,128)(2,1)} %all-gather.3.cloned.1.call-done.early_ref.refs_1_, bf16[5120,1024]{1,0:T(8,128)(2,1)} %all-gather.5.cloned.1.call-done.late_ref.refs_2_, ...), custom_call_target="tpu_custom_call" | custom-call | flops 65000001536 | bytes 195000000 | tf_op jit(solution)/shard_map/final_back/pallas_call | solution.py:670
  406.9 7.0 %fusion.8 = bf16[1024,1024]{1,0:T(8,128)(2,1)S(1)} fusion(f32[1024,1024]{1,0:T(8,128)S(1)} %copy-done.46, bf16[1024,1024]{1,0:T(8,128)(2,1)} %get-tuple-element.105, bf16[1024,1024]{1,0:T(8,128)(2,1)} %get-tuple-element.97), kind=kOutput, calls=%fused_computation.14 | convolution fusion | flops 2168455168 | bytes 10485760 | tf_op jit(solution)/shard_map/td,fd->tf/dot_general | solution.py:1623
  413.9 3.7 convolution_convert_fusion.2.refs_0_
  417.6 34.4 %mlp_back.1 = (bf16[1024,1024]{1,0:T(8,128)(2,1)}, f32[256,1024]{1,0:T(8,128)}, f32[8,1024]{1,0:T(8,128)}) custom-call(bf16[1024,1024]{1,0:T(8,128)(2,1)} %convolution_convert_fusion.2.refs_0_, f32[256,1024]{1,0:T(8,128)} %get-tuple-element.98.refs_1_, f32[6,1024]{1,0:T(8,128)} %refs_7_.1, f32[256,1024]{1,0:T(8,128)} %get-tuple-element.106.refs_3_), custom_call_target="tpu_custom_call" | custom-call | flops 33999998976 | bytes 102000000 | tf_op jit(solution)/shard_map/mlp_back/pallas_call | solution.py:670
  452.1 2.5 convolution_convert_fusion.9.upstream_ref
  454.6 17.4 %attend_back.1 = bf16[1024,768]{1,0:T(8,128)(2,1)S(1)} custom-call(bf16[1024,768]{1,0:T(8,128)(2,1)S(1)} %copy-done.3, s32[1024,1]{1,0:T(8,128)S(1)} %copy.63.starts_ref, bf16[1024,256]{1,0:T(8,128)(2,1)S(1)} %convolution_convert_fusion.9.upstream_ref), custom_call_target="tpu_custom_call" | custom-call | flops 2684354560 | bytes 3145728 | tf_op jit(solution)/shard_map/attend_back/pallas_call | solution.py:870
  472.0 1.5 convolution_convert_fusion.8.refs_5_
  473.5 3.1 convolution_convert_fusion.5.refs_0_
  476.7 3.1 convolution_convert_fusion.6.refs_7_
  479.8 3.8 convolution_convert_fusion.refs_6_
  483.5 4.1 convolution_convert_fusion.1.refs_4_
  487.6 72.8 %attn_back.1 = (bf16[8192,256]{1,0:T(8,128)(2,1)}, f32[8,1024]{1,0:T(8,128)}, f32[512,256]{1,0:T(8,128)}, f32[128,256]{1,0:T(8,128)}, f32[256,512]{1,0:T(8,128)}...) custom-call(bf16[1024,1024]{1,0:T(8,128)(2,1)} %convolution_convert_fusion.5.refs_0_, ...), custom_call_target="tpu_custom_call" | custom-call | flops 70000001024 | bytes 210000000 | tf_op jit(solution)/shard_map/attn_back/pallas_call | solution.py:670
  560.5 2.9 collective-permute-start.2
  564.0 13.6 %scatter.1 = f32[6288,256]{1,0:T(8,128)} custom-call(s32[1]{0:T(128)} %bitcast.2.count_ref, s32[8192]{0:T(1024)} %get-tuple-element.84.key_ref, bf16[6400,256]{1,0:T(8,128)(2,1)} %reduce-scatter.2.cloned.1.call-done.head_ref, bf16[8192,256]{1,0:T(8,128)(2,1)} %get-tuple-element.112.rows_in_ref), custom_call_target="tpu_custom_call" | custom-call | flops 23000000512 | bytes 69000000 | tf_op jit(solution)/shard_map/scatter/pallas_call | solution.py:1355
  577.5 4.6 fusion
  582.1 11.4 %collective-permute-done.2 = bf16[640,256]{1,0:T(8,128)(2,1)S(1)} collective-permute-done((bf16[640,256]{1,0:T(8,128)(2,1)}, bf16[640,256]{1,0:T(8,128)(2,1)S(1)}, u32[]{:S(2)}, u32[]{:S(2)}) %collective-permute-start.2) | collective-permute-done | bytes 327712 | tf_op jit(solution)/shard_map/ppermute | solution.py:1680
  593.5 0.8 fusion.11
  594.3 0.7 fusion.18
  595.0 0.8 fusion.9
  595.7 0.7 fusion.13
  597.1 12.8 %update_stats.1 = (f32[50,128]{1,0:T(8,128)}, f32[2,128]{1,0:T(2,128)}, f32[1,128]{1,0:T(1,128)}, f32[2,128]{1,0:T(2,128)}, f32[4,128]{1,0:T(4,128)}, /*index=5*...) custom-call(f32[50,128]{1,0:T(8,128)} %pad_bitcast_fusion.1.refs_0_,, ...), custom_call_target="tpu_custom_call" | custom-call | flops 12000000000 | bytes 36000000 | tf_op jit(solution)/shard_map/update_stats/pallas_call | solution.py:1139
  610.0 1.4 fusion.35
  611.4 5.5 multiply_reduce_fusion
  616.8 1.4 multiply_reduce_fusion.1
  618.3 1.4 multiply_reduce_fusion.2
  619.7 1.3 multiply_reduce_fusion.7
  621.0 1.4 multiply_reduce_fusion.5
  622.4 11.1 %clip_rates.1 = (f32[8,128]{1,0:T(8,128)}, f32[6,1024]{1,0:T(8,128)}, f32[6,1024]{1,0:T(8,128)}, f32[6,1024]{1,0:T(8,128)}) custom-call(f32[2,128]{1,0:T(2,128)} %bitcast.180, f32[3,128]{1,0:T(4,128)} %bitcast.167, f32[2,128]{1,0:T(2,128)} %bitcast.177, f32[4,128]{1,0:T(4,128)} %bitcast.166, f32[2,128]{1,0:T(2,128)} %bitcast.176, ...), custom_call_target="tpu_custom_call" | custom-call | flops 8000000000 | bytes 24000000 | tf_op jit(solution)/shard_map/clip_rates/pallas_call | solution.py:1228
  633.5 1.4 fusion.36
  634.9 2.3 multiply_subtract_fusion.1
  637.2 2.3 multiply_subtract_fusion.2
  639.4 2.0 multiply_subtract_fusion.4
  641.5 2.2 multiply_subtract_fusion.3
  643.7 9.1 %multiply_subtract_fusion = f32[6288,256]{1,0:T(8,128)} fusion(f32[6288,256]{1,0:T(8,128)} %table_ref.1, f32[]{:T(128)} %bitcast.58, f32[6288,256]{1,0:T(8,128)} %scatter.1, f32[]{:T(128)} %bitcast.40, f32[256]{0:T(256)S(1)} %bitcast.158, f32[6288]{0:T(1024)S(1)} %bitcast.122), kind=kLoop, calls=%fused_computation | loop fusion | flops 8048640 | bytes 19342920 | tf_op jit(solution)/shard_map/sub | solution.py:1733
  (176 shorter events, 16.2 us)
Async XLA Ops:
  7.2 10.2 %copy-start.7 = (f32[512,256]{1,0:T(8,128)S(1)}, f32[512,256]{1,0:T(8,128)}, u32[]{:S(2)}) copy-start(f32[512,256]{1,0:T(8,128)} %param.29) | copy-start | bytes 1572868
  7.2 10.9 %copy-start.16 = (f32[128,256]{1,0:T(8,128)S(1)}, f32[128,256]{1,0:T(8,128)}, u32[]{:S(2)}) copy-start(f32[128,256]{1,0:T(8,128)} %param.27) | copy-start | bytes 393220
  7.2 11.6 %copy-start.39 = (s32[2048]{0:T(1024)S(1)}, s32[2048]{0:T(1024)}, u32[]{:S(2)}) copy-start(s32[2048]{0:T(1024)} %param.21) | copy-start | bytes 24580
  7.2 11.5 %copy-start.28 = (s32[2048]{0:T(1024)S(1)}, s32[2048]{0:T(1024)}, u32[]{:S(2)}) copy-start(s32[2048]{0:T(1024)} %param.24) | copy-start | bytes 24580
  7.2 47.8 %all-gather.3.cloned.1.call-start = ((), (), s32[]{:S(2)}) async-start(), calls=%async_computation.1 | async-start | bytes 3276800 | tf_op jit(solution)/shard_map/all_gather | solution.py:1488
  9.6 233.4 %all-gather.5.cloned.1.call-start = ((), (), s32[]{:S(2)}) async-start(), calls=%async_computation.2 | async-start | bytes 13107200 | tf_op jit(solution)/shard_map/all_gather | solution.py:1537
  13.3 40.0 %collective-permute-start = (bf16[256,896]{1,0:T(8,128)(2,1)S(1)}, bf16[256,896]{1,0:T(8,128)(2,1)S(1)}, u32[]{:S(2)}, u32[]{:S(2)}) collective-permute-start(bf16[256,896]{1,0:T(8,128)(2,1)S(1)} %pad_maximum_fusion.2), channel_id=1, source_target_pairs={{0,4},{1,5},{2,6},{3,7},{4,0},{5,1},{6,2},{7,3},{8,12},{9,13},{10,... | collective-permute-start | bytes 1376264 | tf_op jit(solution)/shard_map/ppermute | solution.py:1476
  18.7 33.1 %collective-permute-start.1 = (bf16[640,256]{1,0:T(8,128)(2,1)S(1)}, bf16[640,256]{1,0:T(8,128)(2,1)S(1)}, u32[]{:S(2)}, u32[]{:S(2)}) collective-permute-start(bf16[640,256]{1,0:T(8,128)(2,1)S(1)} %pad_maximum_fusion.4), channel_id=1, source_target_pairs={{0,4},{1,5},{2,6},{3,7},{4,0},{5,1},{6,2},{7,3},{8,12},{9,13},{10,... | collective-permute-start | bytes 983048 | tf_op jit(solution)/shard_map/ppermute | solution.py:1476
  55.0 69.4 %copy-start.41 = (s32[2048]{0:T(1024)S(1)}, s32[2048]{0:T(1024)}, u32[]{:S(2)}) copy-start(s32[2048]{0:T(1024)} %param.23) | copy-start | bytes 24580
  55.0 69.6 %copy-start.38 = (s32[2048]{0:T(1024)S(1)}, s32[2048]{0:T(1024)}, u32[]{:S(2)}) copy-start(s32[2048]{0:T(1024)} %param.22) | copy-start | bytes 24580
  124.1 439.8 %reduce-scatter.2.cloned.1.call-start = ((), (), s32[]{:S(2)}) async-start(), calls=%async_computation.3 | async-start | bytes 16384000 | tf_op jit(solution)/shard_map/reduce_scatter | solution.py:1605
  125.1 4.5 copy-start.42
  129.6 12.4 %copy-start.2 = (bf16[1024,768]{1,0:T(8,128)(2,1)}, bf16[1024,768]{1,0:T(8,128)(2,1)S(1)}, u32[]{:S(2)}) copy-start(bf16[1024,768]{1,0:T(8,128)(2,1)S(1)} %convolution_convert_fusion.7.mixed_ref) | copy-start | bytes 4718596
  129.6 10.3 %copy-start.18 = (bf16[256,1024]{1,0:T(8,128)(2,1)S(1)}, bf16[256,1024]{1,0:T(8,128)(2,1)}, u32[]{:S(2)}) copy-start(bf16[256,1024]{1,0:T(8,128)(2,1)} %get-tuple-element.93) | copy-start | bytes 1572868
  139.2 0.8 copy-start
  142.0 34.2 %copy-start.50 = (bf16[1024,1024]{1,0:T(8,128)(2,1)S(1)}, bf16[1024,1024]{1,0:T(8,128)(2,1)}, u32[]{:S(2)}) copy-start(bf16[1024,1024]{1,0:T(8,128)(2,1)} %get-tuple-element.96) | copy-start | bytes 6291460
  176.2 4.2 copy-start.54
  180.4 4.0 copy-start.45
  292.4 8.4 %copy-start.23 = (f32[10,1,2048]{2,1,0:T(1,128)S(1)}, f32[10,1,2048]{2,1,0:T(1,128)}, u32[]{:S(2)}) copy-start(f32[10,1,2048]{2,1,0:T(1,128)} %get-tuple-element.121) | copy-start | bytes 245764
  292.4 9.3 %copy-start.13 = (f32[10,1,2048]{2,1,0:T(1,128)S(1)}, f32[10,1,2048]{2,1,0:T(1,128)}, u32[]{:S(2)}) copy-start(f32[10,1,2048]{2,1,0:T(1,128)} %get-tuple-element.101) | copy-start | bytes 245764
  301.7 0.7 copy-start.24
  336.2 0.7 copy-start.29
  337.5 69.4 %copy-start.46 = (f32[1024,1024]{1,0:T(8,128)S(1)}, f32[1024,1024]{1,0:T(8,128)}, u32[]{:S(2)}) copy-start(f32[1024,1024]{1,0:T(8,128)} %copy-done.45) | copy-start | bytes 12582916
  406.9 7.0 %copy-start.51 = (bf16[1024,1024]{1,0:T(8,128)(2,1)S(1)}, bf16[1024,1024]{1,0:T(8,128)(2,1)}, u32[]{:S(2)}) copy-start(bf16[1024,1024]{1,0:T(8,128)(2,1)} %get-tuple-element.96) | copy-start | bytes 6291460
  417.6 34.4 %copy-start.19 = (bf16[256,1024]{1,0:T(8,128)(2,1)S(1)}, bf16[256,1024]{1,0:T(8,128)(2,1)}, u32[]{:S(2)}) copy-start(bf16[256,1024]{1,0:T(8,128)(2,1)} %get-tuple-element.93) | copy-start | bytes 1572868
  452.1 2.5 copy-start.3
  454.5 17.4 %copy-start.1 = (bf16[1024,256]{1,0:T(8,128)(2,1)S(1)}, bf16[1024,256]{1,0:T(8,128)(2,1)}, u32[]{:S(2)}) copy-start(bf16[1024,256]{1,0:T(8,128)(2,1)} %copy-done) | copy-start | bytes 1572868
  454.6 17.4 %copy-start.10 = (bf16[1024,1024]{1,0:T(8,128)(2,1)S(1)}, bf16[1024,1024]{1,0:T(8,128)(2,1)}, u32[]{:S(2)}) copy-start(bf16[1024,1024]{1,0:T(8,128)(2,1)} %get-tuple-element.107) | copy-start | bytes 6291460
  454.6 18.9 %copy-start.49 = (bf16[1024,768]{1,0:T(8,128)(2,1)S(1)}, bf16[1024,768]{1,0:T(8,128)(2,1)}, u32[]{:S(2)}) copy-start(bf16[1024,768]{1,0:T(8,128)(2,1)} %get-tuple-element.90) | copy-start | bytes 4718596
  473.5 3.1 copy-start.48
  476.7 3.1 copy-start.52
  479.8 3.8 copy-start.47
  479.8 3.8 copy-start.53
  487.6 75.8 %copy-start.43 = (f32[4]{0:T(128)S(1)}, f32[4]{0:T(128)}, u32[]{:S(2)}) copy-start(f32[4]{0:T(128)} %get-tuple-element.152) | copy-start | bytes 52
  560.5 33.1 %collective-permute-start.3 = (bf16[256,896]{1,0:T(8,128)(2,1)}, bf16[256,896]{1,0:T(8,128)(2,1)S(1)}, u32[]{:S(2)}, u32[]{:S(2)}) collective-permute-start(bf16[256,896]{1,0:T(8,128)(2,1)} %get-tuple-element.110), channel_id=1, source_target_pairs={{0,4},{1,5},{2,6},{3,7},{4,0},{5,1},{6,2},{7,3},{8,12},{9,13},{10,... | collective-permute-start | bytes 1376264 | tf_op jit(solution)/shard_map/ppermute | solution.py:1680
  560.5 33.0 %collective-permute-start.2 = (bf16[640,256]{1,0:T(8,128)(2,1)}, bf16[640,256]{1,0:T(8,128)(2,1)S(1)}, u32[]{:S(2)}, u32[]{:S(2)}) collective-permute-start(bf16[640,256]{1,0:T(8,128)(2,1)} %get-tuple-element.109), channel_id=1, source_target_pairs={{0,4},{1,5},{2,6},{3,7},{4,0},{5,1},{6,2},{7,3},{8,12},{9,13},{10,... | collective-permute-start | bytes 983048 | tf_op jit(solution)/shard_map/ppermute | solution.py:1680
  577.5 16.0 %copy-start.15 = (f32[512,256]{1,0:T(8,128)S(1)}, f32[512,256]{1,0:T(8,128)}, u32[]{:S(2)}) copy-start(f32[512,256]{1,0:T(8,128)} %get-tuple-element.119) | copy-start | bytes 1572868
  577.5 16.8 %copy-start.22 = (f32[128,256]{1,0:T(8,128)S(1)}, f32[128,256]{1,0:T(8,128)}, u32[]{:S(2)}) copy-start(f32[128,256]{1,0:T(8,128)} %get-tuple-element.116) | copy-start | bytes 393220
  577.5 17.5 %copy-start.14 = (f32[256,512]{1,0:T(8,128)S(1)}, f32[256,512]{1,0:T(8,128)}, u32[]{:S(2)}) copy-start(f32[256,512]{1,0:T(8,128)} %get-tuple-element.118) | copy-start | bytes 1572868
  577.5 18.2 %copy-start.20 = (f32[256,384]{1,0:T(8,128)S(1)}, f32[256,384]{1,0:T(8,128)}, u32[]{:S(2)}) copy-start(f32[256,384]{1,0:T(8,128)} %get-tuple-element.114) | copy-start | bytes 1179652
  594.3 40.6 %copy-start.4 = (f32[512,256]{1,0:T(8,128)}, f32[512,256]{1,0:T(8,128)S(1)}, u32[]{:S(2)}) copy-start(f32[512,256]{1,0:T(8,128)S(1)} %get-tuple-element.231) | copy-start | bytes 1572868
  595.0 44.4 %copy-start.12 = (f32[128,256]{1,0:T(8,128)}, f32[128,256]{1,0:T(8,128)S(1)}, u32[]{:S(2)}) copy-start(f32[128,256]{1,0:T(8,128)S(1)} %get-tuple-element.223) | copy-start | bytes 393220
  595.7 41.4 %copy-start.5 = (f32[256,512]{1,0:T(8,128)}, f32[256,512]{1,0:T(8,128)S(1)}, u32[]{:S(2)}) copy-start(f32[256,512]{1,0:T(8,128)S(1)} %get-tuple-element.227) | copy-start | bytes 1572868
  596.5 45.0 %copy-start.6 = (f32[256,384]{1,0:T(8,128)}, f32[256,384]{1,0:T(8,128)S(1)}, u32[]{:S(2)}) copy-start(f32[256,384]{1,0:T(8,128)S(1)} %get-tuple-element.219) | copy-start | bytes 1179652
  609.9 7.0 %copy-start.30 = (f32[4,128]{1,0:T(4,128)S(1)}, f32[4,128]{1,0:T(4,128)}, u32[]{:S(2)}) copy-start(f32[4,128]{1,0:T(4,128)} %get-tuple-element.135) | copy-start | bytes 6148
  609.9 6.9 %copy-start.33 = (f32[2,128]{1,0:T(2,128)S(1)}, f32[2,128]{1,0:T(2,128)}, u32[]{:S(2)}) copy-start(f32[2,128]{1,0:T(2,128)} %get-tuple-element.136) | copy-start | bytes 3076
  609.9 8.3 %copy-start.31 = (f32[4,128]{1,0:T(4,128)S(1)}, f32[4,128]{1,0:T(4,128)}, u32[]{:S(2)}) copy-start(f32[4,128]{1,0:T(4,128)} %get-tuple-element.134) | copy-start | bytes 6148
  609.9 8.3 %copy-start.34 = (f32[2,128]{1,0:T(2,128)S(1)}, f32[2,128]{1,0:T(2,128)}, u32[]{:S(2)}) copy-start(f32[2,128]{1,0:T(2,128)} %get-tuple-element.133) | copy-start | bytes 3076
  609.9 9.7 %copy-start.35 = (f32[2,128]{1,0:T(2,128)S(1)}, f32[2,128]{1,0:T(2,128)}, u32[]{:S(2)}) copy-start(f32[2,128]{1,0:T(2,128)} %get-tuple-element.132) | copy-start | bytes 3076
  609.9 9.7 %copy-start.40 = (f32[1,128]{1,0:T(1,128)S(1)}, f32[1,128]{1,0:T(1,128)}, u32[]{:S(2)}) copy-start(f32[1,128]{1,0:T(1,128)} %get-tuple-element.131) | copy-start | bytes 1540
  610.0 11.0 %copy-start.32 = (f32[3,128]{1,0:T(4,128)S(1)}, f32[3,128]{1,0:T(4,128)}, u32[]{:S(2)}) copy-start(f32[3,128]{1,0:T(4,128)} %get-tuple-element.130) | copy-start | bytes 4612
  610.0 11.0 %copy-start.36 = (f32[2,128]{1,0:T(2,128)S(1)}, f32[2,128]{1,0:T(2,128)}, u32[]{:S(2)}) copy-start(f32[2,128]{1,0:T(2,128)} %get-tuple-element.129) | copy-start | bytes 3076
  622.4 12.5 %copy-start.8 = (f32[512,256]{1,0:T(8,128)S(1)}, f32[512,256]{1,0:T(8,128)}, u32[]{:S(2)}) copy-start(f32[512,256]{1,0:T(8,128)} %param.29) | copy-start | bytes 1572868
  622.4 14.8 %copy-start.9 = (f32[256,512]{1,0:T(8,128)S(1)}, f32[256,512]{1,0:T(8,128)}, u32[]{:S(2)}) copy-start(f32[256,512]{1,0:T(8,128)} %param.28) | copy-start | bytes 1572868
  622.4 17.0 %copy-start.17 = (f32[128,256]{1,0:T(8,128)S(1)}, f32[128,256]{1,0:T(8,128)}, u32[]{:S(2)}) copy-start(f32[128,256]{1,0:T(8,128)} %param.27) | copy-start | bytes 393220
  622.4 19.1 %copy-start.11 = (f32[256,384]{1,0:T(8,128)S(1)}, f32[256,384]{1,0:T(8,128)}, u32[]{:S(2)}) copy-start(f32[256,384]{1,0:T(8,128)} %param.26) | copy-start | bytes 1179652
  633.5 10.2 %copy-start.21 = (f32[50,128]{1,0:T(8,128)S(1)}, f32[50,128]{1,0:T(8,128)}, u32[]{:S(2)}) copy-start(f32[50,128]{1,0:T(8,128)} %get-tuple-element.126) | copy-start | bytes 76804
  633.5 10.2 %copy-start.37 = (f32[2,128]{1,0:T(2,128)S(1)}, f32[2,128]{1,0:T(2,128)}, u32[]{:S(2)}) copy-start(f32[2,128]{1,0:T(2,128)} %get-tuple-element.127) | copy-start | bytes 3076
  643.7 9.1 %copy-start.44 = (f32[1,128]{1,0:T(1,128)S(1)}, f32[1,128]{1,0:T(1,128)}, u32[]{:S(2)}) copy-start(f32[1,128]{1,0:T(1,128)} %get-tuple-element.125) | copy-start | bytes 1540
  643.7 15.3 %copy-start.27 = (f32[6,1024]{1,0:T(8,128)S(1)}, f32[6,1024]{1,0:T(8,128)}, u32[]{:S(2)}) copy-start(f32[6,1024]{1,0:T(8,128)} %get-tuple-element.235) | copy-start | bytes 73732
  643.7 15.9 %copy-start.26 = (f32[6,1024]{1,0:T(8,128)S(1)}, f32[6,1024]{1,0:T(8,128)}, u32[]{:S(2)}) copy-start(f32[6,1024]{1,0:T(8,128)} %get-tuple-element.236) | copy-start | bytes 73732
  643.7 16.5 %copy-start.25 = (f32[6,1024]{1,0:T(8,128)S(1)}, f32[6,1024]{1,0:T(8,128)}, u32[]{:S(2)}) copy-start(f32[6,1024]{1,0:T(8,128)} %get-tuple-element.237) | copy-start | bytes 73732
Sparse Core Ops, SparseCore 0:
  9.9 43.5 all-gather.2
  124.2 108.4 all-gather.4
  336.3 124.5 reduce-scatter.1
